TPU v7x, 128 devices: a whole 4x4x4 slice. The times are simulated.
128 devices in a mesh: slab: 32 (over z_lo, y, x), col: 4 (over z_hi, core).
Axes of the slice: x: 4, y: 4, z: 4 (z_hi: 2, z_lo: 2; z = z_hi * 2 + z_lo), core: 2. Of those that a mesh axis runs over, the one named last changes fastest.
Arguments:
- hamiltonian_blocks: bfloat16 [512, 9, 128, 128], P('slab'), may hold values from -0.0625 to 0.0625
- block_columns: int32 [512, 9], P('slab'), may hold values from 0 to 511, as said below
- probe: bfloat16 [65536, 2048], P('slab', 'col'), may hold values from -6 to 6
- previous: float32 [65536, 2048], P('slab', 'col'), may hold values from -6 to 6
- current: float32 [65536, 2048], P('slab', 'col'), may hold values from -6 to 6
- orbital_weight: float32 [65536], P('slab'), may hold values from 0.1 to 10
Outputs:
- last_previous: float32 [65536, 2048], P('slab', 'col')
- last_current: float32 [65536, 2048], P('slab', 'col')
- moments: float32 [3, 2048], P(None, 'col')
Inputs may be any that keep to these rules, and one draw needn't show every extreme that they name: `block_columns`: the 9 entries of a row are distinct block columns within 5 of the row's own block row, counted cyclically modulo 512; they include the row itself and the block rows 5 before and 5 after it.
All inputs are finite; a program needn't handle non-finite values.
Results may differ from a plain program's by a relative error of at most 0.0024.
Values may be sent and summed in bfloat16 or wider, within the bound.
No kernel may reach another device: no remote copies, remote signals or barrier semaphores. Data moves between devices by JAX's collectives and lax.ppermute only.
A program may use at most 192 MiB of HBM per device.

v0:
```python
import functools
import jax
import jax.numpy as jnp
from jax import lax
from jax.experimental import pallas as pl
from jax.experimental.pallas import tpu as pltpu
from jax.sharding import PartitionSpec as P

BAND = 5
TERMS = 3
CHUNKS = 2
F32 = jnp.float32
BF16 = jnp.bfloat16
VMEM = pl.BlockSpec(memory_space=pltpu.VMEM)
SMEM = pl.BlockSpec(memory_space=pltpu.SMEM)
HBM = pl.BlockSpec(memory_space=pltpu.HBM)


def params(**more):
    return pltpu.CompilerParams(vmem_limit_bytes=12 * 1024 * 1024, **more)


def cost(flops, moved):
    return pl.CostEstimate(flops=flops, bytes_accessed=moved, transcendentals=0)


def edge_kernel(first, cols, rim, _, current, low, high, held, sems):
    rows = current.shape[0]
    copies = [
        pltpu.make_async_copy(
            current.at[pl.ds(start, rim), pl.ds(first, cols)], held.at[side], sems.at[side]
        )
        for side, start in enumerate((0, rows - rim))
    ]
    for copy in copies:
        copy.start()
    for side, out in enumerate((low, high)):
        copies[side].wait()
        out[...] = held[side].astype(BF16)


def band_kernel(_, places, blocks, banded, held, sems):
    rows_blk, slots, width, _ = blocks.shape

    def fetch(pair):
        two = pl.ds(2 * pair, 2)
        return pltpu.make_async_copy(blocks.at[two], held.at[two], sems.at[pair])

    for pair in range(rows_blk // 2):
        fetch(pair).start()

    def one_pair(pair, _):
        banded[pair] = jnp.zeros(banded.shape[1:], BF16)
        fetch(pair).wait()
        for half in range(2):
            row = 2 * pair + half
            for slot in range(slots):
                at = pl.multiple_of((places[row, slot] + half) * width, width)
                banded[pair, pl.ds(half * width, width), pl.ds(at, width)] = held[row, slot]
        return 0

    lax.fori_loop(0, rows_blk // 2, one_pair, 0)


def weight_kernel(scale, _, orbital, probe, weights):
    lanes = orbital.shape[1]
    for block in range(orbital.shape[0]):
        here = pl.ds(block * lanes, lanes)
        column = jnp.broadcast_to(orbital[block : block + 1, :] * scale, (lanes, lanes)).T
        for j in range(probe.shape[1] // lanes):
            there = pl.ds(j * lanes, lanes)
            weights[here, there] = column * probe[here, there].astype(F32)


def fold(x):
    return jnp.sum(x.reshape(-1, 8, x.shape[-1]), axis=0)


def middle_kernel(sources, first, cols, width, rows_blk, _, banded, weights, *refs):
    source, previous = refs[:sources], refs[sources]
    upcoming, *inner, partial, x = refs[sources + 1 + (first > 0) :]
    columns = pl.ds(first, cols)
    rim = BAND * width
    rows = rows_blk * width
    if sources == 1:
        x[...] = source[0][:, columns].astype(BF16)
    else:
        x[0:rim] = source[0][...]
        x[rim : rows - rim] = source[1][...]
        x[rows - rim : rows] = source[2][...]
    total = jnp.zeros((8, cols), F32)
    for pair in range(rows_blk // 2):
        start = 2 * pair - BAND
        low, high = max(start, 0), min(start + 2 * BAND + 2, rows_blk)
        product = jnp.dot(
            banded[pair, :, (low - start) * width : (high - start) * width],
            x[low * width : high * width],
            preferred_element_type=F32,
        )
        here = pl.ds(2 * pair * width, 2 * width)
        result = 2.0 * product - previous[here, columns]
        upcoming[here, columns] = result
        a = max(2 * pair, BAND)
        b = min(2 * pair + 2, rows_blk - BAND)
        if a < b:
            piece = result[(a - 2 * pair) * width : (b - 2 * pair) * width]
            for out in inner:
                out[(a - BAND) * width : (b - BAND) * width] = piece.astype(BF16)
            total = total + fold(piece * weights[a * width : b * width, columns])
    partial[...] = total


def rim_parts(rows_blk):
    parts = []
    for pair in range(rows_blk // 2):
        start = 2 * pair - BAND
        if 2 * pair < BAND:
            parts.append((0, pair, 0, min(2, BAND - 2 * pair), 0, -start, BAND + start))
    for pair in range(rows_blk // 2):
        start = 2 * pair - BAND
        first = max(2 * pair, rows_blk - BAND)
        if first < 2 * pair + 2:
            parts.append((1, pair, first - 2 * pair, 2, rows_blk - start, 2 * BAND + 2, 0))
    return parts


def rim_kernel(kind, first, cols, width, rows_blk, _, banded, weights, low, high, begun, partial, *refs):
    halos = (low, high)
    earlier = refs[: TERMS * CHUNKS - 1] if kind == "final" else ()
    upcoming, *edges, moments = refs[len(earlier) :]
    columns = pl.ds(first, cols)
    rim = BAND * width
    rows = rows_blk * width
    total = partial[...]
    for side, pair, a, b, left, right, at in rim_parts(rows_blk):
        product = jnp.dot(
            banded[pair, a * width : b * width, left * width : right * width],
            halos[side][at * width : (at + right - left) * width],
            preferred_element_type=F32,
        )
        top = (2 * pair + a) * width
        here = pl.ds(top, (b - a) * width)
        result = begun[here, columns] + 2.0 * product
        upcoming[here, columns] = result
        if edges:
            base = top - (0 if side == 0 else rows - rim)
            edges[side][base : base + (b - a) * width] = result.astype(BF16)
        total = total + fold(result * weights[here, columns])
    if kind == "final":
        lanes = moments.shape[2]
        parts = []
        for one in [*(ref[...] for ref in earlier), total]:
            one = jnp.sum(one, axis=0, keepdims=True)
            parts += [one[:, j * lanes : (j + 1) * lanes] for j in range(cols // lanes)]
        moments[...] = jnp.broadcast_to(jnp.concatenate(parts, axis=0)[None], moments.shape)
    else:
        moments[...] = total


def copies_of(parts, source, target, sems):
    copies = [
        pltpu.make_async_copy(source.at[part], target.at[part], sems.at[i])
        for i, part in enumerate(parts)
    ]
    for copy in copies:
        copy.start()
    return copies


def store_kernel(rim, cols, _, previous, current, out_previous, out_current, done, whole_sem, sems):
    rows, all_cols = current.shape
    held = all_cols - cols
    parts = [
        (pl.ds(0, rows), pl.ds(0, held)),
        (pl.ds(rim, rows - 2 * rim), pl.ds(held, cols)),
    ]
    copies = copies_of(parts, current, out_current, sems)
    copies += copies_of([pl.ds(0, rows)], previous, out_previous, whole_sem)
    done[...] = jnp.zeros(done.shape, F32)
    for copy in copies:
        copy.wait()


def sum_kernel(rim, cols, parts, current, _, out, out_current, sems):
    rows, all_cols = current.shape
    columns = pl.ds(all_cols - cols, cols)
    rims = [(pl.ds(0, rim), columns), (pl.ds(rows - rim, rim), columns)]
    copies = copies_of(rims, current, out_current, sems)
    lanes = parts.shape[2]
    total = jnp.sum(parts[...], axis=0)
    each = out.shape[1] // lanes
    for term in range(out.shape[0]):
        for j in range(each):
            out[term : term + 1, j * lanes : (j + 1) * lanes] = total[term * each + j][None]
    for copy in copies:
        copy.wait()


def in_hbm(x):
    return pltpu.with_memory_space_constraint(x, pltpu.HBM)


def local(hamiltonian_blocks, block_columns, probe, previous, current, orbital_weight):
    rows_blk, slots, width, _ = hamiltonian_blocks.shape
    rows, all_cols = current.shape
    cols = all_cols // CHUNKS
    rim = BAND * width
    slabs = lax.axis_size("slab")
    total_blocks = rows_blk * slabs
    onward = [(i, (i + 1) % slabs) for i in range(slabs)]
    backward = [(target, source) for source, target in onward]
    shape = jax.ShapeDtypeStruct
    edge_shape = shape((rim, cols), BF16)
    full_shape = shape((rows, all_cols), F32)
    part_shape = shape((8, cols), F32)
    flops = 2 * rows * cols * 9 * width

    def exchange(low, high):
        return lax.ppermute(high, "slab", onward), lax.ppermute(low, "slab", backward)

    def edges(token, chunk):
        return pl.pallas_call(
            functools.partial(edge_kernel, chunk * cols, cols, rim),
            out_shape=(edge_shape, edge_shape),
            in_specs=[VMEM, HBM],
            out_specs=(VMEM, VMEM),
            scratch_shapes=[pltpu.VMEM((2, rim, cols), F32), pltpu.SemaphoreType.DMA((2,))],
            compiler_params=params(),
            cost_estimate=cost(0, 6 * 2 * rim * cols),
            name="edges",
        )(token, in_hbm(current))

    def middle(token, term, chunk):
        args = [token, banded, weights, *sources[chunk], terms[term]]
        aliases = {}
        if chunk:
            aliases = {len(args): 0}
            args.append(terms[term + 2])
        outs = (full_shape, shape((rows - 2 * rim, cols), BF16), part_shape)
        if term == TERMS - 1:
            outs = (full_shape, part_shape)
        return pl.pallas_call(
            functools.partial(
                middle_kernel, len(sources[chunk]), chunk * cols, cols, width, rows_blk
            ),
            out_shape=outs,
            in_specs=[VMEM] * len(args),
            out_specs=(VMEM,) * len(outs),
            scratch_shapes=[pltpu.VMEM((rows, cols), BF16)],
            input_output_aliases=aliases,
            compiler_params=params(),
            cost_estimate=cost(flops, 8 * 1024 * 1024),
            name="middle",
        )(*args)

    def rims(token, term, chunk):
        args = [token, banded, weights, *halos[chunk], terms[term + 2], begun[chunk][-1]]
        kind = "inner"
        outs = (full_shape, edge_shape, edge_shape, part_shape)
        if term == TERMS - 1:
            kind = "last"
            outs = (full_shape, part_shape)
            if chunk == CHUNKS - 1:
                kind = "final"
                args += sums
                outs = (full_shape, shape((slabs, TERMS * all_cols // 128, 128), F32))
        return pl.pallas_call(
            functools.partial(rim_kernel, kind, chunk * cols, cols, width, rows_blk),
            out_shape=outs,
            in_specs=[VMEM] * len(args),
            out_specs=(VMEM,) * len(outs),
            input_output_aliases={5: 0},
            compiler_params=params(),
            cost_estimate=cost(flops // 5, 2 * 1024 * 1024),
            name="rims",
        )(*args)

    first_row = lax.axis_index("slab") * rows_blk
    own_row = first_row + jnp.arange(rows_blk, dtype=jnp.int32)[:, None]
    places = (block_columns - own_row + BAND + total_blocks) % total_blocks
    pairs = rows_blk // 2

    halos = [None] * CHUNKS
    opening = edges(jnp.zeros((8, 128), F32), 0)
    halos[0] = exchange(*opening)
    banded = pl.pallas_call(
        band_kernel,
        out_shape=shape((pairs, 2 * width, (2 * BAND + 2) * width), BF16),
        in_specs=[VMEM, SMEM, HBM],
        out_specs=VMEM,
        scratch_shapes=[
            pltpu.VMEM(hamiltonian_blocks.shape, BF16),
            pltpu.SemaphoreType.DMA((pairs,)),
        ],
        compiler_params=params(),
        cost_estimate=cost(0, 12 * 1024 * 1024),
        name="band",
    )(opening[0], places, in_hbm(hamiltonian_blocks))
    token = banded
    for chunk in range(1, CHUNKS):
        opening = edges(token, chunk)
        halos[chunk] = exchange(*opening)
        token = opening[0]
    weights = pl.pallas_call(
        functools.partial(weight_kernel, 1.0 / (total_blocks * width)),
        out_shape=full_shape,
        in_specs=[VMEM] * 3,
        out_specs=VMEM,
        compiler_params=params(),
        cost_estimate=cost(0, 4 * 1024 * 1024),
        name="weights",
    )(token, orbital_weight.reshape(rows_blk, width), probe)

    terms = [previous, current] + [None] * TERMS
    sources = [(current,)] * CHUNKS
    begun = [None] * CHUNKS
    sums = []
    order = [(term, chunk) for term in range(TERMS) for chunk in range(CHUNKS)]

    def begin(token, term, chunk):
        terms[term + 2], *begun[chunk] = middle(token, term, chunk)
        return begun[chunk][-1]

    token = begin(weights, *order[0])
    for step, (term, chunk) in enumerate(order):
        terms[term + 2], *sent, token = rims(token, term, chunk)
        if sent:
            halos[chunk] = exchange(*sent)
            sources[chunk] = (sent[0], begun[chunk][0], sent[1])
        sums.append(token)
        if step + 1 < len(order):
            token = begin(token, *order[step + 1])
        if step + 2 == len(order):
            last_previous, last_current, token = pl.pallas_call(
                functools.partial(store_kernel, rim, cols),
                out_shape=(full_shape, full_shape, shape((8, 128), F32)),
                in_specs=[VMEM] * 3,
                out_specs=(HBM, HBM, VMEM),
                scratch_shapes=[pltpu.SemaphoreType.DMA((1,)), pltpu.SemaphoreType.DMA((2,))],
                compiler_params=params(),
                cost_estimate=cost(0, 16 * 1024 * 1024),
                name="store",
            )(token, terms[-2], terms[-1])
    gathered = lax.all_to_all(sums[-1], "slab", 0, 0)
    moments, last_current = pl.pallas_call(
        functools.partial(sum_kernel, rim, cols),
        out_shape=(shape((TERMS, all_cols), F32), full_shape),
        in_specs=[VMEM, VMEM, HBM],
        out_specs=(VMEM, HBM),
        scratch_shapes=[pltpu.SemaphoreType.DMA((2,))],
        input_output_aliases={2: 1},
        compiler_params=params(),
        name="sums",
    )(gathered, terms[-1], last_current)
    return last_previous, last_current, moments


def solution(mesh):
    return jax.shard_map(
        local,
        mesh=mesh,
        in_specs=(
            P("slab", None, None, None),
            P("slab", None),
            P("slab", "col"),
            P("slab", "col"),
            P("slab", "col"),
            P("slab"),
        ),
        out_specs=(P("slab", "col"), P("slab", "col"), P(None, "col")),
        check_vma=False,
    )
```

profile of v0, /device:TPU:0, one launch (start us, length us, event | category | flops | bytes accessed | tf_op | source)
XLA Modules:
  0.0 83.6 jit_solution(16659310353893854273)
XLA Ops:
  0.7 1.3 %edges.2 = (bf16[640,256]{1,0:T(8,128)(2,1)S(1)}, bf16[640,256]{1,0:T(8,128)(2,1)S(1)}) custom-call(f32[8,128]{1,0:T(8,128)S(1)} %broadcast_in_dim.4._, f32[2048,512]{1,0:T(8,128)} %refs_3_.3), custom_call_target="tpu_custom_call" | custom-call | bytes 1966080 | tf_op jit(solution)/shard_map/edges/pallas_call | solution.py:222
  2.0 6.7 %collective-permute-start.1 = (bf16[640,256]{1,0:T(8,128)(2,1)S(1)}, bf16[640,256]{1,0:T(8,128)(2,1)S(1)}, u32[]{:S(2)}, u32[]{:S(2)}) collective-permute-start(bf16[640,256]{1,0:T(8,128)(2,1)S(1)} %get-tuple-element.48._), channel_id=1, source_target_pairs={{4,0},{8,4},{12,8},{16,12},{20,16},{24,20},{28,24},{32,28},{36,32}... | collective-permute-start | bytes 983048 | tf_op jit(solution)/shard_map/ppermute | solution.py:219
  8.7 0.1 add_select_fusion.places
  8.8 3.2 %band.1._.banded = bf16[8,256,1536]{2,1,0:T(8,128)(2,1)S(1)} custom-call(bf16[640,256]{1,0:T(8,128)(2,1)S(1)} %get-tuple-element.48._, s32[16,9]{1,0:T(8,128)S(1)} %add_select_fusion.places, bf16[16,9,128,128]{3,2,1,0:T(8,128)(2,1)} %blocks.1), custom_call_target="tpu_custom_call" | custom-call | bytes 12582912 | tf_op jit(solution)/shard_map/band/pallas_call | solution.py:286
  12.0 1.5 %edges.3 = (bf16[640,256]{1,0:T(8,128)(2,1)S(1)}, bf16[640,256]{1,0:T(8,128)(2,1)S(1)}) custom-call(bf16[8,256,1536]{2,1,0:T(8,128)(2,1)S(1)} %band.1._.banded, f32[2048,512]{1,0:T(8,128)} %refs_3_.3), custom_call_target="tpu_custom_call" | custom-call | bytes 1966080 | tf_op jit(solution)/shard_map/edges/pallas_call | solution.py:222
  13.5 6.3 %collective-permute-start.3 = (bf16[640,256]{1,0:T(8,128)(2,1)S(1)}, bf16[640,256]{1,0:T(8,128)(2,1)S(1)}, u32[]{:S(2)}, u32[]{:S(2)}) collective-permute-start(bf16[640,256]{1,0:T(8,128)(2,1)S(1)} %get-tuple-element.49._), channel_id=1, source_target_pairs={{4,0},{8,4},{12,8},{16,12},{20,16},{24,20},{28,24},{32,28},{36,32}... | collective-permute-start | bytes 983048 | tf_op jit(solution)/shard_map/ppermute | solution.py:219
  19.8 0.3 weights.1._
  20.2 1.6 %middle.6 = (f32[2048,512]{1,0:T(8,128)S(1)}, bf16[768,256]{1,0:T(8,128)(2,1)S(1)}, f32[8,256]{1,0:T(8,128)S(1)}) custom-call(f32[2048,512]{1,0:T(8,128)S(1)} %weights.1._, bf16[8,256,1536]{2,1,0:T(8,128)(2,1)S(1)} %band.1._.banded, f32[2048,512]{1,0:T(8,128)S(1)} %weights.1._, f32[2048,512]{1,0:T(8,128)S(1)} %copy-done, f32[2048,512]{1,0:T(8,128)S(1)} %copy-done.1), custom_call_target="tpu_custom_call" | custom-call | flops 1207959552 | bytes 8388608 | tf_op jit(solution)/shard_map/middle/pallas_call | solution.py:242
  21.8 0.3 collective-permute-done.low
  22.1 0.8 rims.6
  22.9 0.1 collective-permute-start.4
  22.9 6.2 %collective-permute-start.5 = (bf16[640,256]{1,0:T(8,128)(2,1)S(1)}, bf16[640,256]{1,0:T(8,128)(2,1)S(1)}, u32[]{:S(2)}, u32[]{:S(2)}) collective-permute-start(bf16[640,256]{1,0:T(8,128)(2,1)S(1)} %get-tuple-element.59.refs_0_), channel_id=1, source_target_pairs={{4,0},{8,4},{12,8},{16,12},{20,16},{24,20},{28,24},{32,28},{36,32}... | collective-permute-start | bytes 983048 | tf_op jit(solution)/shard_map/ppermute | solution.py:219
  29.2 1.6 %middle.7 = (f32[2048,512]{1,0:T(8,128)S(1)}, bf16[768,256]{1,0:T(8,128)(2,1)S(1)}, f32[8,256]{1,0:T(8,128)S(1)}) custom-call(f32[8,256]{1,0:T(8,128)S(1)} %get-tuple-element.53._.refs_0_, bf16[8,256,1536]{2,1,0:T(8,128)(2,1)S(1)} %band.1._.banded, f32[2048,512]{1,0:T(8,128)S(1)} %weights.1._, ...), custom_call_target="tpu_custom_call", output_to_operand_aliasing={{0}: (5, {})} | custom-call | flops 1207959552 | bytes 8388608 | tf_op jit(solution)/shard_map/middle/pallas_call | solution.py:242
  30.8 3.9 %collective-permute-done.2.low = bf16[640,256]{1,0:T(8,128)(2,1)S(1)} collective-permute-done((bf16[640,256]{1,0:T(8,128)(2,1)S(1)}, bf16[640,256]{1,0:T(8,128)(2,1)S(1)}, u32[]{:S(2)}, u32[]{:S(2)}) %collective-permute-start.2) | collective-permute-done | bytes 327712 | tf_op jit(solution)/shard_map/ppermute | solution.py:219
  34.7 0.8 rims.7
  35.5 0.1 collective-permute-start.6
  35.5 6.2 %collective-permute-start.7 = (bf16[640,256]{1,0:T(8,128)(2,1)S(1)}, bf16[640,256]{1,0:T(8,128)(2,1)S(1)}, u32[]{:S(2)}, u32[]{:S(2)}) collective-permute-start(bf16[640,256]{1,0:T(8,128)(2,1)S(1)} %get-tuple-element.65.refs_0_), channel_id=1, source_target_pairs={{4,0},{8,4},{12,8},{16,12},{20,16},{24,20},{28,24},{32,28},{36,32}... | collective-permute-start | bytes 983048 | tf_op jit(solution)/shard_map/ppermute | solution.py:219
  41.8 1.6 %middle.8 = (f32[2048,512]{1,0:T(8,128)S(1)}, bf16[768,256]{1,0:T(8,128)(2,1)S(1)}, f32[8,256]{1,0:T(8,128)S(1)}) custom-call(f32[8,256]{1,0:T(8,128)S(1)} %get-tuple-element.58._.refs_1_, bf16[8,256,1536]{2,1,0:T(8,128)(2,1)S(1)} %band.1._.banded, f32[2048,512]{1,0:T(8,128)S(1)} %weights.1._, bf16[640,256]{1,0:T(8,128)(2,1)S(1)} %get-tuple-element.59.refs_0_, ...), custom_call_target="tpu_custom_call" | custom-call | flops 1207959552 | bytes 8388608 | tf_op jit(solution)/shard_map/middle/pallas_call | solution.py:242
  43.4 0.8 rims.8
  44.2 0.1 collective-permute-start.8
  44.2 6.2 %collective-permute-start.9 = (bf16[640,256]{1,0:T(8,128)(2,1)S(1)}, bf16[640,256]{1,0:T(8,128)(2,1)S(1)}, u32[]{:S(2)}, u32[]{:S(2)}) collective-permute-start(bf16[640,256]{1,0:T(8,128)(2,1)S(1)} %get-tuple-element.72.refs_0_), channel_id=1, source_target_pairs={{4,0},{8,4},{12,8},{16,12},{20,16},{24,20},{28,24},{32,28},{36,32}... | collective-permute-start | bytes 983048 | tf_op jit(solution)/shard_map/ppermute | solution.py:219
  50.5 1.6 %middle.9 = (f32[2048,512]{1,0:T(8,128)S(1)}, bf16[768,256]{1,0:T(8,128)(2,1)S(1)}, f32[8,256]{1,0:T(8,128)S(1)}) custom-call(f32[8,256]{1,0:T(8,128)S(1)} %get-tuple-element.64._.refs_2_, bf16[8,256,1536]{2,1,0:T(8,128)(2,1)S(1)} %band.1._.banded, f32[2048,512]{1,0:T(8,128)S(1)} %weights.1._, ...), custom_call_target="tpu_custom_call", output_to_operand_aliasing={{0}: (7, {})} | custom-call | flops 1207959552 | bytes 8388608 | tf_op jit(solution)/shard_map/middle/pallas_call | solution.py:242
  52.1 0.8 rims.9
  52.9 0.3 collective-permute-start.10
  53.1 6.2 %collective-permute-start.11 = (bf16[640,256]{1,0:T(8,128)(2,1)S(1)}, bf16[640,256]{1,0:T(8,128)(2,1)S(1)}, u32[]{:S(2)}, u32[]{:S(2)}) collective-permute-start(bf16[640,256]{1,0:T(8,128)(2,1)S(1)} %get-tuple-element.79.refs_0_), channel_id=1, source_target_pairs={{4,0},{8,4},{12,8},{16,12},{20,16},{24,20},{28,24},{32,28},{36,32}... | collective-permute-start | bytes 983048 | tf_op jit(solution)/shard_map/ppermute | solution.py:219
  59.4 1.6 %middle.10 = (f32[2048,512]{1,0:T(8,128)S(1)}, f32[8,256]{1,0:T(8,128)S(1)}) custom-call(f32[8,256]{1,0:T(8,128)S(1)} %get-tuple-element.71._.refs_3_, bf16[8,256,1536]{2,1,0:T(8,128)(2,1)S(1)} %band.1._.banded, f32[2048,512]{1,0:T(8,128)S(1)} %weights.1._, bf16[640,256]{1,0:T(8,128)(2,1)S(1)} %get-tuple-element.72.refs_0_, ...), custom_call_target="tpu_custom_call" | custom-call | flops 1207959552 | bytes 8388608 | tf_op jit(solution)/shard_map/middle/pallas_call | solution.py:242
  61.0 0.7 rims.10
  61.7 1.6 %middle.11 = (f32[2048,512]{1,0:T(8,128)S(1)}, f32[8,256]{1,0:T(8,128)S(1)}) custom-call(f32[8,256]{1,0:T(8,128)S(1)} %get-tuple-element.78._.refs_4_, bf16[8,256,1536]{2,1,0:T(8,128)(2,1)S(1)} %band.1._.banded, f32[2048,512]{1,0:T(8,128)S(1)} %weights.1._, bf16[640,256]{1,0:T(8,128)(2,1)S(1)} %get-tuple-element.79.refs_0_, ...), custom_call_target="tpu_custom_call", output_to_operand_aliasing={{0}: (7, {})} | custom-call | flops 1207959552 | bytes 8388608 | tf_op jit(solution)/shard_map/middle/pallas_call | solution.py:242
  63.3 3.0 %store.1 = (f32[2048,512]{1,0:T(8,128)}, f32[2048,512]{1,0:T(8,128)}, f32[8,128]{1,0:T(8,128)S(1)}) custom-call(f32[8,256]{1,0:T(8,128)S(1)} %get-tuple-element.83._.partial, f32[2048,512]{1,0:T(8,128)S(1)} %get-tuple-element.84.previous, f32[2048,512]{1,0:T(8,128)S(1)} %get-tuple-element.85.current.begun), custom_call_target="tpu_custom_call" | custom-call | bytes 16777216 | tf_op jit(solution)/shard_map/store/pallas_call | solution.py:334
  66.3 0.7 rims.11
  67.0 14.7 %all_to_all.5.parts = f32[32,12,128]{2,1,0:T(8,128)S(1)} all-to-all(f32[32,12,128]{2,1,0:T(8,128)S(1)} %get-tuple-element.88), channel_id=1, replica_groups=mesh['slab'=32,'col'=4] {'slab'}, dimensions={0} | all-to-all | bytes 393216 | tf_op jit(solution)/shard_map/all_to_all | solution.py:344
  81.8 1.7 %sums.1 = (f32[3,512]{1,0:T(4,128)}, f32[2048,512]{1,0:T(8,128)}) custom-call(f32[32,12,128]{2,1,0:T(8,128)S(1)} %all_to_all.5.parts, f32[2048,512]{1,0:T(8,128)S(1)} %get-tuple-element.89.current, f32[2048,512]{1,0:T(8,128)} %get-tuple-element.90._), custom_call_target="tpu_custom_call", output_to_operand_aliasing={{1}: (2, {})} | custom-call | tf_op jit(solution)/shard_map/sums/pallas_call | solution.py:345
  (24 shorter events, 0.1 us)
Async XLA Ops:
  0.6 8.1 %copy-start.4 = (s32[16,9]{1,0:T(8,128)S(1)}, s32[16,9]{1,0:T(8,128)}, u32[]{:S(2)}) copy-start(s32[16,9]{1,0:T(8,128)} %param.7) | copy-start | bytes 1732
  2.0 19.8 %collective-permute-start.1 = (bf16[640,256]{1,0:T(8,128)(2,1)S(1)}, bf16[640,256]{1,0:T(8,128)(2,1)S(1)}, u32[]{:S(2)}, u32[]{:S(2)}) collective-permute-start(bf16[640,256]{1,0:T(8,128)(2,1)S(1)} %get-tuple-element.48._), channel_id=1, source_target_pairs={{4,0},{8,4},{12,8},{16,12},{20,16},{24,20},{28,24},{32,28},{36,32}... | collective-permute-start | bytes 983048 | tf_op jit(solution)/shard_map/ppermute | solution.py:219
  8.7 13.4 %collective-permute-start = (bf16[640,256]{1,0:T(8,128)(2,1)S(1)}, bf16[640,256]{1,0:T(8,128)(2,1)S(1)}, u32[]{:S(2)}, u32[]{:S(2)}) collective-permute-start(bf16[640,256]{1,0:T(8,128)(2,1)S(1)} %get-tuple-element.51), channel_id=1, source_target_pairs={{0,4},{4,8},{8,12},{12,16},{16,20},{20,24},{24,28},{28,32},{32,36}... | collective-permute-start | bytes 983048 | tf_op jit(solution)/shard_map/ppermute | solution.py:219
  12.0 7.9 %copy-start.2 = (bf16[2048,512]{1,0:T(8,128)(2,1)S(1)}, bf16[2048,512]{1,0:T(8,128)(2,1)}, u32[]{:S(2)}) copy-start(bf16[2048,512]{1,0:T(8,128)(2,1)} %probe.1) | copy-start | bytes 6291460
  12.0 7.8 %copy-start.3 = (f32[2048]{0:T(1024)S(1)}, f32[2048]{0:T(1024)}, u32[]{:S(2)}) copy-start(f32[2048]{0:T(1024)} %param.11) | copy-start | bytes 24580
  12.0 8.2 %copy-start.1 = (f32[2048,512]{1,0:T(8,128)S(1)}, f32[2048,512]{1,0:T(8,128)}, u32[]{:S(2)}) copy-start(f32[2048,512]{1,0:T(8,128)} %refs_1_.3) | copy-start | bytes 12582916
  13.5 6.7 %copy-start = (f32[2048,512]{1,0:T(8,128)S(1)}, f32[2048,512]{1,0:T(8,128)}, u32[]{:S(2)}) copy-start(f32[2048,512]{1,0:T(8,128)} %refs_3_.3) | copy-start | bytes 12582916
  13.5 17.3 %collective-permute-start.3 = (bf16[640,256]{1,0:T(8,128)(2,1)S(1)}, bf16[640,256]{1,0:T(8,128)(2,1)S(1)}, u32[]{:S(2)}, u32[]{:S(2)}) collective-permute-start(bf16[640,256]{1,0:T(8,128)(2,1)S(1)} %get-tuple-element.49._), channel_id=1, source_target_pairs={{4,0},{8,4},{12,8},{16,12},{20,16},{24,20},{28,24},{32,28},{36,32}... | collective-permute-start | bytes 983048 | tf_op jit(solution)/shard_map/ppermute | solution.py:219
  19.8 14.9 %collective-permute-start.2 = (bf16[640,256]{1,0:T(8,128)(2,1)S(1)}, bf16[640,256]{1,0:T(8,128)(2,1)S(1)}, u32[]{:S(2)}, u32[]{:S(2)}) collective-permute-start(bf16[640,256]{1,0:T(8,128)(2,1)S(1)} %get-tuple-element.56), channel_id=1, source_target_pairs={{0,4},{4,8},{8,12},{12,16},{16,20},{20,24},{24,28},{28,32},{32,36}... | collective-permute-start | bytes 983048 | tf_op jit(solution)/shard_map/ppermute | solution.py:219
  22.9 20.5 %collective-permute-start.4 = (bf16[640,256]{1,0:T(8,128)(2,1)S(1)}, bf16[640,256]{1,0:T(8,128)(2,1)S(1)}, u32[]{:S(2)}, u32[]{:S(2)}) collective-permute-start(bf16[640,256]{1,0:T(8,128)(2,1)S(1)} %get-tuple-element.61.refs_2_), channel_id=1, source_target_pairs={{0,4},{4,8},{8,12},{12,16},{16,20},{20,24},{24,28},{28,32},{32,36}... | collective-permute-start | bytes 983048 | tf_op jit(solution)/shard_map/ppermute | solution.py:219
  22.9 20.4 %collective-permute-start.5 = (bf16[640,256]{1,0:T(8,128)(2,1)S(1)}, bf16[640,256]{1,0:T(8,128)(2,1)S(1)}, u32[]{:S(2)}, u32[]{:S(2)}) collective-permute-start(bf16[640,256]{1,0:T(8,128)(2,1)S(1)} %get-tuple-element.59.refs_0_), channel_id=1, source_target_pairs={{4,0},{8,4},{12,8},{16,12},{20,16},{24,20},{28,24},{32,28},{36,32}... | collective-permute-start | bytes 983048 | tf_op jit(solution)/shard_map/ppermute | solution.py:219
  35.5 16.6 %collective-permute-start.6 = (bf16[640,256]{1,0:T(8,128)(2,1)S(1)}, bf16[640,256]{1,0:T(8,128)(2,1)S(1)}, u32[]{:S(2)}, u32[]{:S(2)}) collective-permute-start(bf16[640,256]{1,0:T(8,128)(2,1)S(1)} %get-tuple-element.67.refs_2_), channel_id=1, source_target_pairs={{0,4},{4,8},{8,12},{12,16},{16,20},{20,24},{24,28},{28,32},{32,36}... | collective-permute-start | bytes 983048 | tf_op jit(solution)/shard_map/ppermute | solution.py:219
  35.5 16.6 %collective-permute-start.7 = (bf16[640,256]{1,0:T(8,128)(2,1)S(1)}, bf16[640,256]{1,0:T(8,128)(2,1)S(1)}, u32[]{:S(2)}, u32[]{:S(2)}) collective-permute-start(bf16[640,256]{1,0:T(8,128)(2,1)S(1)} %get-tuple-element.65.refs_0_), channel_id=1, source_target_pairs={{4,0},{8,4},{12,8},{16,12},{20,16},{24,20},{28,24},{32,28},{36,32}... | collective-permute-start | bytes 983048 | tf_op jit(solution)/shard_map/ppermute | solution.py:219
  44.2 16.8 %collective-permute-start.8 = (bf16[640,256]{1,0:T(8,128)(2,1)S(1)}, bf16[640,256]{1,0:T(8,128)(2,1)S(1)}, u32[]{:S(2)}, u32[]{:S(2)}) collective-permute-start(bf16[640,256]{1,0:T(8,128)(2,1)S(1)} %get-tuple-element.74.refs_2_), channel_id=1, source_target_pairs={{0,4},{4,8},{8,12},{12,16},{16,20},{20,24},{24,28},{28,32},{32,36}... | collective-permute-start | bytes 983048 | tf_op jit(solution)/shard_map/ppermute | solution.py:219
  44.2 16.7 %collective-permute-start.9 = (bf16[640,256]{1,0:T(8,128)(2,1)S(1)}, bf16[640,256]{1,0:T(8,128)(2,1)S(1)}, u32[]{:S(2)}, u32[]{:S(2)}) collective-permute-start(bf16[640,256]{1,0:T(8,128)(2,1)S(1)} %get-tuple-element.72.refs_0_), channel_id=1, source_target_pairs={{4,0},{8,4},{12,8},{16,12},{20,16},{24,20},{28,24},{32,28},{36,32}... | collective-permute-start | bytes 983048 | tf_op jit(solution)/shard_map/ppermute | solution.py:219
  52.9 13.4 %collective-permute-start.10 = (bf16[640,256]{1,0:T(8,128)(2,1)S(1)}, bf16[640,256]{1,0:T(8,128)(2,1)S(1)}, u32[]{:S(2)}, u32[]{:S(2)}) collective-permute-start(bf16[640,256]{1,0:T(8,128)(2,1)S(1)} %get-tuple-element.81.refs_2_), channel_id=1, source_target_pairs={{0,4},{4,8},{8,12},{12,16},{16,20},{20,24},{24,28},{28,32},{32,36}... | collective-permute-start | bytes 983048 | tf_op jit(solution)/shard_map/ppermute | solution.py:219
  53.1 13.2 %collective-permute-start.11 = (bf16[640,256]{1,0:T(8,128)(2,1)S(1)}, bf16[640,256]{1,0:T(8,128)(2,1)S(1)}, u32[]{:S(2)}, u32[]{:S(2)}) collective-permute-start(bf16[640,256]{1,0:T(8,128)(2,1)S(1)} %get-tuple-element.79.refs_0_), channel_id=1, source_target_pairs={{4,0},{8,4},{12,8},{16,12},{20,16},{24,20},{28,24},{32,28},{36,32}... | collective-permute-start | bytes 983048 | tf_op jit(solution)/shard_map/ppermute | solution.py:219
where the time goes:
time: 83.8 us; the launch traced here: 83.6 us
  starting transfers between devices  38.4 us (46%)
  Pallas kernels  25 us (30%)
  blocking collectives  14.7 us (18%)
  waiting for transfers between devices  4.22 us (5%)
  between operations  1.1 us (1%)
    ppermute x6, starting transfers between devices, exchange(): lax.ppermute(low, 'slab', backward)  37.9 us
    all_to_all x1, blocking collectives, local(): gathered = lax.all_to_all(sums[-1], 'slab', 0, 0)  14.7 us
    pallas_call x6, Pallas kernels, middle(): pl.pallas_call(functools.partial(middle_kernel, len(sources[chunk]), chun...  9.57 us
    pallas_call x6, Pallas kernels, rims(): pl.pallas_call(functools.partial(rim_kernel, kind, chunk * cols, cols, wi...  4.42 us
    ppermute x6, waiting for transfers between devices, exchange(): lax.ppermute(high, 'slab', onward)  4.2 us
    pallas_call x1, Pallas kernels, local(): pl.pallas_call(band_kernel, out_shape=shape((pairs, 2 * width, (2 * BAND...  3.16 us
    pallas_call x1, Pallas kernels, local(): pl.pallas_call(functools.partial(store_kernel, rim, cols), out_shape=(ful...  2.99 us
    pallas_call x2, Pallas kernels, edges(): pl.pallas_call(functools.partial(edge_kernel, chunk * cols, cols, rim), o...  2.83 us
  transfers between devices with their start and end apart: 12, of which 2 were waited for; matrix products, arithmetic and copies ran while one was open for 0% of the time, Pallas kernels for 25%

commit v1 on v0

--- a/solution.py
+++ b/solution.py
@@ -24,7 +24,21 @@
     return pl.CostEstimate(flops=flops, bytes_accessed=moved, transcendentals=0)
 
 
-def edge_kernel(first, cols, rim, _, current, low, high, held, sems):
+def put(odd, side, pairs, at, value):
+    for parity in range(2):
+
+        @pl.when(odd[0] == parity)
+        def _():
+            pairs[(side + parity + 1) % 2][at] = value
+
+
+def pick(odd, side, pairs, at):
+    evens, odds = pairs[0][at], pairs[1][at]
+    taken = (odd[0] == 1) if side == 0 else (odd[0] == 0)
+    return jnp.where(taken, evens, odds)
+
+
+def edge_kernel(first, cols, rim, odd, _, current, evens, odds, held, sems):
     rows = current.shape[0]
     copies = [
         pltpu.make_async_copy(
@@ -34,9 +48,9 @@
     ]
     for copy in copies:
         copy.start()
-    for side, out in enumerate((low, high)):
+    for side in range(2):
         copies[side].wait()
-        out[...] = held[side].astype(BF16)
+        put(odd, side, (evens, odds), slice(None), held[side].astype(BF16))
 
 
 def band_kernel(_, places, blocks, banded, held, sems):
@@ -76,7 +90,7 @@
     return jnp.sum(x.reshape(-1, 8, x.shape[-1]), axis=0)
 
 
-def middle_kernel(sources, first, cols, width, rows_blk, _, banded, weights, *refs):
+def middle_kernel(sources, first, cols, width, rows_blk, odd, _, banded, weights, *refs):
     source, previous = refs[:sources], refs[sources]
     upcoming, *inner, partial, x = refs[sources + 1 + (first > 0) :]
     columns = pl.ds(first, cols)
@@ -85,9 +99,15 @@
     if sources == 1:
         x[...] = source[0][:, columns].astype(BF16)
     else:
-        x[0:rim] = source[0][...]
-        x[rim : rows - rim] = source[1][...]
-        x[rows - rim : rows] = source[2][...]
+        evens, inside, odds = source
+        x[rim : rows - rim] = inside[...]
+        for parity in range(2):
+
+            @pl.when(odd[0] == parity)
+            def _():
+                x[0:rim] = (odds, evens)[parity][...]
+                x[rows - rim : rows] = (evens, odds)[parity][...]
+
     total = jnp.zeros((8, cols), F32)
     for pair in range(rows_blk // 2):
         start = 2 * pair - BAND
@@ -124,8 +144,7 @@
     return parts
 
 
-def rim_kernel(kind, first, cols, width, rows_blk, _, banded, weights, low, high, begun, partial, *refs):
-    halos = (low, high)
+def rim_kernel(kind, first, cols, width, rows_blk, odd, _, banded, weights, evens, odds, begun, partial, *refs):
     earlier = refs[: TERMS * CHUNKS - 1] if kind == "final" else ()
     upcoming, *edges, moments = refs[len(earlier) :]
     columns = pl.ds(first, cols)
@@ -135,7 +154,7 @@
     for side, pair, a, b, left, right, at in rim_parts(rows_blk):
         product = jnp.dot(
             banded[pair, a * width : b * width, left * width : right * width],
-            halos[side][at * width : (at + right - left) * width],
+            pick(odd, side, (evens, odds), slice(at * width, (at + right - left) * width)),
             preferred_element_type=F32,
         )
         top = (2 * pair + a) * width
@@ -144,7 +163,7 @@
         upcoming[here, columns] = result
         if edges:
             base = top - (0 if side == 0 else rows - rim)
-            edges[side][base : base + (b - a) * width] = result.astype(BF16)
+            put(odd, side, edges, slice(base, base + (b - a) * width), result.astype(BF16))
         total = total + fold(result * weights[here, columns])
     if kind == "final":
         lanes = moments.shape[2]
@@ -207,31 +226,33 @@
     rim = BAND * width
     slabs = lax.axis_size("slab")
     total_blocks = rows_blk * slabs
-    onward = [(i, (i + 1) % slabs) for i in range(slabs)]
-    backward = [(target, source) for source, target in onward]
+    odd = lax.axis_index("slab")[None] & 1
+    pairs_of = [[(i, i ^ 1) for i in range(slabs)]]
+    pairs_of.append([((i + 1) % slabs, (k + 1) % slabs) for i, k in pairs_of[0]])
     shape = jax.ShapeDtypeStruct
     edge_shape = shape((rim, cols), BF16)
     full_shape = shape((rows, all_cols), F32)
     part_shape = shape((8, cols), F32)
     flops = 2 * rows * cols * 9 * width
 
-    def exchange(low, high):
-        return lax.ppermute(high, "slab", onward), lax.ppermute(low, "slab", backward)
+    def exchange(evens, odds):
+        ahead = lax.ppermute(odds, "slab", pairs_of[1])
+        return lax.ppermute(evens, "slab", pairs_of[0]), ahead
 
     def edges(token, chunk):
         return pl.pallas_call(
             functools.partial(edge_kernel, chunk * cols, cols, rim),
             out_shape=(edge_shape, edge_shape),
-            in_specs=[VMEM, HBM],
+            in_specs=[SMEM, VMEM, HBM],
             out_specs=(VMEM, VMEM),
             scratch_shapes=[pltpu.VMEM((2, rim, cols), F32), pltpu.SemaphoreType.DMA((2,))],
             compiler_params=params(),
             cost_estimate=cost(0, 6 * 2 * rim * cols),
             name="edges",
-        )(token, in_hbm(current))
+        )(odd, token, in_hbm(current))
 
     def middle(token, term, chunk):
-        args = [token, banded, weights, *sources[chunk], terms[term]]
+        args = [odd, token, banded, weights, *sources[chunk], terms[term]]
         aliases = {}
         if chunk:
             aliases = {len(args): 0}
@@ -244,7 +265,7 @@
                 middle_kernel, len(sources[chunk]), chunk * cols, cols, width, rows_blk
             ),
             out_shape=outs,
-            in_specs=[VMEM] * len(args),
+            in_specs=[SMEM] + [VMEM] * (len(args) - 1),
             out_specs=(VMEM,) * len(outs),
             scratch_shapes=[pltpu.VMEM((rows, cols), BF16)],
             input_output_aliases=aliases,
@@ -254,7 +275,7 @@
         )(*args)
 
     def rims(token, term, chunk):
-        args = [token, banded, weights, *halos[chunk], terms[term + 2], begun[chunk][-1]]
+        args = [odd, token, banded, weights, *halos[chunk], terms[term + 2], begun[chunk][-1]]
         kind = "inner"
         outs = (full_shape, edge_shape, edge_shape, part_shape)
         if term == TERMS - 1:
@@ -267,9 +288,9 @@
         return pl.pallas_call(
             functools.partial(rim_kernel, kind, chunk * cols, cols, width, rows_blk),
             out_shape=outs,
-            in_specs=[VMEM] * len(args),
+            in_specs=[SMEM] + [VMEM] * (len(args) - 1),
             out_specs=(VMEM,) * len(outs),
-            input_output_aliases={5: 0},
+            input_output_aliases={6: 0},
             compiler_params=params(),
             cost_estimate=cost(flops // 5, 2 * 1024 * 1024),
             name="rims",

time: 83.8 us -> 72.3 us (0.86)
  starting transfers between devices: 38.4 us -> 22.7 us
  Pallas kernels: 25 us -> 29.9 us
  blocking collectives: 14.7 us -> 13.2 us
  local copies, waits for them, and re-layouts: 0.03 us -> 1.49 us
    ppermute x12, starting transfers between devices: 38.4 us -> 22.7 us  [the longest x6 20.6 us: exchange(): ahead = lax.ppermute(odds, 'slab', pairs_of[1])]
    pallas_call x6, Pallas kernels: 4.42 us -> 8.84 us  [rims(): pl.pallas_call(functools.partial(rim_kernel, kind, chunk * cols, cols, wi...]
    all_to_all x1, blocking collectives: 14.7 us -> 13.2 us  [local(): gathered = lax.all_to_all(sums[-1], 'slab', 0, 0)]
    unnamed x10, local copies, waits for them, and re-layouts: 0.03 us -> 1.49 us
  transfers between devices with their start and end apart: 12 -> 12, of which waited for: 2 -> 5; matrix products, arithmetic and copies ran while one was open for 0% -> 0% of each run, Pallas kernels for 25% -> 36%
where the time goes in v1:
time: 72.3 us; the launch traced here: 72.1 us
  Pallas kernels  29.9 us (41%)
  starting transfers between devices  22.7 us (31%)
  blocking collectives  13.2 us (18%)
  waiting for transfers between devices  3.78 us (5%)
  local copies, waits for them, and re-layouts  1.49 us (2%)
  between operations  1.05 us (1%)
    ppermute x6, starting transfers between devices, exchange(): ahead = lax.ppermute(odds, 'slab', pairs_of[1])  20.6 us
    all_to_all x1, blocking collectives, local(): gathered = lax.all_to_all(sums[-1], 'slab', 0, 0)  13.2 us
    pallas_call x6, Pallas kernels, middle(): pl.pallas_call(functools.partial(middle_kernel, len(sources[chunk]), chun...  9.99 us
    pallas_call x6, Pallas kernels, rims(): pl.pallas_call(functools.partial(rim_kernel, kind, chunk * cols, cols, wi...  8.84 us
    ppermute x6, waiting for transfers between devices, exchange(): ahead = lax.ppermute(odds, 'slab', pairs_of[1])  3.77 us
    pallas_call x1, Pallas kernels, local(): pl.pallas_call(band_kernel, out_shape=shape((pairs, 2 * width, (2 * BAND...  3.16 us
    pallas_call x1, Pallas kernels, local(): pl.pallas_call(functools.partial(store_kernel, rim, cols), out_shape=(ful...  2.99 us
    pallas_call x2, Pallas kernels, edges(): pl.pallas_call(functools.partial(edge_kernel, chunk * cols, cols, rim), o...  2.9 us
  transfers between devices with their start and end apart: 12, of which 5 were waited for; matrix products, arithmetic and copies ran while one was open for 0% of the time, Pallas kernels for 36%

profile of v1, /device:TPU:0, one launch (start us, length us, event | category | flops | bytes accessed | tf_op | source)
XLA Modules:
  0.0 72.1 jit_solution(8840073535530633617)
XLA Ops:
  0.7 1.4 %edges.2 = (bf16[640,256]{1,0:T(8,128)(2,1)S(1)}, bf16[640,256]{1,0:T(8,128)(2,1)S(1)}) custom-call(s32[1]{0:T(128)} %bitcast.odd, f32[8,128]{1,0:T(8,128)S(1)} %broadcast_in_dim.2._, f32[2048,512]{1,0:T(8,128)} %refs_3_.3), custom_call_target="tpu_custom_call" | custom-call | bytes 1966080 | tf_op jit(solution)/shard_map/edges/pallas_call | solution.py:243
  2.0 1.6 %collective-permute-start = (bf16[640,256]{1,0:T(8,128)(2,1)S(1)}, bf16[640,256]{1,0:T(8,128)(2,1)S(1)}, u32[]{:S(2)}, u32[]{:S(2)}) collective-permute-start(bf16[640,256]{1,0:T(8,128)(2,1)S(1)} %get-tuple-element.48._), channel_id=1, source_target_pairs={{0,4},{4,0},{8,12},{12,8},{16,20},{20,16},{24,28},{28,24},{32,36},... | collective-permute-start | bytes 983048 | tf_op jit(solution)/shard_map/ppermute | solution.py:240
  3.7 5.9 %collective-permute-start.1 = (bf16[640,256]{1,0:T(8,128)(2,1)S(1)}, bf16[640,256]{1,0:T(8,128)(2,1)S(1)}, u32[]{:S(2)}, u32[]{:S(2)}) collective-permute-start(bf16[640,256]{1,0:T(8,128)(2,1)S(1)} %get-tuple-element.51), channel_id=1, source_target_pairs={{4,8},{8,4},{12,16},{16,12},{20,24},{24,20},{28,32},{32,28},{36,40... | collective-permute-start | bytes 983048 | tf_op jit(solution)/shard_map/ppermute | solution.py:239
  9.7 3.2 %band.1._.banded = bf16[8,256,1536]{2,1,0:T(8,128)(2,1)S(1)} custom-call(bf16[640,256]{1,0:T(8,128)(2,1)S(1)} %get-tuple-element.48._, s32[16,9]{1,0:T(8,128)S(1)} %add_select_fusion.places, bf16[16,9,128,128]{3,2,1,0:T(8,128)(2,1)} %blocks.1), custom_call_target="tpu_custom_call" | custom-call | bytes 12582912 | tf_op jit(solution)/shard_map/band/pallas_call | solution.py:307
  12.9 1.5 %edges.3 = (bf16[640,256]{1,0:T(8,128)(2,1)S(1)}, bf16[640,256]{1,0:T(8,128)(2,1)S(1)}) custom-call(s32[1]{0:T(128)} %bitcast.odd, bf16[8,256,1536]{2,1,0:T(8,128)(2,1)S(1)} %band.1._.banded, f32[2048,512]{1,0:T(8,128)} %refs_3_.3), custom_call_target="tpu_custom_call" | custom-call | bytes 1966080 | tf_op jit(solution)/shard_map/edges/pallas_call | solution.py:243
  14.5 1.2 %collective-permute-start.3 = (bf16[640,256]{1,0:T(8,128)(2,1)S(1)}, bf16[640,256]{1,0:T(8,128)(2,1)S(1)}, u32[]{:S(2)}, u32[]{:S(2)}) collective-permute-start(bf16[640,256]{1,0:T(8,128)(2,1)S(1)} %get-tuple-element.56), channel_id=1, source_target_pairs={{4,8},{8,4},{12,16},{16,12},{20,24},{24,20},{28,32},{32,28},{36,40... | collective-permute-start | bytes 983048 | tf_op jit(solution)/shard_map/ppermute | solution.py:239
  15.7 0.3 weights.1._
  16.1 1.4 %copy-done = f32[2048,512]{1,0:T(8,128)S(1)} copy-done((f32[2048,512]{1,0:T(8,128)S(1)}, f32[2048,512]{1,0:T(8,128)}, u32[]{:S(2)}) %copy-start) | copy-done | bytes 4194328
  17.5 1.6 %middle.6 = (f32[2048,512]{1,0:T(8,128)S(1)}, bf16[768,256]{1,0:T(8,128)(2,1)S(1)}, f32[8,256]{1,0:T(8,128)S(1)}) custom-call(s32[1]{0:T(128)} %bitcast.odd, f32[2048,512]{1,0:T(8,128)S(1)} %weights.1._, bf16[8,256,1536]{2,1,0:T(8,128)(2,1)S(1)} %band.1._.banded, f32[2048,512]{1,0:T(8,128)S(1)} %weights.1._, f32[2048,512]{1,0:T(8,128)S(1)} %copy-done, ...), custom_call_target="tpu_custom_call" | custom-call | flops 1207959552 | bytes 8388608 | tf_op jit(solution)/shard_map/middle/pallas_call | solution.py:263
  19.2 1.8 %rims.6 = (f32[2048,512]{1,0:T(8,128)S(1)}, bf16[640,256]{1,0:T(8,128)(2,1)S(1)}, bf16[640,256]{1,0:T(8,128)(2,1)S(1)}, f32[8,256]{1,0:T(8,128)S(1)}) custom-call(s32[1]{0:T(128)} %bitcast.odd, f32[8,256]{1,0:T(8,128)S(1)} %get-tuple-element.50._.partial, bf16[8,256,1536]{2,1,0:T(8,128)(2,1)S(1)} %band.1._.banded, ...), custom_call_target="tpu_custom_call", output_to_operand_aliasing={{0}: (6, {})} | custom-call | flops 241591904 | bytes 2097152 | tf_op jit(solution)/shard_map/rims/pallas_call | solution.py:288
  21.1 5.0 %collective-permute-start.5 = (bf16[640,256]{1,0:T(8,128)(2,1)S(1)}, bf16[640,256]{1,0:T(8,128)(2,1)S(1)}, u32[]{:S(2)}, u32[]{:S(2)}) collective-permute-start(bf16[640,256]{1,0:T(8,128)(2,1)S(1)} %get-tuple-element.61.refs_2_), channel_id=1, source_target_pairs={{4,8},{8,4},{12,16},{16,12},{20,24},{24,20},{28,32},{32,28},{36,40... | collective-permute-start | bytes 983048 | tf_op jit(solution)/shard_map/ppermute | solution.py:239
  26.1 1.6 %middle.7 = (f32[2048,512]{1,0:T(8,128)S(1)}, bf16[768,256]{1,0:T(8,128)(2,1)S(1)}, f32[8,256]{1,0:T(8,128)S(1)}) custom-call(s32[1]{0:T(128)} %bitcast.odd, f32[8,256]{1,0:T(8,128)S(1)} %get-tuple-element.53._.refs_0_, bf16[8,256,1536]{2,1,0:T(8,128)(2,1)S(1)} %band.1._.banded, f32[2048,512]{1,0:T(8,128)S(1)} %weights.1._, ...), custom_call_target="tpu_custom_call", output_to_operand_aliasing={{0}: (6, {})} | custom-call | flops 1207959552 | bytes 8388608 | tf_op jit(solution)/shard_map/middle/pallas_call | solution.py:263
  27.7 0.4 collective-permute-done.3.odds
  28.1 1.8 %rims.7 = (f32[2048,512]{1,0:T(8,128)S(1)}, bf16[640,256]{1,0:T(8,128)(2,1)S(1)}, bf16[640,256]{1,0:T(8,128)(2,1)S(1)}, f32[8,256]{1,0:T(8,128)S(1)}) custom-call(s32[1]{0:T(128)} %bitcast.odd, f32[8,256]{1,0:T(8,128)S(1)} %get-tuple-element.55._.partial, bf16[8,256,1536]{2,1,0:T(8,128)(2,1)S(1)} %band.1._.banded, ...), custom_call_target="tpu_custom_call", output_to_operand_aliasing={{0}: (6, {})} | custom-call | flops 241591904 | bytes 2097152 | tf_op jit(solution)/shard_map/rims/pallas_call | solution.py:288
  30.0 2.0 %collective-permute-start.7 = (bf16[640,256]{1,0:T(8,128)(2,1)S(1)}, bf16[640,256]{1,0:T(8,128)(2,1)S(1)}, u32[]{:S(2)}, u32[]{:S(2)}) collective-permute-start(bf16[640,256]{1,0:T(8,128)(2,1)S(1)} %get-tuple-element.67.refs_2_), channel_id=1, source_target_pairs={{4,8},{8,4},{12,16},{16,12},{20,24},{24,20},{28,32},{32,28},{36,40... | collective-permute-start | bytes 983048 | tf_op jit(solution)/shard_map/ppermute | solution.py:239
  31.9 1.7 %middle.8 = (f32[2048,512]{1,0:T(8,128)S(1)}, bf16[768,256]{1,0:T(8,128)(2,1)S(1)}, f32[8,256]{1,0:T(8,128)S(1)}) custom-call(s32[1]{0:T(128)} %bitcast.odd, f32[8,256]{1,0:T(8,128)S(1)} %get-tuple-element.58._.refs_1_, bf16[8,256,1536]{2,1,0:T(8,128)(2,1)S(1)} %band.1._.banded, f32[2048,512]{1,0:T(8,128)S(1)} %weights.1._, ...), custom_call_target="tpu_custom_call" | custom-call | flops 1207959552 | bytes 8388608 | tf_op jit(solution)/shard_map/middle/pallas_call | solution.py:263
  33.7 1.1 %collective-permute-done.5.odds = bf16[640,256]{1,0:T(8,128)(2,1)S(1)} collective-permute-done((bf16[640,256]{1,0:T(8,128)(2,1)S(1)}, bf16[640,256]{1,0:T(8,128)(2,1)S(1)}, u32[]{:S(2)}, u32[]{:S(2)}) %collective-permute-start.5) | collective-permute-done | bytes 327712 | tf_op jit(solution)/shard_map/ppermute | solution.py:239
  34.7 1.8 %rims.8 = (f32[2048,512]{1,0:T(8,128)S(1)}, bf16[640,256]{1,0:T(8,128)(2,1)S(1)}, bf16[640,256]{1,0:T(8,128)(2,1)S(1)}, f32[8,256]{1,0:T(8,128)S(1)}) custom-call(s32[1]{0:T(128)} %bitcast.odd, f32[8,256]{1,0:T(8,128)S(1)} %get-tuple-element.62._.partial, bf16[8,256,1536]{2,1,0:T(8,128)(2,1)S(1)} %band.1._.banded, ...), custom_call_target="tpu_custom_call", output_to_operand_aliasing={{0}: (6, {})} | custom-call | flops 241591904 | bytes 2097152 | tf_op jit(solution)/shard_map/rims/pallas_call | solution.py:288
  36.7 3.3 %collective-permute-start.9 = (bf16[640,256]{1,0:T(8,128)(2,1)S(1)}, bf16[640,256]{1,0:T(8,128)(2,1)S(1)}, u32[]{:S(2)}, u32[]{:S(2)}) collective-permute-start(bf16[640,256]{1,0:T(8,128)(2,1)S(1)} %get-tuple-element.74.refs_2_), channel_id=1, source_target_pairs={{4,8},{8,4},{12,16},{16,12},{20,24},{24,20},{28,32},{32,28},{36,40... | collective-permute-start | bytes 983048 | tf_op jit(solution)/shard_map/ppermute | solution.py:239
  40.0 1.7 %middle.9 = (f32[2048,512]{1,0:T(8,128)S(1)}, bf16[768,256]{1,0:T(8,128)(2,1)S(1)}, f32[8,256]{1,0:T(8,128)S(1)}) custom-call(s32[1]{0:T(128)} %bitcast.odd, f32[8,256]{1,0:T(8,128)S(1)} %get-tuple-element.64._.refs_2_, bf16[8,256,1536]{2,1,0:T(8,128)(2,1)S(1)} %band.1._.banded, f32[2048,512]{1,0:T(8,128)S(1)} %weights.1._, ...), custom_call_target="tpu_custom_call", output_to_operand_aliasing={{0}: (8, {})} | custom-call | flops 1207959552 | bytes 8388608 | tf_op jit(solution)/shard_map/middle/pallas_call | solution.py:263
  41.7 0.2 collective-permute-done.7.odds
  41.9 2.0 %rims.9 = (f32[2048,512]{1,0:T(8,128)S(1)}, bf16[640,256]{1,0:T(8,128)(2,1)S(1)}, bf16[640,256]{1,0:T(8,128)(2,1)S(1)}, f32[8,256]{1,0:T(8,128)S(1)}) custom-call(s32[1]{0:T(128)} %bitcast.odd, f32[8,256]{1,0:T(8,128)S(1)} %get-tuple-element.69._.partial, bf16[8,256,1536]{2,1,0:T(8,128)(2,1)S(1)} %band.1._.banded, ...), custom_call_target="tpu_custom_call", output_to_operand_aliasing={{0}: (6, {})} | custom-call | flops 241591904 | bytes 2097152 | tf_op jit(solution)/shard_map/rims/pallas_call | solution.py:288
  43.9 3.2 %collective-permute-start.11 = (bf16[640,256]{1,0:T(8,128)(2,1)S(1)}, bf16[640,256]{1,0:T(8,128)(2,1)S(1)}, u32[]{:S(2)}, u32[]{:S(2)}) collective-permute-start(bf16[640,256]{1,0:T(8,128)(2,1)S(1)} %get-tuple-element.81.refs_2_), channel_id=1, source_target_pairs={{4,8},{8,4},{12,16},{16,12},{20,24},{24,20},{28,32},{32,28},{36,40... | collective-permute-start | bytes 983048 | tf_op jit(solution)/shard_map/ppermute | solution.py:239
  47.1 1.7 %middle.10 = (f32[2048,512]{1,0:T(8,128)S(1)}, f32[8,256]{1,0:T(8,128)S(1)}) custom-call(s32[1]{0:T(128)} %bitcast.odd, f32[8,256]{1,0:T(8,128)S(1)} %get-tuple-element.71._.refs_3_, bf16[8,256,1536]{2,1,0:T(8,128)(2,1)S(1)} %band.1._.banded, f32[2048,512]{1,0:T(8,128)S(1)} %weights.1._, bf16[640,256]{1,0:T(8,128)(2,1)S(1)} %get-tuple-element.72.refs_0_, ...), custom_call_target="tpu_custom_call" | custom-call | flops 1207959552 | bytes 8388608 | tf_op jit(solution)/shard_map/middle/pallas_call | solution.py:263
  48.8 1.8 %collective-permute-done.9.odds = bf16[640,256]{1,0:T(8,128)(2,1)S(1)} collective-permute-done((bf16[640,256]{1,0:T(8,128)(2,1)S(1)}, bf16[640,256]{1,0:T(8,128)(2,1)S(1)}, u32[]{:S(2)}, u32[]{:S(2)}) %collective-permute-start.9) | collective-permute-done | bytes 327712 | tf_op jit(solution)/shard_map/ppermute | solution.py:239
  50.6 0.7 rims.10
  51.3 1.7 %middle.11 = (f32[2048,512]{1,0:T(8,128)S(1)}, f32[8,256]{1,0:T(8,128)S(1)}) custom-call(s32[1]{0:T(128)} %bitcast.odd, f32[8,256]{1,0:T(8,128)S(1)} %get-tuple-element.78._.refs_4_, bf16[8,256,1536]{2,1,0:T(8,128)(2,1)S(1)} %band.1._.banded, f32[2048,512]{1,0:T(8,128)S(1)} %weights.1._, ...), custom_call_target="tpu_custom_call", output_to_operand_aliasing={{0}: (8, {})} | custom-call | flops 1207959552 | bytes 8388608 | tf_op jit(solution)/shard_map/middle/pallas_call | solution.py:263
  53.0 3.0 %store.1 = (f32[2048,512]{1,0:T(8,128)}, f32[2048,512]{1,0:T(8,128)}, f32[8,128]{1,0:T(8,128)S(1)}) custom-call(f32[8,256]{1,0:T(8,128)S(1)} %get-tuple-element.83._.partial, f32[2048,512]{1,0:T(8,128)S(1)} %get-tuple-element.84.previous, f32[2048,512]{1,0:T(8,128)S(1)} %get-tuple-element.85.current.begun), custom_call_target="tpu_custom_call" | custom-call | bytes 16777216 | tf_op jit(solution)/shard_map/store/pallas_call | solution.py:355
  56.0 0.4 collective-permute-done.11.odds
  56.4 0.7 %rims.11 = (f32[2048,512]{1,0:T(8,128)S(1)}, f32[32,12,128]{2,1,0:T(8,128)S(1)}) custom-call(s32[1]{0:T(128)} %bitcast.odd, f32[8,128]{1,0:T(8,128)S(1)} %get-tuple-element.87._, bf16[8,256,1536]{2,1,0:T(8,128)(2,1)S(1)} %band.1._.banded, f32[2048,512]{1,0:T(8,128)S(1)} %weights.1._, ...), custom_call_target="tpu_custom_call", output_to_operand_aliasing={{0}: (6, {})} | custom-call | flops 241591904 | bytes 2097152 | tf_op jit(solution)/shard_map/rims/pallas_call | solution.py:288
  57.1 13.2 %all_to_all.5.parts = f32[32,12,128]{2,1,0:T(8,128)S(1)} all-to-all(f32[32,12,128]{2,1,0:T(8,128)S(1)} %get-tuple-element.88), channel_id=1, replica_groups=mesh['slab'=32,'col'=4] {'slab'}, dimensions={0} | all-to-all | bytes 393216 | tf_op jit(solution)/shard_map/all_to_all | solution.py:365
  70.3 1.7 %sums.1 = (f32[3,512]{1,0:T(4,128)}, f32[2048,512]{1,0:T(8,128)}) custom-call(f32[32,12,128]{2,1,0:T(8,128)S(1)} %all_to_all.5.parts, f32[2048,512]{1,0:T(8,128)S(1)} %get-tuple-element.89.current, f32[2048,512]{1,0:T(8,128)} %get-tuple-element.90._), custom_call_target="tpu_custom_call", output_to_operand_aliasing={{1}: (2, {})} | custom-call | tf_op jit(solution)/shard_map/sums/pallas_call | solution.py:366
  (24 shorter events, 0.6 us)
Async XLA Ops:
  0.6 9.0 %copy-start.4 = (s32[16,9]{1,0:T(8,128)S(1)}, s32[16,9]{1,0:T(8,128)}, u32[]{:S(2)}) copy-start(s32[16,9]{1,0:T(8,128)} %param.7) | copy-start | bytes 1732
  2.0 17.1 %collective-permute-start = (bf16[640,256]{1,0:T(8,128)(2,1)S(1)}, bf16[640,256]{1,0:T(8,128)(2,1)S(1)}, u32[]{:S(2)}, u32[]{:S(2)}) collective-permute-start(bf16[640,256]{1,0:T(8,128)(2,1)S(1)} %get-tuple-element.48._), channel_id=1, source_target_pairs={{0,4},{4,0},{8,12},{12,8},{16,20},{20,16},{24,28},{28,24},{32,36},... | collective-permute-start | bytes 983048 | tf_op jit(solution)/shard_map/ppermute | solution.py:240
  3.7 15.5 %collective-permute-start.1 = (bf16[640,256]{1,0:T(8,128)(2,1)S(1)}, bf16[640,256]{1,0:T(8,128)(2,1)S(1)}, u32[]{:S(2)}, u32[]{:S(2)}) collective-permute-start(bf16[640,256]{1,0:T(8,128)(2,1)S(1)} %get-tuple-element.51), channel_id=1, source_target_pairs={{4,8},{8,4},{12,16},{16,12},{20,24},{24,20},{28,32},{32,28},{36,40... | collective-permute-start | bytes 983048 | tf_op jit(solution)/shard_map/ppermute | solution.py:239
  12.8 2.9 %copy-start.2 = (bf16[2048,512]{1,0:T(8,128)(2,1)S(1)}, bf16[2048,512]{1,0:T(8,128)(2,1)}, u32[]{:S(2)}) copy-start(bf16[2048,512]{1,0:T(8,128)(2,1)} %probe.1) | copy-start | bytes 6291460
  12.9 2.9 %copy-start.3 = (f32[2048]{0:T(1024)S(1)}, f32[2048]{0:T(1024)}, u32[]{:S(2)}) copy-start(f32[2048]{0:T(1024)} %param.11) | copy-start | bytes 24580
  12.9 3.2 %copy-start.1 = (f32[2048,512]{1,0:T(8,128)S(1)}, f32[2048,512]{1,0:T(8,128)}, u32[]{:S(2)}) copy-start(f32[2048,512]{1,0:T(8,128)} %refs_1_.3) | copy-start | bytes 12582916
  14.4 3.1 %copy-start = (f32[2048,512]{1,0:T(8,128)S(1)}, f32[2048,512]{1,0:T(8,128)}, u32[]{:S(2)}) copy-start(f32[2048,512]{1,0:T(8,128)} %refs_3_.3) | copy-start | bytes 12582916
  14.4 13.3 %collective-permute-start.2 = (bf16[640,256]{1,0:T(8,128)(2,1)S(1)}, bf16[640,256]{1,0:T(8,128)(2,1)S(1)}, u32[]{:S(2)}, u32[]{:S(2)}) collective-permute-start(bf16[640,256]{1,0:T(8,128)(2,1)S(1)} %get-tuple-element.49._), channel_id=1, source_target_pairs={{0,4},{4,0},{8,12},{12,8},{16,20},{20,16},{24,28},{28,24},{32,36},... | collective-permute-start | bytes 983048 | tf_op jit(solution)/shard_map/ppermute | solution.py:240
  14.5 13.6 %collective-permute-start.3 = (bf16[640,256]{1,0:T(8,128)(2,1)S(1)}, bf16[640,256]{1,0:T(8,128)(2,1)S(1)}, u32[]{:S(2)}, u32[]{:S(2)}) collective-permute-start(bf16[640,256]{1,0:T(8,128)(2,1)S(1)} %get-tuple-element.56), channel_id=1, source_target_pairs={{4,8},{8,4},{12,16},{16,12},{20,24},{24,20},{28,32},{32,28},{36,40... | collective-permute-start | bytes 983048 | tf_op jit(solution)/shard_map/ppermute | solution.py:239
  21.0 12.6 %collective-permute-start.4 = (bf16[640,256]{1,0:T(8,128)(2,1)S(1)}, bf16[640,256]{1,0:T(8,128)(2,1)S(1)}, u32[]{:S(2)}, u32[]{:S(2)}) collective-permute-start(bf16[640,256]{1,0:T(8,128)(2,1)S(1)} %get-tuple-element.59.refs_0_), channel_id=1, source_target_pairs={{0,4},{4,0},{8,12},{12,8},{16,20},{20,16},{24,28},{28,24},{32,36},... | collective-permute-start | bytes 983048 | tf_op jit(solution)/shard_map/ppermute | solution.py:240
  21.1 13.6 %collective-permute-start.5 = (bf16[640,256]{1,0:T(8,128)(2,1)S(1)}, bf16[640,256]{1,0:T(8,128)(2,1)S(1)}, u32[]{:S(2)}, u32[]{:S(2)}) collective-permute-start(bf16[640,256]{1,0:T(8,128)(2,1)S(1)} %get-tuple-element.61.refs_2_), channel_id=1, source_target_pairs={{4,8},{8,4},{12,16},{16,12},{20,24},{24,20},{28,32},{32,28},{36,40... | collective-permute-start | bytes 983048 | tf_op jit(solution)/shard_map/ppermute | solution.py:239
  29.9 11.8 %collective-permute-start.6 = (bf16[640,256]{1,0:T(8,128)(2,1)S(1)}, bf16[640,256]{1,0:T(8,128)(2,1)S(1)}, u32[]{:S(2)}, u32[]{:S(2)}) collective-permute-start(bf16[640,256]{1,0:T(8,128)(2,1)S(1)} %get-tuple-element.65.refs_0_), channel_id=1, source_target_pairs={{0,4},{4,0},{8,12},{12,8},{16,20},{20,16},{24,28},{28,24},{32,36},... | collective-permute-start | bytes 983048 | tf_op jit(solution)/shard_map/ppermute | solution.py:240
  30.0 11.9 %collective-permute-start.7 = (bf16[640,256]{1,0:T(8,128)(2,1)S(1)}, bf16[640,256]{1,0:T(8,128)(2,1)S(1)}, u32[]{:S(2)}, u32[]{:S(2)}) collective-permute-start(bf16[640,256]{1,0:T(8,128)(2,1)S(1)} %get-tuple-element.67.refs_2_), channel_id=1, source_target_pairs={{4,8},{8,4},{12,16},{16,12},{20,24},{24,20},{28,32},{32,28},{36,40... | collective-permute-start | bytes 983048 | tf_op jit(solution)/shard_map/ppermute | solution.py:239
  36.6 12.2 %collective-permute-start.8 = (bf16[640,256]{1,0:T(8,128)(2,1)S(1)}, bf16[640,256]{1,0:T(8,128)(2,1)S(1)}, u32[]{:S(2)}, u32[]{:S(2)}) collective-permute-start(bf16[640,256]{1,0:T(8,128)(2,1)S(1)} %get-tuple-element.72.refs_0_), channel_id=1, source_target_pairs={{0,4},{4,0},{8,12},{12,8},{16,20},{20,16},{24,28},{28,24},{32,36},... | collective-permute-start | bytes 983048 | tf_op jit(solution)/shard_map/ppermute | solution.py:240
  36.7 13.9 %collective-permute-start.9 = (bf16[640,256]{1,0:T(8,128)(2,1)S(1)}, bf16[640,256]{1,0:T(8,128)(2,1)S(1)}, u32[]{:S(2)}, u32[]{:S(2)}) collective-permute-start(bf16[640,256]{1,0:T(8,128)(2,1)S(1)} %get-tuple-element.74.refs_2_), channel_id=1, source_target_pairs={{4,8},{8,4},{12,16},{16,12},{20,24},{24,20},{28,32},{32,28},{36,40... | collective-permute-start | bytes 983048 | tf_op jit(solution)/shard_map/ppermute | solution.py:239
  43.8 12.2 %collective-permute-start.10 = (bf16[640,256]{1,0:T(8,128)(2,1)S(1)}, bf16[640,256]{1,0:T(8,128)(2,1)S(1)}, u32[]{:S(2)}, u32[]{:S(2)}) collective-permute-start(bf16[640,256]{1,0:T(8,128)(2,1)S(1)} %get-tuple-element.79.refs_0_), channel_id=1, source_target_pairs={{0,4},{4,0},{8,12},{12,8},{16,20},{20,16},{24,28},{28,24},{32,36},... | collective-permute-start | bytes 983048 | tf_op jit(solution)/shard_map/ppermute | solution.py:240
  43.9 12.5 %collective-permute-start.11 = (bf16[640,256]{1,0:T(8,128)(2,1)S(1)}, bf16[640,256]{1,0:T(8,128)(2,1)S(1)}, u32[]{:S(2)}, u32[]{:S(2)}) collective-permute-start(bf16[640,256]{1,0:T(8,128)(2,1)S(1)} %get-tuple-element.81.refs_2_), channel_id=1, source_target_pairs={{4,8},{8,4},{12,16},{16,12},{20,24},{24,20},{28,32},{32,28},{36,40... | collective-permute-start | bytes 983048 | tf_op jit(solution)/shard_map/ppermute | solution.py:239

commit v2 on v1

--- a/solution.py
+++ b/solution.py
@@ -24,12 +24,13 @@
     return pl.CostEstimate(flops=flops, bytes_accessed=moved, transcendentals=0)
 
 
-def put(odd, side, pairs, at, value):
+def hand_out(odd, rims, evens, odds):
     for parity in range(2):
 
         @pl.when(odd[0] == parity)
         def _():
-            pairs[(side + parity + 1) % 2][at] = value
+            evens[...] = rims[1 - parity].astype(BF16)
+            odds[...] = rims[parity].astype(BF16)
 
 
 def pick(odd, side, pairs, at):
@@ -38,23 +39,33 @@
     return jnp.where(taken, evens, odds)
 
 
-def edge_kernel(first, cols, rim, odd, _, current, evens, odds, held, sems):
+def fetch_rims(current, first, cols, held, sems):
+    rim = held.shape[1]
     rows = current.shape[0]
+    piece = rim // sems.shape[1]
     copies = [
         pltpu.make_async_copy(
-            current.at[pl.ds(start, rim), pl.ds(first, cols)], held.at[side], sems.at[side]
+            current.at[pl.ds(start + i * piece, piece), pl.ds(first, cols)],
+            held.at[side, pl.ds(i * piece, piece)],
+            sems.at[side, i],
         )
         for side, start in enumerate((0, rows - rim))
+        for i in range(sems.shape[1])
     ]
     for copy in copies:
         copy.start()
-    for side in range(2):
-        copies[side].wait()
-        put(odd, side, (evens, odds), slice(None), held[side].astype(BF16))
-
-
-def band_kernel(_, places, blocks, banded, held, sems):
+    return copies
+
+
+def edge_kernel(first, cols, odd, current, evens, odds, held, sems):
+    for copy in fetch_rims(current, first, cols, held, sems):
+        copy.wait()
+    hand_out(odd, held, evens, odds)
+
+
+def band_kernel(first, cols, odd, _, places, blocks, current, banded, evens, odds, held, sems, rims, rim_sems):
     rows_blk, slots, width, _ = blocks.shape
+    copies = fetch_rims(current, first, cols, rims, rim_sems)
 
     def fetch(pair):
         two = pl.ds(2 * pair, 2)
@@ -62,6 +73,9 @@
 
     for pair in range(rows_blk // 2):
         fetch(pair).start()
+    for copy in copies:
+        copy.wait()
+    hand_out(odd, rims, evens, odds)
 
     def one_pair(pair, _):
         banded[pair] = jnp.zeros(banded.shape[1:], BF16)
@@ -144,9 +158,10 @@
     return parts
 
 
-def rim_kernel(kind, first, cols, width, rows_blk, odd, _, banded, weights, evens, odds, begun, partial, *refs):
+def rim_kernel(kind, first, cols, width, rows_blk, odd, _, banded, weights, odds, evens, begun, partial, *refs):
     earlier = refs[: TERMS * CHUNKS - 1] if kind == "final" else ()
-    upcoming, *edges, moments = refs[len(earlier) :]
+    upcoming, moments = refs[len(earlier) : len(earlier) + 2]
+    sent = refs[len(earlier) + 2 :]
     columns = pl.ds(first, cols)
     rim = BAND * width
     rows = rows_blk * width
@@ -161,10 +176,12 @@
         here = pl.ds(top, (b - a) * width)
         result = begun[here, columns] + 2.0 * product
         upcoming[here, columns] = result
-        if edges:
+        if sent:
             base = top - (0 if side == 0 else rows - rim)
-            put(odd, side, edges, slice(base, base + (b - a) * width), result.astype(BF16))
+            sent[2][side, base : base + (b - a) * width] = result.astype(BF16)
         total = total + fold(result * weights[here, columns])
+    if sent:
+        hand_out(odd, sent[2], *sent[:2])
     if kind == "final":
         lanes = moments.shape[2]
         parts = []
@@ -237,19 +254,7 @@
 
     def exchange(evens, odds):
         ahead = lax.ppermute(odds, "slab", pairs_of[1])
-        return lax.ppermute(evens, "slab", pairs_of[0]), ahead
-
-    def edges(token, chunk):
-        return pl.pallas_call(
-            functools.partial(edge_kernel, chunk * cols, cols, rim),
-            out_shape=(edge_shape, edge_shape),
-            in_specs=[SMEM, VMEM, HBM],
-            out_specs=(VMEM, VMEM),
-            scratch_shapes=[pltpu.VMEM((2, rim, cols), F32), pltpu.SemaphoreType.DMA((2,))],
-            compiler_params=params(),
-            cost_estimate=cost(0, 6 * 2 * rim * cols),
-            name="edges",
-        )(odd, token, in_hbm(current))
+        return ahead, lax.ppermute(evens, "slab", pairs_of[0])
 
     def middle(token, term, chunk):
         args = [odd, token, banded, weights, *sources[chunk], terms[term]]
@@ -277,9 +282,11 @@
     def rims(token, term, chunk):
         args = [odd, token, banded, weights, *halos[chunk], terms[term + 2], begun[chunk][-1]]
         kind = "inner"
-        outs = (full_shape, edge_shape, edge_shape, part_shape)
+        outs = (full_shape, part_shape, edge_shape, edge_shape)
+        scratch = [pltpu.VMEM((2, rim, cols), BF16)]
         if term == TERMS - 1:
             kind = "last"
+            scratch = []
             outs = (full_shape, part_shape)
             if chunk == CHUNKS - 1:
                 kind = "final"
@@ -290,6 +297,7 @@
             out_shape=outs,
             in_specs=[SMEM] + [VMEM] * (len(args) - 1),
             out_specs=(VMEM,) * len(outs),
+            scratch_shapes=scratch,
             input_output_aliases={6: 0},
             compiler_params=params(),
             cost_estimate=cost(flops // 5, 2 * 1024 * 1024),
@@ -301,27 +309,37 @@
     places = (block_columns - own_row + BAND + total_blocks) % total_blocks
     pairs = rows_blk // 2
 
-    halos = [None] * CHUNKS
-    opening = edges(jnp.zeros((8, 128), F32), 0)
-    halos[0] = exchange(*opening)
-    banded = pl.pallas_call(
-        band_kernel,
-        out_shape=shape((pairs, 2 * width, (2 * BAND + 2) * width), BF16),
-        in_specs=[VMEM, SMEM, HBM],
-        out_specs=VMEM,
+    rim_scratch = [pltpu.VMEM((2, rim, cols), F32), pltpu.SemaphoreType.DMA((2, BAND))]
+    opening = pl.pallas_call(
+        functools.partial(edge_kernel, 0, cols),
+        out_shape=(edge_shape, edge_shape),
+        in_specs=[SMEM, HBM],
+        out_specs=(VMEM, VMEM),
+        scratch_shapes=rim_scratch,
+        compiler_params=params(),
+        cost_estimate=cost(0, 6 * 2 * rim * cols),
+        name="edges",
+    )(odd, in_hbm(current))
+    halos = [exchange(*opening)]
+    banded, *opening = pl.pallas_call(
+        functools.partial(band_kernel, cols, cols),
+        out_shape=(
+            shape((pairs, 2 * width, (2 * BAND + 2) * width), BF16),
+            edge_shape,
+            edge_shape,
+        ),
+        in_specs=[SMEM, VMEM, SMEM, HBM, HBM],
+        out_specs=(VMEM,) * 3,
         scratch_shapes=[
             pltpu.VMEM(hamiltonian_blocks.shape, BF16),
             pltpu.SemaphoreType.DMA((pairs,)),
+            *rim_scratch,
         ],
         compiler_params=params(),
         cost_estimate=cost(0, 12 * 1024 * 1024),
         name="band",
-    )(opening[0], places, in_hbm(hamiltonian_blocks))
-    token = banded
-    for chunk in range(1, CHUNKS):
-        opening = edges(token, chunk)
-        halos[chunk] = exchange(*opening)
-        token = opening[0]
+    )(odd, opening[1], places, in_hbm(hamiltonian_blocks), in_hbm(current))
+    halos.append(exchange(*opening))
     weights = pl.pallas_call(
         functools.partial(weight_kernel, 1.0 / (total_blocks * width)),
         out_shape=full_shape,
@@ -330,7 +348,7 @@
         compiler_params=params(),
         cost_estimate=cost(0, 4 * 1024 * 1024),
         name="weights",
-    )(token, orbital_weight.reshape(rows_blk, width), probe)
+    )(opening[1], orbital_weight.reshape(rows_blk, width), probe)
 
     terms = [previous, current] + [None] * TERMS
     sources = [(current,)] * CHUNKS
@@ -344,7 +362,7 @@
 
     token = begin(weights, *order[0])
     for step, (term, chunk) in enumerate(order):
-        terms[term + 2], *sent, token = rims(token, term, chunk)
+        terms[term + 2], token, *sent = rims(token, term, chunk)
         if sent:
             halos[chunk] = exchange(*sent)
             sources[chunk] = (sent[0], begun[chunk][0], sent[1])

time: 72.3 us -> 71.4 us (0.988)
  waiting for transfers between devices: 3.78 us -> 10.7 us
  Pallas kernels: 29.9 us -> 26.5 us
  starting transfers between devices: 22.7 us -> 20.8 us
  local copies, waits for them, and re-layouts: 1.49 us -> 0.03 us
  blocking collectives: 13.2 us -> 12.1 us
    ppermute x6, waiting for transfers between devices: 3.77 us -> 10.3 us  [exchange(): ahead = lax.ppermute(odds, 'slab', pairs_of[1])]
    pallas_call x6, Pallas kernels: 8.84 us -> 4.77 us  [rims(): pl.pallas_call(functools.partial(rim_kernel, kind, chunk * cols, cols, wi...]
    unnamed x10, local copies, waits for them, and re-layouts: 1.49 us -> 0.03 us
    ppermute x6, starting transfers between devices: 2.08 us -> 0.77 us  [exchange(): return (ahead, lax.ppermute(evens, 'slab', pairs_of[0]))]
    all_to_all x1, blocking collectives: 13.2 us -> 12.1 us  [local(): gathered = lax.all_to_all(sums[-1], 'slab', 0, 0)]
    pallas_call x3 -> x2, Pallas kernels: 6.06 us -> 6.73 us  [the longest x1 5.21 us: local(): pl.pallas_call(functools.partial(band_kernel, cols, cols), out_shape=(sha...]
  transfers between devices with their start and end apart: 12 -> 12, of which waited for: 5 -> 5; matrix products, arithmetic and copies ran while one was open for 0% -> 0% of each run, Pallas kernels for 36% -> 32%
where the time goes in v2:
time: 71.4 us; the launch traced here: 71.2 us
  Pallas kernels  26.5 us (37%)
  starting transfers between devices  20.8 us (29%)
  blocking collectives  12.1 us (17%)
  waiting for transfers between devices  10.7 us (15%)
  between operations  1.01 us (1%)
    ppermute x6, starting transfers between devices, exchange(): ahead = lax.ppermute(odds, 'slab', pairs_of[1])  20 us
    all_to_all x1, blocking collectives, local(): gathered = lax.all_to_all(sums[-1], 'slab', 0, 0)  12.1 us
    ppermute x6, waiting for transfers between devices, exchange(): ahead = lax.ppermute(odds, 'slab', pairs_of[1])  10.3 us
    pallas_call x6, Pallas kernels, middle(): pl.pallas_call(functools.partial(middle_kernel, len(sources[chunk]), chun...  9.99 us
    pallas_call x1, Pallas kernels, local(): pl.pallas_call(functools.partial(band_kernel, cols, cols), out_shape=(sha...  5.21 us
    pallas_call x6, Pallas kernels, rims(): pl.pallas_call(functools.partial(rim_kernel, kind, chunk * cols, cols, wi...  4.77 us
    pallas_call x1, Pallas kernels, local(): pl.pallas_call(functools.partial(store_kernel, rim, cols), out_shape=(ful...  2.99 us
    pallas_call x1, Pallas kernels, local(): pl.pallas_call(functools.partial(sum_kernel, rim, cols), out_shape=(shape...  1.67 us
  transfers between devices with their start and end apart: 12, of which 5 were waited for; matrix products, arithmetic and copies ran while one was open for 0% of the time, Pallas kernels for 32%

profile of v2, /device:TPU:0, one launch (start us, length us, event | category | flops | bytes accessed | tf_op | source)
XLA Modules:
  0.0 71.2 jit_solution(5483479214953521400)
XLA Ops:
  0.6 1.5 %edges.1 = (bf16[640,256]{1,0:T(8,128)(2,1)S(1)}, bf16[640,256]{1,0:T(8,128)(2,1)S(1)}) custom-call(s32[1]{0:T(128)} %bitcast.odd, f32[2048,512]{1,0:T(8,128)} %refs_3_.3), custom_call_target="tpu_custom_call" | custom-call | bytes 1966080 | tf_op jit(solution)/shard_map/edges/pallas_call | solution.py:313
  2.2 6.7 %collective-permute-start = (bf16[640,256]{1,0:T(8,128)(2,1)S(1)}, bf16[640,256]{1,0:T(8,128)(2,1)S(1)}, u32[]{:S(2)}, u32[]{:S(2)}) collective-permute-start(bf16[640,256]{1,0:T(8,128)(2,1)S(1)} %get-tuple-element.49._), channel_id=1, source_target_pairs={{4,8},{8,4},{12,16},{16,12},{20,24},{24,20},{28,32},{32,28},{36,40... | collective-permute-start | bytes 983048 | tf_op jit(solution)/shard_map/ppermute | solution.py:256
  8.9 0.1 add_select_fusion.places
  9.0 0.0 copy-start.1
  9.0 5.2 %band.1 = (bf16[8,256,1536]{2,1,0:T(8,128)(2,1)S(1)}, bf16[640,256]{1,0:T(8,128)(2,1)S(1)}, bf16[640,256]{1,0:T(8,128)(2,1)S(1)}) custom-call(s32[1]{0:T(128)} %bitcast.odd, bf16[640,256]{1,0:T(8,128)(2,1)S(1)} %get-tuple-element.49._, s32[16,9]{1,0:T(8,128)S(1)} %add_select_fusion.places, bf16[16,9,128,128]{3,2,1,0:T(8,128)(2,1)} %blocks.1, f32[2048,512]{1,0:T(8,128)} %refs_3_.3), custom_call_target="tpu_custom_call" | custom-call | bytes 12582912 | tf_op jit(solution)/shard_map/band/pallas_call | solution.py:324
  14.2 1.4 %collective-permute-start.2 = (bf16[640,256]{1,0:T(8,128)(2,1)S(1)}, bf16[640,256]{1,0:T(8,128)(2,1)S(1)}, u32[]{:S(2)}, u32[]{:S(2)}) collective-permute-start(bf16[640,256]{1,0:T(8,128)(2,1)S(1)} %get-tuple-element.50._), channel_id=1, source_target_pairs={{4,8},{8,4},{12,16},{16,12},{20,24},{24,20},{28,32},{32,28},{36,40... | collective-permute-start | bytes 983048 | tf_op jit(solution)/shard_map/ppermute | solution.py:256
  15.7 0.8 %collective-permute-start.3 = (bf16[640,256]{1,0:T(8,128)(2,1)S(1)}, bf16[640,256]{1,0:T(8,128)(2,1)S(1)}, u32[]{:S(2)}, u32[]{:S(2)}) collective-permute-start(bf16[640,256]{1,0:T(8,128)(2,1)S(1)} %get-tuple-element.58), channel_id=1, source_target_pairs={{0,4},{4,0},{8,12},{12,8},{16,20},{20,16},{24,28},{28,24},{32,36},... | collective-permute-start | bytes 983048 | tf_op jit(solution)/shard_map/ppermute | solution.py:257
  16.4 0.3 weights.1._
  16.8 1.6 %middle.6 = (f32[2048,512]{1,0:T(8,128)S(1)}, bf16[768,256]{1,0:T(8,128)(2,1)S(1)}, f32[8,256]{1,0:T(8,128)S(1)}) custom-call(s32[1]{0:T(128)} %bitcast.odd, f32[2048,512]{1,0:T(8,128)S(1)} %weights.1._, bf16[8,256,1536]{2,1,0:T(8,128)(2,1)S(1)} %get-tuple-element.51.banded, f32[2048,512]{1,0:T(8,128)S(1)} %weights.1._, f32[2048,512]{1,0:T(8,128)S(1)} %copy-done, ...), custom_call_target="tpu_custom_call" | custom-call | flops 1207959552 | bytes 8388608 | tf_op jit(solution)/shard_map/middle/pallas_call | solution.py:268
  18.4 0.4 collective-permute-done.1.evens
  18.8 0.8 %rims.6 = (f32[2048,512]{1,0:T(8,128)S(1)}, f32[8,256]{1,0:T(8,128)S(1)}, bf16[640,256]{1,0:T(8,128)(2,1)S(1)}, bf16[640,256]{1,0:T(8,128)(2,1)S(1)}) custom-call(s32[1]{0:T(128)} %bitcast.odd, f32[8,256]{1,0:T(8,128)S(1)} %get-tuple-element.52._.partial, bf16[8,256,1536]{2,1,0:T(8,128)(2,1)S(1)} %get-tuple-element.51.banded, ...), custom_call_target="tpu_custom_call", output_to_operand_aliasing={{0}: (6, {})} | custom-call | flops 241591904 | bytes 2097152 | tf_op jit(solution)/shard_map/rims/pallas_call | solution.py:295
  19.6 4.6 %collective-permute-start.4 = (bf16[640,256]{1,0:T(8,128)(2,1)S(1)}, bf16[640,256]{1,0:T(8,128)(2,1)S(1)}, u32[]{:S(2)}, u32[]{:S(2)}) collective-permute-start(bf16[640,256]{1,0:T(8,128)(2,1)S(1)} %get-tuple-element.63.refs_2_), channel_id=1, source_target_pairs={{4,8},{8,4},{12,16},{16,12},{20,24},{24,20},{28,32},{32,28},{36,40... | collective-permute-start | bytes 983048 | tf_op jit(solution)/shard_map/ppermute | solution.py:256
  24.2 1.6 %middle.7 = (f32[2048,512]{1,0:T(8,128)S(1)}, bf16[768,256]{1,0:T(8,128)(2,1)S(1)}, f32[8,256]{1,0:T(8,128)S(1)}) custom-call(s32[1]{0:T(128)} %bitcast.odd, f32[8,256]{1,0:T(8,128)S(1)} %get-tuple-element.55._.refs_0_, bf16[8,256,1536]{2,1,0:T(8,128)(2,1)S(1)} %get-tuple-element.51.banded, ...), custom_call_target="tpu_custom_call", output_to_operand_aliasing={{0}: (6, {})} | custom-call | flops 1207959552 | bytes 8388608 | tf_op jit(solution)/shard_map/middle/pallas_call | solution.py:268
  25.9 3.3 %collective-permute-done.2.odds = bf16[640,256]{1,0:T(8,128)(2,1)S(1)} collective-permute-done((bf16[640,256]{1,0:T(8,128)(2,1)S(1)}, bf16[640,256]{1,0:T(8,128)(2,1)S(1)}, u32[]{:S(2)}, u32[]{:S(2)}) %collective-permute-start.2) | collective-permute-done | bytes 327712 | tf_op jit(solution)/shard_map/ppermute | solution.py:256
  29.2 0.8 %rims.7 = (f32[2048,512]{1,0:T(8,128)S(1)}, f32[8,256]{1,0:T(8,128)S(1)}, bf16[640,256]{1,0:T(8,128)(2,1)S(1)}, bf16[640,256]{1,0:T(8,128)(2,1)S(1)}) custom-call(s32[1]{0:T(128)} %bitcast.odd, f32[8,256]{1,0:T(8,128)S(1)} %get-tuple-element.57._.partial, bf16[8,256,1536]{2,1,0:T(8,128)(2,1)S(1)} %get-tuple-element.51.banded, ...), custom_call_target="tpu_custom_call", output_to_operand_aliasing={{0}: (6, {})} | custom-call | flops 241591904 | bytes 2097152 | tf_op jit(solution)/shard_map/rims/pallas_call | solution.py:295
  30.0 2.1 %collective-permute-start.6 = (bf16[640,256]{1,0:T(8,128)(2,1)S(1)}, bf16[640,256]{1,0:T(8,128)(2,1)S(1)}, u32[]{:S(2)}, u32[]{:S(2)}) collective-permute-start(bf16[640,256]{1,0:T(8,128)(2,1)S(1)} %get-tuple-element.69.refs_2_), channel_id=1, source_target_pairs={{4,8},{8,4},{12,16},{16,12},{20,24},{24,20},{28,32},{32,28},{36,40... | collective-permute-start | bytes 983048 | tf_op jit(solution)/shard_map/ppermute | solution.py:256
  32.1 1.7 %middle.8 = (f32[2048,512]{1,0:T(8,128)S(1)}, bf16[768,256]{1,0:T(8,128)(2,1)S(1)}, f32[8,256]{1,0:T(8,128)S(1)}) custom-call(s32[1]{0:T(128)} %bitcast.odd, f32[8,256]{1,0:T(8,128)S(1)} %get-tuple-element.60._.refs_1_, bf16[8,256,1536]{2,1,0:T(8,128)(2,1)S(1)} %get-tuple-element.51.banded, f32[2048,512]{1,0:T(8,128)S(1)} %weights.1._, ...), custom_call_target="tpu_custom_call" | custom-call | flops 1207959552 | bytes 8388608 | tf_op jit(solution)/shard_map/middle/pallas_call | solution.py:268
  33.8 1.5 %collective-permute-done.4.odds = bf16[640,256]{1,0:T(8,128)(2,1)S(1)} collective-permute-done((bf16[640,256]{1,0:T(8,128)(2,1)S(1)}, bf16[640,256]{1,0:T(8,128)(2,1)S(1)}, u32[]{:S(2)}, u32[]{:S(2)}) %collective-permute-start.4) | collective-permute-done | bytes 327712 | tf_op jit(solution)/shard_map/ppermute | solution.py:256
  35.3 0.8 %rims.8 = (f32[2048,512]{1,0:T(8,128)S(1)}, f32[8,256]{1,0:T(8,128)S(1)}, bf16[640,256]{1,0:T(8,128)(2,1)S(1)}, bf16[640,256]{1,0:T(8,128)(2,1)S(1)}) custom-call(s32[1]{0:T(128)} %bitcast.odd, f32[8,256]{1,0:T(8,128)S(1)} %get-tuple-element.64._.partial, bf16[8,256,1536]{2,1,0:T(8,128)(2,1)S(1)} %get-tuple-element.51.banded, ...), custom_call_target="tpu_custom_call", output_to_operand_aliasing={{0}: (6, {})} | custom-call | flops 241591904 | bytes 2097152 | tf_op jit(solution)/shard_map/rims/pallas_call | solution.py:295
  36.2 2.8 %collective-permute-start.8 = (bf16[640,256]{1,0:T(8,128)(2,1)S(1)}, bf16[640,256]{1,0:T(8,128)(2,1)S(1)}, u32[]{:S(2)}, u32[]{:S(2)}) collective-permute-start(bf16[640,256]{1,0:T(8,128)(2,1)S(1)} %get-tuple-element.76.refs_2_), channel_id=1, source_target_pairs={{4,8},{8,4},{12,16},{16,12},{20,24},{24,20},{28,32},{32,28},{36,40... | collective-permute-start | bytes 983048 | tf_op jit(solution)/shard_map/ppermute | solution.py:256
  39.0 1.7 %middle.9 = (f32[2048,512]{1,0:T(8,128)S(1)}, bf16[768,256]{1,0:T(8,128)(2,1)S(1)}, f32[8,256]{1,0:T(8,128)S(1)}) custom-call(s32[1]{0:T(128)} %bitcast.odd, f32[8,256]{1,0:T(8,128)S(1)} %get-tuple-element.66._.refs_2_, bf16[8,256,1536]{2,1,0:T(8,128)(2,1)S(1)} %get-tuple-element.51.banded, ...), custom_call_target="tpu_custom_call", output_to_operand_aliasing={{0}: (8, {})} | custom-call | flops 1207959552 | bytes 8388608 | tf_op jit(solution)/shard_map/middle/pallas_call | solution.py:268
  40.7 1.6 %collective-permute-done.6.odds = bf16[640,256]{1,0:T(8,128)(2,1)S(1)} collective-permute-done((bf16[640,256]{1,0:T(8,128)(2,1)S(1)}, bf16[640,256]{1,0:T(8,128)(2,1)S(1)}, u32[]{:S(2)}, u32[]{:S(2)}) %collective-permute-start.6) | collective-permute-done | bytes 327712 | tf_op jit(solution)/shard_map/ppermute | solution.py:256
  42.3 0.8 %rims.9 = (f32[2048,512]{1,0:T(8,128)S(1)}, f32[8,256]{1,0:T(8,128)S(1)}, bf16[640,256]{1,0:T(8,128)(2,1)S(1)}, bf16[640,256]{1,0:T(8,128)(2,1)S(1)}) custom-call(s32[1]{0:T(128)} %bitcast.odd, f32[8,256]{1,0:T(8,128)S(1)} %get-tuple-element.71._.partial, bf16[8,256,1536]{2,1,0:T(8,128)(2,1)S(1)} %get-tuple-element.51.banded, ...), custom_call_target="tpu_custom_call", output_to_operand_aliasing={{0}: (6, {})} | custom-call | flops 241591904 | bytes 2097152 | tf_op jit(solution)/shard_map/rims/pallas_call | solution.py:295
  43.2 2.3 %collective-permute-start.10 = (bf16[640,256]{1,0:T(8,128)(2,1)S(1)}, bf16[640,256]{1,0:T(8,128)(2,1)S(1)}, u32[]{:S(2)}, u32[]{:S(2)}) collective-permute-start(bf16[640,256]{1,0:T(8,128)(2,1)S(1)} %get-tuple-element.83.refs_2_), channel_id=1, source_target_pairs={{4,8},{8,4},{12,16},{16,12},{20,24},{24,20},{28,32},{32,28},{36,40... | collective-permute-start | bytes 983048 | tf_op jit(solution)/shard_map/ppermute | solution.py:256
  45.5 1.7 %middle.10 = (f32[2048,512]{1,0:T(8,128)S(1)}, f32[8,256]{1,0:T(8,128)S(1)}) custom-call(s32[1]{0:T(128)} %bitcast.odd, f32[8,256]{1,0:T(8,128)S(1)} %get-tuple-element.73._.refs_3_, bf16[8,256,1536]{2,1,0:T(8,128)(2,1)S(1)} %get-tuple-element.51.banded, f32[2048,512]{1,0:T(8,128)S(1)} %weights.1._, bf16[640,256]{1,0:T(8,128)(2,1)S(1)} %get-tuple-element.74.refs_0_, ...), custom_call_target="tpu_custom_call" | custom-call | flops 1207959552 | bytes 8388608 | tf_op jit(solution)/shard_map/middle/pallas_call | solution.py:268
  47.2 3.9 %collective-permute-done.8.odds = bf16[640,256]{1,0:T(8,128)(2,1)S(1)} collective-permute-done((bf16[640,256]{1,0:T(8,128)(2,1)S(1)}, bf16[640,256]{1,0:T(8,128)(2,1)S(1)}, u32[]{:S(2)}, u32[]{:S(2)}) %collective-permute-start.8) | collective-permute-done | bytes 327712 | tf_op jit(solution)/shard_map/ppermute | solution.py:256
  51.1 0.7 rims.10
  51.8 1.7 %middle.11 = (f32[2048,512]{1,0:T(8,128)S(1)}, f32[8,256]{1,0:T(8,128)S(1)}) custom-call(s32[1]{0:T(128)} %bitcast.odd, f32[8,256]{1,0:T(8,128)S(1)} %get-tuple-element.80._.refs_4_, bf16[8,256,1536]{2,1,0:T(8,128)(2,1)S(1)} %get-tuple-element.51.banded, f32[2048,512]{1,0:T(8,128)S(1)} %weights.1._, ...), custom_call_target="tpu_custom_call", output_to_operand_aliasing={{0}: (8, {})} | custom-call | flops 1207959552 | bytes 8388608 | tf_op jit(solution)/shard_map/middle/pallas_call | solution.py:268
  53.5 3.0 %store.1 = (f32[2048,512]{1,0:T(8,128)}, f32[2048,512]{1,0:T(8,128)}, f32[8,128]{1,0:T(8,128)S(1)}) custom-call(f32[8,256]{1,0:T(8,128)S(1)} %get-tuple-element.85._.partial, f32[2048,512]{1,0:T(8,128)S(1)} %get-tuple-element.86.previous, f32[2048,512]{1,0:T(8,128)S(1)} %get-tuple-element.87.current.begun), custom_call_target="tpu_custom_call" | custom-call | bytes 16777216 | tf_op jit(solution)/shard_map/store/pallas_call | solution.py:373
  56.5 0.7 %rims.11 = (f32[2048,512]{1,0:T(8,128)S(1)}, f32[32,12,128]{2,1,0:T(8,128)S(1)}) custom-call(s32[1]{0:T(128)} %bitcast.odd, f32[8,128]{1,0:T(8,128)S(1)} %get-tuple-element.89._, bf16[8,256,1536]{2,1,0:T(8,128)(2,1)S(1)} %get-tuple-element.51.banded, f32[2048,512]{1,0:T(8,128)S(1)} %weights.1._, ...), custom_call_target="tpu_custom_call", output_to_operand_aliasing={{0}: (6, {})} | custom-call | flops 241591904 | bytes 2097152 | tf_op jit(solution)/shard_map/rims/pallas_call | solution.py:295
  57.3 12.1 %all_to_all.5.parts = f32[32,12,128]{2,1,0:T(8,128)S(1)} all-to-all(f32[32,12,128]{2,1,0:T(8,128)S(1)} %get-tuple-element.90), channel_id=1, replica_groups=mesh['slab'=32,'col'=4] {'slab'}, dimensions={0} | all-to-all | bytes 393216 | tf_op jit(solution)/shard_map/all_to_all | solution.py:383
  69.4 1.7 %sums.1 = (f32[3,512]{1,0:T(4,128)}, f32[2048,512]{1,0:T(8,128)}) custom-call(f32[32,12,128]{2,1,0:T(8,128)S(1)} %all_to_all.5.parts, f32[2048,512]{1,0:T(8,128)S(1)} %get-tuple-element.91.current, f32[2048,512]{1,0:T(8,128)} %get-tuple-element.92._), custom_call_target="tpu_custom_call", output_to_operand_aliasing={{1}: (2, {})} | custom-call | tf_op jit(solution)/shard_map/sums/pallas_call | solution.py:384
  (22 shorter events, 0.1 us)
Async XLA Ops:
  0.6 8.3 %copy-start.4 = (s32[16,9]{1,0:T(8,128)S(1)}, s32[16,9]{1,0:T(8,128)}, u32[]{:S(2)}) copy-start(s32[16,9]{1,0:T(8,128)} %param.7) | copy-start | bytes 1732
  2.2 16.3 %collective-permute-start = (bf16[640,256]{1,0:T(8,128)(2,1)S(1)}, bf16[640,256]{1,0:T(8,128)(2,1)S(1)}, u32[]{:S(2)}, u32[]{:S(2)}) collective-permute-start(bf16[640,256]{1,0:T(8,128)(2,1)S(1)} %get-tuple-element.49._), channel_id=1, source_target_pairs={{4,8},{8,4},{12,16},{16,12},{20,24},{24,20},{28,32},{32,28},{36,40... | collective-permute-start | bytes 983048 | tf_op jit(solution)/shard_map/ppermute | solution.py:256
  8.9 9.9 %collective-permute-start.1 = (bf16[640,256]{1,0:T(8,128)(2,1)S(1)}, bf16[640,256]{1,0:T(8,128)(2,1)S(1)}, u32[]{:S(2)}, u32[]{:S(2)}) collective-permute-start(bf16[640,256]{1,0:T(8,128)(2,1)S(1)} %get-tuple-element.53), channel_id=1, source_target_pairs={{0,4},{4,0},{8,12},{12,8},{16,20},{20,16},{24,28},{28,24},{32,36},... | collective-permute-start | bytes 983048 | tf_op jit(solution)/shard_map/ppermute | solution.py:257
  9.0 7.4 %copy-start.2 = (bf16[2048,512]{1,0:T(8,128)(2,1)S(1)}, bf16[2048,512]{1,0:T(8,128)(2,1)}, u32[]{:S(2)}) copy-start(bf16[2048,512]{1,0:T(8,128)(2,1)} %probe.1) | copy-start | bytes 6291460
  9.0 7.4 %copy-start.3 = (f32[2048]{0:T(1024)S(1)}, f32[2048]{0:T(1024)}, u32[]{:S(2)}) copy-start(f32[2048]{0:T(1024)} %param.11) | copy-start | bytes 24580
  9.0 7.8 %copy-start.1 = (f32[2048,512]{1,0:T(8,128)S(1)}, f32[2048,512]{1,0:T(8,128)}, u32[]{:S(2)}) copy-start(f32[2048,512]{1,0:T(8,128)} %refs_1_.3) | copy-start | bytes 12582916
  14.2 2.6 %copy-start = (f32[2048,512]{1,0:T(8,128)S(1)}, f32[2048,512]{1,0:T(8,128)}, u32[]{:S(2)}) copy-start(f32[2048,512]{1,0:T(8,128)} %refs_3_.3) | copy-start | bytes 12582916
  14.2 14.9 %collective-permute-start.2 = (bf16[640,256]{1,0:T(8,128)(2,1)S(1)}, bf16[640,256]{1,0:T(8,128)(2,1)S(1)}, u32[]{:S(2)}, u32[]{:S(2)}) collective-permute-start(bf16[640,256]{1,0:T(8,128)(2,1)S(1)} %get-tuple-element.50._), channel_id=1, source_target_pairs={{4,8},{8,4},{12,16},{16,12},{20,24},{24,20},{28,32},{32,28},{36,40... | collective-permute-start | bytes 983048 | tf_op jit(solution)/shard_map/ppermute | solution.py:256
  15.7 13.5 %collective-permute-start.3 = (bf16[640,256]{1,0:T(8,128)(2,1)S(1)}, bf16[640,256]{1,0:T(8,128)(2,1)S(1)}, u32[]{:S(2)}, u32[]{:S(2)}) collective-permute-start(bf16[640,256]{1,0:T(8,128)(2,1)S(1)} %get-tuple-element.58), channel_id=1, source_target_pairs={{0,4},{4,0},{8,12},{12,8},{16,20},{20,16},{24,28},{28,24},{32,36},... | collective-permute-start | bytes 983048 | tf_op jit(solution)/shard_map/ppermute | solution.py:257
  19.6 15.7 %collective-permute-start.4 = (bf16[640,256]{1,0:T(8,128)(2,1)S(1)}, bf16[640,256]{1,0:T(8,128)(2,1)S(1)}, u32[]{:S(2)}, u32[]{:S(2)}) collective-permute-start(bf16[640,256]{1,0:T(8,128)(2,1)S(1)} %get-tuple-element.63.refs_2_), channel_id=1, source_target_pairs={{4,8},{8,4},{12,16},{16,12},{20,24},{24,20},{28,32},{32,28},{36,40... | collective-permute-start | bytes 983048 | tf_op jit(solution)/shard_map/ppermute | solution.py:256
  24.2 11.1 %collective-permute-start.5 = (bf16[640,256]{1,0:T(8,128)(2,1)S(1)}, bf16[640,256]{1,0:T(8,128)(2,1)S(1)}, u32[]{:S(2)}, u32[]{:S(2)}) collective-permute-start(bf16[640,256]{1,0:T(8,128)(2,1)S(1)} %get-tuple-element.61.refs_0_), channel_id=1, source_target_pairs={{0,4},{4,0},{8,12},{12,8},{16,20},{20,16},{24,28},{28,24},{32,36},... | collective-permute-start | bytes 983048 | tf_op jit(solution)/shard_map/ppermute | solution.py:257
  30.0 12.3 %collective-permute-start.6 = (bf16[640,256]{1,0:T(8,128)(2,1)S(1)}, bf16[640,256]{1,0:T(8,128)(2,1)S(1)}, u32[]{:S(2)}, u32[]{:S(2)}) collective-permute-start(bf16[640,256]{1,0:T(8,128)(2,1)S(1)} %get-tuple-element.69.refs_2_), channel_id=1, source_target_pairs={{4,8},{8,4},{12,16},{16,12},{20,24},{24,20},{28,32},{32,28},{36,40... | collective-permute-start | bytes 983048 | tf_op jit(solution)/shard_map/ppermute | solution.py:256
  32.1 10.2 %collective-permute-start.7 = (bf16[640,256]{1,0:T(8,128)(2,1)S(1)}, bf16[640,256]{1,0:T(8,128)(2,1)S(1)}, u32[]{:S(2)}, u32[]{:S(2)}) collective-permute-start(bf16[640,256]{1,0:T(8,128)(2,1)S(1)} %get-tuple-element.67.refs_0_), channel_id=1, source_target_pairs={{0,4},{4,0},{8,12},{12,8},{16,20},{20,16},{24,28},{28,24},{32,36},... | collective-permute-start | bytes 983048 | tf_op jit(solution)/shard_map/ppermute | solution.py:257
  36.2 14.9 %collective-permute-start.8 = (bf16[640,256]{1,0:T(8,128)(2,1)S(1)}, bf16[640,256]{1,0:T(8,128)(2,1)S(1)}, u32[]{:S(2)}, u32[]{:S(2)}) collective-permute-start(bf16[640,256]{1,0:T(8,128)(2,1)S(1)} %get-tuple-element.76.refs_2_), channel_id=1, source_target_pairs={{4,8},{8,4},{12,16},{16,12},{20,24},{24,20},{28,32},{32,28},{36,40... | collective-permute-start | bytes 983048 | tf_op jit(solution)/shard_map/ppermute | solution.py:256
  39.0 12.1 %collective-permute-start.9 = (bf16[640,256]{1,0:T(8,128)(2,1)S(1)}, bf16[640,256]{1,0:T(8,128)(2,1)S(1)}, u32[]{:S(2)}, u32[]{:S(2)}) collective-permute-start(bf16[640,256]{1,0:T(8,128)(2,1)S(1)} %get-tuple-element.74.refs_0_), channel_id=1, source_target_pairs={{0,4},{4,0},{8,12},{12,8},{16,20},{20,16},{24,28},{28,24},{32,36},... | collective-permute-start | bytes 983048 | tf_op jit(solution)/shard_map/ppermute | solution.py:257
  43.2 13.4 %collective-permute-start.10 = (bf16[640,256]{1,0:T(8,128)(2,1)S(1)}, bf16[640,256]{1,0:T(8,128)(2,1)S(1)}, u32[]{:S(2)}, u32[]{:S(2)}) collective-permute-start(bf16[640,256]{1,0:T(8,128)(2,1)S(1)} %get-tuple-element.83.refs_2_), channel_id=1, source_target_pairs={{4,8},{8,4},{12,16},{16,12},{20,24},{24,20},{28,32},{32,28},{36,40... | collective-permute-start | bytes 983048 | tf_op jit(solution)/shard_map/ppermute | solution.py:256
  45.5 11.0 %collective-permute-start.11 = (bf16[640,256]{1,0:T(8,128)(2,1)S(1)}, bf16[640,256]{1,0:T(8,128)(2,1)S(1)}, u32[]{:S(2)}, u32[]{:S(2)}) collective-permute-start(bf16[640,256]{1,0:T(8,128)(2,1)S(1)} %get-tuple-element.81.refs_0_), channel_id=1, source_target_pairs={{0,4},{4,0},{8,12},{12,8},{16,20},{20,16},{24,28},{28,24},{32,36},... | collective-permute-start | bytes 983048 | tf_op jit(solution)/shard_map/ppermute | solution.py:257

commit v3 on v2

--- a/solution.py
+++ b/solution.py
@@ -24,13 +24,12 @@
     return pl.CostEstimate(flops=flops, bytes_accessed=moved, transcendentals=0)
 
 
-def hand_out(odd, rims, evens, odds):
+def hand_out(odd, take, evens, odds):
     for parity in range(2):
 
         @pl.when(odd[0] == parity)
         def _():
-            evens[...] = rims[1 - parity].astype(BF16)
-            odds[...] = rims[parity].astype(BF16)
+            take((odds, evens) if parity == 0 else (evens, odds))
 
 
 def pick(odd, side, pairs, at):
@@ -54,18 +53,24 @@
     ]
     for copy in copies:
         copy.start()
-    return copies
+
+    def take(targets):
+        for k, copy in enumerate(copies):
+            side, i = divmod(k, sems.shape[1])
+            here = slice(i * piece, (i + 1) * piece)
+            copy.wait()
+            targets[side][here] = held[side, here].astype(BF16)
+
+    return take
 
 
 def edge_kernel(first, cols, odd, current, evens, odds, held, sems):
-    for copy in fetch_rims(current, first, cols, held, sems):
-        copy.wait()
-    hand_out(odd, held, evens, odds)
+    hand_out(odd, fetch_rims(current, first, cols, held, sems), evens, odds)
 
 
 def band_kernel(first, cols, odd, _, places, blocks, current, banded, evens, odds, held, sems, rims, rim_sems):
     rows_blk, slots, width, _ = blocks.shape
-    copies = fetch_rims(current, first, cols, rims, rim_sems)
+    take = fetch_rims(current, first, cols, rims, rim_sems)
 
     def fetch(pair):
         two = pl.ds(2 * pair, 2)
@@ -73,9 +78,7 @@
 
     for pair in range(rows_blk // 2):
         fetch(pair).start()
-    for copy in copies:
-        copy.wait()
-    hand_out(odd, rims, evens, odds)
+    hand_out(odd, take, evens, odds)
 
     def one_pair(pair, _):
         banded[pair] = jnp.zeros(banded.shape[1:], BF16)
@@ -148,88 +151,101 @@
     parts = []
     for pair in range(rows_blk // 2):
         start = 2 * pair - BAND
-        if 2 * pair < BAND:
-            parts.append((0, pair, 0, min(2, BAND - 2 * pair), 0, -start, BAND + start))
-    for pair in range(rows_blk // 2):
-        start = 2 * pair - BAND
         first = max(2 * pair, rows_blk - BAND)
         if first < 2 * pair + 2:
             parts.append((1, pair, first - 2 * pair, 2, rows_blk - start, 2 * BAND + 2, 0))
+    for pair in range(rows_blk // 2):
+        start = 2 * pair - BAND
+        if 2 * pair < BAND:
+            parts.append((0, pair, 0, min(2, BAND - 2 * pair), 0, -start, BAND + start))
     return parts
 
 
-def rim_kernel(kind, first, cols, width, rows_blk, odd, _, banded, weights, odds, evens, begun, partial, *refs):
-    earlier = refs[: TERMS * CHUNKS - 1] if kind == "final" else ()
-    upcoming, moments = refs[len(earlier) : len(earlier) + 2]
-    sent = refs[len(earlier) + 2 :]
+def rim_sums(first, cols, width, rows_blk, odd, banded, weights, evens, odds, begun, partial, keep):
     columns = pl.ds(first, cols)
-    rim = BAND * width
-    rows = rows_blk * width
     total = partial[...]
-    for side, pair, a, b, left, right, at in rim_parts(rows_blk):
+    for part, (side, pair, a, b, left, right, at) in enumerate(rim_parts(rows_blk)):
         product = jnp.dot(
             banded[pair, a * width : b * width, left * width : right * width],
             pick(odd, side, (evens, odds), slice(at * width, (at + right - left) * width)),
             preferred_element_type=F32,
         )
-        top = (2 * pair + a) * width
-        here = pl.ds(top, (b - a) * width)
+        here = pl.ds((2 * pair + a) * width, (b - a) * width)
         result = begun[here, columns] + 2.0 * product
+        keep(part, side, here, columns, result)
+        total = total + fold(result * weights[here, columns])
+    return total
+
+
+def rim_kernel(first, cols, width, rows_blk, odd, _, banded, weights, odds_in, evens_in, begun, partial, *refs):
+    upcoming, moments, evens, odds, rims = refs
+    rim = rims.shape[1]
+    rows = rows_blk * width
+
+    def keep(part, side, here, columns, result):
         upcoming[here, columns] = result
-        if sent:
-            base = top - (0 if side == 0 else rows - rim)
-            sent[2][side, base : base + (b - a) * width] = result.astype(BF16)
-        total = total + fold(result * weights[here, columns])
-    if sent:
-        hand_out(odd, sent[2], *sent[:2])
-    if kind == "final":
-        lanes = moments.shape[2]
-        parts = []
-        for one in [*(ref[...] for ref in earlier), total]:
-            one = jnp.sum(one, axis=0, keepdims=True)
-            parts += [one[:, j * lanes : (j + 1) * lanes] for j in range(cols // lanes)]
-        moments[...] = jnp.broadcast_to(jnp.concatenate(parts, axis=0)[None], moments.shape)
+        base = here.start - (0 if side == 0 else rows - rim)
+        rims[side, base : base + here.size] = result.astype(BF16)
+
+    moments[...] = rim_sums(
+        first, cols, width, rows_blk, odd, banded, weights, evens_in, odds_in, begun, partial, keep
+    )
+
+    def take(targets):
+        for side in range(2):
+            targets[side][...] = rims[side]
+
+    hand_out(odd, take, evens, odds)
+
+
+def last_rim_kernel(count, first, cols, width, rows_blk, odd, _, banded, weights, odds_in, evens_in, begun, partial, *refs):
+    earlier, (out, moments, *tail, held, sems) = refs[:count], refs[count + 1 :]
+    copies = []
+
+    def keep(part, side, here, columns, result):
+        if tail and part == len(rim_parts(rows_blk)) - 1:
+            tail[0][...] = result
+            return
+        slot = held.at[part, pl.ds(0, here.size)]
+        slot[...] = result
+        copies.append(pltpu.make_async_copy(slot, out.at[here, columns], sems.at[part]))
+        copies[-1].start()
+
+    total = rim_sums(
+        first, cols, width, rows_blk, odd, banded, weights, evens_in, odds_in, begun, partial, keep
+    )
+    if tail:
+        parts = [jnp.sum(one, axis=0, keepdims=True) for one in [*(ref[...] for ref in earlier), total]]
+        row = jnp.concatenate(parts, axis=1)
+        for slab in range(moments.shape[0]):
+            moments[slab] = row
     else:
         moments[...] = total
-
-
-def copies_of(parts, source, target, sems):
+    for copy in copies:
+        copy.wait()
+
+
+def store_kernel(rim, _, previous, current, out_previous, out_current, sems):
+    inside = pl.ds(rim, current.shape[0] - 2 * rim)
     copies = [
-        pltpu.make_async_copy(source.at[part], target.at[part], sems.at[i])
-        for i, part in enumerate(parts)
+        pltpu.make_async_copy(previous, out_previous, sems.at[0]),
+        pltpu.make_async_copy(current.at[inside], out_current.at[inside], sems.at[1]),
     ]
     for copy in copies:
         copy.start()
-    return copies
-
-
-def store_kernel(rim, cols, _, previous, current, out_previous, out_current, done, whole_sem, sems):
-    rows, all_cols = current.shape
-    held = all_cols - cols
-    parts = [
-        (pl.ds(0, rows), pl.ds(0, held)),
-        (pl.ds(rim, rows - 2 * rim), pl.ds(held, cols)),
-    ]
-    copies = copies_of(parts, current, out_current, sems)
-    copies += copies_of([pl.ds(0, rows)], previous, out_previous, whole_sem)
-    done[...] = jnp.zeros(done.shape, F32)
     for copy in copies:
         copy.wait()
 
 
-def sum_kernel(rim, cols, parts, current, _, out, out_current, sems):
-    rows, all_cols = current.shape
-    columns = pl.ds(all_cols - cols, cols)
-    rims = [(pl.ds(0, rim), columns), (pl.ds(rows - rim, rim), columns)]
-    copies = copies_of(rims, current, out_current, sems)
-    lanes = parts.shape[2]
+def sum_kernel(top, first, parts, tail, _, out, out_current, sem):
+    rows, cols = tail.shape
+    copy = pltpu.make_async_copy(tail, out_current.at[pl.ds(top, rows), pl.ds(first, cols)], sem)
+    copy.start()
     total = jnp.sum(parts[...], axis=0)
-    each = out.shape[1] // lanes
+    every = out.shape[1]
     for term in range(out.shape[0]):
-        for j in range(each):
-            out[term : term + 1, j * lanes : (j + 1) * lanes] = total[term * each + j][None]
-    for copy in copies:
-        copy.wait()
+        out[term : term + 1] = total[:, term * every : (term + 1) * every]
+    copy.wait()
 
 
 def in_hbm(x):
@@ -281,24 +297,36 @@
 
     def rims(token, term, chunk):
         args = [odd, token, banded, weights, *halos[chunk], terms[term + 2], begun[chunk][-1]]
-        kind = "inner"
-        outs = (full_shape, part_shape, edge_shape, edge_shape)
-        scratch = [pltpu.VMEM((2, rim, cols), BF16)]
-        if term == TERMS - 1:
-            kind = "last"
-            scratch = []
+        specs = [SMEM] + [VMEM] * (len(args) - 1)
+        bound = (chunk * cols, cols, width, rows_blk)
+        if term < TERMS - 1:
+            kernel = functools.partial(rim_kernel, *bound)
+            outs = (full_shape, part_shape, edge_shape, edge_shape)
+            out_specs = (VMEM,) * 4
+            scratch = [pltpu.VMEM((2, rim, cols), BF16)]
+            aliases = {6: 0}
+        else:
+            final = chunk == CHUNKS - 1
+            if final:
+                args += sums
+                specs += [VMEM] * len(sums)
+            kernel = functools.partial(last_rim_kernel, len(sums) if final else 0, *bound)
+            aliases = {len(args): 0}
+            args.append(outputs[1])
+            specs.append(HBM)
             outs = (full_shape, part_shape)
-            if chunk == CHUNKS - 1:
-                kind = "final"
-                args += sums
-                outs = (full_shape, shape((slabs, TERMS * all_cols // 128, 128), F32))
+            if final:
+                outs = (full_shape, shape((slabs, 1, TERMS * all_cols), F32), shape((tail, cols), F32))
+            out_specs = (HBM,) + (VMEM,) * (len(outs) - 1)
+            count = len(rim_parts(rows_blk))
+            scratch = [pltpu.VMEM((count, 2 * width, cols), F32), pltpu.SemaphoreType.DMA((count,))]
         return pl.pallas_call(
-            functools.partial(rim_kernel, kind, chunk * cols, cols, width, rows_blk),
+            kernel,
             out_shape=outs,
-            in_specs=[SMEM] + [VMEM] * (len(args) - 1),
-            out_specs=(VMEM,) * len(outs),
+            in_specs=specs,
+            out_specs=out_specs,
             scratch_shapes=scratch,
-            input_output_aliases={6: 0},
+            input_output_aliases=aliases,
             compiler_params=params(),
             cost_estimate=cost(flops // 5, 2 * 1024 * 1024),
             name="rims",
@@ -355,6 +383,10 @@
     begun = [None] * CHUNKS
     sums = []
     order = [(term, chunk) for term in range(TERMS) for chunk in range(CHUNKS)]
+    ahead = len(order) - CHUNKS
+    _, pair, low, high, *_ = rim_parts(rows_blk)[-1]
+    top, tail = (2 * pair + low) * width, (high - low) * width
+    outputs = None
 
     def begin(token, term, chunk):
         terms[term + 2], *begun[chunk] = middle(token, term, chunk)
@@ -362,36 +394,41 @@
 
     token = begin(weights, *order[0])
     for step, (term, chunk) in enumerate(order):
-        terms[term + 2], token, *sent = rims(token, term, chunk)
-        if sent:
+        if step < ahead:
+            terms[term + 2], token, *sent = rims(token, term, chunk)
             halos[chunk] = exchange(*sent)
             sources[chunk] = (sent[0], begun[chunk][0], sent[1])
+        else:
+            last_current, token, *ends = rims(token, term, chunk)
+            outputs = (outputs[0], last_current)
         sums.append(token)
-        if step + 1 < len(order):
+        if step + 1 < ahead:
             token = begin(token, *order[step + 1])
-        if step + 2 == len(order):
-            last_previous, last_current, token = pl.pallas_call(
-                functools.partial(store_kernel, rim, cols),
-                out_shape=(full_shape, full_shape, shape((8, 128), F32)),
+        elif step + 1 == ahead:
+            for item in order[ahead:]:
+                token = begin(token, *item)
+            outputs = pl.pallas_call(
+                functools.partial(store_kernel, rim),
+                out_shape=(full_shape, full_shape),
                 in_specs=[VMEM] * 3,
-                out_specs=(HBM, HBM, VMEM),
-                scratch_shapes=[pltpu.SemaphoreType.DMA((1,)), pltpu.SemaphoreType.DMA((2,))],
+                out_specs=(HBM, HBM),
+                scratch_shapes=[pltpu.SemaphoreType.DMA((2,))],
                 compiler_params=params(),
                 cost_estimate=cost(0, 16 * 1024 * 1024),
                 name="store",
             )(token, terms[-2], terms[-1])
     gathered = lax.all_to_all(sums[-1], "slab", 0, 0)
     moments, last_current = pl.pallas_call(
-        functools.partial(sum_kernel, rim, cols),
+        functools.partial(sum_kernel, top, all_cols - cols),
         out_shape=(shape((TERMS, all_cols), F32), full_shape),
         in_specs=[VMEM, VMEM, HBM],
         out_specs=(VMEM, HBM),
-        scratch_shapes=[pltpu.SemaphoreType.DMA((2,))],
+        scratch_shapes=[pltpu.SemaphoreType.DMA],
         input_output_aliases={2: 1},
         compiler_params=params(),
         name="sums",
-    )(gathered, terms[-1], last_current)
-    return last_previous, last_current, moments
+    )(gathered, ends[0], outputs[1])
+    return outputs[0], last_current, moments
 
 
 def solution(mesh):

time: 71.4 us -> 71.4 us (level)
    ppermute x6, waiting for transfers between devices: 10.3 us -> 9.55 us  [exchange(): ahead = lax.ppermute(odds, 'slab', pairs_of[1])]
  transfers between devices with their start and end apart: 12 -> 12, of which waited for: 5 -> 5; matrix products, arithmetic and copies ran while one was open for 0% -> 0% of each run, Pallas kernels for 32% -> 31%
where the time goes in v3:
time: 71.4 us; the launch traced here: 71.3 us
  Pallas kernels  26.5 us (37%)
  starting transfers between devices  20.8 us (29%)
  blocking collectives  12.8 us (18%)
  waiting for transfers between devices  10 us (14%)
  between operations  1.02 us (1%)
    ppermute x6, starting transfers between devices, exchange(): ahead = lax.ppermute(odds, 'slab', pairs_of[1])  20 us
    all_to_all x1, blocking collectives, local(): gathered = lax.all_to_all(sums[-1], 'slab', 0, 0)  12.8 us
    pallas_call x6, Pallas kernels, middle(): pl.pallas_call(functools.partial(middle_kernel, len(sources[chunk]), chun...  9.99 us
    ppermute x6, waiting for transfers between devices, exchange(): ahead = lax.ppermute(odds, 'slab', pairs_of[1])  9.55 us
    pallas_call x6, Pallas kernels, rims(): pl.pallas_call(kernel, out_shape=outs, in_specs=specs, out_specs=out_spec...  5.8 us
    pallas_call x1, Pallas kernels, local(): pl.pallas_call(functools.partial(band_kernel, cols, cols), out_shape=(sha...  5.14 us
    pallas_call x1, Pallas kernels, local(): pl.pallas_call(functools.partial(store_kernel, rim), out_shape=(full_shap...  2.54 us
    pallas_call x1, Pallas kernels, local(): pl.pallas_call(functools.partial(edge_kernel, 0, cols), out_shape=(edge_s...  1.46 us
  transfers between devices with their start and end apart: 12, of which 5 were waited for; matrix products, arithmetic and copies ran while one was open for 0% of the time, Pallas kernels for 31%

profile of v3, /device:TPU:0, one launch (start us, length us, event | category | flops | bytes accessed | tf_op | source)
XLA Modules:
  0.0 71.3 jit_solution(12086630503498820237)
XLA Ops:
  0.6 1.5 %edges.1 = (bf16[640,256]{1,0:T(8,128)(2,1)S(1)}, bf16[640,256]{1,0:T(8,128)(2,1)S(1)}) custom-call(s32[1]{0:T(128)} %bitcast.odd, f32[2048,512]{1,0:T(8,128)} %refs_3_.3), custom_call_target="tpu_custom_call" | custom-call | bytes 1966080 | tf_op jit(solution)/shard_map/edges/pallas_call | solution.py:341
  2.1 6.7 %collective-permute-start = (bf16[640,256]{1,0:T(8,128)(2,1)S(1)}, bf16[640,256]{1,0:T(8,128)(2,1)S(1)}, u32[]{:S(2)}, u32[]{:S(2)}) collective-permute-start(bf16[640,256]{1,0:T(8,128)(2,1)S(1)} %get-tuple-element.49._), channel_id=1, source_target_pairs={{4,8},{8,4},{12,16},{16,12},{20,24},{24,20},{28,32},{32,28},{36,40... | collective-permute-start | bytes 983048 | tf_op jit(solution)/shard_map/ppermute | solution.py:272
  8.8 0.1 add_select_fusion.places
  8.9 0.0 copy-start.3
  9.0 5.1 %band.1 = (bf16[8,256,1536]{2,1,0:T(8,128)(2,1)S(1)}, bf16[640,256]{1,0:T(8,128)(2,1)S(1)}, bf16[640,256]{1,0:T(8,128)(2,1)S(1)}) custom-call(s32[1]{0:T(128)} %bitcast.odd, bf16[640,256]{1,0:T(8,128)(2,1)S(1)} %get-tuple-element.49._, s32[16,9]{1,0:T(8,128)S(1)} %add_select_fusion.places, bf16[16,9,128,128]{3,2,1,0:T(8,128)(2,1)} %blocks.1, f32[2048,512]{1,0:T(8,128)} %refs_3_.3), custom_call_target="tpu_custom_call" | custom-call | bytes 12582912 | tf_op jit(solution)/shard_map/band/pallas_call | solution.py:352
  14.1 1.4 %collective-permute-start.2 = (bf16[640,256]{1,0:T(8,128)(2,1)S(1)}, bf16[640,256]{1,0:T(8,128)(2,1)S(1)}, u32[]{:S(2)}, u32[]{:S(2)}) collective-permute-start(bf16[640,256]{1,0:T(8,128)(2,1)S(1)} %get-tuple-element.50._), channel_id=1, source_target_pairs={{4,8},{8,4},{12,16},{16,12},{20,24},{24,20},{28,32},{32,28},{36,40... | collective-permute-start | bytes 983048 | tf_op jit(solution)/shard_map/ppermute | solution.py:272
  15.6 0.8 %collective-permute-start.3 = (bf16[640,256]{1,0:T(8,128)(2,1)S(1)}, bf16[640,256]{1,0:T(8,128)(2,1)S(1)}, u32[]{:S(2)}, u32[]{:S(2)}) collective-permute-start(bf16[640,256]{1,0:T(8,128)(2,1)S(1)} %get-tuple-element.58), channel_id=1, source_target_pairs={{0,4},{4,0},{8,12},{12,8},{16,20},{20,16},{24,28},{28,24},{32,36},... | collective-permute-start | bytes 983048 | tf_op jit(solution)/shard_map/ppermute | solution.py:273
  16.3 0.3 weights.1._
  16.7 1.6 %middle.6 = (f32[2048,512]{1,0:T(8,128)S(1)}, bf16[768,256]{1,0:T(8,128)(2,1)S(1)}, f32[8,256]{1,0:T(8,128)S(1)}) custom-call(s32[1]{0:T(128)} %bitcast.odd, f32[2048,512]{1,0:T(8,128)S(1)} %weights.1._, bf16[8,256,1536]{2,1,0:T(8,128)(2,1)S(1)} %get-tuple-element.51.banded, f32[2048,512]{1,0:T(8,128)S(1)} %weights.1._, f32[2048,512]{1,0:T(8,128)S(1)} %copy-done, ...), custom_call_target="tpu_custom_call" | custom-call | flops 1207959552 | bytes 8388608 | tf_op jit(solution)/shard_map/middle/pallas_call | solution.py:284
  18.3 0.5 collective-permute-done.1.evens_in
  18.8 0.8 %rims.6 = (f32[2048,512]{1,0:T(8,128)S(1)}, f32[8,256]{1,0:T(8,128)S(1)}, bf16[640,256]{1,0:T(8,128)(2,1)S(1)}, bf16[640,256]{1,0:T(8,128)(2,1)S(1)}) custom-call(s32[1]{0:T(128)} %bitcast.odd, f32[8,256]{1,0:T(8,128)S(1)} %get-tuple-element.52._.partial, bf16[8,256,1536]{2,1,0:T(8,128)(2,1)S(1)} %get-tuple-element.51.banded, ...), custom_call_target="tpu_custom_call", output_to_operand_aliasing={{0}: (6, {})} | custom-call | flops 241591904 | bytes 2097152 | tf_op jit(solution)/shard_map/rims/pallas_call | solution.py:323
  19.6 4.6 %collective-permute-start.4 = (bf16[640,256]{1,0:T(8,128)(2,1)S(1)}, bf16[640,256]{1,0:T(8,128)(2,1)S(1)}, u32[]{:S(2)}, u32[]{:S(2)}) collective-permute-start(bf16[640,256]{1,0:T(8,128)(2,1)S(1)} %get-tuple-element.63.refs_2_), channel_id=1, source_target_pairs={{4,8},{8,4},{12,16},{16,12},{20,24},{24,20},{28,32},{32,28},{36,40... | collective-permute-start | bytes 983048 | tf_op jit(solution)/shard_map/ppermute | solution.py:272
  24.2 1.6 %middle.7 = (f32[2048,512]{1,0:T(8,128)S(1)}, bf16[768,256]{1,0:T(8,128)(2,1)S(1)}, f32[8,256]{1,0:T(8,128)S(1)}) custom-call(s32[1]{0:T(128)} %bitcast.odd, f32[8,256]{1,0:T(8,128)S(1)} %get-tuple-element.55._.refs_0_, bf16[8,256,1536]{2,1,0:T(8,128)(2,1)S(1)} %get-tuple-element.51.banded, ...), custom_call_target="tpu_custom_call", output_to_operand_aliasing={{0}: (6, {})} | custom-call | flops 1207959552 | bytes 8388608 | tf_op jit(solution)/shard_map/middle/pallas_call | solution.py:284
  25.8 3.3 %collective-permute-done.2.odds_in = bf16[640,256]{1,0:T(8,128)(2,1)S(1)} collective-permute-done((bf16[640,256]{1,0:T(8,128)(2,1)S(1)}, bf16[640,256]{1,0:T(8,128)(2,1)S(1)}, u32[]{:S(2)}, u32[]{:S(2)}) %collective-permute-start.2) | collective-permute-done | bytes 327712 | tf_op jit(solution)/shard_map/ppermute | solution.py:272
  29.1 0.8 %rims.7 = (f32[2048,512]{1,0:T(8,128)S(1)}, f32[8,256]{1,0:T(8,128)S(1)}, bf16[640,256]{1,0:T(8,128)(2,1)S(1)}, bf16[640,256]{1,0:T(8,128)(2,1)S(1)}) custom-call(s32[1]{0:T(128)} %bitcast.odd, f32[8,256]{1,0:T(8,128)S(1)} %get-tuple-element.57._.partial, bf16[8,256,1536]{2,1,0:T(8,128)(2,1)S(1)} %get-tuple-element.51.banded, ...), custom_call_target="tpu_custom_call", output_to_operand_aliasing={{0}: (6, {})} | custom-call | flops 241591904 | bytes 2097152 | tf_op jit(solution)/shard_map/rims/pallas_call | solution.py:323
  29.8 2.1 %collective-permute-start.6 = (bf16[640,256]{1,0:T(8,128)(2,1)S(1)}, bf16[640,256]{1,0:T(8,128)(2,1)S(1)}, u32[]{:S(2)}, u32[]{:S(2)}) collective-permute-start(bf16[640,256]{1,0:T(8,128)(2,1)S(1)} %get-tuple-element.69.refs_2_), channel_id=1, source_target_pairs={{4,8},{8,4},{12,16},{16,12},{20,24},{24,20},{28,32},{32,28},{36,40... | collective-permute-start | bytes 983048 | tf_op jit(solution)/shard_map/ppermute | solution.py:272
  31.9 1.7 %middle.8 = (f32[2048,512]{1,0:T(8,128)S(1)}, bf16[768,256]{1,0:T(8,128)(2,1)S(1)}, f32[8,256]{1,0:T(8,128)S(1)}) custom-call(s32[1]{0:T(128)} %bitcast.odd, f32[8,256]{1,0:T(8,128)S(1)} %get-tuple-element.60._.refs_1_, bf16[8,256,1536]{2,1,0:T(8,128)(2,1)S(1)} %get-tuple-element.51.banded, f32[2048,512]{1,0:T(8,128)S(1)} %weights.1._, ...), custom_call_target="tpu_custom_call" | custom-call | flops 1207959552 | bytes 8388608 | tf_op jit(solution)/shard_map/middle/pallas_call | solution.py:284
  33.6 1.6 %collective-permute-done.4.odds_in = bf16[640,256]{1,0:T(8,128)(2,1)S(1)} collective-permute-done((bf16[640,256]{1,0:T(8,128)(2,1)S(1)}, bf16[640,256]{1,0:T(8,128)(2,1)S(1)}, u32[]{:S(2)}, u32[]{:S(2)}) %collective-permute-start.4) | collective-permute-done | bytes 327712 | tf_op jit(solution)/shard_map/ppermute | solution.py:272
  35.3 0.8 %rims.8 = (f32[2048,512]{1,0:T(8,128)S(1)}, f32[8,256]{1,0:T(8,128)S(1)}, bf16[640,256]{1,0:T(8,128)(2,1)S(1)}, bf16[640,256]{1,0:T(8,128)(2,1)S(1)}) custom-call(s32[1]{0:T(128)} %bitcast.odd, f32[8,256]{1,0:T(8,128)S(1)} %get-tuple-element.64._.partial, bf16[8,256,1536]{2,1,0:T(8,128)(2,1)S(1)} %get-tuple-element.51.banded, ...), custom_call_target="tpu_custom_call", output_to_operand_aliasing={{0}: (6, {})} | custom-call | flops 241591904 | bytes 2097152 | tf_op jit(solution)/shard_map/rims/pallas_call | solution.py:323
  36.0 2.7 %collective-permute-start.8 = (bf16[640,256]{1,0:T(8,128)(2,1)S(1)}, bf16[640,256]{1,0:T(8,128)(2,1)S(1)}, u32[]{:S(2)}, u32[]{:S(2)}) collective-permute-start(bf16[640,256]{1,0:T(8,128)(2,1)S(1)} %get-tuple-element.76.refs_2_), channel_id=1, source_target_pairs={{4,8},{8,4},{12,16},{16,12},{20,24},{24,20},{28,32},{32,28},{36,40... | collective-permute-start | bytes 983048 | tf_op jit(solution)/shard_map/ppermute | solution.py:272
  38.7 1.7 %middle.9 = (f32[2048,512]{1,0:T(8,128)S(1)}, bf16[768,256]{1,0:T(8,128)(2,1)S(1)}, f32[8,256]{1,0:T(8,128)S(1)}) custom-call(s32[1]{0:T(128)} %bitcast.odd, f32[8,256]{1,0:T(8,128)S(1)} %get-tuple-element.66._.refs_2_, bf16[8,256,1536]{2,1,0:T(8,128)(2,1)S(1)} %get-tuple-element.51.banded, ...), custom_call_target="tpu_custom_call", output_to_operand_aliasing={{0}: (8, {})} | custom-call | flops 1207959552 | bytes 8388608 | tf_op jit(solution)/shard_map/middle/pallas_call | solution.py:284
  40.4 1.9 %collective-permute-done.6.odds_in = bf16[640,256]{1,0:T(8,128)(2,1)S(1)} collective-permute-done((bf16[640,256]{1,0:T(8,128)(2,1)S(1)}, bf16[640,256]{1,0:T(8,128)(2,1)S(1)}, u32[]{:S(2)}, u32[]{:S(2)}) %collective-permute-start.6) | collective-permute-done | bytes 327712 | tf_op jit(solution)/shard_map/ppermute | solution.py:272
  42.3 0.8 %rims.9 = (f32[2048,512]{1,0:T(8,128)S(1)}, f32[8,256]{1,0:T(8,128)S(1)}, bf16[640,256]{1,0:T(8,128)(2,1)S(1)}, bf16[640,256]{1,0:T(8,128)(2,1)S(1)}) custom-call(s32[1]{0:T(128)} %bitcast.odd, f32[8,256]{1,0:T(8,128)S(1)} %get-tuple-element.71._.partial, bf16[8,256,1536]{2,1,0:T(8,128)(2,1)S(1)} %get-tuple-element.51.banded, ...), custom_call_target="tpu_custom_call", output_to_operand_aliasing={{0}: (6, {})} | custom-call | flops 241591904 | bytes 2097152 | tf_op jit(solution)/shard_map/rims/pallas_call | solution.py:323
  43.1 2.4 %collective-permute-start.10 = (bf16[640,256]{1,0:T(8,128)(2,1)S(1)}, bf16[640,256]{1,0:T(8,128)(2,1)S(1)}, u32[]{:S(2)}, u32[]{:S(2)}) collective-permute-start(bf16[640,256]{1,0:T(8,128)(2,1)S(1)} %get-tuple-element.81.refs_2_), channel_id=1, source_target_pairs={{4,8},{8,4},{12,16},{16,12},{20,24},{24,20},{28,32},{32,28},{36,40... | collective-permute-start | bytes 983048 | tf_op jit(solution)/shard_map/ppermute | solution.py:272
  45.5 1.7 %middle.10 = (f32[2048,512]{1,0:T(8,128)S(1)}, f32[8,256]{1,0:T(8,128)S(1)}) custom-call(s32[1]{0:T(128)} %bitcast.odd, f32[8,256]{1,0:T(8,128)S(1)} %get-tuple-element.73._.refs_3_, bf16[8,256,1536]{2,1,0:T(8,128)(2,1)S(1)} %get-tuple-element.51.banded, f32[2048,512]{1,0:T(8,128)S(1)} %weights.1._, bf16[640,256]{1,0:T(8,128)(2,1)S(1)} %get-tuple-element.74.refs_0_, ...), custom_call_target="tpu_custom_call" | custom-call | flops 1207959552 | bytes 8388608 | tf_op jit(solution)/shard_map/middle/pallas_call | solution.py:284
  47.2 1.7 %middle.11 = (f32[2048,512]{1,0:T(8,128)S(1)}, f32[8,256]{1,0:T(8,128)S(1)}) custom-call(s32[1]{0:T(128)} %bitcast.odd, f32[8,256]{1,0:T(8,128)S(1)} %get-tuple-element.78._.partial, bf16[8,256,1536]{2,1,0:T(8,128)(2,1)S(1)} %get-tuple-element.51.banded, f32[2048,512]{1,0:T(8,128)S(1)} %weights.1._, ...), custom_call_target="tpu_custom_call", output_to_operand_aliasing={{0}: (8, {})} | custom-call | flops 1207959552 | bytes 8388608 | tf_op jit(solution)/shard_map/middle/pallas_call | solution.py:284
  48.9 2.5 %store.1 = (f32[2048,512]{1,0:T(8,128)}, f32[2048,512]{1,0:T(8,128)}) custom-call(f32[8,256]{1,0:T(8,128)S(1)} %get-tuple-element.83._.partial, f32[2048,512]{1,0:T(8,128)S(1)} %get-tuple-element.84.previous, f32[2048,512]{1,0:T(8,128)S(1)} %get-tuple-element.85.current.begun), custom_call_target="tpu_custom_call" | custom-call | bytes 16777216 | tf_op jit(solution)/shard_map/store/pallas_call | solution.py:410
  51.5 1.4 %rims.10 = (f32[2048,512]{1,0:T(8,128)}, f32[8,256]{1,0:T(8,128)S(1)}) custom-call(s32[1]{0:T(128)} %bitcast.odd, f32[8,256]{1,0:T(8,128)S(1)} %get-tuple-element.83._.partial, bf16[8,256,1536]{2,1,0:T(8,128)(2,1)S(1)} %get-tuple-element.51.banded, f32[2048,512]{1,0:T(8,128)S(1)} %weights.1._, ...), custom_call_target="tpu_custom_call", output_to_operand_aliasing={{0}: (8, {})} | custom-call | flops 241591904 | bytes 2097152 | tf_op jit(solution)/shard_map/rims/pallas_call | solution.py:323
  52.9 2.8 %collective-permute-done.10.odds_in = bf16[640,256]{1,0:T(8,128)(2,1)S(1)} collective-permute-done((bf16[640,256]{1,0:T(8,128)(2,1)S(1)}, bf16[640,256]{1,0:T(8,128)(2,1)S(1)}, u32[]{:S(2)}, u32[]{:S(2)}) %collective-permute-start.10) | collective-permute-done | bytes 327712 | tf_op jit(solution)/shard_map/ppermute | solution.py:272
  55.7 1.4 %rims.11 = (f32[2048,512]{1,0:T(8,128)}, f32[32,1,1536]{2,1,0:T(1,128)S(1)}, f32[128,256]{1,0:T(8,128)S(1)}) custom-call(s32[1]{0:T(128)} %bitcast.odd, f32[8,256]{1,0:T(8,128)S(1)} %get-tuple-element.88._.refs_4_, bf16[8,256,1536]{2,1,0:T(8,128)(2,1)S(1)} %get-tuple-element.51.banded, f32[2048,512]{1,0:T(8,128)S(1)} %weights.1._, ...), custom_call_target="tpu_custom_call", output_to_operand_aliasing={{0}: (13, {})} | custom-call | flops 241591904 | bytes 2097152 | tf_op jit(solution)/shard_map/rims/pallas_call | solution.py:323
  57.0 12.8 %all_to_all.5.parts = f32[32,1,1536]{2,1,0:T(1,128)S(1)} all-to-all(f32[32,1,1536]{2,1,0:T(1,128)S(1)} %get-tuple-element.90), channel_id=1, replica_groups=mesh['slab'=32,'col'=4] {'slab'}, dimensions={0} | all-to-all | bytes 393216 | tf_op jit(solution)/shard_map/all_to_all | solution.py:420
  69.8 1.3 %sums.1 = (f32[3,512]{1,0:T(4,128)}, f32[2048,512]{1,0:T(8,128)}) custom-call(f32[32,1,1536]{2,1,0:T(1,128)S(1)} %all_to_all.5.parts, f32[128,256]{1,0:T(8,128)S(1)} %get-tuple-element.91.tail, f32[2048,512]{1,0:T(8,128)} %get-tuple-element.92._), custom_call_target="tpu_custom_call", output_to_operand_aliasing={{1}: (2, {})} | custom-call | tf_op jit(solution)/shard_map/sums/pallas_call | solution.py:421
  (22 shorter events, 0.1 us)
Async XLA Ops:
  0.6 8.2 %copy-start.4 = (s32[16,9]{1,0:T(8,128)S(1)}, s32[16,9]{1,0:T(8,128)}, u32[]{:S(2)}) copy-start(s32[16,9]{1,0:T(8,128)} %param.7) | copy-start | bytes 1732
  2.1 16.2 %collective-permute-start = (bf16[640,256]{1,0:T(8,128)(2,1)S(1)}, bf16[640,256]{1,0:T(8,128)(2,1)S(1)}, u32[]{:S(2)}, u32[]{:S(2)}) collective-permute-start(bf16[640,256]{1,0:T(8,128)(2,1)S(1)} %get-tuple-element.49._), channel_id=1, source_target_pairs={{4,8},{8,4},{12,16},{16,12},{20,24},{24,20},{28,32},{32,28},{36,40... | collective-permute-start | bytes 983048 | tf_op jit(solution)/shard_map/ppermute | solution.py:272
  8.8 10.0 %collective-permute-start.1 = (bf16[640,256]{1,0:T(8,128)(2,1)S(1)}, bf16[640,256]{1,0:T(8,128)(2,1)S(1)}, u32[]{:S(2)}, u32[]{:S(2)}) collective-permute-start(bf16[640,256]{1,0:T(8,128)(2,1)S(1)} %get-tuple-element.53), channel_id=1, source_target_pairs={{0,4},{4,0},{8,12},{12,8},{16,20},{20,16},{24,28},{28,24},{32,36},... | collective-permute-start | bytes 983048 | tf_op jit(solution)/shard_map/ppermute | solution.py:273
  8.9 7.4 %copy-start.2 = (bf16[2048,512]{1,0:T(8,128)(2,1)S(1)}, bf16[2048,512]{1,0:T(8,128)(2,1)}, u32[]{:S(2)}) copy-start(bf16[2048,512]{1,0:T(8,128)(2,1)} %probe.1) | copy-start | bytes 6291460
  8.9 7.4 %copy-start.3 = (f32[2048]{0:T(1024)S(1)}, f32[2048]{0:T(1024)}, u32[]{:S(2)}) copy-start(f32[2048]{0:T(1024)} %param.11) | copy-start | bytes 24580
  8.9 7.7 %copy-start.1 = (f32[2048,512]{1,0:T(8,128)S(1)}, f32[2048,512]{1,0:T(8,128)}, u32[]{:S(2)}) copy-start(f32[2048,512]{1,0:T(8,128)} %refs_1_.3) | copy-start | bytes 12582916
  14.1 2.6 %copy-start = (f32[2048,512]{1,0:T(8,128)S(1)}, f32[2048,512]{1,0:T(8,128)}, u32[]{:S(2)}) copy-start(f32[2048,512]{1,0:T(8,128)} %refs_3_.3) | copy-start | bytes 12582916
  14.1 14.9 %collective-permute-start.2 = (bf16[640,256]{1,0:T(8,128)(2,1)S(1)}, bf16[640,256]{1,0:T(8,128)(2,1)S(1)}, u32[]{:S(2)}, u32[]{:S(2)}) collective-permute-start(bf16[640,256]{1,0:T(8,128)(2,1)S(1)} %get-tuple-element.50._), channel_id=1, source_target_pairs={{4,8},{8,4},{12,16},{16,12},{20,24},{24,20},{28,32},{32,28},{36,40... | collective-permute-start | bytes 983048 | tf_op jit(solution)/shard_map/ppermute | solution.py:272
  15.6 13.5 %collective-permute-start.3 = (bf16[640,256]{1,0:T(8,128)(2,1)S(1)}, bf16[640,256]{1,0:T(8,128)(2,1)S(1)}, u32[]{:S(2)}, u32[]{:S(2)}) collective-permute-start(bf16[640,256]{1,0:T(8,128)(2,1)S(1)} %get-tuple-element.58), channel_id=1, source_target_pairs={{0,4},{4,0},{8,12},{12,8},{16,20},{20,16},{24,28},{28,24},{32,36},... | collective-permute-start | bytes 983048 | tf_op jit(solution)/shard_map/ppermute | solution.py:273
  19.6 15.7 %collective-permute-start.4 = (bf16[640,256]{1,0:T(8,128)(2,1)S(1)}, bf16[640,256]{1,0:T(8,128)(2,1)S(1)}, u32[]{:S(2)}, u32[]{:S(2)}) collective-permute-start(bf16[640,256]{1,0:T(8,128)(2,1)S(1)} %get-tuple-element.63.refs_2_), channel_id=1, source_target_pairs={{4,8},{8,4},{12,16},{16,12},{20,24},{24,20},{28,32},{32,28},{36,40... | collective-permute-start | bytes 983048 | tf_op jit(solution)/shard_map/ppermute | solution.py:272
  24.2 11.1 %collective-permute-start.5 = (bf16[640,256]{1,0:T(8,128)(2,1)S(1)}, bf16[640,256]{1,0:T(8,128)(2,1)S(1)}, u32[]{:S(2)}, u32[]{:S(2)}) collective-permute-start(bf16[640,256]{1,0:T(8,128)(2,1)S(1)} %get-tuple-element.61.refs_0_), channel_id=1, source_target_pairs={{0,4},{4,0},{8,12},{12,8},{16,20},{20,16},{24,28},{28,24},{32,36},... | collective-permute-start | bytes 983048 | tf_op jit(solution)/shard_map/ppermute | solution.py:273
  29.8 12.5 %collective-permute-start.6 = (bf16[640,256]{1,0:T(8,128)(2,1)S(1)}, bf16[640,256]{1,0:T(8,128)(2,1)S(1)}, u32[]{:S(2)}, u32[]{:S(2)}) collective-permute-start(bf16[640,256]{1,0:T(8,128)(2,1)S(1)} %get-tuple-element.69.refs_2_), channel_id=1, source_target_pairs={{4,8},{8,4},{12,16},{16,12},{20,24},{24,20},{28,32},{32,28},{36,40... | collective-permute-start | bytes 983048 | tf_op jit(solution)/shard_map/ppermute | solution.py:272
  31.9 10.3 %collective-permute-start.7 = (bf16[640,256]{1,0:T(8,128)(2,1)S(1)}, bf16[640,256]{1,0:T(8,128)(2,1)S(1)}, u32[]{:S(2)}, u32[]{:S(2)}) collective-permute-start(bf16[640,256]{1,0:T(8,128)(2,1)S(1)} %get-tuple-element.67.refs_0_), channel_id=1, source_target_pairs={{0,4},{4,0},{8,12},{12,8},{16,20},{20,16},{24,28},{28,24},{32,36},... | collective-permute-start | bytes 983048 | tf_op jit(solution)/shard_map/ppermute | solution.py:273
  36.0 15.4 %collective-permute-start.8 = (bf16[640,256]{1,0:T(8,128)(2,1)S(1)}, bf16[640,256]{1,0:T(8,128)(2,1)S(1)}, u32[]{:S(2)}, u32[]{:S(2)}) collective-permute-start(bf16[640,256]{1,0:T(8,128)(2,1)S(1)} %get-tuple-element.76.refs_2_), channel_id=1, source_target_pairs={{4,8},{8,4},{12,16},{16,12},{20,24},{24,20},{28,32},{32,28},{36,40... | collective-permute-start | bytes 983048 | tf_op jit(solution)/shard_map/ppermute | solution.py:272
  38.7 12.8 %collective-permute-start.9 = (bf16[640,256]{1,0:T(8,128)(2,1)S(1)}, bf16[640,256]{1,0:T(8,128)(2,1)S(1)}, u32[]{:S(2)}, u32[]{:S(2)}) collective-permute-start(bf16[640,256]{1,0:T(8,128)(2,1)S(1)} %get-tuple-element.74.refs_0_), channel_id=1, source_target_pairs={{0,4},{4,0},{8,12},{12,8},{16,20},{20,16},{24,28},{28,24},{32,36},... | collective-permute-start | bytes 983048 | tf_op jit(solution)/shard_map/ppermute | solution.py:273
  43.1 12.6 %collective-permute-start.10 = (bf16[640,256]{1,0:T(8,128)(2,1)S(1)}, bf16[640,256]{1,0:T(8,128)(2,1)S(1)}, u32[]{:S(2)}, u32[]{:S(2)}) collective-permute-start(bf16[640,256]{1,0:T(8,128)(2,1)S(1)} %get-tuple-element.81.refs_2_), channel_id=1, source_target_pairs={{4,8},{8,4},{12,16},{16,12},{20,24},{24,20},{28,32},{32,28},{36,40... | collective-permute-start | bytes 983048 | tf_op jit(solution)/shard_map/ppermute | solution.py:272
  45.5 10.2 %collective-permute-start.11 = (bf16[640,256]{1,0:T(8,128)(2,1)S(1)}, bf16[640,256]{1,0:T(8,128)(2,1)S(1)}, u32[]{:S(2)}, u32[]{:S(2)}) collective-permute-start(bf16[640,256]{1,0:T(8,128)(2,1)S(1)} %get-tuple-element.79.refs_0_), channel_id=1, source_target_pairs={{0,4},{4,0},{8,12},{12,8},{16,20},{20,16},{24,28},{28,24},{32,36},... | collective-permute-start | bytes 983048 | tf_op jit(solution)/shard_map/ppermute | solution.py:273

commit v4 on v3

--- a/solution.py
+++ b/solution.py
@@ -109,11 +109,19 @@
 
 def middle_kernel(sources, first, cols, width, rows_blk, odd, _, banded, weights, *refs):
     source, previous = refs[:sources], refs[sources]
-    upcoming, *inner, partial, x = refs[sources + 1 + (first > 0) :]
+    results = refs[sources + 1 + (first > 0) :]
+    if sources == 1:
+        *results, held, sems = results
+    upcoming, *inner, partial, x = results
     columns = pl.ds(first, cols)
     rim = BAND * width
     rows = rows_blk * width
     if sources == 1:
+        copies = []
+        for pair in range(rows_blk // 2):
+            two = pl.ds(2 * pair * width, 2 * width)
+            copies.append(pltpu.make_async_copy(previous.at[two, columns], held.at[two], sems.at[pair]))
+            copies[-1].start()
         x[...] = source[0][:, columns].astype(BF16)
     else:
         evens, inside, odds = source
@@ -135,7 +143,12 @@
             preferred_element_type=F32,
         )
         here = pl.ds(2 * pair * width, 2 * width)
-        result = 2.0 * product - previous[here, columns]
+        if sources == 1:
+            copies[pair].wait()
+            before = held[here]
+        else:
+            before = previous[here, columns]
+        result = 2.0 * product - before
         upcoming[here, columns] = result
         a = max(2 * pair, BAND)
         b = min(2 * pair + 2, rows_blk - BAND)
@@ -198,31 +211,37 @@
     hand_out(odd, take, evens, odds)
 
 
-def last_rim_kernel(count, first, cols, width, rows_blk, odd, _, banded, weights, odds_in, evens_in, begun, partial, *refs):
-    earlier, (out, moments, *tail, held, sems) = refs[:count], refs[count + 1 :]
+def store_rim_kernel(first, cols, width, rows_blk, odd, _, banded, weights, odds_in, evens_in, begun, partial, __, out, moments, held, sems):
     copies = []
 
     def keep(part, side, here, columns, result):
-        if tail and part == len(rim_parts(rows_blk)) - 1:
-            tail[0][...] = result
-            return
         slot = held.at[part, pl.ds(0, here.size)]
         slot[...] = result
         copies.append(pltpu.make_async_copy(slot, out.at[here, columns], sems.at[part]))
         copies[-1].start()
 
+    moments[...] = rim_sums(
+        first, cols, width, rows_blk, odd, banded, weights, evens_in, odds_in, begun, partial, keep
+    )
+    for copy in copies:
+        copy.wait()
+
+
+def last_rim_kernel(first, cols, width, rows_blk, odd, _, banded, weights, odds_in, evens_in, begun, partial, *refs):
+    *earlier, moments, rims = refs
+    rim = rims.shape[1]
+
+    def keep(part, side, here, columns, result):
+        base = here.start - (0 if side == 0 else rows_blk * width - rim)
+        rims[side, base : base + here.size] = result
+
     total = rim_sums(
         first, cols, width, rows_blk, odd, banded, weights, evens_in, odds_in, begun, partial, keep
     )
-    if tail:
-        parts = [jnp.sum(one, axis=0, keepdims=True) for one in [*(ref[...] for ref in earlier), total]]
-        row = jnp.concatenate(parts, axis=1)
-        for slab in range(moments.shape[0]):
-            moments[slab] = row
-    else:
-        moments[...] = total
-    for copy in copies:
-        copy.wait()
+    parts = [jnp.sum(one, axis=0, keepdims=True) for one in [*(ref[...] for ref in earlier), total]]
+    row = jnp.concatenate(parts, axis=1)
+    for slab in range(moments.shape[0]):
+        moments[slab] = row
 
 
 def store_kernel(rim, _, previous, current, out_previous, out_current, sems):
@@ -237,15 +256,25 @@
         copy.wait()
 
 
-def sum_kernel(top, first, parts, tail, _, out, out_current, sem):
-    rows, cols = tail.shape
-    copy = pltpu.make_async_copy(tail, out_current.at[pl.ds(top, rows), pl.ds(first, cols)], sem)
-    copy.start()
+def sum_kernel(first, parts, rims, _, out, out_current, held, sems):
+    _, rim, cols = rims.shape
+    starts = (0, out_current.shape[0] - rim)
+    copies = [
+        pltpu.make_async_copy(
+            rims.at[side], out_current.at[pl.ds(start, rim), pl.ds(first, cols)], sems.at[side]
+        )
+        for side, start in enumerate(starts)
+    ]
+    for copy in copies:
+        copy.start()
     total = jnp.sum(parts[...], axis=0)
-    every = out.shape[1]
-    for term in range(out.shape[0]):
-        out[term : term + 1] = total[:, term * every : (term + 1) * every]
-    copy.wait()
+    every = held.shape[1]
+    for term in range(held.shape[0]):
+        held[term : term + 1] = total[:, term * every : (term + 1) * every]
+    copies.append(pltpu.make_async_copy(held, out, sems.at[2]))
+    copies[-1].start()
+    for copy in copies:
+        copy.wait()
 
 
 def in_hbm(x):
@@ -274,10 +303,16 @@
 
     def middle(token, term, chunk):
         args = [odd, token, banded, weights, *sources[chunk], terms[term]]
+        specs = [SMEM] + [VMEM] * (len(args) - 1)
+        scratch = [pltpu.VMEM((rows, cols), BF16)]
+        if term == 0:
+            args[-1], specs[-1] = in_hbm(previous), HBM
+            scratch += [pltpu.VMEM((rows, cols), F32), pltpu.SemaphoreType.DMA((pairs,))]
         aliases = {}
         if chunk:
             aliases = {len(args): 0}
             args.append(terms[term + 2])
+            specs.append(VMEM)
         outs = (full_shape, shape((rows - 2 * rim, cols), BF16), part_shape)
         if term == TERMS - 1:
             outs = (full_shape, part_shape)
@@ -286,9 +321,9 @@
                 middle_kernel, len(sources[chunk]), chunk * cols, cols, width, rows_blk
             ),
             out_shape=outs,
-            in_specs=[SMEM] + [VMEM] * (len(args) - 1),
+            in_specs=specs,
             out_specs=(VMEM,) * len(outs),
-            scratch_shapes=[pltpu.VMEM((rows, cols), BF16)],
+            scratch_shapes=scratch,
             input_output_aliases=aliases,
             compiler_params=params(),
             cost_estimate=cost(flops, 8 * 1024 * 1024),
@@ -305,21 +340,23 @@
             out_specs = (VMEM,) * 4
             scratch = [pltpu.VMEM((2, rim, cols), BF16)]
             aliases = {6: 0}
-        else:
-            final = chunk == CHUNKS - 1
-            if final:
-                args += sums
-                specs += [VMEM] * len(sums)
-            kernel = functools.partial(last_rim_kernel, len(sums) if final else 0, *bound)
+        elif chunk < CHUNKS - 1:
+            kernel = functools.partial(store_rim_kernel, *bound)
             aliases = {len(args): 0}
             args.append(outputs[1])
             specs.append(HBM)
             outs = (full_shape, part_shape)
-            if final:
-                outs = (full_shape, shape((slabs, 1, TERMS * all_cols), F32), shape((tail, cols), F32))
-            out_specs = (HBM,) + (VMEM,) * (len(outs) - 1)
+            out_specs = (HBM, VMEM)
             count = len(rim_parts(rows_blk))
             scratch = [pltpu.VMEM((count, 2 * width, cols), F32), pltpu.SemaphoreType.DMA((count,))]
+        else:
+            kernel = functools.partial(last_rim_kernel, *bound)
+            aliases = {}
+            args += sums
+            specs += [VMEM] * len(sums)
+            outs = (shape((slabs, 1, TERMS * all_cols), F32), shape((2, rim, cols), F32))
+            out_specs = (VMEM, VMEM)
+            scratch = []
         return pl.pallas_call(
             kernel,
             out_shape=outs,
@@ -384,8 +421,6 @@
     sums = []
     order = [(term, chunk) for term in range(TERMS) for chunk in range(CHUNKS)]
     ahead = len(order) - CHUNKS
-    _, pair, low, high, *_ = rim_parts(rows_blk)[-1]
-    top, tail = (2 * pair + low) * width, (high - low) * width
     outputs = None
 
     def begin(token, term, chunk):
@@ -398,9 +433,11 @@
             terms[term + 2], token, *sent = rims(token, term, chunk)
             halos[chunk] = exchange(*sent)
             sources[chunk] = (sent[0], begun[chunk][0], sent[1])
+        elif step + 1 < len(order):
+            last_current, token = rims(token, term, chunk)
+            outputs = (outputs[0], last_current)
         else:
-            last_current, token, *ends = rims(token, term, chunk)
-            outputs = (outputs[0], last_current)
+            scattered, ends = rims(token, term, chunk)
         sums.append(token)
         if step + 1 < ahead:
             token = begin(token, *order[step + 1])
@@ -417,17 +454,18 @@
                 cost_estimate=cost(0, 16 * 1024 * 1024),
                 name="store",
             )(token, terms[-2], terms[-1])
-    gathered = lax.all_to_all(sums[-1], "slab", 0, 0)
+    gathered = lax.all_to_all(scattered, "slab", 0, 0)
+    moments_shape = shape((TERMS, all_cols), F32)
     moments, last_current = pl.pallas_call(
-        functools.partial(sum_kernel, top, all_cols - cols),
-        out_shape=(shape((TERMS, all_cols), F32), full_shape),
+        functools.partial(sum_kernel, all_cols - cols),
+        out_shape=(moments_shape, full_shape),
         in_specs=[VMEM, VMEM, HBM],
-        out_specs=(VMEM, HBM),
-        scratch_shapes=[pltpu.SemaphoreType.DMA],
+        out_specs=(HBM, HBM),
+        scratch_shapes=[pltpu.VMEM(moments_shape.shape, F32), pltpu.SemaphoreType.DMA((3,))],
         input_output_aliases={2: 1},
         compiler_params=params(),
         name="sums",
-    )(gathered, ends[0], outputs[1])
+    )(gathered, ends, outputs[1])
     return outputs[0], last_current, moments
 
 

time: 71.4 us -> 75.4 us (1.056)
  Pallas kernels: 26.5 us -> 32.2 us
  waiting for transfers between devices: 10 us -> 6.1 us
  blocking collectives: 12.8 us -> 14 us
  starting transfers between devices: 20.8 us -> 21.7 us
    pallas_call x6, Pallas kernels: 9.99 us -> 17 us  [middle(): pl.pallas_call(functools.partial(middle_kernel, len(sources[chunk]), chun...]
    ppermute x6, waiting for transfers between devices: 9.55 us -> 6.08 us  [exchange(): ahead = lax.ppermute(odds, 'slab', pairs_of[1])]
    all_to_all x1, blocking collectives: 12.8 us -> 14 us  [local(): gathered = lax.all_to_all(scattered, 'slab', 0, 0)]
    ppermute x6, starting transfers between devices: 20 us -> 20.9 us  [exchange(): ahead = lax.ppermute(odds, 'slab', pairs_of[1])]
    pallas_call x6, Pallas kernels: 5.8 us -> 5.02 us  [rims(): pl.pallas_call(kernel, out_shape=outs, in_specs=specs, out_specs=out_spec...]
  transfers between devices with their start and end apart: 12 -> 12, of which waited for: 5 -> 2; matrix products, arithmetic and copies ran while one was open for 0% -> 0% of each run, Pallas kernels for 31% -> 39%
where the time goes in v4:
time: 75.4 us; the launch traced here: 75.2 us
  Pallas kernels  32.2 us (43%)
  starting transfers between devices  21.7 us (29%)
  blocking collectives  14 us (19%)
  waiting for transfers between devices  6.1 us (8%)
  between operations  1.04 us (1%)
    ppermute x6, starting transfers between devices, exchange(): ahead = lax.ppermute(odds, 'slab', pairs_of[1])  20.9 us
    pallas_call x6, Pallas kernels, middle(): pl.pallas_call(functools.partial(middle_kernel, len(sources[chunk]), chun...  17 us
    all_to_all x1, blocking collectives, local(): gathered = lax.all_to_all(scattered, 'slab', 0, 0)  14 us
    ppermute x6, waiting for transfers between devices, exchange(): ahead = lax.ppermute(odds, 'slab', pairs_of[1])  6.08 us
    pallas_call x6, Pallas kernels, rims(): pl.pallas_call(kernel, out_shape=outs, in_specs=specs, out_specs=out_spec...  5.02 us
    pallas_call x1, Pallas kernels, local(): pl.pallas_call(functools.partial(band_kernel, cols, cols), out_shape=(sha...  4.81 us
    pallas_call x1, Pallas kernels, local(): pl.pallas_call(functools.partial(store_kernel, rim), out_shape=(full_shap...  2.54 us
  transfers between devices with their start and end apart: 12, of which 2 were waited for; matrix products, arithmetic and copies ran while one was open for 0% of the time, Pallas kernels for 39%

profile of v4, /device:TPU:0, one launch (start us, length us, event | category | flops | bytes accessed | tf_op | source)
XLA Modules:
  0.0 75.2 jit_solution(11353703656830528409)
XLA Ops:
  0.6 1.5 %edges.1 = (bf16[640,256]{1,0:T(8,128)(2,1)S(1)}, bf16[640,256]{1,0:T(8,128)(2,1)S(1)}) custom-call(s32[1]{0:T(128)} %bitcast.odd, f32[2048,512]{1,0:T(8,128)} %refs_3_.3), custom_call_target="tpu_custom_call" | custom-call | bytes 1966080 | tf_op jit(solution)/shard_map/edges/pallas_call | solution.py:378
  2.1 6.7 %collective-permute-start = (bf16[640,256]{1,0:T(8,128)(2,1)S(1)}, bf16[640,256]{1,0:T(8,128)(2,1)S(1)}, u32[]{:S(2)}, u32[]{:S(2)}) collective-permute-start(bf16[640,256]{1,0:T(8,128)(2,1)S(1)} %get-tuple-element.48._), channel_id=1, source_target_pairs={{4,8},{8,4},{12,16},{16,12},{20,24},{24,20},{28,32},{32,28},{36,40... | collective-permute-start | bytes 983048 | tf_op jit(solution)/shard_map/ppermute | solution.py:301
  8.8 0.1 add_select_fusion.places
  8.9 0.0 copy-start.2
  8.9 4.8 %band.1 = (bf16[8,256,1536]{2,1,0:T(8,128)(2,1)S(1)}, bf16[640,256]{1,0:T(8,128)(2,1)S(1)}, bf16[640,256]{1,0:T(8,128)(2,1)S(1)}) custom-call(s32[1]{0:T(128)} %bitcast.odd, bf16[640,256]{1,0:T(8,128)(2,1)S(1)} %get-tuple-element.48._, s32[16,9]{1,0:T(8,128)S(1)} %add_select_fusion.places, bf16[16,9,128,128]{3,2,1,0:T(8,128)(2,1)} %blocks.1, f32[2048,512]{1,0:T(8,128)} %refs_3_.3), custom_call_target="tpu_custom_call" | custom-call | bytes 12582912 | tf_op jit(solution)/shard_map/band/pallas_call | solution.py:389
  13.8 0.0 copy-start
  13.8 1.4 %collective-permute-start.2 = (bf16[640,256]{1,0:T(8,128)(2,1)S(1)}, bf16[640,256]{1,0:T(8,128)(2,1)S(1)}, u32[]{:S(2)}, u32[]{:S(2)}) collective-permute-start(bf16[640,256]{1,0:T(8,128)(2,1)S(1)} %get-tuple-element.49._), channel_id=1, source_target_pairs={{4,8},{8,4},{12,16},{16,12},{20,24},{24,20},{28,32},{32,28},{36,40... | collective-permute-start | bytes 983048 | tf_op jit(solution)/shard_map/ppermute | solution.py:301
  15.2 0.8 %collective-permute-start.3 = (bf16[640,256]{1,0:T(8,128)(2,1)S(1)}, bf16[640,256]{1,0:T(8,128)(2,1)S(1)}, u32[]{:S(2)}, u32[]{:S(2)}) collective-permute-start(bf16[640,256]{1,0:T(8,128)(2,1)S(1)} %get-tuple-element.57), channel_id=1, source_target_pairs={{0,4},{4,0},{8,12},{12,8},{16,20},{20,16},{24,28},{28,24},{32,36},... | collective-permute-start | bytes 983048 | tf_op jit(solution)/shard_map/ppermute | solution.py:302
  16.0 0.3 weights.1._
  16.3 5.0 %middle.6 = (f32[2048,512]{1,0:T(8,128)S(1)}, bf16[768,256]{1,0:T(8,128)(2,1)S(1)}, f32[8,256]{1,0:T(8,128)S(1)}) custom-call(s32[1]{0:T(128)} %bitcast.odd, f32[2048,512]{1,0:T(8,128)S(1)} %weights.1._, bf16[8,256,1536]{2,1,0:T(8,128)(2,1)S(1)} %get-tuple-element.50.banded, f32[2048,512]{1,0:T(8,128)S(1)} %weights.1._, f32[2048,512]{1,0:T(8,128)S(1)} %copy-done, ...), custom_call_target="tpu_custom_call" | custom-call | flops 1207959552 | bytes 8388608 | tf_op jit(solution)/shard_map/middle/pallas_call | solution.py:319
  21.4 0.0 collective-permute-done.odds_in
  21.4 0.8 %rims.6 = (f32[2048,512]{1,0:T(8,128)S(1)}, f32[8,256]{1,0:T(8,128)S(1)}, bf16[640,256]{1,0:T(8,128)(2,1)S(1)}, bf16[640,256]{1,0:T(8,128)(2,1)S(1)}) custom-call(s32[1]{0:T(128)} %bitcast.odd, f32[8,256]{1,0:T(8,128)S(1)} %get-tuple-element.51._.partial, bf16[8,256,1536]{2,1,0:T(8,128)(2,1)S(1)} %get-tuple-element.50.banded, ...), custom_call_target="tpu_custom_call", output_to_operand_aliasing={{0}: (6, {})} | custom-call | flops 241591904 | bytes 2097152 | tf_op jit(solution)/shard_map/rims/pallas_call | solution.py:360
  22.2 4.2 %collective-permute-start.4 = (bf16[640,256]{1,0:T(8,128)(2,1)S(1)}, bf16[640,256]{1,0:T(8,128)(2,1)S(1)}, u32[]{:S(2)}, u32[]{:S(2)}) collective-permute-start(bf16[640,256]{1,0:T(8,128)(2,1)S(1)} %get-tuple-element.62.refs_2_), channel_id=1, source_target_pairs={{4,8},{8,4},{12,16},{16,12},{20,24},{24,20},{28,32},{32,28},{36,40... | collective-permute-start | bytes 983048 | tf_op jit(solution)/shard_map/ppermute | solution.py:301
  26.4 5.0 %middle.7 = (f32[2048,512]{1,0:T(8,128)S(1)}, bf16[768,256]{1,0:T(8,128)(2,1)S(1)}, f32[8,256]{1,0:T(8,128)S(1)}) custom-call(s32[1]{0:T(128)} %bitcast.odd, f32[8,256]{1,0:T(8,128)S(1)} %get-tuple-element.54._.refs_0_, bf16[8,256,1536]{2,1,0:T(8,128)(2,1)S(1)} %get-tuple-element.50.banded, ...), custom_call_target="tpu_custom_call", output_to_operand_aliasing={{0}: (6, {})} | custom-call | flops 1207959552 | bytes 8388608 | tf_op jit(solution)/shard_map/middle/pallas_call | solution.py:319
  31.4 0.8 %rims.7 = (f32[2048,512]{1,0:T(8,128)S(1)}, f32[8,256]{1,0:T(8,128)S(1)}, bf16[640,256]{1,0:T(8,128)(2,1)S(1)}, bf16[640,256]{1,0:T(8,128)(2,1)S(1)}) custom-call(s32[1]{0:T(128)} %bitcast.odd, f32[8,256]{1,0:T(8,128)S(1)} %get-tuple-element.56._.partial, bf16[8,256,1536]{2,1,0:T(8,128)(2,1)S(1)} %get-tuple-element.50.banded, ...), custom_call_target="tpu_custom_call", output_to_operand_aliasing={{0}: (6, {})} | custom-call | flops 241591904 | bytes 2097152 | tf_op jit(solution)/shard_map/rims/pallas_call | solution.py:360
  32.2 2.2 %collective-permute-start.6 = (bf16[640,256]{1,0:T(8,128)(2,1)S(1)}, bf16[640,256]{1,0:T(8,128)(2,1)S(1)}, u32[]{:S(2)}, u32[]{:S(2)}) collective-permute-start(bf16[640,256]{1,0:T(8,128)(2,1)S(1)} %get-tuple-element.68.refs_2_), channel_id=1, source_target_pairs={{4,8},{8,4},{12,16},{16,12},{20,24},{24,20},{28,32},{32,28},{36,40... | collective-permute-start | bytes 983048 | tf_op jit(solution)/shard_map/ppermute | solution.py:301
  34.4 0.0 collective-permute-start.7
  34.4 1.7 %middle.8 = (f32[2048,512]{1,0:T(8,128)S(1)}, bf16[768,256]{1,0:T(8,128)(2,1)S(1)}, f32[8,256]{1,0:T(8,128)S(1)}) custom-call(s32[1]{0:T(128)} %bitcast.odd, f32[8,256]{1,0:T(8,128)S(1)} %get-tuple-element.59._.refs_1_, bf16[8,256,1536]{2,1,0:T(8,128)(2,1)S(1)} %get-tuple-element.50.banded, f32[2048,512]{1,0:T(8,128)S(1)} %weights.1._, ...), custom_call_target="tpu_custom_call" | custom-call | flops 1207959552 | bytes 8388608 | tf_op jit(solution)/shard_map/middle/pallas_call | solution.py:319
  36.1 0.8 %rims.8 = (f32[2048,512]{1,0:T(8,128)S(1)}, f32[8,256]{1,0:T(8,128)S(1)}, bf16[640,256]{1,0:T(8,128)(2,1)S(1)}, bf16[640,256]{1,0:T(8,128)(2,1)S(1)}) custom-call(s32[1]{0:T(128)} %bitcast.odd, f32[8,256]{1,0:T(8,128)S(1)} %get-tuple-element.63._.partial, bf16[8,256,1536]{2,1,0:T(8,128)(2,1)S(1)} %get-tuple-element.50.banded, ...), custom_call_target="tpu_custom_call", output_to_operand_aliasing={{0}: (6, {})} | custom-call | flops 241591904 | bytes 2097152 | tf_op jit(solution)/shard_map/rims/pallas_call | solution.py:360
  36.9 4.2 %collective-permute-start.8 = (bf16[640,256]{1,0:T(8,128)(2,1)S(1)}, bf16[640,256]{1,0:T(8,128)(2,1)S(1)}, u32[]{:S(2)}, u32[]{:S(2)}) collective-permute-start(bf16[640,256]{1,0:T(8,128)(2,1)S(1)} %get-tuple-element.75.refs_2_), channel_id=1, source_target_pairs={{4,8},{8,4},{12,16},{16,12},{20,24},{24,20},{28,32},{32,28},{36,40... | collective-permute-start | bytes 983048 | tf_op jit(solution)/shard_map/ppermute | solution.py:301
  41.1 1.9 %middle.9 = (f32[2048,512]{1,0:T(8,128)S(1)}, bf16[768,256]{1,0:T(8,128)(2,1)S(1)}, f32[8,256]{1,0:T(8,128)S(1)}) custom-call(s32[1]{0:T(128)} %bitcast.odd, f32[8,256]{1,0:T(8,128)S(1)} %get-tuple-element.65._.refs_2_, bf16[8,256,1536]{2,1,0:T(8,128)(2,1)S(1)} %get-tuple-element.50.banded, ...), custom_call_target="tpu_custom_call", output_to_operand_aliasing={{0}: (8, {})} | custom-call | flops 1207959552 | bytes 8388608 | tf_op jit(solution)/shard_map/middle/pallas_call | solution.py:319
  43.0 4.2 %collective-permute-done.6.odds_in = bf16[640,256]{1,0:T(8,128)(2,1)S(1)} collective-permute-done((bf16[640,256]{1,0:T(8,128)(2,1)S(1)}, bf16[640,256]{1,0:T(8,128)(2,1)S(1)}, u32[]{:S(2)}, u32[]{:S(2)}) %collective-permute-start.6) | collective-permute-done | bytes 327712 | tf_op jit(solution)/shard_map/ppermute | solution.py:301
  47.2 0.8 %rims.9 = (f32[2048,512]{1,0:T(8,128)S(1)}, f32[8,256]{1,0:T(8,128)S(1)}, bf16[640,256]{1,0:T(8,128)(2,1)S(1)}, bf16[640,256]{1,0:T(8,128)(2,1)S(1)}) custom-call(s32[1]{0:T(128)} %bitcast.odd, f32[8,256]{1,0:T(8,128)S(1)} %get-tuple-element.70._.partial, bf16[8,256,1536]{2,1,0:T(8,128)(2,1)S(1)} %get-tuple-element.50.banded, ...), custom_call_target="tpu_custom_call", output_to_operand_aliasing={{0}: (6, {})} | custom-call | flops 241591904 | bytes 2097152 | tf_op jit(solution)/shard_map/rims/pallas_call | solution.py:360
  47.9 2.1 %collective-permute-start.10 = (bf16[640,256]{1,0:T(8,128)(2,1)S(1)}, bf16[640,256]{1,0:T(8,128)(2,1)S(1)}, u32[]{:S(2)}, u32[]{:S(2)}) collective-permute-start(bf16[640,256]{1,0:T(8,128)(2,1)S(1)} %get-tuple-element.80.refs_2_), channel_id=1, source_target_pairs={{4,8},{8,4},{12,16},{16,12},{20,24},{24,20},{28,32},{32,28},{36,40... | collective-permute-start | bytes 983048 | tf_op jit(solution)/shard_map/ppermute | solution.py:301
  50.1 1.7 %middle.10 = (f32[2048,512]{1,0:T(8,128)S(1)}, f32[8,256]{1,0:T(8,128)S(1)}) custom-call(s32[1]{0:T(128)} %bitcast.odd, f32[8,256]{1,0:T(8,128)S(1)} %get-tuple-element.72._.refs_3_, bf16[8,256,1536]{2,1,0:T(8,128)(2,1)S(1)} %get-tuple-element.50.banded, f32[2048,512]{1,0:T(8,128)S(1)} %weights.1._, bf16[640,256]{1,0:T(8,128)(2,1)S(1)} %get-tuple-element.73.refs_0_, ...), custom_call_target="tpu_custom_call" | custom-call | flops 1207959552 | bytes 8388608 | tf_op jit(solution)/shard_map/middle/pallas_call | solution.py:319
  51.7 1.7 %middle.11 = (f32[2048,512]{1,0:T(8,128)S(1)}, f32[8,256]{1,0:T(8,128)S(1)}) custom-call(s32[1]{0:T(128)} %bitcast.odd, f32[8,256]{1,0:T(8,128)S(1)} %get-tuple-element.77._.partial, bf16[8,256,1536]{2,1,0:T(8,128)(2,1)S(1)} %get-tuple-element.50.banded, f32[2048,512]{1,0:T(8,128)S(1)} %weights.1._, ...), custom_call_target="tpu_custom_call", output_to_operand_aliasing={{0}: (8, {})} | custom-call | flops 1207959552 | bytes 8388608 | tf_op jit(solution)/shard_map/middle/pallas_call | solution.py:319
  53.4 2.5 %store.1 = (f32[2048,512]{1,0:T(8,128)}, f32[2048,512]{1,0:T(8,128)}) custom-call(f32[8,256]{1,0:T(8,128)S(1)} %get-tuple-element.82._.partial, f32[2048,512]{1,0:T(8,128)S(1)} %get-tuple-element.83.previous, f32[2048,512]{1,0:T(8,128)S(1)} %get-tuple-element.84.current.begun), custom_call_target="tpu_custom_call" | custom-call | bytes 16777216 | tf_op jit(solution)/shard_map/store/pallas_call | solution.py:447
  56.0 1.4 %rims.10 = (f32[2048,512]{1,0:T(8,128)}, f32[8,256]{1,0:T(8,128)S(1)}) custom-call(s32[1]{0:T(128)} %bitcast.odd, f32[8,256]{1,0:T(8,128)S(1)} %get-tuple-element.82._.partial, bf16[8,256,1536]{2,1,0:T(8,128)(2,1)S(1)} %get-tuple-element.50.banded, f32[2048,512]{1,0:T(8,128)S(1)} %weights.1._, ...), custom_call_target="tpu_custom_call", output_to_operand_aliasing={{0}: (8, {})} | custom-call | flops 241591904 | bytes 2097152 | tf_op jit(solution)/shard_map/rims/pallas_call | solution.py:360
  57.4 1.9 %collective-permute-done.10.odds_in = bf16[640,256]{1,0:T(8,128)(2,1)S(1)} collective-permute-done((bf16[640,256]{1,0:T(8,128)(2,1)S(1)}, bf16[640,256]{1,0:T(8,128)(2,1)S(1)}, u32[]{:S(2)}, u32[]{:S(2)}) %collective-permute-start.10) | collective-permute-done | bytes 327712 | tf_op jit(solution)/shard_map/ppermute | solution.py:301
  59.3 0.6 rims.11
  59.9 14.0 %all_to_all.5.parts = f32[32,1,1536]{2,1,0:T(1,128)S(1)} all-to-all(f32[32,1,1536]{2,1,0:T(1,128)S(1)} %get-tuple-element.88), channel_id=1, replica_groups=mesh['slab'=32,'col'=4] {'slab'}, dimensions={0} | all-to-all | bytes 393216 | tf_op jit(solution)/shard_map/all_to_all | solution.py:457
  73.9 1.1 %sums.1 = (f32[3,512]{1,0:T(4,128)}, f32[2048,512]{1,0:T(8,128)}) custom-call(f32[32,1,1536]{2,1,0:T(1,128)S(1)} %all_to_all.5.parts, f32[2,640,256]{2,1,0:T(8,128)S(1)} %get-tuple-element.89.rims, f32[2048,512]{1,0:T(8,128)} %get-tuple-element.90._), custom_call_target="tpu_custom_call", output_to_operand_aliasing={{1}: (2, {})} | custom-call | tf_op jit(solution)/shard_map/sums/pallas_call | solution.py:459
  (20 shorter events, 0.0 us)
Async XLA Ops:
  0.6 8.2 %copy-start.3 = (s32[16,9]{1,0:T(8,128)S(1)}, s32[16,9]{1,0:T(8,128)}, u32[]{:S(2)}) copy-start(s32[16,9]{1,0:T(8,128)} %param.7) | copy-start | bytes 1732
  2.1 19.3 %collective-permute-start = (bf16[640,256]{1,0:T(8,128)(2,1)S(1)}, bf16[640,256]{1,0:T(8,128)(2,1)S(1)}, u32[]{:S(2)}, u32[]{:S(2)}) collective-permute-start(bf16[640,256]{1,0:T(8,128)(2,1)S(1)} %get-tuple-element.48._), channel_id=1, source_target_pairs={{4,8},{8,4},{12,16},{16,12},{20,24},{24,20},{28,32},{32,28},{36,40... | collective-permute-start | bytes 983048 | tf_op jit(solution)/shard_map/ppermute | solution.py:301
  8.8 12.5 %collective-permute-start.1 = (bf16[640,256]{1,0:T(8,128)(2,1)S(1)}, bf16[640,256]{1,0:T(8,128)(2,1)S(1)}, u32[]{:S(2)}, u32[]{:S(2)}) collective-permute-start(bf16[640,256]{1,0:T(8,128)(2,1)S(1)} %get-tuple-element.52), channel_id=1, source_target_pairs={{0,4},{4,0},{8,12},{12,8},{16,20},{20,16},{24,28},{28,24},{32,36},... | collective-permute-start | bytes 983048 | tf_op jit(solution)/shard_map/ppermute | solution.py:302
  8.9 7.0 %copy-start.1 = (bf16[2048,512]{1,0:T(8,128)(2,1)S(1)}, bf16[2048,512]{1,0:T(8,128)(2,1)}, u32[]{:S(2)}) copy-start(bf16[2048,512]{1,0:T(8,128)(2,1)} %probe.1) | copy-start | bytes 6291460
  8.9 7.0 %copy-start.2 = (f32[2048]{0:T(1024)S(1)}, f32[2048]{0:T(1024)}, u32[]{:S(2)}) copy-start(f32[2048]{0:T(1024)} %param.11) | copy-start | bytes 24580
  13.8 2.6 %copy-start = (f32[2048,512]{1,0:T(8,128)S(1)}, f32[2048,512]{1,0:T(8,128)}, u32[]{:S(2)}) copy-start(f32[2048,512]{1,0:T(8,128)} %refs_3_.3) | copy-start | bytes 12582916
  13.8 17.6 %collective-permute-start.2 = (bf16[640,256]{1,0:T(8,128)(2,1)S(1)}, bf16[640,256]{1,0:T(8,128)(2,1)S(1)}, u32[]{:S(2)}, u32[]{:S(2)}) collective-permute-start(bf16[640,256]{1,0:T(8,128)(2,1)S(1)} %get-tuple-element.49._), channel_id=1, source_target_pairs={{4,8},{8,4},{12,16},{16,12},{20,24},{24,20},{28,32},{32,28},{36,40... | collective-permute-start | bytes 983048 | tf_op jit(solution)/shard_map/ppermute | solution.py:301
  15.2 16.2 %collective-permute-start.3 = (bf16[640,256]{1,0:T(8,128)(2,1)S(1)}, bf16[640,256]{1,0:T(8,128)(2,1)S(1)}, u32[]{:S(2)}, u32[]{:S(2)}) collective-permute-start(bf16[640,256]{1,0:T(8,128)(2,1)S(1)} %get-tuple-element.57), channel_id=1, source_target_pairs={{0,4},{4,0},{8,12},{12,8},{16,20},{20,16},{24,28},{28,24},{32,36},... | collective-permute-start | bytes 983048 | tf_op jit(solution)/shard_map/ppermute | solution.py:302
  22.2 13.9 %collective-permute-start.4 = (bf16[640,256]{1,0:T(8,128)(2,1)S(1)}, bf16[640,256]{1,0:T(8,128)(2,1)S(1)}, u32[]{:S(2)}, u32[]{:S(2)}) collective-permute-start(bf16[640,256]{1,0:T(8,128)(2,1)S(1)} %get-tuple-element.62.refs_2_), channel_id=1, source_target_pairs={{4,8},{8,4},{12,16},{16,12},{20,24},{24,20},{28,32},{32,28},{36,40... | collective-permute-start | bytes 983048 | tf_op jit(solution)/shard_map/ppermute | solution.py:301
  26.4 9.7 %collective-permute-start.5 = (bf16[640,256]{1,0:T(8,128)(2,1)S(1)}, bf16[640,256]{1,0:T(8,128)(2,1)S(1)}, u32[]{:S(2)}, u32[]{:S(2)}) collective-permute-start(bf16[640,256]{1,0:T(8,128)(2,1)S(1)} %get-tuple-element.60.refs_0_), channel_id=1, source_target_pairs={{0,4},{4,0},{8,12},{12,8},{16,20},{20,16},{24,28},{28,24},{32,36},... | collective-permute-start | bytes 983048 | tf_op jit(solution)/shard_map/ppermute | solution.py:302
  32.2 14.9 %collective-permute-start.6 = (bf16[640,256]{1,0:T(8,128)(2,1)S(1)}, bf16[640,256]{1,0:T(8,128)(2,1)S(1)}, u32[]{:S(2)}, u32[]{:S(2)}) collective-permute-start(bf16[640,256]{1,0:T(8,128)(2,1)S(1)} %get-tuple-element.68.refs_2_), channel_id=1, source_target_pairs={{4,8},{8,4},{12,16},{16,12},{20,24},{24,20},{28,32},{32,28},{36,40... | collective-permute-start | bytes 983048 | tf_op jit(solution)/shard_map/ppermute | solution.py:301
  34.4 12.8 %collective-permute-start.7 = (bf16[640,256]{1,0:T(8,128)(2,1)S(1)}, bf16[640,256]{1,0:T(8,128)(2,1)S(1)}, u32[]{:S(2)}, u32[]{:S(2)}) collective-permute-start(bf16[640,256]{1,0:T(8,128)(2,1)S(1)} %get-tuple-element.66.refs_0_), channel_id=1, source_target_pairs={{0,4},{4,0},{8,12},{12,8},{16,20},{20,16},{24,28},{28,24},{32,36},... | collective-permute-start | bytes 983048 | tf_op jit(solution)/shard_map/ppermute | solution.py:302
  36.9 19.1 %collective-permute-start.8 = (bf16[640,256]{1,0:T(8,128)(2,1)S(1)}, bf16[640,256]{1,0:T(8,128)(2,1)S(1)}, u32[]{:S(2)}, u32[]{:S(2)}) collective-permute-start(bf16[640,256]{1,0:T(8,128)(2,1)S(1)} %get-tuple-element.75.refs_2_), channel_id=1, source_target_pairs={{4,8},{8,4},{12,16},{16,12},{20,24},{24,20},{28,32},{32,28},{36,40... | collective-permute-start | bytes 983048 | tf_op jit(solution)/shard_map/ppermute | solution.py:301
  41.1 14.9 %collective-permute-start.9 = (bf16[640,256]{1,0:T(8,128)(2,1)S(1)}, bf16[640,256]{1,0:T(8,128)(2,1)S(1)}, u32[]{:S(2)}, u32[]{:S(2)}) collective-permute-start(bf16[640,256]{1,0:T(8,128)(2,1)S(1)} %get-tuple-element.73.refs_0_), channel_id=1, source_target_pairs={{0,4},{4,0},{8,12},{12,8},{16,20},{20,16},{24,28},{28,24},{32,36},... | collective-permute-start | bytes 983048 | tf_op jit(solution)/shard_map/ppermute | solution.py:302
  47.9 11.4 %collective-permute-start.10 = (bf16[640,256]{1,0:T(8,128)(2,1)S(1)}, bf16[640,256]{1,0:T(8,128)(2,1)S(1)}, u32[]{:S(2)}, u32[]{:S(2)}) collective-permute-start(bf16[640,256]{1,0:T(8,128)(2,1)S(1)} %get-tuple-element.80.refs_2_), channel_id=1, source_target_pairs={{4,8},{8,4},{12,16},{16,12},{20,24},{24,20},{28,32},{32,28},{36,40... | collective-permute-start | bytes 983048 | tf_op jit(solution)/shard_map/ppermute | solution.py:301
  50.1 9.3 %collective-permute-start.11 = (bf16[640,256]{1,0:T(8,128)(2,1)S(1)}, bf16[640,256]{1,0:T(8,128)(2,1)S(1)}, u32[]{:S(2)}, u32[]{:S(2)}) collective-permute-start(bf16[640,256]{1,0:T(8,128)(2,1)S(1)} %get-tuple-element.78.refs_0_), channel_id=1, source_target_pairs={{0,4},{4,0},{8,12},{12,8},{16,20},{20,16},{24,28},{28,24},{32,36},... | collective-permute-start | bytes 983048 | tf_op jit(solution)/shard_map/ppermute | solution.py:302

commit v5 on v4

--- a/solution.py
+++ b/solution.py
@@ -109,19 +109,11 @@
 
 def middle_kernel(sources, first, cols, width, rows_blk, odd, _, banded, weights, *refs):
     source, previous = refs[:sources], refs[sources]
-    results = refs[sources + 1 + (first > 0) :]
-    if sources == 1:
-        *results, held, sems = results
-    upcoming, *inner, partial, x = results
+    upcoming, *inner, partial, x = refs[sources + 1 + (first > 0) :]
     columns = pl.ds(first, cols)
     rim = BAND * width
     rows = rows_blk * width
     if sources == 1:
-        copies = []
-        for pair in range(rows_blk // 2):
-            two = pl.ds(2 * pair * width, 2 * width)
-            copies.append(pltpu.make_async_copy(previous.at[two, columns], held.at[two], sems.at[pair]))
-            copies[-1].start()
         x[...] = source[0][:, columns].astype(BF16)
     else:
         evens, inside, odds = source
@@ -143,12 +135,7 @@
             preferred_element_type=F32,
         )
         here = pl.ds(2 * pair * width, 2 * width)
-        if sources == 1:
-            copies[pair].wait()
-            before = held[here]
-        else:
-            before = previous[here, columns]
-        result = 2.0 * product - before
+        result = 2.0 * product - previous[here, columns]
         upcoming[here, columns] = result
         a = max(2 * pair, BAND)
         b = min(2 * pair + 2, rows_blk - BAND)
@@ -303,16 +290,10 @@
 
     def middle(token, term, chunk):
         args = [odd, token, banded, weights, *sources[chunk], terms[term]]
-        specs = [SMEM] + [VMEM] * (len(args) - 1)
-        scratch = [pltpu.VMEM((rows, cols), BF16)]
-        if term == 0:
-            args[-1], specs[-1] = in_hbm(previous), HBM
-            scratch += [pltpu.VMEM((rows, cols), F32), pltpu.SemaphoreType.DMA((pairs,))]
         aliases = {}
         if chunk:
             aliases = {len(args): 0}
             args.append(terms[term + 2])
-            specs.append(VMEM)
         outs = (full_shape, shape((rows - 2 * rim, cols), BF16), part_shape)
         if term == TERMS - 1:
             outs = (full_shape, part_shape)
@@ -321,9 +302,9 @@
                 middle_kernel, len(sources[chunk]), chunk * cols, cols, width, rows_blk
             ),
             out_shape=outs,
-            in_specs=specs,
+            in_specs=[SMEM] + [VMEM] * (len(args) - 1),
             out_specs=(VMEM,) * len(outs),
-            scratch_shapes=scratch,
+            scratch_shapes=[pltpu.VMEM((rows, cols), BF16)],
             input_output_aliases=aliases,
             compiler_params=params(),
             cost_estimate=cost(flops, 8 * 1024 * 1024),

time: 75.4 us -> 70.5 us (0.935)
  Pallas kernels: 32.2 us -> 25.6 us
  waiting for transfers between devices: 6.1 us -> 10 us
  blocking collectives: 14 us -> 12.8 us
  starting transfers between devices: 21.7 us -> 20.8 us
    pallas_call x6, Pallas kernels: 17 us -> 9.99 us  [middle(): pl.pallas_call(functools.partial(middle_kernel, len(sources[chunk]), chun...]
    ppermute x6, waiting for transfers between devices: 6.08 us -> 9.55 us  [exchange(): ahead = lax.ppermute(odds, 'slab', pairs_of[1])]
    all_to_all x1, blocking collectives: 14 us -> 12.8 us  [local(): gathered = lax.all_to_all(scattered, 'slab', 0, 0)]
    ppermute x6, starting transfers between devices: 20.9 us -> 20 us  [exchange(): ahead = lax.ppermute(odds, 'slab', pairs_of[1])]
  transfers between devices with their start and end apart: 12 -> 12, of which waited for: 2 -> 5; matrix products, arithmetic and copies ran while one was open for 0% -> 0% of each run, Pallas kernels for 39% -> 32%
where the time goes in v5:
time: 70.5 us; the launch traced here: 70.3 us
  Pallas kernels  25.6 us (36%)
  starting transfers between devices  20.8 us (30%)
  blocking collectives  12.8 us (18%)
  waiting for transfers between devices  10 us (14%)
  between operations  1.01 us (1%)
    ppermute x6, starting transfers between devices, exchange(): ahead = lax.ppermute(odds, 'slab', pairs_of[1])  20 us
    all_to_all x1, blocking collectives, local(): gathered = lax.all_to_all(scattered, 'slab', 0, 0)  12.8 us
    pallas_call x6, Pallas kernels, middle(): pl.pallas_call(functools.partial(middle_kernel, len(sources[chunk]), chun...  9.99 us
    ppermute x6, waiting for transfers between devices, exchange(): ahead = lax.ppermute(odds, 'slab', pairs_of[1])  9.55 us
    pallas_call x1, Pallas kernels, local(): pl.pallas_call(functools.partial(band_kernel, cols, cols), out_shape=(sha...  5.14 us
    pallas_call x6, Pallas kernels, rims(): pl.pallas_call(kernel, out_shape=outs, in_specs=specs, out_specs=out_spec...  5.02 us
    pallas_call x1, Pallas kernels, local(): pl.pallas_call(functools.partial(store_kernel, rim), out_shape=(full_shap...  2.54 us
    pallas_call x1, Pallas kernels, local(): pl.pallas_call(functools.partial(edge_kernel, 0, cols), out_shape=(edge_s...  1.46 us
  transfers between devices with their start and end apart: 12, of which 5 were waited for; matrix products, arithmetic and copies ran while one was open for 0% of the time, Pallas kernels for 32%

profile of v5, /device:TPU:0, one launch (start us, length us, event | category | flops | bytes accessed | tf_op | source)
XLA Modules:
  0.0 70.3 jit_solution(14393058295503986961)
XLA Ops:
  0.6 1.5 %edges.1 = (bf16[640,256]{1,0:T(8,128)(2,1)S(1)}, bf16[640,256]{1,0:T(8,128)(2,1)S(1)}) custom-call(s32[1]{0:T(128)} %bitcast.odd, f32[2048,512]{1,0:T(8,128)} %refs_3_.3), custom_call_target="tpu_custom_call" | custom-call | bytes 1966080 | tf_op jit(solution)/shard_map/edges/pallas_call | solution.py:359
  2.1 6.7 %collective-permute-start = (bf16[640,256]{1,0:T(8,128)(2,1)S(1)}, bf16[640,256]{1,0:T(8,128)(2,1)S(1)}, u32[]{:S(2)}, u32[]{:S(2)}) collective-permute-start(bf16[640,256]{1,0:T(8,128)(2,1)S(1)} %get-tuple-element.48._), channel_id=1, source_target_pairs={{4,8},{8,4},{12,16},{16,12},{20,24},{24,20},{28,32},{32,28},{36,40... | collective-permute-start | bytes 983048 | tf_op jit(solution)/shard_map/ppermute | solution.py:288
  8.8 0.1 add_select_fusion.places
  8.9 0.0 copy-start.3
  9.0 5.1 %band.1 = (bf16[8,256,1536]{2,1,0:T(8,128)(2,1)S(1)}, bf16[640,256]{1,0:T(8,128)(2,1)S(1)}, bf16[640,256]{1,0:T(8,128)(2,1)S(1)}) custom-call(s32[1]{0:T(128)} %bitcast.odd, bf16[640,256]{1,0:T(8,128)(2,1)S(1)} %get-tuple-element.48._, s32[16,9]{1,0:T(8,128)S(1)} %add_select_fusion.places, bf16[16,9,128,128]{3,2,1,0:T(8,128)(2,1)} %blocks.1, f32[2048,512]{1,0:T(8,128)} %refs_3_.3), custom_call_target="tpu_custom_call" | custom-call | bytes 12582912 | tf_op jit(solution)/shard_map/band/pallas_call | solution.py:370
  14.1 1.4 %collective-permute-start.2 = (bf16[640,256]{1,0:T(8,128)(2,1)S(1)}, bf16[640,256]{1,0:T(8,128)(2,1)S(1)}, u32[]{:S(2)}, u32[]{:S(2)}) collective-permute-start(bf16[640,256]{1,0:T(8,128)(2,1)S(1)} %get-tuple-element.49._), channel_id=1, source_target_pairs={{4,8},{8,4},{12,16},{16,12},{20,24},{24,20},{28,32},{32,28},{36,40... | collective-permute-start | bytes 983048 | tf_op jit(solution)/shard_map/ppermute | solution.py:288
  15.6 0.8 %collective-permute-start.3 = (bf16[640,256]{1,0:T(8,128)(2,1)S(1)}, bf16[640,256]{1,0:T(8,128)(2,1)S(1)}, u32[]{:S(2)}, u32[]{:S(2)}) collective-permute-start(bf16[640,256]{1,0:T(8,128)(2,1)S(1)} %get-tuple-element.57), channel_id=1, source_target_pairs={{0,4},{4,0},{8,12},{12,8},{16,20},{20,16},{24,28},{28,24},{32,36},... | collective-permute-start | bytes 983048 | tf_op jit(solution)/shard_map/ppermute | solution.py:289
  16.3 0.3 weights.1._
  16.7 1.6 %middle.6 = (f32[2048,512]{1,0:T(8,128)S(1)}, bf16[768,256]{1,0:T(8,128)(2,1)S(1)}, f32[8,256]{1,0:T(8,128)S(1)}) custom-call(s32[1]{0:T(128)} %bitcast.odd, f32[2048,512]{1,0:T(8,128)S(1)} %weights.1._, bf16[8,256,1536]{2,1,0:T(8,128)(2,1)S(1)} %get-tuple-element.50.banded, f32[2048,512]{1,0:T(8,128)S(1)} %weights.1._, f32[2048,512]{1,0:T(8,128)S(1)} %copy-done, ...), custom_call_target="tpu_custom_call" | custom-call | flops 1207959552 | bytes 8388608 | tf_op jit(solution)/shard_map/middle/pallas_call | solution.py:300
  18.3 0.5 collective-permute-done.1.evens_in
  18.8 0.8 %rims.6 = (f32[2048,512]{1,0:T(8,128)S(1)}, f32[8,256]{1,0:T(8,128)S(1)}, bf16[640,256]{1,0:T(8,128)(2,1)S(1)}, bf16[640,256]{1,0:T(8,128)(2,1)S(1)}) custom-call(s32[1]{0:T(128)} %bitcast.odd, f32[8,256]{1,0:T(8,128)S(1)} %get-tuple-element.51._.partial, bf16[8,256,1536]{2,1,0:T(8,128)(2,1)S(1)} %get-tuple-element.50.banded, ...), custom_call_target="tpu_custom_call", output_to_operand_aliasing={{0}: (6, {})} | custom-call | flops 241591904 | bytes 2097152 | tf_op jit(solution)/shard_map/rims/pallas_call | solution.py:341
  19.6 4.6 %collective-permute-start.4 = (bf16[640,256]{1,0:T(8,128)(2,1)S(1)}, bf16[640,256]{1,0:T(8,128)(2,1)S(1)}, u32[]{:S(2)}, u32[]{:S(2)}) collective-permute-start(bf16[640,256]{1,0:T(8,128)(2,1)S(1)} %get-tuple-element.62.refs_2_), channel_id=1, source_target_pairs={{4,8},{8,4},{12,16},{16,12},{20,24},{24,20},{28,32},{32,28},{36,40... | collective-permute-start | bytes 983048 | tf_op jit(solution)/shard_map/ppermute | solution.py:288
  24.2 1.6 %middle.7 = (f32[2048,512]{1,0:T(8,128)S(1)}, bf16[768,256]{1,0:T(8,128)(2,1)S(1)}, f32[8,256]{1,0:T(8,128)S(1)}) custom-call(s32[1]{0:T(128)} %bitcast.odd, f32[8,256]{1,0:T(8,128)S(1)} %get-tuple-element.54._.refs_0_, bf16[8,256,1536]{2,1,0:T(8,128)(2,1)S(1)} %get-tuple-element.50.banded, ...), custom_call_target="tpu_custom_call", output_to_operand_aliasing={{0}: (6, {})} | custom-call | flops 1207959552 | bytes 8388608 | tf_op jit(solution)/shard_map/middle/pallas_call | solution.py:300
  25.8 3.3 %collective-permute-done.2.odds_in = bf16[640,256]{1,0:T(8,128)(2,1)S(1)} collective-permute-done((bf16[640,256]{1,0:T(8,128)(2,1)S(1)}, bf16[640,256]{1,0:T(8,128)(2,1)S(1)}, u32[]{:S(2)}, u32[]{:S(2)}) %collective-permute-start.2) | collective-permute-done | bytes 327712 | tf_op jit(solution)/shard_map/ppermute | solution.py:288
  29.1 0.8 %rims.7 = (f32[2048,512]{1,0:T(8,128)S(1)}, f32[8,256]{1,0:T(8,128)S(1)}, bf16[640,256]{1,0:T(8,128)(2,1)S(1)}, bf16[640,256]{1,0:T(8,128)(2,1)S(1)}) custom-call(s32[1]{0:T(128)} %bitcast.odd, f32[8,256]{1,0:T(8,128)S(1)} %get-tuple-element.56._.partial, bf16[8,256,1536]{2,1,0:T(8,128)(2,1)S(1)} %get-tuple-element.50.banded, ...), custom_call_target="tpu_custom_call", output_to_operand_aliasing={{0}: (6, {})} | custom-call | flops 241591904 | bytes 2097152 | tf_op jit(solution)/shard_map/rims/pallas_call | solution.py:341
  29.8 2.1 %collective-permute-start.6 = (bf16[640,256]{1,0:T(8,128)(2,1)S(1)}, bf16[640,256]{1,0:T(8,128)(2,1)S(1)}, u32[]{:S(2)}, u32[]{:S(2)}) collective-permute-start(bf16[640,256]{1,0:T(8,128)(2,1)S(1)} %get-tuple-element.68.refs_2_), channel_id=1, source_target_pairs={{4,8},{8,4},{12,16},{16,12},{20,24},{24,20},{28,32},{32,28},{36,40... | collective-permute-start | bytes 983048 | tf_op jit(solution)/shard_map/ppermute | solution.py:288
  31.9 1.7 %middle.8 = (f32[2048,512]{1,0:T(8,128)S(1)}, bf16[768,256]{1,0:T(8,128)(2,1)S(1)}, f32[8,256]{1,0:T(8,128)S(1)}) custom-call(s32[1]{0:T(128)} %bitcast.odd, f32[8,256]{1,0:T(8,128)S(1)} %get-tuple-element.59._.refs_1_, bf16[8,256,1536]{2,1,0:T(8,128)(2,1)S(1)} %get-tuple-element.50.banded, f32[2048,512]{1,0:T(8,128)S(1)} %weights.1._, ...), custom_call_target="tpu_custom_call" | custom-call | flops 1207959552 | bytes 8388608 | tf_op jit(solution)/shard_map/middle/pallas_call | solution.py:300
  33.6 1.6 %collective-permute-done.4.odds_in = bf16[640,256]{1,0:T(8,128)(2,1)S(1)} collective-permute-done((bf16[640,256]{1,0:T(8,128)(2,1)S(1)}, bf16[640,256]{1,0:T(8,128)(2,1)S(1)}, u32[]{:S(2)}, u32[]{:S(2)}) %collective-permute-start.4) | collective-permute-done | bytes 327712 | tf_op jit(solution)/shard_map/ppermute | solution.py:288
  35.3 0.8 %rims.8 = (f32[2048,512]{1,0:T(8,128)S(1)}, f32[8,256]{1,0:T(8,128)S(1)}, bf16[640,256]{1,0:T(8,128)(2,1)S(1)}, bf16[640,256]{1,0:T(8,128)(2,1)S(1)}) custom-call(s32[1]{0:T(128)} %bitcast.odd, f32[8,256]{1,0:T(8,128)S(1)} %get-tuple-element.63._.partial, bf16[8,256,1536]{2,1,0:T(8,128)(2,1)S(1)} %get-tuple-element.50.banded, ...), custom_call_target="tpu_custom_call", output_to_operand_aliasing={{0}: (6, {})} | custom-call | flops 241591904 | bytes 2097152 | tf_op jit(solution)/shard_map/rims/pallas_call | solution.py:341
  36.0 2.7 %collective-permute-start.8 = (bf16[640,256]{1,0:T(8,128)(2,1)S(1)}, bf16[640,256]{1,0:T(8,128)(2,1)S(1)}, u32[]{:S(2)}, u32[]{:S(2)}) collective-permute-start(bf16[640,256]{1,0:T(8,128)(2,1)S(1)} %get-tuple-element.75.refs_2_), channel_id=1, source_target_pairs={{4,8},{8,4},{12,16},{16,12},{20,24},{24,20},{28,32},{32,28},{36,40... | collective-permute-start | bytes 983048 | tf_op jit(solution)/shard_map/ppermute | solution.py:288
  38.7 1.7 %middle.9 = (f32[2048,512]{1,0:T(8,128)S(1)}, bf16[768,256]{1,0:T(8,128)(2,1)S(1)}, f32[8,256]{1,0:T(8,128)S(1)}) custom-call(s32[1]{0:T(128)} %bitcast.odd, f32[8,256]{1,0:T(8,128)S(1)} %get-tuple-element.65._.refs_2_, bf16[8,256,1536]{2,1,0:T(8,128)(2,1)S(1)} %get-tuple-element.50.banded, ...), custom_call_target="tpu_custom_call", output_to_operand_aliasing={{0}: (8, {})} | custom-call | flops 1207959552 | bytes 8388608 | tf_op jit(solution)/shard_map/middle/pallas_call | solution.py:300
  40.4 1.9 %collective-permute-done.6.odds_in = bf16[640,256]{1,0:T(8,128)(2,1)S(1)} collective-permute-done((bf16[640,256]{1,0:T(8,128)(2,1)S(1)}, bf16[640,256]{1,0:T(8,128)(2,1)S(1)}, u32[]{:S(2)}, u32[]{:S(2)}) %collective-permute-start.6) | collective-permute-done | bytes 327712 | tf_op jit(solution)/shard_map/ppermute | solution.py:288
  42.3 0.8 %rims.9 = (f32[2048,512]{1,0:T(8,128)S(1)}, f32[8,256]{1,0:T(8,128)S(1)}, bf16[640,256]{1,0:T(8,128)(2,1)S(1)}, bf16[640,256]{1,0:T(8,128)(2,1)S(1)}) custom-call(s32[1]{0:T(128)} %bitcast.odd, f32[8,256]{1,0:T(8,128)S(1)} %get-tuple-element.70._.partial, bf16[8,256,1536]{2,1,0:T(8,128)(2,1)S(1)} %get-tuple-element.50.banded, ...), custom_call_target="tpu_custom_call", output_to_operand_aliasing={{0}: (6, {})} | custom-call | flops 241591904 | bytes 2097152 | tf_op jit(solution)/shard_map/rims/pallas_call | solution.py:341
  43.1 2.4 %collective-permute-start.10 = (bf16[640,256]{1,0:T(8,128)(2,1)S(1)}, bf16[640,256]{1,0:T(8,128)(2,1)S(1)}, u32[]{:S(2)}, u32[]{:S(2)}) collective-permute-start(bf16[640,256]{1,0:T(8,128)(2,1)S(1)} %get-tuple-element.80.refs_2_), channel_id=1, source_target_pairs={{4,8},{8,4},{12,16},{16,12},{20,24},{24,20},{28,32},{32,28},{36,40... | collective-permute-start | bytes 983048 | tf_op jit(solution)/shard_map/ppermute | solution.py:288
  45.5 1.7 %middle.10 = (f32[2048,512]{1,0:T(8,128)S(1)}, f32[8,256]{1,0:T(8,128)S(1)}) custom-call(s32[1]{0:T(128)} %bitcast.odd, f32[8,256]{1,0:T(8,128)S(1)} %get-tuple-element.72._.refs_3_, bf16[8,256,1536]{2,1,0:T(8,128)(2,1)S(1)} %get-tuple-element.50.banded, f32[2048,512]{1,0:T(8,128)S(1)} %weights.1._, bf16[640,256]{1,0:T(8,128)(2,1)S(1)} %get-tuple-element.73.refs_0_, ...), custom_call_target="tpu_custom_call" | custom-call | flops 1207959552 | bytes 8388608 | tf_op jit(solution)/shard_map/middle/pallas_call | solution.py:300
  47.2 1.7 %middle.11 = (f32[2048,512]{1,0:T(8,128)S(1)}, f32[8,256]{1,0:T(8,128)S(1)}) custom-call(s32[1]{0:T(128)} %bitcast.odd, f32[8,256]{1,0:T(8,128)S(1)} %get-tuple-element.77._.partial, bf16[8,256,1536]{2,1,0:T(8,128)(2,1)S(1)} %get-tuple-element.50.banded, f32[2048,512]{1,0:T(8,128)S(1)} %weights.1._, ...), custom_call_target="tpu_custom_call", output_to_operand_aliasing={{0}: (8, {})} | custom-call | flops 1207959552 | bytes 8388608 | tf_op jit(solution)/shard_map/middle/pallas_call | solution.py:300
  48.9 2.5 %store.1 = (f32[2048,512]{1,0:T(8,128)}, f32[2048,512]{1,0:T(8,128)}) custom-call(f32[8,256]{1,0:T(8,128)S(1)} %get-tuple-element.82._.partial, f32[2048,512]{1,0:T(8,128)S(1)} %get-tuple-element.83.previous, f32[2048,512]{1,0:T(8,128)S(1)} %get-tuple-element.84.current.begun), custom_call_target="tpu_custom_call" | custom-call | bytes 16777216 | tf_op jit(solution)/shard_map/store/pallas_call | solution.py:428
  51.5 1.4 %rims.10 = (f32[2048,512]{1,0:T(8,128)}, f32[8,256]{1,0:T(8,128)S(1)}) custom-call(s32[1]{0:T(128)} %bitcast.odd, f32[8,256]{1,0:T(8,128)S(1)} %get-tuple-element.82._.partial, bf16[8,256,1536]{2,1,0:T(8,128)(2,1)S(1)} %get-tuple-element.50.banded, f32[2048,512]{1,0:T(8,128)S(1)} %weights.1._, ...), custom_call_target="tpu_custom_call", output_to_operand_aliasing={{0}: (8, {})} | custom-call | flops 241591904 | bytes 2097152 | tf_op jit(solution)/shard_map/rims/pallas_call | solution.py:341
  52.9 2.8 %collective-permute-done.10.odds_in = bf16[640,256]{1,0:T(8,128)(2,1)S(1)} collective-permute-done((bf16[640,256]{1,0:T(8,128)(2,1)S(1)}, bf16[640,256]{1,0:T(8,128)(2,1)S(1)}, u32[]{:S(2)}, u32[]{:S(2)}) %collective-permute-start.10) | collective-permute-done | bytes 327712 | tf_op jit(solution)/shard_map/ppermute | solution.py:288
  55.7 0.6 rims.11
  56.3 12.8 %all_to_all.5.parts = f32[32,1,1536]{2,1,0:T(1,128)S(1)} all-to-all(f32[32,1,1536]{2,1,0:T(1,128)S(1)} %get-tuple-element.88), channel_id=1, replica_groups=mesh['slab'=32,'col'=4] {'slab'}, dimensions={0} | all-to-all | bytes 393216 | tf_op jit(solution)/shard_map/all_to_all | solution.py:438
  69.0 1.1 %sums.1 = (f32[3,512]{1,0:T(4,128)}, f32[2048,512]{1,0:T(8,128)}) custom-call(f32[32,1,1536]{2,1,0:T(1,128)S(1)} %all_to_all.5.parts, f32[2,640,256]{2,1,0:T(8,128)S(1)} %get-tuple-element.89.rims, f32[2048,512]{1,0:T(8,128)} %get-tuple-element.90._), custom_call_target="tpu_custom_call", output_to_operand_aliasing={{1}: (2, {})} | custom-call | tf_op jit(solution)/shard_map/sums/pallas_call | solution.py:440
  (22 shorter events, 0.1 us)
Async XLA Ops:
  0.6 8.2 %copy-start.4 = (s32[16,9]{1,0:T(8,128)S(1)}, s32[16,9]{1,0:T(8,128)}, u32[]{:S(2)}) copy-start(s32[16,9]{1,0:T(8,128)} %param.7) | copy-start | bytes 1732
  2.1 16.2 %collective-permute-start = (bf16[640,256]{1,0:T(8,128)(2,1)S(1)}, bf16[640,256]{1,0:T(8,128)(2,1)S(1)}, u32[]{:S(2)}, u32[]{:S(2)}) collective-permute-start(bf16[640,256]{1,0:T(8,128)(2,1)S(1)} %get-tuple-element.48._), channel_id=1, source_target_pairs={{4,8},{8,4},{12,16},{16,12},{20,24},{24,20},{28,32},{32,28},{36,40... | collective-permute-start | bytes 983048 | tf_op jit(solution)/shard_map/ppermute | solution.py:288
  8.8 10.0 %collective-permute-start.1 = (bf16[640,256]{1,0:T(8,128)(2,1)S(1)}, bf16[640,256]{1,0:T(8,128)(2,1)S(1)}, u32[]{:S(2)}, u32[]{:S(2)}) collective-permute-start(bf16[640,256]{1,0:T(8,128)(2,1)S(1)} %get-tuple-element.52), channel_id=1, source_target_pairs={{0,4},{4,0},{8,12},{12,8},{16,20},{20,16},{24,28},{28,24},{32,36},... | collective-permute-start | bytes 983048 | tf_op jit(solution)/shard_map/ppermute | solution.py:289
  8.9 7.4 %copy-start.2 = (bf16[2048,512]{1,0:T(8,128)(2,1)S(1)}, bf16[2048,512]{1,0:T(8,128)(2,1)}, u32[]{:S(2)}) copy-start(bf16[2048,512]{1,0:T(8,128)(2,1)} %probe.1) | copy-start | bytes 6291460
  8.9 7.4 %copy-start.3 = (f32[2048]{0:T(1024)S(1)}, f32[2048]{0:T(1024)}, u32[]{:S(2)}) copy-start(f32[2048]{0:T(1024)} %param.11) | copy-start | bytes 24580
  8.9 7.7 %copy-start.1 = (f32[2048,512]{1,0:T(8,128)S(1)}, f32[2048,512]{1,0:T(8,128)}, u32[]{:S(2)}) copy-start(f32[2048,512]{1,0:T(8,128)} %refs_1_.3) | copy-start | bytes 12582916
  14.1 2.6 %copy-start = (f32[2048,512]{1,0:T(8,128)S(1)}, f32[2048,512]{1,0:T(8,128)}, u32[]{:S(2)}) copy-start(f32[2048,512]{1,0:T(8,128)} %refs_3_.3) | copy-start | bytes 12582916
  14.1 14.9 %collective-permute-start.2 = (bf16[640,256]{1,0:T(8,128)(2,1)S(1)}, bf16[640,256]{1,0:T(8,128)(2,1)S(1)}, u32[]{:S(2)}, u32[]{:S(2)}) collective-permute-start(bf16[640,256]{1,0:T(8,128)(2,1)S(1)} %get-tuple-element.49._), channel_id=1, source_target_pairs={{4,8},{8,4},{12,16},{16,12},{20,24},{24,20},{28,32},{32,28},{36,40... | collective-permute-start | bytes 983048 | tf_op jit(solution)/shard_map/ppermute | solution.py:288
  15.6 13.5 %collective-permute-start.3 = (bf16[640,256]{1,0:T(8,128)(2,1)S(1)}, bf16[640,256]{1,0:T(8,128)(2,1)S(1)}, u32[]{:S(2)}, u32[]{:S(2)}) collective-permute-start(bf16[640,256]{1,0:T(8,128)(2,1)S(1)} %get-tuple-element.57), channel_id=1, source_target_pairs={{0,4},{4,0},{8,12},{12,8},{16,20},{20,16},{24,28},{28,24},{32,36},... | collective-permute-start | bytes 983048 | tf_op jit(solution)/shard_map/ppermute | solution.py:289
  19.6 15.7 %collective-permute-start.4 = (bf16[640,256]{1,0:T(8,128)(2,1)S(1)}, bf16[640,256]{1,0:T(8,128)(2,1)S(1)}, u32[]{:S(2)}, u32[]{:S(2)}) collective-permute-start(bf16[640,256]{1,0:T(8,128)(2,1)S(1)} %get-tuple-element.62.refs_2_), channel_id=1, source_target_pairs={{4,8},{8,4},{12,16},{16,12},{20,24},{24,20},{28,32},{32,28},{36,40... | collective-permute-start | bytes 983048 | tf_op jit(solution)/shard_map/ppermute | solution.py:288
  24.2 11.1 %collective-permute-start.5 = (bf16[640,256]{1,0:T(8,128)(2,1)S(1)}, bf16[640,256]{1,0:T(8,128)(2,1)S(1)}, u32[]{:S(2)}, u32[]{:S(2)}) collective-permute-start(bf16[640,256]{1,0:T(8,128)(2,1)S(1)} %get-tuple-element.60.refs_0_), channel_id=1, source_target_pairs={{0,4},{4,0},{8,12},{12,8},{16,20},{20,16},{24,28},{28,24},{32,36},... | collective-permute-start | bytes 983048 | tf_op jit(solution)/shard_map/ppermute | solution.py:289
  29.8 12.5 %collective-permute-start.6 = (bf16[640,256]{1,0:T(8,128)(2,1)S(1)}, bf16[640,256]{1,0:T(8,128)(2,1)S(1)}, u32[]{:S(2)}, u32[]{:S(2)}) collective-permute-start(bf16[640,256]{1,0:T(8,128)(2,1)S(1)} %get-tuple-element.68.refs_2_), channel_id=1, source_target_pairs={{4,8},{8,4},{12,16},{16,12},{20,24},{24,20},{28,32},{32,28},{36,40... | collective-permute-start | bytes 983048 | tf_op jit(solution)/shard_map/ppermute | solution.py:288
  31.9 10.3 %collective-permute-start.7 = (bf16[640,256]{1,0:T(8,128)(2,1)S(1)}, bf16[640,256]{1,0:T(8,128)(2,1)S(1)}, u32[]{:S(2)}, u32[]{:S(2)}) collective-permute-start(bf16[640,256]{1,0:T(8,128)(2,1)S(1)} %get-tuple-element.66.refs_0_), channel_id=1, source_target_pairs={{0,4},{4,0},{8,12},{12,8},{16,20},{20,16},{24,28},{28,24},{32,36},... | collective-permute-start | bytes 983048 | tf_op jit(solution)/shard_map/ppermute | solution.py:289
  36.0 15.4 %collective-permute-start.8 = (bf16[640,256]{1,0:T(8,128)(2,1)S(1)}, bf16[640,256]{1,0:T(8,128)(2,1)S(1)}, u32[]{:S(2)}, u32[]{:S(2)}) collective-permute-start(bf16[640,256]{1,0:T(8,128)(2,1)S(1)} %get-tuple-element.75.refs_2_), channel_id=1, source_target_pairs={{4,8},{8,4},{12,16},{16,12},{20,24},{24,20},{28,32},{32,28},{36,40... | collective-permute-start | bytes 983048 | tf_op jit(solution)/shard_map/ppermute | solution.py:288
  38.7 12.8 %collective-permute-start.9 = (bf16[640,256]{1,0:T(8,128)(2,1)S(1)}, bf16[640,256]{1,0:T(8,128)(2,1)S(1)}, u32[]{:S(2)}, u32[]{:S(2)}) collective-permute-start(bf16[640,256]{1,0:T(8,128)(2,1)S(1)} %get-tuple-element.73.refs_0_), channel_id=1, source_target_pairs={{0,4},{4,0},{8,12},{12,8},{16,20},{20,16},{24,28},{28,24},{32,36},... | collective-permute-start | bytes 983048 | tf_op jit(solution)/shard_map/ppermute | solution.py:289
  43.1 12.6 %collective-permute-start.10 = (bf16[640,256]{1,0:T(8,128)(2,1)S(1)}, bf16[640,256]{1,0:T(8,128)(2,1)S(1)}, u32[]{:S(2)}, u32[]{:S(2)}) collective-permute-start(bf16[640,256]{1,0:T(8,128)(2,1)S(1)} %get-tuple-element.80.refs_2_), channel_id=1, source_target_pairs={{4,8},{8,4},{12,16},{16,12},{20,24},{24,20},{28,32},{32,28},{36,40... | collective-permute-start | bytes 983048 | tf_op jit(solution)/shard_map/ppermute | solution.py:288
  45.5 10.2 %collective-permute-start.11 = (bf16[640,256]{1,0:T(8,128)(2,1)S(1)}, bf16[640,256]{1,0:T(8,128)(2,1)S(1)}, u32[]{:S(2)}, u32[]{:S(2)}) collective-permute-start(bf16[640,256]{1,0:T(8,128)(2,1)S(1)} %get-tuple-element.78.refs_0_), channel_id=1, source_target_pairs={{0,4},{4,0},{8,12},{12,8},{16,20},{20,16},{24,28},{28,24},{32,36},... | collective-permute-start | bytes 983048 | tf_op jit(solution)/shard_map/ppermute | solution.py:289

commit v6 on v5

--- a/solution.py
+++ b/solution.py
@@ -68,29 +68,25 @@
     hand_out(odd, fetch_rims(current, first, cols, held, sems), evens, odds)
 
 
-def band_kernel(first, cols, odd, _, places, blocks, current, banded, evens, odds, held, sems, rims, rim_sems):
+def band_kernel(first, cols, odd, _, places, blocks, current, banded, evens, odds, sems, rims, rim_sems):
     rows_blk, slots, width, _ = blocks.shape
     take = fetch_rims(current, first, cols, rims, rim_sems)
 
-    def fetch(pair):
-        two = pl.ds(2 * pair, 2)
-        return pltpu.make_async_copy(blocks.at[two], held.at[two], sems.at[pair])
-
-    for pair in range(rows_blk // 2):
-        fetch(pair).start()
-    hand_out(odd, take, evens, odds)
-
     def one_pair(pair, _):
         banded[pair] = jnp.zeros(banded.shape[1:], BF16)
-        fetch(pair).wait()
         for half in range(2):
             row = 2 * pair + half
             for slot in range(slots):
                 at = pl.multiple_of((places[row, slot] + half) * width, width)
-                banded[pair, pl.ds(half * width, width), pl.ds(at, width)] = held[row, slot]
+                target = banded.at[pair, pl.ds(half * width, width), pl.ds(at, width)]
+                pltpu.make_async_copy(blocks.at[row, slot], target, sems.at[pair]).start()
         return 0
 
     lax.fori_loop(0, rows_blk // 2, one_pair, 0)
+    hand_out(odd, take, evens, odds)
+    for pair in range(rows_blk // 2):
+        bytes_of = banded.at[pair, :, pl.ds(0, slots * width)]
+        pltpu.make_async_copy(bytes_of, bytes_of, sems.at[pair]).wait()
 
 
 def weight_kernel(scale, _, orbital, probe, weights):
@@ -377,7 +373,6 @@
         in_specs=[SMEM, VMEM, SMEM, HBM, HBM],
         out_specs=(VMEM,) * 3,
         scratch_shapes=[
-            pltpu.VMEM(hamiltonian_blocks.shape, BF16),
             pltpu.SemaphoreType.DMA((pairs,)),
             *rim_scratch,
         ],

time: 70.5 us -> 69.9 us (level)
  waiting for transfers between devices: 10 us -> 8.28 us
  starting transfers between devices: 20.8 us -> 22.5 us
  Pallas kernels: 25.6 us -> 24.3 us
    ppermute x6, waiting for transfers between devices: 9.55 us -> 5.85 us  [exchange(): ahead = lax.ppermute(odds, 'slab', pairs_of[1])]
    ppermute x6, waiting for transfers between devices: 0.49 us -> 2.42 us  [exchange(): return (ahead, lax.ppermute(evens, 'slab', pairs_of[0]))]
    ppermute x6, starting transfers between devices: 20 us -> 21.8 us  [exchange(): ahead = lax.ppermute(odds, 'slab', pairs_of[1])]
    pallas_call x1, Pallas kernels: 5.14 us -> 3.87 us  [local(): pl.pallas_call(functools.partial(band_kernel, cols, cols), out_shape=(sha...]
    all_to_all x1, blocking collectives: 12.8 us -> 13.5 us  [local(): gathered = lax.all_to_all(scattered, 'slab', 0, 0)]
  transfers between devices with their start and end apart: 12 -> 12, of which waited for: 5 -> 5; matrix products, arithmetic and copies ran while one was open for 0% -> 0% of each run, Pallas kernels for 32% -> 30%
where the time goes in v6:
time: 69.9 us; the launch traced here: 69.7 us
  Pallas kernels  24.3 us (35%)
  starting transfers between devices  22.5 us (32%)
  blocking collectives  13.5 us (19%)
  waiting for transfers between devices  8.28 us (12%)
  between operations  1.01 us (1%)
    ppermute x6, starting transfers between devices, exchange(): ahead = lax.ppermute(odds, 'slab', pairs_of[1])  21.8 us
    all_to_all x1, blocking collectives, local(): gathered = lax.all_to_all(scattered, 'slab', 0, 0)  13.5 us
    pallas_call x6, Pallas kernels, middle(): pl.pallas_call(functools.partial(middle_kernel, len(sources[chunk]), chun...  9.99 us
    ppermute x6, waiting for transfers between devices, exchange(): ahead = lax.ppermute(odds, 'slab', pairs_of[1])  5.85 us
    pallas_call x6, Pallas kernels, rims(): pl.pallas_call(kernel, out_shape=outs, in_specs=specs, out_specs=out_spec...  5.02 us
    pallas_call x1, Pallas kernels, local(): pl.pallas_call(functools.partial(band_kernel, cols, cols), out_shape=(sha...  3.87 us
    pallas_call x1, Pallas kernels, local(): pl.pallas_call(functools.partial(store_kernel, rim), out_shape=(full_shap...  2.54 us
    ppermute x6, waiting for transfers between devices, exchange(): return (ahead, lax.ppermute(evens, 'slab', pairs_of[0]))  2.42 us
  transfers between devices with their start and end apart: 12, of which 5 were waited for; matrix products, arithmetic and copies ran while one was open for 0% of the time, Pallas kernels for 30%

profile of v6, /device:TPU:0, one launch (start us, length us, event | category | flops | bytes accessed | tf_op | source)
XLA Modules:
  0.0 69.7 jit_solution(15025834475267176151)
XLA Ops:
  0.6 1.5 %edges.1 = (bf16[640,256]{1,0:T(8,128)(2,1)S(1)}, bf16[640,256]{1,0:T(8,128)(2,1)S(1)}) custom-call(s32[1]{0:T(128)} %bitcast.odd, f32[2048,512]{1,0:T(8,128)} %refs_3_.3), custom_call_target="tpu_custom_call" | custom-call | bytes 1966080 | tf_op jit(solution)/shard_map/edges/pallas_call | solution.py:355
  2.1 6.7 %collective-permute-start = (bf16[640,256]{1,0:T(8,128)(2,1)S(1)}, bf16[640,256]{1,0:T(8,128)(2,1)S(1)}, u32[]{:S(2)}, u32[]{:S(2)}) collective-permute-start(bf16[640,256]{1,0:T(8,128)(2,1)S(1)} %get-tuple-element.48._), channel_id=1, source_target_pairs={{4,8},{8,4},{12,16},{16,12},{20,24},{24,20},{28,32},{32,28},{36,40... | collective-permute-start | bytes 983048 | tf_op jit(solution)/shard_map/ppermute | solution.py:284
  8.8 0.1 add_select_fusion.places
  8.9 0.0 copy-start.3
  9.0 3.9 %band.1 = (bf16[8,256,1536]{2,1,0:T(8,128)(2,1)S(1)}, bf16[640,256]{1,0:T(8,128)(2,1)S(1)}, bf16[640,256]{1,0:T(8,128)(2,1)S(1)}) custom-call(s32[1]{0:T(128)} %bitcast.odd, bf16[640,256]{1,0:T(8,128)(2,1)S(1)} %get-tuple-element.48._, s32[16,9]{1,0:T(8,128)S(1)} %add_select_fusion.places, bf16[16,9,128,128]{3,2,1,0:T(8,128)(2,1)} %blocks.1, f32[2048,512]{1,0:T(8,128)} %refs_3_.3), custom_call_target="tpu_custom_call" | custom-call | bytes 12582912 | tf_op jit(solution)/shard_map/band/pallas_call | solution.py:366
  12.9 1.4 %collective-permute-start.2 = (bf16[640,256]{1,0:T(8,128)(2,1)S(1)}, bf16[640,256]{1,0:T(8,128)(2,1)S(1)}, u32[]{:S(2)}, u32[]{:S(2)}) collective-permute-start(bf16[640,256]{1,0:T(8,128)(2,1)S(1)} %get-tuple-element.49._), channel_id=1, source_target_pairs={{4,8},{8,4},{12,16},{16,12},{20,24},{24,20},{28,32},{32,28},{36,40... | collective-permute-start | bytes 983048 | tf_op jit(solution)/shard_map/ppermute | solution.py:284
  14.3 0.8 %collective-permute-start.3 = (bf16[640,256]{1,0:T(8,128)(2,1)S(1)}, bf16[640,256]{1,0:T(8,128)(2,1)S(1)}, u32[]{:S(2)}, u32[]{:S(2)}) collective-permute-start(bf16[640,256]{1,0:T(8,128)(2,1)S(1)} %get-tuple-element.57), channel_id=1, source_target_pairs={{0,4},{4,0},{8,12},{12,8},{16,20},{20,16},{24,28},{28,24},{32,36},... | collective-permute-start | bytes 983048 | tf_op jit(solution)/shard_map/ppermute | solution.py:285
  15.1 0.3 weights.1._
  15.4 1.6 %middle.6 = (f32[2048,512]{1,0:T(8,128)S(1)}, bf16[768,256]{1,0:T(8,128)(2,1)S(1)}, f32[8,256]{1,0:T(8,128)S(1)}) custom-call(s32[1]{0:T(128)} %bitcast.odd, f32[2048,512]{1,0:T(8,128)S(1)} %weights.1._, bf16[8,256,1536]{2,1,0:T(8,128)(2,1)S(1)} %get-tuple-element.50.banded, f32[2048,512]{1,0:T(8,128)S(1)} %weights.1._, f32[2048,512]{1,0:T(8,128)S(1)} %copy-done, ...), custom_call_target="tpu_custom_call" | custom-call | flops 1207959552 | bytes 8388608 | tf_op jit(solution)/shard_map/middle/pallas_call | solution.py:296
  17.1 2.4 %collective-permute-done.1.evens_in = bf16[640,256]{1,0:T(8,128)(2,1)S(1)} collective-permute-done((bf16[640,256]{1,0:T(8,128)(2,1)S(1)}, bf16[640,256]{1,0:T(8,128)(2,1)S(1)}, u32[]{:S(2)}, u32[]{:S(2)}) %collective-permute-start.1) | collective-permute-done | bytes 327712 | tf_op jit(solution)/shard_map/ppermute | solution.py:285
  19.5 0.8 %rims.6 = (f32[2048,512]{1,0:T(8,128)S(1)}, f32[8,256]{1,0:T(8,128)S(1)}, bf16[640,256]{1,0:T(8,128)(2,1)S(1)}, bf16[640,256]{1,0:T(8,128)(2,1)S(1)}) custom-call(s32[1]{0:T(128)} %bitcast.odd, f32[8,256]{1,0:T(8,128)S(1)} %get-tuple-element.51._.partial, bf16[8,256,1536]{2,1,0:T(8,128)(2,1)S(1)} %get-tuple-element.50.banded, ...), custom_call_target="tpu_custom_call", output_to_operand_aliasing={{0}: (6, {})} | custom-call | flops 241591904 | bytes 2097152 | tf_op jit(solution)/shard_map/rims/pallas_call | solution.py:337
  20.2 4.3 %collective-permute-start.4 = (bf16[640,256]{1,0:T(8,128)(2,1)S(1)}, bf16[640,256]{1,0:T(8,128)(2,1)S(1)}, u32[]{:S(2)}, u32[]{:S(2)}) collective-permute-start(bf16[640,256]{1,0:T(8,128)(2,1)S(1)} %get-tuple-element.62.refs_2_), channel_id=1, source_target_pairs={{4,8},{8,4},{12,16},{16,12},{20,24},{24,20},{28,32},{32,28},{36,40... | collective-permute-start | bytes 983048 | tf_op jit(solution)/shard_map/ppermute | solution.py:284
  24.5 1.6 %middle.7 = (f32[2048,512]{1,0:T(8,128)S(1)}, bf16[768,256]{1,0:T(8,128)(2,1)S(1)}, f32[8,256]{1,0:T(8,128)S(1)}) custom-call(s32[1]{0:T(128)} %bitcast.odd, f32[8,256]{1,0:T(8,128)S(1)} %get-tuple-element.54._.refs_0_, bf16[8,256,1536]{2,1,0:T(8,128)(2,1)S(1)} %get-tuple-element.50.banded, ...), custom_call_target="tpu_custom_call", output_to_operand_aliasing={{0}: (6, {})} | custom-call | flops 1207959552 | bytes 8388608 | tf_op jit(solution)/shard_map/middle/pallas_call | solution.py:296
  26.2 1.6 %collective-permute-done.2.odds_in = bf16[640,256]{1,0:T(8,128)(2,1)S(1)} collective-permute-done((bf16[640,256]{1,0:T(8,128)(2,1)S(1)}, bf16[640,256]{1,0:T(8,128)(2,1)S(1)}, u32[]{:S(2)}, u32[]{:S(2)}) %collective-permute-start.2) | collective-permute-done | bytes 327712 | tf_op jit(solution)/shard_map/ppermute | solution.py:284
  27.8 0.8 %rims.7 = (f32[2048,512]{1,0:T(8,128)S(1)}, f32[8,256]{1,0:T(8,128)S(1)}, bf16[640,256]{1,0:T(8,128)(2,1)S(1)}, bf16[640,256]{1,0:T(8,128)(2,1)S(1)}) custom-call(s32[1]{0:T(128)} %bitcast.odd, f32[8,256]{1,0:T(8,128)S(1)} %get-tuple-element.56._.partial, bf16[8,256,1536]{2,1,0:T(8,128)(2,1)S(1)} %get-tuple-element.50.banded, ...), custom_call_target="tpu_custom_call", output_to_operand_aliasing={{0}: (6, {})} | custom-call | flops 241591904 | bytes 2097152 | tf_op jit(solution)/shard_map/rims/pallas_call | solution.py:337
  28.6 2.1 %collective-permute-start.6 = (bf16[640,256]{1,0:T(8,128)(2,1)S(1)}, bf16[640,256]{1,0:T(8,128)(2,1)S(1)}, u32[]{:S(2)}, u32[]{:S(2)}) collective-permute-start(bf16[640,256]{1,0:T(8,128)(2,1)S(1)} %get-tuple-element.68.refs_2_), channel_id=1, source_target_pairs={{4,8},{8,4},{12,16},{16,12},{20,24},{24,20},{28,32},{32,28},{36,40... | collective-permute-start | bytes 983048 | tf_op jit(solution)/shard_map/ppermute | solution.py:284
  30.7 1.7 %middle.8 = (f32[2048,512]{1,0:T(8,128)S(1)}, bf16[768,256]{1,0:T(8,128)(2,1)S(1)}, f32[8,256]{1,0:T(8,128)S(1)}) custom-call(s32[1]{0:T(128)} %bitcast.odd, f32[8,256]{1,0:T(8,128)S(1)} %get-tuple-element.59._.refs_1_, bf16[8,256,1536]{2,1,0:T(8,128)(2,1)S(1)} %get-tuple-element.50.banded, f32[2048,512]{1,0:T(8,128)S(1)} %weights.1._, ...), custom_call_target="tpu_custom_call" | custom-call | flops 1207959552 | bytes 8388608 | tf_op jit(solution)/shard_map/middle/pallas_call | solution.py:296
  32.4 1.6 %collective-permute-done.4.odds_in = bf16[640,256]{1,0:T(8,128)(2,1)S(1)} collective-permute-done((bf16[640,256]{1,0:T(8,128)(2,1)S(1)}, bf16[640,256]{1,0:T(8,128)(2,1)S(1)}, u32[]{:S(2)}, u32[]{:S(2)}) %collective-permute-start.4) | collective-permute-done | bytes 327712 | tf_op jit(solution)/shard_map/ppermute | solution.py:284
  34.0 0.8 %rims.8 = (f32[2048,512]{1,0:T(8,128)S(1)}, f32[8,256]{1,0:T(8,128)S(1)}, bf16[640,256]{1,0:T(8,128)(2,1)S(1)}, bf16[640,256]{1,0:T(8,128)(2,1)S(1)}) custom-call(s32[1]{0:T(128)} %bitcast.odd, f32[8,256]{1,0:T(8,128)S(1)} %get-tuple-element.63._.partial, bf16[8,256,1536]{2,1,0:T(8,128)(2,1)S(1)} %get-tuple-element.50.banded, ...), custom_call_target="tpu_custom_call", output_to_operand_aliasing={{0}: (6, {})} | custom-call | flops 241591904 | bytes 2097152 | tf_op jit(solution)/shard_map/rims/pallas_call | solution.py:337
  34.8 3.0 %collective-permute-start.8 = (bf16[640,256]{1,0:T(8,128)(2,1)S(1)}, bf16[640,256]{1,0:T(8,128)(2,1)S(1)}, u32[]{:S(2)}, u32[]{:S(2)}) collective-permute-start(bf16[640,256]{1,0:T(8,128)(2,1)S(1)} %get-tuple-element.75.refs_2_), channel_id=1, source_target_pairs={{4,8},{8,4},{12,16},{16,12},{20,24},{24,20},{28,32},{32,28},{36,40... | collective-permute-start | bytes 983048 | tf_op jit(solution)/shard_map/ppermute | solution.py:284
  37.7 1.7 %middle.9 = (f32[2048,512]{1,0:T(8,128)S(1)}, bf16[768,256]{1,0:T(8,128)(2,1)S(1)}, f32[8,256]{1,0:T(8,128)S(1)}) custom-call(s32[1]{0:T(128)} %bitcast.odd, f32[8,256]{1,0:T(8,128)S(1)} %get-tuple-element.65._.refs_2_, bf16[8,256,1536]{2,1,0:T(8,128)(2,1)S(1)} %get-tuple-element.50.banded, ...), custom_call_target="tpu_custom_call", output_to_operand_aliasing={{0}: (8, {})} | custom-call | flops 1207959552 | bytes 8388608 | tf_op jit(solution)/shard_map/middle/pallas_call | solution.py:296
  39.4 2.0 %collective-permute-done.6.odds_in = bf16[640,256]{1,0:T(8,128)(2,1)S(1)} collective-permute-done((bf16[640,256]{1,0:T(8,128)(2,1)S(1)}, bf16[640,256]{1,0:T(8,128)(2,1)S(1)}, u32[]{:S(2)}, u32[]{:S(2)}) %collective-permute-start.6) | collective-permute-done | bytes 327712 | tf_op jit(solution)/shard_map/ppermute | solution.py:284
  41.4 0.8 %rims.9 = (f32[2048,512]{1,0:T(8,128)S(1)}, f32[8,256]{1,0:T(8,128)S(1)}, bf16[640,256]{1,0:T(8,128)(2,1)S(1)}, bf16[640,256]{1,0:T(8,128)(2,1)S(1)}) custom-call(s32[1]{0:T(128)} %bitcast.odd, f32[8,256]{1,0:T(8,128)S(1)} %get-tuple-element.70._.partial, bf16[8,256,1536]{2,1,0:T(8,128)(2,1)S(1)} %get-tuple-element.50.banded, ...), custom_call_target="tpu_custom_call", output_to_operand_aliasing={{0}: (6, {})} | custom-call | flops 241591904 | bytes 2097152 | tf_op jit(solution)/shard_map/rims/pallas_call | solution.py:337
  42.2 4.2 %collective-permute-start.10 = (bf16[640,256]{1,0:T(8,128)(2,1)S(1)}, bf16[640,256]{1,0:T(8,128)(2,1)S(1)}, u32[]{:S(2)}, u32[]{:S(2)}) collective-permute-start(bf16[640,256]{1,0:T(8,128)(2,1)S(1)} %get-tuple-element.80.refs_2_), channel_id=1, source_target_pairs={{4,8},{8,4},{12,16},{16,12},{20,24},{24,20},{28,32},{32,28},{36,40... | collective-permute-start | bytes 983048 | tf_op jit(solution)/shard_map/ppermute | solution.py:284
  46.4 1.7 %middle.10 = (f32[2048,512]{1,0:T(8,128)S(1)}, f32[8,256]{1,0:T(8,128)S(1)}) custom-call(s32[1]{0:T(128)} %bitcast.odd, f32[8,256]{1,0:T(8,128)S(1)} %get-tuple-element.72._.refs_3_, bf16[8,256,1536]{2,1,0:T(8,128)(2,1)S(1)} %get-tuple-element.50.banded, f32[2048,512]{1,0:T(8,128)S(1)} %weights.1._, bf16[640,256]{1,0:T(8,128)(2,1)S(1)} %get-tuple-element.73.refs_0_, ...), custom_call_target="tpu_custom_call" | custom-call | flops 1207959552 | bytes 8388608 | tf_op jit(solution)/shard_map/middle/pallas_call | solution.py:296
  48.1 1.7 %middle.11 = (f32[2048,512]{1,0:T(8,128)S(1)}, f32[8,256]{1,0:T(8,128)S(1)}) custom-call(s32[1]{0:T(128)} %bitcast.odd, f32[8,256]{1,0:T(8,128)S(1)} %get-tuple-element.77._.partial, bf16[8,256,1536]{2,1,0:T(8,128)(2,1)S(1)} %get-tuple-element.50.banded, f32[2048,512]{1,0:T(8,128)S(1)} %weights.1._, ...), custom_call_target="tpu_custom_call", output_to_operand_aliasing={{0}: (8, {})} | custom-call | flops 1207959552 | bytes 8388608 | tf_op jit(solution)/shard_map/middle/pallas_call | solution.py:296
  49.8 2.5 %store.1 = (f32[2048,512]{1,0:T(8,128)}, f32[2048,512]{1,0:T(8,128)}) custom-call(f32[8,256]{1,0:T(8,128)S(1)} %get-tuple-element.82._.partial, f32[2048,512]{1,0:T(8,128)S(1)} %get-tuple-element.83.previous, f32[2048,512]{1,0:T(8,128)S(1)} %get-tuple-element.84.current.begun), custom_call_target="tpu_custom_call" | custom-call | bytes 16777216 | tf_op jit(solution)/shard_map/store/pallas_call | solution.py:423
  52.4 1.4 %rims.10 = (f32[2048,512]{1,0:T(8,128)}, f32[8,256]{1,0:T(8,128)S(1)}) custom-call(s32[1]{0:T(128)} %bitcast.odd, f32[8,256]{1,0:T(8,128)S(1)} %get-tuple-element.82._.partial, bf16[8,256,1536]{2,1,0:T(8,128)(2,1)S(1)} %get-tuple-element.50.banded, f32[2048,512]{1,0:T(8,128)S(1)} %weights.1._, ...), custom_call_target="tpu_custom_call", output_to_operand_aliasing={{0}: (8, {})} | custom-call | flops 241591904 | bytes 2097152 | tf_op jit(solution)/shard_map/rims/pallas_call | solution.py:337
  53.8 0.6 collective-permute-done.10.odds_in
  54.4 0.6 rims.11
  55.0 13.5 %all_to_all.5.parts = f32[32,1,1536]{2,1,0:T(1,128)S(1)} all-to-all(f32[32,1,1536]{2,1,0:T(1,128)S(1)} %get-tuple-element.88), channel_id=1, replica_groups=mesh['slab'=32,'col'=4] {'slab'}, dimensions={0} | all-to-all | bytes 393216 | tf_op jit(solution)/shard_map/all_to_all | solution.py:433
  68.5 1.1 %sums.1 = (f32[3,512]{1,0:T(4,128)}, f32[2048,512]{1,0:T(8,128)}) custom-call(f32[32,1,1536]{2,1,0:T(1,128)S(1)} %all_to_all.5.parts, f32[2,640,256]{2,1,0:T(8,128)S(1)} %get-tuple-element.89.rims, f32[2048,512]{1,0:T(8,128)} %get-tuple-element.90._), custom_call_target="tpu_custom_call", output_to_operand_aliasing={{1}: (2, {})} | custom-call | tf_op jit(solution)/shard_map/sums/pallas_call | solution.py:435
  (22 shorter events, 0.1 us)
Async XLA Ops:
  0.6 8.2 %copy-start.4 = (s32[16,9]{1,0:T(8,128)S(1)}, s32[16,9]{1,0:T(8,128)}, u32[]{:S(2)}) copy-start(s32[16,9]{1,0:T(8,128)} %param.7) | copy-start | bytes 1732
  2.1 14.9 %collective-permute-start = (bf16[640,256]{1,0:T(8,128)(2,1)S(1)}, bf16[640,256]{1,0:T(8,128)(2,1)S(1)}, u32[]{:S(2)}, u32[]{:S(2)}) collective-permute-start(bf16[640,256]{1,0:T(8,128)(2,1)S(1)} %get-tuple-element.48._), channel_id=1, source_target_pairs={{4,8},{8,4},{12,16},{16,12},{20,24},{24,20},{28,32},{32,28},{36,40... | collective-permute-start | bytes 983048 | tf_op jit(solution)/shard_map/ppermute | solution.py:284
  8.8 10.6 %collective-permute-start.1 = (bf16[640,256]{1,0:T(8,128)(2,1)S(1)}, bf16[640,256]{1,0:T(8,128)(2,1)S(1)}, u32[]{:S(2)}, u32[]{:S(2)}) collective-permute-start(bf16[640,256]{1,0:T(8,128)(2,1)S(1)} %get-tuple-element.52), channel_id=1, source_target_pairs={{0,4},{4,0},{8,12},{12,8},{16,20},{20,16},{24,28},{28,24},{32,36},... | collective-permute-start | bytes 983048 | tf_op jit(solution)/shard_map/ppermute | solution.py:285
  8.9 6.1 %copy-start.2 = (bf16[2048,512]{1,0:T(8,128)(2,1)S(1)}, bf16[2048,512]{1,0:T(8,128)(2,1)}, u32[]{:S(2)}) copy-start(bf16[2048,512]{1,0:T(8,128)(2,1)} %probe.1) | copy-start | bytes 6291460
  8.9 6.1 %copy-start.3 = (f32[2048]{0:T(1024)S(1)}, f32[2048]{0:T(1024)}, u32[]{:S(2)}) copy-start(f32[2048]{0:T(1024)} %param.11) | copy-start | bytes 24580
  8.9 6.5 %copy-start.1 = (f32[2048,512]{1,0:T(8,128)S(1)}, f32[2048,512]{1,0:T(8,128)}, u32[]{:S(2)}) copy-start(f32[2048,512]{1,0:T(8,128)} %refs_1_.3) | copy-start | bytes 12582916
  12.8 2.6 %copy-start = (f32[2048,512]{1,0:T(8,128)S(1)}, f32[2048,512]{1,0:T(8,128)}, u32[]{:S(2)}) copy-start(f32[2048,512]{1,0:T(8,128)} %refs_3_.3) | copy-start | bytes 12582916
  12.9 14.9 %collective-permute-start.2 = (bf16[640,256]{1,0:T(8,128)(2,1)S(1)}, bf16[640,256]{1,0:T(8,128)(2,1)S(1)}, u32[]{:S(2)}, u32[]{:S(2)}) collective-permute-start(bf16[640,256]{1,0:T(8,128)(2,1)S(1)} %get-tuple-element.49._), channel_id=1, source_target_pairs={{4,8},{8,4},{12,16},{16,12},{20,24},{24,20},{28,32},{32,28},{36,40... | collective-permute-start | bytes 983048 | tf_op jit(solution)/shard_map/ppermute | solution.py:284
  14.3 13.5 %collective-permute-start.3 = (bf16[640,256]{1,0:T(8,128)(2,1)S(1)}, bf16[640,256]{1,0:T(8,128)(2,1)S(1)}, u32[]{:S(2)}, u32[]{:S(2)}) collective-permute-start(bf16[640,256]{1,0:T(8,128)(2,1)S(1)} %get-tuple-element.57), channel_id=1, source_target_pairs={{0,4},{4,0},{8,12},{12,8},{16,20},{20,16},{24,28},{28,24},{32,36},... | collective-permute-start | bytes 983048 | tf_op jit(solution)/shard_map/ppermute | solution.py:285
  20.2 13.7 %collective-permute-start.4 = (bf16[640,256]{1,0:T(8,128)(2,1)S(1)}, bf16[640,256]{1,0:T(8,128)(2,1)S(1)}, u32[]{:S(2)}, u32[]{:S(2)}) collective-permute-start(bf16[640,256]{1,0:T(8,128)(2,1)S(1)} %get-tuple-element.62.refs_2_), channel_id=1, source_target_pairs={{4,8},{8,4},{12,16},{16,12},{20,24},{24,20},{28,32},{32,28},{36,40... | collective-permute-start | bytes 983048 | tf_op jit(solution)/shard_map/ppermute | solution.py:284
  24.5 9.5 %collective-permute-start.5 = (bf16[640,256]{1,0:T(8,128)(2,1)S(1)}, bf16[640,256]{1,0:T(8,128)(2,1)S(1)}, u32[]{:S(2)}, u32[]{:S(2)}) collective-permute-start(bf16[640,256]{1,0:T(8,128)(2,1)S(1)} %get-tuple-element.60.refs_0_), channel_id=1, source_target_pairs={{0,4},{4,0},{8,12},{12,8},{16,20},{20,16},{24,28},{28,24},{32,36},... | collective-permute-start | bytes 983048 | tf_op jit(solution)/shard_map/ppermute | solution.py:285
  28.6 12.8 %collective-permute-start.6 = (bf16[640,256]{1,0:T(8,128)(2,1)S(1)}, bf16[640,256]{1,0:T(8,128)(2,1)S(1)}, u32[]{:S(2)}, u32[]{:S(2)}) collective-permute-start(bf16[640,256]{1,0:T(8,128)(2,1)S(1)} %get-tuple-element.68.refs_2_), channel_id=1, source_target_pairs={{4,8},{8,4},{12,16},{16,12},{20,24},{24,20},{28,32},{32,28},{36,40... | collective-permute-start | bytes 983048 | tf_op jit(solution)/shard_map/ppermute | solution.py:284
  30.7 10.7 %collective-permute-start.7 = (bf16[640,256]{1,0:T(8,128)(2,1)S(1)}, bf16[640,256]{1,0:T(8,128)(2,1)S(1)}, u32[]{:S(2)}, u32[]{:S(2)}) collective-permute-start(bf16[640,256]{1,0:T(8,128)(2,1)S(1)} %get-tuple-element.66.refs_0_), channel_id=1, source_target_pairs={{0,4},{4,0},{8,12},{12,8},{16,20},{20,16},{24,28},{28,24},{32,36},... | collective-permute-start | bytes 983048 | tf_op jit(solution)/shard_map/ppermute | solution.py:285
  34.8 17.6 %collective-permute-start.8 = (bf16[640,256]{1,0:T(8,128)(2,1)S(1)}, bf16[640,256]{1,0:T(8,128)(2,1)S(1)}, u32[]{:S(2)}, u32[]{:S(2)}) collective-permute-start(bf16[640,256]{1,0:T(8,128)(2,1)S(1)} %get-tuple-element.75.refs_2_), channel_id=1, source_target_pairs={{4,8},{8,4},{12,16},{16,12},{20,24},{24,20},{28,32},{32,28},{36,40... | collective-permute-start | bytes 983048 | tf_op jit(solution)/shard_map/ppermute | solution.py:284
  37.7 14.7 %collective-permute-start.9 = (bf16[640,256]{1,0:T(8,128)(2,1)S(1)}, bf16[640,256]{1,0:T(8,128)(2,1)S(1)}, u32[]{:S(2)}, u32[]{:S(2)}) collective-permute-start(bf16[640,256]{1,0:T(8,128)(2,1)S(1)} %get-tuple-element.73.refs_0_), channel_id=1, source_target_pairs={{0,4},{4,0},{8,12},{12,8},{16,20},{20,16},{24,28},{28,24},{32,36},... | collective-permute-start | bytes 983048 | tf_op jit(solution)/shard_map/ppermute | solution.py:285
  42.2 12.2 %collective-permute-start.10 = (bf16[640,256]{1,0:T(8,128)(2,1)S(1)}, bf16[640,256]{1,0:T(8,128)(2,1)S(1)}, u32[]{:S(2)}, u32[]{:S(2)}) collective-permute-start(bf16[640,256]{1,0:T(8,128)(2,1)S(1)} %get-tuple-element.80.refs_2_), channel_id=1, source_target_pairs={{4,8},{8,4},{12,16},{16,12},{20,24},{24,20},{28,32},{32,28},{36,40... | collective-permute-start | bytes 983048 | tf_op jit(solution)/shard_map/ppermute | solution.py:284
  46.4 8.0 %collective-permute-start.11 = (bf16[640,256]{1,0:T(8,128)(2,1)S(1)}, bf16[640,256]{1,0:T(8,128)(2,1)S(1)}, u32[]{:S(2)}, u32[]{:S(2)}) collective-permute-start(bf16[640,256]{1,0:T(8,128)(2,1)S(1)} %get-tuple-element.78.refs_0_), channel_id=1, source_target_pairs={{0,4},{4,0},{8,12},{12,8},{16,20},{20,16},{24,28},{28,24},{32,36},... | collective-permute-start | bytes 983048 | tf_op jit(solution)/shard_map/ppermute | solution.py:285

commit v7 on v6

--- a/solution.py
+++ b/solution.py
@@ -173,7 +173,7 @@
     return total
 
 
-def rim_kernel(first, cols, width, rows_blk, odd, _, banded, weights, odds_in, evens_in, begun, partial, *refs):
+def rim_kernel(first, cols, width, rows_blk, odd, _, banded, weights, evens_in, odds_in, begun, partial, *refs):
     upcoming, moments, evens, odds, rims = refs
     rim = rims.shape[1]
     rows = rows_blk * width
@@ -194,7 +194,7 @@
     hand_out(odd, take, evens, odds)
 
 
-def store_rim_kernel(first, cols, width, rows_blk, odd, _, banded, weights, odds_in, evens_in, begun, partial, __, out, moments, held, sems):
+def store_rim_kernel(first, cols, width, rows_blk, odd, _, banded, weights, evens_in, odds_in, begun, partial, __, out, moments, held, sems):
     copies = []
 
     def keep(part, side, here, columns, result):
@@ -210,7 +210,7 @@
         copy.wait()
 
 
-def last_rim_kernel(first, cols, width, rows_blk, odd, _, banded, weights, odds_in, evens_in, begun, partial, *refs):
+def last_rim_kernel(first, cols, width, rows_blk, odd, _, banded, weights, evens_in, odds_in, begun, partial, *refs):
     *earlier, moments, rims = refs
     rim = rims.shape[1]
 
@@ -281,8 +281,7 @@
     flops = 2 * rows * cols * 9 * width
 
     def exchange(evens, odds):
-        ahead = lax.ppermute(odds, "slab", pairs_of[1])
-        return ahead, lax.ppermute(evens, "slab", pairs_of[0])
+        return lax.ppermute(evens, "slab", pairs_of[0]), lax.ppermute(odds, "slab", pairs_of[1])
 
     def middle(token, term, chunk):
         args = [odd, token, banded, weights, *sources[chunk], terms[term]]

time: 69.9 us -> 70.3 us (level)
  starting transfers between devices: 22.5 us -> 24.1 us
  waiting for transfers between devices: 8.28 us -> 6.7 us
    ppermute x12, waiting for transfers between devices: 8.28 us -> 6.7 us  [the longest x6 4.42 us: exchange(): lax.ppermute(evens, 'slab', pairs_of[0])]
    ppermute x12, starting transfers between devices: 22.5 us -> 24.1 us  [the longest x6 23 us: exchange(): lax.ppermute(odds, 'slab', pairs_of[1])]
  transfers between devices with their start and end apart: 12 -> 12, of which waited for: 5 -> 7; matrix products, arithmetic and copies ran while one was open for 0% -> 0% of each run, Pallas kernels for 30% -> 30%
where the time goes in v7:
time: 70.3 us; the launch traced here: 70.1 us
  Pallas kernels  24.3 us (35%)
  starting transfers between devices  24.1 us (34%)
  blocking collectives  13.9 us (20%)
  waiting for transfers between devices  6.7 us (10%)
  between operations  1.05 us (1%)
    ppermute x6, starting transfers between devices, exchange(): lax.ppermute(odds, 'slab', pairs_of[1])  23 us
    all_to_all x1, blocking collectives, local(): gathered = lax.all_to_all(scattered, 'slab', 0, 0)  13.9 us
    pallas_call x6, Pallas kernels, middle(): pl.pallas_call(functools.partial(middle_kernel, len(sources[chunk]), chun...  9.99 us
    pallas_call x6, Pallas kernels, rims(): pl.pallas_call(kernel, out_shape=outs, in_specs=specs, out_specs=out_spec...  5.01 us
    ppermute x6, waiting for transfers between devices, exchange(): lax.ppermute(evens, 'slab', pairs_of[0])  4.42 us
    pallas_call x1, Pallas kernels, local(): pl.pallas_call(functools.partial(band_kernel, cols, cols), out_shape=(sha...  3.87 us
    pallas_call x1, Pallas kernels, local(): pl.pallas_call(functools.partial(store_kernel, rim), out_shape=(full_shap...  2.54 us
    ppermute x6, waiting for transfers between devices, exchange(): lax.ppermute(odds, 'slab', pairs_of[1])  2.28 us
  transfers between devices with their start and end apart: 12, of which 7 were waited for; matrix products, arithmetic and copies ran while one was open for 0% of the time, Pallas kernels for 30%

profile of v7, /device:TPU:0, one launch (start us, length us, event | category | flops | bytes accessed | tf_op | source)
XLA Modules:
  0.0 70.1 jit_solution(15412889904506699044)
XLA Ops:
  0.6 1.5 %edges.1 = (bf16[640,256]{1,0:T(8,128)(2,1)S(1)}, bf16[640,256]{1,0:T(8,128)(2,1)S(1)}) custom-call(s32[1]{0:T(128)} %bitcast.odd, f32[2048,512]{1,0:T(8,128)} %refs_3_.3), custom_call_target="tpu_custom_call" | custom-call | bytes 1966080 | tf_op jit(solution)/shard_map/edges/pallas_call | solution.py:354
  2.1 6.7 %collective-permute-start.1 = (bf16[640,256]{1,0:T(8,128)(2,1)S(1)}, bf16[640,256]{1,0:T(8,128)(2,1)S(1)}, u32[]{:S(2)}, u32[]{:S(2)}) collective-permute-start(bf16[640,256]{1,0:T(8,128)(2,1)S(1)} %get-tuple-element.48._), channel_id=1, source_target_pairs={{4,8},{8,4},{12,16},{16,12},{20,24},{24,20},{28,32},{32,28},{36,40... | collective-permute-start | bytes 983048 | tf_op jit(solution)/shard_map/ppermute | solution.py:284
  9.0 3.9 %band.1 = (bf16[8,256,1536]{2,1,0:T(8,128)(2,1)S(1)}, bf16[640,256]{1,0:T(8,128)(2,1)S(1)}, bf16[640,256]{1,0:T(8,128)(2,1)S(1)}) custom-call(s32[1]{0:T(128)} %bitcast.odd, bf16[640,256]{1,0:T(8,128)(2,1)S(1)} %get-tuple-element.48._, s32[16,9]{1,0:T(8,128)S(1)} %add_select_fusion.places, bf16[16,9,128,128]{3,2,1,0:T(8,128)(2,1)} %blocks.1, f32[2048,512]{1,0:T(8,128)} %refs_3_.3), custom_call_target="tpu_custom_call" | custom-call | bytes 12582912 | tf_op jit(solution)/shard_map/band/pallas_call | solution.py:365
  12.9 1.4 %collective-permute-start.3 = (bf16[640,256]{1,0:T(8,128)(2,1)S(1)}, bf16[640,256]{1,0:T(8,128)(2,1)S(1)}, u32[]{:S(2)}, u32[]{:S(2)}) collective-permute-start(bf16[640,256]{1,0:T(8,128)(2,1)S(1)} %get-tuple-element.49._), channel_id=1, source_target_pairs={{4,8},{8,4},{12,16},{16,12},{20,24},{24,20},{28,32},{32,28},{36,40... | collective-permute-start | bytes 983048 | tf_op jit(solution)/shard_map/ppermute | solution.py:284
  14.3 0.8 %collective-permute-start.2 = (bf16[640,256]{1,0:T(8,128)(2,1)S(1)}, bf16[640,256]{1,0:T(8,128)(2,1)S(1)}, u32[]{:S(2)}, u32[]{:S(2)}) collective-permute-start(bf16[640,256]{1,0:T(8,128)(2,1)S(1)} %get-tuple-element.57), channel_id=1, source_target_pairs={{0,4},{4,0},{8,12},{12,8},{16,20},{20,16},{24,28},{28,24},{32,36},... | collective-permute-start | bytes 983048 | tf_op jit(solution)/shard_map/ppermute | solution.py:284
  15.1 0.3 weights.1._
  15.4 1.6 %middle.6 = (f32[2048,512]{1,0:T(8,128)S(1)}, bf16[768,256]{1,0:T(8,128)(2,1)S(1)}, f32[8,256]{1,0:T(8,128)S(1)}) custom-call(s32[1]{0:T(128)} %bitcast.odd, f32[2048,512]{1,0:T(8,128)S(1)} %weights.1._, bf16[8,256,1536]{2,1,0:T(8,128)(2,1)S(1)} %get-tuple-element.50.banded, f32[2048,512]{1,0:T(8,128)S(1)} %weights.1._, f32[2048,512]{1,0:T(8,128)S(1)} %copy-done, ...), custom_call_target="tpu_custom_call" | custom-call | flops 1207959552 | bytes 8388608 | tf_op jit(solution)/shard_map/middle/pallas_call | solution.py:295
  17.1 2.4 %collective-permute-done.evens_in = bf16[640,256]{1,0:T(8,128)(2,1)S(1)} collective-permute-done((bf16[640,256]{1,0:T(8,128)(2,1)S(1)}, bf16[640,256]{1,0:T(8,128)(2,1)S(1)}, u32[]{:S(2)}, u32[]{:S(2)}) %collective-permute-start) | collective-permute-done | bytes 327712 | tf_op jit(solution)/shard_map/ppermute | solution.py:284
  19.5 0.8 %rims.6 = (f32[2048,512]{1,0:T(8,128)S(1)}, f32[8,256]{1,0:T(8,128)S(1)}, bf16[640,256]{1,0:T(8,128)(2,1)S(1)}, bf16[640,256]{1,0:T(8,128)(2,1)S(1)}) custom-call(s32[1]{0:T(128)} %bitcast.odd, f32[8,256]{1,0:T(8,128)S(1)} %get-tuple-element.51._.partial, bf16[8,256,1536]{2,1,0:T(8,128)(2,1)S(1)} %get-tuple-element.50.banded, ...), custom_call_target="tpu_custom_call", output_to_operand_aliasing={{0}: (6, {})} | custom-call | flops 241591904 | bytes 2097152 | tf_op jit(solution)/shard_map/rims/pallas_call | solution.py:336
  20.3 4.3 %collective-permute-start.5 = (bf16[640,256]{1,0:T(8,128)(2,1)S(1)}, bf16[640,256]{1,0:T(8,128)(2,1)S(1)}, u32[]{:S(2)}, u32[]{:S(2)}) collective-permute-start(bf16[640,256]{1,0:T(8,128)(2,1)S(1)} %get-tuple-element.62.refs_2_), channel_id=1, source_target_pairs={{4,8},{8,4},{12,16},{16,12},{20,24},{24,20},{28,32},{32,28},{36,40... | collective-permute-start | bytes 983048 | tf_op jit(solution)/shard_map/ppermute | solution.py:284
  24.6 1.6 %middle.7 = (f32[2048,512]{1,0:T(8,128)S(1)}, bf16[768,256]{1,0:T(8,128)(2,1)S(1)}, f32[8,256]{1,0:T(8,128)S(1)}) custom-call(s32[1]{0:T(128)} %bitcast.odd, f32[8,256]{1,0:T(8,128)S(1)} %get-tuple-element.54._.refs_0_, bf16[8,256,1536]{2,1,0:T(8,128)(2,1)S(1)} %get-tuple-element.50.banded, ...), custom_call_target="tpu_custom_call", output_to_operand_aliasing={{0}: (6, {})} | custom-call | flops 1207959552 | bytes 8388608 | tf_op jit(solution)/shard_map/middle/pallas_call | solution.py:295
  26.2 0.8 %collective-permute-done.3.odds_in = bf16[640,256]{1,0:T(8,128)(2,1)S(1)} collective-permute-done((bf16[640,256]{1,0:T(8,128)(2,1)S(1)}, bf16[640,256]{1,0:T(8,128)(2,1)S(1)}, u32[]{:S(2)}, u32[]{:S(2)}) %collective-permute-start.3) | collective-permute-done | bytes 327712 | tf_op jit(solution)/shard_map/ppermute | solution.py:284
  27.0 0.8 %rims.7 = (f32[2048,512]{1,0:T(8,128)S(1)}, f32[8,256]{1,0:T(8,128)S(1)}, bf16[640,256]{1,0:T(8,128)(2,1)S(1)}, bf16[640,256]{1,0:T(8,128)(2,1)S(1)}) custom-call(s32[1]{0:T(128)} %bitcast.odd, f32[8,256]{1,0:T(8,128)S(1)} %get-tuple-element.56._.partial, bf16[8,256,1536]{2,1,0:T(8,128)(2,1)S(1)} %get-tuple-element.50.banded, ...), custom_call_target="tpu_custom_call", output_to_operand_aliasing={{0}: (6, {})} | custom-call | flops 241591904 | bytes 2097152 | tf_op jit(solution)/shard_map/rims/pallas_call | solution.py:336
  27.9 2.9 %collective-permute-start.7 = (bf16[640,256]{1,0:T(8,128)(2,1)S(1)}, bf16[640,256]{1,0:T(8,128)(2,1)S(1)}, u32[]{:S(2)}, u32[]{:S(2)}) collective-permute-start(bf16[640,256]{1,0:T(8,128)(2,1)S(1)} %get-tuple-element.68.refs_2_), channel_id=1, source_target_pairs={{4,8},{8,4},{12,16},{16,12},{20,24},{24,20},{28,32},{32,28},{36,40... | collective-permute-start | bytes 983048 | tf_op jit(solution)/shard_map/ppermute | solution.py:284
  30.8 1.7 %middle.8 = (f32[2048,512]{1,0:T(8,128)S(1)}, bf16[768,256]{1,0:T(8,128)(2,1)S(1)}, f32[8,256]{1,0:T(8,128)S(1)}) custom-call(s32[1]{0:T(128)} %bitcast.odd, f32[8,256]{1,0:T(8,128)S(1)} %get-tuple-element.59._.refs_1_, bf16[8,256,1536]{2,1,0:T(8,128)(2,1)S(1)} %get-tuple-element.50.banded, f32[2048,512]{1,0:T(8,128)S(1)} %weights.1._, ...), custom_call_target="tpu_custom_call" | custom-call | flops 1207959552 | bytes 8388608 | tf_op jit(solution)/shard_map/middle/pallas_call | solution.py:295
  32.5 1.1 %collective-permute-done.4.evens_in = bf16[640,256]{1,0:T(8,128)(2,1)S(1)} collective-permute-done((bf16[640,256]{1,0:T(8,128)(2,1)S(1)}, bf16[640,256]{1,0:T(8,128)(2,1)S(1)}, u32[]{:S(2)}, u32[]{:S(2)}) %collective-permute-start.4) | collective-permute-done | bytes 327712 | tf_op jit(solution)/shard_map/ppermute | solution.py:284
  33.5 0.4 collective-permute-done.5.odds_in
  33.9 0.8 %rims.8 = (f32[2048,512]{1,0:T(8,128)S(1)}, f32[8,256]{1,0:T(8,128)S(1)}, bf16[640,256]{1,0:T(8,128)(2,1)S(1)}, bf16[640,256]{1,0:T(8,128)(2,1)S(1)}) custom-call(s32[1]{0:T(128)} %bitcast.odd, f32[8,256]{1,0:T(8,128)S(1)} %get-tuple-element.63._.partial, bf16[8,256,1536]{2,1,0:T(8,128)(2,1)S(1)} %get-tuple-element.50.banded, ...), custom_call_target="tpu_custom_call", output_to_operand_aliasing={{0}: (6, {})} | custom-call | flops 241591904 | bytes 2097152 | tf_op jit(solution)/shard_map/rims/pallas_call | solution.py:336
  34.8 3.2 %collective-permute-start.9 = (bf16[640,256]{1,0:T(8,128)(2,1)S(1)}, bf16[640,256]{1,0:T(8,128)(2,1)S(1)}, u32[]{:S(2)}, u32[]{:S(2)}) collective-permute-start(bf16[640,256]{1,0:T(8,128)(2,1)S(1)} %get-tuple-element.75.refs_2_), channel_id=1, source_target_pairs={{4,8},{8,4},{12,16},{16,12},{20,24},{24,20},{28,32},{32,28},{36,40... | collective-permute-start | bytes 983048 | tf_op jit(solution)/shard_map/ppermute | solution.py:284
  37.9 1.7 %middle.9 = (f32[2048,512]{1,0:T(8,128)S(1)}, bf16[768,256]{1,0:T(8,128)(2,1)S(1)}, f32[8,256]{1,0:T(8,128)S(1)}) custom-call(s32[1]{0:T(128)} %bitcast.odd, f32[8,256]{1,0:T(8,128)S(1)} %get-tuple-element.65._.refs_2_, bf16[8,256,1536]{2,1,0:T(8,128)(2,1)S(1)} %get-tuple-element.50.banded, ...), custom_call_target="tpu_custom_call", output_to_operand_aliasing={{0}: (8, {})} | custom-call | flops 1207959552 | bytes 8388608 | tf_op jit(solution)/shard_map/middle/pallas_call | solution.py:295
  39.6 0.9 %collective-permute-done.6.evens_in = bf16[640,256]{1,0:T(8,128)(2,1)S(1)} collective-permute-done((bf16[640,256]{1,0:T(8,128)(2,1)S(1)}, bf16[640,256]{1,0:T(8,128)(2,1)S(1)}, u32[]{:S(2)}, u32[]{:S(2)}) %collective-permute-start.6) | collective-permute-done | bytes 327712 | tf_op jit(solution)/shard_map/ppermute | solution.py:284
  40.5 0.9 %collective-permute-done.7.odds_in = bf16[640,256]{1,0:T(8,128)(2,1)S(1)} collective-permute-done((bf16[640,256]{1,0:T(8,128)(2,1)S(1)}, bf16[640,256]{1,0:T(8,128)(2,1)S(1)}, u32[]{:S(2)}, u32[]{:S(2)}) %collective-permute-start.7) | collective-permute-done | bytes 327712 | tf_op jit(solution)/shard_map/ppermute | solution.py:284
  41.4 0.8 %rims.9 = (f32[2048,512]{1,0:T(8,128)S(1)}, f32[8,256]{1,0:T(8,128)S(1)}, bf16[640,256]{1,0:T(8,128)(2,1)S(1)}, bf16[640,256]{1,0:T(8,128)(2,1)S(1)}) custom-call(s32[1]{0:T(128)} %bitcast.odd, f32[8,256]{1,0:T(8,128)S(1)} %get-tuple-element.70._.partial, bf16[8,256,1536]{2,1,0:T(8,128)(2,1)S(1)} %get-tuple-element.50.banded, ...), custom_call_target="tpu_custom_call", output_to_operand_aliasing={{0}: (6, {})} | custom-call | flops 241591904 | bytes 2097152 | tf_op jit(solution)/shard_map/rims/pallas_call | solution.py:336
  42.3 4.5 %collective-permute-start.11 = (bf16[640,256]{1,0:T(8,128)(2,1)S(1)}, bf16[640,256]{1,0:T(8,128)(2,1)S(1)}, u32[]{:S(2)}, u32[]{:S(2)}) collective-permute-start(bf16[640,256]{1,0:T(8,128)(2,1)S(1)} %get-tuple-element.80.refs_2_), channel_id=1, source_target_pairs={{4,8},{8,4},{12,16},{16,12},{20,24},{24,20},{28,32},{32,28},{36,40... | collective-permute-start | bytes 983048 | tf_op jit(solution)/shard_map/ppermute | solution.py:284
  46.8 1.7 %middle.10 = (f32[2048,512]{1,0:T(8,128)S(1)}, f32[8,256]{1,0:T(8,128)S(1)}) custom-call(s32[1]{0:T(128)} %bitcast.odd, f32[8,256]{1,0:T(8,128)S(1)} %get-tuple-element.72._.refs_3_, bf16[8,256,1536]{2,1,0:T(8,128)(2,1)S(1)} %get-tuple-element.50.banded, f32[2048,512]{1,0:T(8,128)S(1)} %weights.1._, bf16[640,256]{1,0:T(8,128)(2,1)S(1)} %get-tuple-element.73.refs_0_, ...), custom_call_target="tpu_custom_call" | custom-call | flops 1207959552 | bytes 8388608 | tf_op jit(solution)/shard_map/middle/pallas_call | solution.py:295
  48.5 1.7 %middle.11 = (f32[2048,512]{1,0:T(8,128)S(1)}, f32[8,256]{1,0:T(8,128)S(1)}) custom-call(s32[1]{0:T(128)} %bitcast.odd, f32[8,256]{1,0:T(8,128)S(1)} %get-tuple-element.77._.partial, bf16[8,256,1536]{2,1,0:T(8,128)(2,1)S(1)} %get-tuple-element.50.banded, f32[2048,512]{1,0:T(8,128)S(1)} %weights.1._, ...), custom_call_target="tpu_custom_call", output_to_operand_aliasing={{0}: (8, {})} | custom-call | flops 1207959552 | bytes 8388608 | tf_op jit(solution)/shard_map/middle/pallas_call | solution.py:295
  50.2 2.5 %store.1 = (f32[2048,512]{1,0:T(8,128)}, f32[2048,512]{1,0:T(8,128)}) custom-call(f32[8,256]{1,0:T(8,128)S(1)} %get-tuple-element.82._.partial, f32[2048,512]{1,0:T(8,128)S(1)} %get-tuple-element.83.previous, f32[2048,512]{1,0:T(8,128)S(1)} %get-tuple-element.84.current.begun), custom_call_target="tpu_custom_call" | custom-call | bytes 16777216 | tf_op jit(solution)/shard_map/store/pallas_call | solution.py:422
  52.7 1.4 %rims.10 = (f32[2048,512]{1,0:T(8,128)}, f32[8,256]{1,0:T(8,128)S(1)}) custom-call(s32[1]{0:T(128)} %bitcast.odd, f32[8,256]{1,0:T(8,128)S(1)} %get-tuple-element.82._.partial, bf16[8,256,1536]{2,1,0:T(8,128)(2,1)S(1)} %get-tuple-element.50.banded, f32[2048,512]{1,0:T(8,128)S(1)} %weights.1._, ...), custom_call_target="tpu_custom_call", output_to_operand_aliasing={{0}: (8, {})} | custom-call | flops 241591904 | bytes 2097152 | tf_op jit(solution)/shard_map/rims/pallas_call | solution.py:336
  54.1 0.3 collective-permute-done.11.odds_in
  54.4 0.6 rims.11
  55.0 13.9 %all_to_all.5.parts = f32[32,1,1536]{2,1,0:T(1,128)S(1)} all-to-all(f32[32,1,1536]{2,1,0:T(1,128)S(1)} %get-tuple-element.88), channel_id=1, replica_groups=mesh['slab'=32,'col'=4] {'slab'}, dimensions={0} | all-to-all | bytes 393216 | tf_op jit(solution)/shard_map/all_to_all | solution.py:432
  68.9 1.1 %sums.1 = (f32[3,512]{1,0:T(4,128)}, f32[2048,512]{1,0:T(8,128)}) custom-call(f32[32,1,1536]{2,1,0:T(1,128)S(1)} %all_to_all.5.parts, f32[2,640,256]{2,1,0:T(8,128)S(1)} %get-tuple-element.89.rims, f32[2048,512]{1,0:T(8,128)} %get-tuple-element.90._), custom_call_target="tpu_custom_call", output_to_operand_aliasing={{1}: (2, {})} | custom-call | tf_op jit(solution)/shard_map/sums/pallas_call | solution.py:434
  (22 shorter events, 0.5 us)
Async XLA Ops:
  0.6 8.2 %copy-start.4 = (s32[16,9]{1,0:T(8,128)S(1)}, s32[16,9]{1,0:T(8,128)}, u32[]{:S(2)}) copy-start(s32[16,9]{1,0:T(8,128)} %param.7) | copy-start | bytes 1732
  2.1 14.9 %collective-permute-start.1 = (bf16[640,256]{1,0:T(8,128)(2,1)S(1)}, bf16[640,256]{1,0:T(8,128)(2,1)S(1)}, u32[]{:S(2)}, u32[]{:S(2)}) collective-permute-start(bf16[640,256]{1,0:T(8,128)(2,1)S(1)} %get-tuple-element.48._), channel_id=1, source_target_pairs={{4,8},{8,4},{12,16},{16,12},{20,24},{24,20},{28,32},{32,28},{36,40... | collective-permute-start | bytes 983048 | tf_op jit(solution)/shard_map/ppermute | solution.py:284
  8.8 10.6 %collective-permute-start = (bf16[640,256]{1,0:T(8,128)(2,1)S(1)}, bf16[640,256]{1,0:T(8,128)(2,1)S(1)}, u32[]{:S(2)}, u32[]{:S(2)}) collective-permute-start(bf16[640,256]{1,0:T(8,128)(2,1)S(1)} %get-tuple-element.52), channel_id=1, source_target_pairs={{0,4},{4,0},{8,12},{12,8},{16,20},{20,16},{24,28},{28,24},{32,36},... | collective-permute-start | bytes 983048 | tf_op jit(solution)/shard_map/ppermute | solution.py:284
  8.9 6.1 %copy-start.2 = (bf16[2048,512]{1,0:T(8,128)(2,1)S(1)}, bf16[2048,512]{1,0:T(8,128)(2,1)}, u32[]{:S(2)}) copy-start(bf16[2048,512]{1,0:T(8,128)(2,1)} %probe.1) | copy-start | bytes 6291460
  8.9 6.1 %copy-start.3 = (f32[2048]{0:T(1024)S(1)}, f32[2048]{0:T(1024)}, u32[]{:S(2)}) copy-start(f32[2048]{0:T(1024)} %param.11) | copy-start | bytes 24580
  8.9 6.5 %copy-start.1 = (f32[2048,512]{1,0:T(8,128)S(1)}, f32[2048,512]{1,0:T(8,128)}, u32[]{:S(2)}) copy-start(f32[2048,512]{1,0:T(8,128)} %refs_1_.3) | copy-start | bytes 12582916
  12.8 2.6 %copy-start = (f32[2048,512]{1,0:T(8,128)S(1)}, f32[2048,512]{1,0:T(8,128)}, u32[]{:S(2)}) copy-start(f32[2048,512]{1,0:T(8,128)} %refs_3_.3) | copy-start | bytes 12582916
  12.9 14.1 %collective-permute-start.3 = (bf16[640,256]{1,0:T(8,128)(2,1)S(1)}, bf16[640,256]{1,0:T(8,128)(2,1)S(1)}, u32[]{:S(2)}, u32[]{:S(2)}) collective-permute-start(bf16[640,256]{1,0:T(8,128)(2,1)S(1)} %get-tuple-element.49._), channel_id=1, source_target_pairs={{4,8},{8,4},{12,16},{16,12},{20,24},{24,20},{28,32},{32,28},{36,40... | collective-permute-start | bytes 983048 | tf_op jit(solution)/shard_map/ppermute | solution.py:284
  14.3 12.7 %collective-permute-start.2 = (bf16[640,256]{1,0:T(8,128)(2,1)S(1)}, bf16[640,256]{1,0:T(8,128)(2,1)S(1)}, u32[]{:S(2)}, u32[]{:S(2)}) collective-permute-start(bf16[640,256]{1,0:T(8,128)(2,1)S(1)} %get-tuple-element.57), channel_id=1, source_target_pairs={{0,4},{4,0},{8,12},{12,8},{16,20},{20,16},{24,28},{28,24},{32,36},... | collective-permute-start | bytes 983048 | tf_op jit(solution)/shard_map/ppermute | solution.py:284
  20.2 13.3 %collective-permute-start.4 = (bf16[640,256]{1,0:T(8,128)(2,1)S(1)}, bf16[640,256]{1,0:T(8,128)(2,1)S(1)}, u32[]{:S(2)}, u32[]{:S(2)}) collective-permute-start(bf16[640,256]{1,0:T(8,128)(2,1)S(1)} %get-tuple-element.60.refs_0_), channel_id=1, source_target_pairs={{0,4},{4,0},{8,12},{12,8},{16,20},{20,16},{24,28},{28,24},{32,36},... | collective-permute-start | bytes 983048 | tf_op jit(solution)/shard_map/ppermute | solution.py:284
  20.3 13.6 %collective-permute-start.5 = (bf16[640,256]{1,0:T(8,128)(2,1)S(1)}, bf16[640,256]{1,0:T(8,128)(2,1)S(1)}, u32[]{:S(2)}, u32[]{:S(2)}) collective-permute-start(bf16[640,256]{1,0:T(8,128)(2,1)S(1)} %get-tuple-element.62.refs_2_), channel_id=1, source_target_pairs={{4,8},{8,4},{12,16},{16,12},{20,24},{24,20},{28,32},{32,28},{36,40... | collective-permute-start | bytes 983048 | tf_op jit(solution)/shard_map/ppermute | solution.py:284
  27.8 12.8 %collective-permute-start.6 = (bf16[640,256]{1,0:T(8,128)(2,1)S(1)}, bf16[640,256]{1,0:T(8,128)(2,1)S(1)}, u32[]{:S(2)}, u32[]{:S(2)}) collective-permute-start(bf16[640,256]{1,0:T(8,128)(2,1)S(1)} %get-tuple-element.66.refs_0_), channel_id=1, source_target_pairs={{0,4},{4,0},{8,12},{12,8},{16,20},{20,16},{24,28},{28,24},{32,36},... | collective-permute-start | bytes 983048 | tf_op jit(solution)/shard_map/ppermute | solution.py:284
  27.9 13.5 %collective-permute-start.7 = (bf16[640,256]{1,0:T(8,128)(2,1)S(1)}, bf16[640,256]{1,0:T(8,128)(2,1)S(1)}, u32[]{:S(2)}, u32[]{:S(2)}) collective-permute-start(bf16[640,256]{1,0:T(8,128)(2,1)S(1)} %get-tuple-element.68.refs_2_), channel_id=1, source_target_pairs={{4,8},{8,4},{12,16},{16,12},{20,24},{24,20},{28,32},{32,28},{36,40... | collective-permute-start | bytes 983048 | tf_op jit(solution)/shard_map/ppermute | solution.py:284
  34.7 18.1 %collective-permute-start.8 = (bf16[640,256]{1,0:T(8,128)(2,1)S(1)}, bf16[640,256]{1,0:T(8,128)(2,1)S(1)}, u32[]{:S(2)}, u32[]{:S(2)}) collective-permute-start(bf16[640,256]{1,0:T(8,128)(2,1)S(1)} %get-tuple-element.73.refs_0_), channel_id=1, source_target_pairs={{0,4},{4,0},{8,12},{12,8},{16,20},{20,16},{24,28},{28,24},{32,36},... | collective-permute-start | bytes 983048 | tf_op jit(solution)/shard_map/ppermute | solution.py:284
  34.8 18.0 %collective-permute-start.9 = (bf16[640,256]{1,0:T(8,128)(2,1)S(1)}, bf16[640,256]{1,0:T(8,128)(2,1)S(1)}, u32[]{:S(2)}, u32[]{:S(2)}) collective-permute-start(bf16[640,256]{1,0:T(8,128)(2,1)S(1)} %get-tuple-element.75.refs_2_), channel_id=1, source_target_pairs={{4,8},{8,4},{12,16},{16,12},{20,24},{24,20},{28,32},{32,28},{36,40... | collective-permute-start | bytes 983048 | tf_op jit(solution)/shard_map/ppermute | solution.py:284
  42.2 12.0 %collective-permute-start.10 = (bf16[640,256]{1,0:T(8,128)(2,1)S(1)}, bf16[640,256]{1,0:T(8,128)(2,1)S(1)}, u32[]{:S(2)}, u32[]{:S(2)}) collective-permute-start(bf16[640,256]{1,0:T(8,128)(2,1)S(1)} %get-tuple-element.78.refs_0_), channel_id=1, source_target_pairs={{0,4},{4,0},{8,12},{12,8},{16,20},{20,16},{24,28},{28,24},{32,36},... | collective-permute-start | bytes 983048 | tf_op jit(solution)/shard_map/ppermute | solution.py:284
  42.3 12.1 %collective-permute-start.11 = (bf16[640,256]{1,0:T(8,128)(2,1)S(1)}, bf16[640,256]{1,0:T(8,128)(2,1)S(1)}, u32[]{:S(2)}, u32[]{:S(2)}) collective-permute-start(bf16[640,256]{1,0:T(8,128)(2,1)S(1)} %get-tuple-element.80.refs_2_), channel_id=1, source_target_pairs={{4,8},{8,4},{12,16},{16,12},{20,24},{24,20},{28,32},{32,28},{36,40... | collective-permute-start | bytes 983048 | tf_op jit(solution)/shard_map/ppermute | solution.py:284

commit v8 on v7

--- a/solution.py
+++ b/solution.py
@@ -64,29 +64,49 @@
     return take
 
 
-def edge_kernel(first, cols, odd, current, evens, odds, held, sems):
-    hand_out(odd, fetch_rims(current, first, cols, held, sems), evens, odds)
-
-
-def band_kernel(first, cols, odd, _, places, blocks, current, banded, evens, odds, sems, rims, rim_sems):
+def place_blocks(total, slab, columns, blocks, banded, held, sem, sems):
     rows_blk, slots, width, _ = blocks.shape
-    take = fetch_rims(current, first, cols, rims, rim_sems)
+    load = pltpu.make_async_copy(columns, held, sem)
+    load.start()
+    load.wait()
+
+    def place(row, slot):
+        at = held[row, slot] - (slab[0] * rows_blk + row) + BAND
+        at = jnp.where(at < 0, at + total, at)
+        return jnp.where(at >= total, at - total, at)
 
     def one_pair(pair, _):
         banded[pair] = jnp.zeros(banded.shape[1:], BF16)
         for half in range(2):
             row = 2 * pair + half
             for slot in range(slots):
-                at = pl.multiple_of((places[row, slot] + half) * width, width)
+                at = pl.multiple_of((place(row, slot) + half) * width, width)
                 target = banded.at[pair, pl.ds(half * width, width), pl.ds(at, width)]
                 pltpu.make_async_copy(blocks.at[row, slot], target, sems.at[pair]).start()
         return 0
 
     lax.fori_loop(0, rows_blk // 2, one_pair, 0)
-    hand_out(odd, take, evens, odds)
     for pair in range(rows_blk // 2):
         bytes_of = banded.at[pair, :, pl.ds(0, slots * width)]
         pltpu.make_async_copy(bytes_of, bytes_of, sems.at[pair]).wait()
+
+
+def edge_kernel(first, cols, total, slab, core, columns, blocks, current, banded, evens, odds, held, rim_sems, *rest):
+    hand_out([slab[0] & 1], fetch_rims(current, first, cols, held, rim_sems), evens, odds)
+
+    @pl.when(core[0] == 1)
+    def _():
+        place_blocks(total, slab, columns, blocks, banded, *rest)
+
+
+def band_kernel(first, cols, total, slab, core, _, columns, blocks, current, begun, banded, evens, odds, held, rim_sems, *rest):
+    take = fetch_rims(current, first, cols, held, rim_sems)
+
+    @pl.when(core[0] == 0)
+    def _():
+        place_blocks(total, slab, columns, blocks, banded, *rest)
+
+    hand_out([slab[0] & 1], take, evens, odds)
 
 
 def weight_kernel(scale, _, orbital, probe, weights):
@@ -271,7 +291,8 @@
     rim = BAND * width
     slabs = lax.axis_size("slab")
     total_blocks = rows_blk * slabs
-    odd = lax.axis_index("slab")[None] & 1
+    slab = lax.axis_index("slab")[None]
+    odd = slab & 1
     pairs_of = [[(i, i ^ 1) for i in range(slabs)]]
     pairs_of.append([((i + 1) % slabs, (k + 1) % slabs) for i, k in pairs_of[0]])
     shape = jax.ShapeDtypeStruct
@@ -345,40 +366,40 @@
             name="rims",
         )(*args)
 
-    first_row = lax.axis_index("slab") * rows_blk
-    own_row = first_row + jnp.arange(rows_blk, dtype=jnp.int32)[:, None]
-    places = (block_columns - own_row + BAND + total_blocks) % total_blocks
     pairs = rows_blk // 2
 
-    rim_scratch = [pltpu.VMEM((2, rim, cols), F32), pltpu.SemaphoreType.DMA((2, BAND))]
-    opening = pl.pallas_call(
-        functools.partial(edge_kernel, 0, cols),
-        out_shape=(edge_shape, edge_shape),
-        in_specs=[SMEM, HBM],
-        out_specs=(VMEM, VMEM),
-        scratch_shapes=rim_scratch,
+    core = lax.axis_index("col")[None] & 1
+    band_shape = shape((pairs, 2 * width, (2 * BAND + 2) * width), BF16)
+    opening_scratch = [
+        pltpu.VMEM((2, rim, cols), F32),
+        pltpu.SemaphoreType.DMA((2, BAND)),
+        pltpu.SMEM(block_columns.shape, jnp.int32),
+        pltpu.SemaphoreType.DMA,
+        pltpu.SemaphoreType.DMA((pairs,)),
+    ]
+    in_main = (in_hbm(block_columns), in_hbm(hamiltonian_blocks), in_hbm(current))
+    banded, *opening = pl.pallas_call(
+        functools.partial(edge_kernel, 0, cols, total_blocks),
+        out_shape=(band_shape, edge_shape, edge_shape),
+        in_specs=[SMEM, SMEM, HBM, HBM, HBM],
+        out_specs=(VMEM,) * 3,
+        scratch_shapes=opening_scratch,
         compiler_params=params(),
         cost_estimate=cost(0, 6 * 2 * rim * cols),
         name="edges",
-    )(odd, in_hbm(current))
+    )(slab, core, *in_main)
     halos = [exchange(*opening)]
     banded, *opening = pl.pallas_call(
-        functools.partial(band_kernel, cols, cols),
-        out_shape=(
-            shape((pairs, 2 * width, (2 * BAND + 2) * width), BF16),
-            edge_shape,
-            edge_shape,
-        ),
-        in_specs=[SMEM, VMEM, SMEM, HBM, HBM],
+        functools.partial(band_kernel, cols, cols, total_blocks),
+        out_shape=(band_shape, edge_shape, edge_shape),
+        in_specs=[SMEM, SMEM, VMEM, HBM, HBM, HBM, VMEM],
         out_specs=(VMEM,) * 3,
-        scratch_shapes=[
-            pltpu.SemaphoreType.DMA((pairs,)),
-            *rim_scratch,
-        ],
+        scratch_shapes=opening_scratch,
+        input_output_aliases={6: 0},
         compiler_params=params(),
         cost_estimate=cost(0, 12 * 1024 * 1024),
         name="band",
-    )(odd, opening[1], places, in_hbm(hamiltonian_blocks), in_hbm(current))
+    )(slab, core, opening[1], *in_main, banded)
     halos.append(exchange(*opening))
     weights = pl.pallas_call(
         functools.partial(weight_kernel, 1.0 / (total_blocks * width)),

time: 70.3 us -> 74 us (1.053)
  starting transfers between devices: 24.1 us -> 26.1 us
  Pallas kernels: 24.3 us -> 25.1 us
    ppermute x6, waiting for transfers between devices: 2.28 us -> 6.71 us  [exchange(): lax.ppermute(odds, 'slab', pairs_of[1])]
    ppermute x6, waiting for transfers between devices: 4.42 us -> 0.16 us  [exchange(): lax.ppermute(evens, 'slab', pairs_of[0])]
    ppermute x6, starting transfers between devices: 1.1 us -> 2.7 us  [exchange(): lax.ppermute(evens, 'slab', pairs_of[0])]
  transfers between devices with their start and end apart: 12 -> 12, of which waited for: 7 -> 5; matrix products, arithmetic and copies ran while one was open for 0% -> 0% of each run, Pallas kernels for 30% -> 30%
where the time goes in v8:
time: 74 us; the launch traced here: 73.7 us
  starting transfers between devices  26.1 us (35%)
  Pallas kernels  25.1 us (34%)
  blocking collectives  14.6 us (20%)
  waiting for transfers between devices  6.87 us (9%)
  between operations  1.03 us (1%)
    ppermute x6, starting transfers between devices, exchange(): lax.ppermute(odds, 'slab', pairs_of[1])  23.4 us
    all_to_all x1, blocking collectives, local(): gathered = lax.all_to_all(scattered, 'slab', 0, 0)  14.6 us
    pallas_call x6, Pallas kernels, middle(): pl.pallas_call(functools.partial(middle_kernel, len(sources[chunk]), chun...  10.2 us
    ppermute x6, waiting for transfers between devices, exchange(): lax.ppermute(odds, 'slab', pairs_of[1])  6.71 us
    pallas_call x6, Pallas kernels, rims(): pl.pallas_call(kernel, out_shape=outs, in_specs=specs, out_specs=out_spec...  5.08 us
    pallas_call x1, Pallas kernels, local(): pl.pallas_call(functools.partial(band_kernel, cols, cols, total_blocks),...  4.3 us
    ppermute x6, starting transfers between devices, exchange(): lax.ppermute(evens, 'slab', pairs_of[0])  2.7 us
    pallas_call x1, Pallas kernels, local(): pl.pallas_call(functools.partial(store_kernel, rim), out_shape=(full_shap...  2.54 us
  transfers between devices with their start and end apart: 12, of which 5 were waited for; matrix products, arithmetic and copies ran while one was open for 0% of the time, Pallas kernels for 30%

profile of v8, /device:TPU:0, one launch (start us, length us, event | category | flops | bytes accessed | tf_op | source)
XLA Modules:
  0.0 73.7 jit_solution(12226983083338183052)
XLA Ops:
  0.6 1.5 %edges.1 = (bf16[8,256,1536]{2,1,0:T(8,128)(2,1)S(1)}, bf16[640,256]{1,0:T(8,128)(2,1)S(1)}, bf16[640,256]{1,0:T(8,128)(2,1)S(1)}) custom-call(s32[1]{0:T(128)} %bitcast.slab, s32[1]{0:T(128)} %bitcast.1.core, s32[16,9]{1,0:T(8,128)} %columns.3, bf16[16,9,128,128]{3,2,1,0:T(8,128)(2,1)} %blocks.3, f32[2048,512]{1,0:T(8,128)} %refs_3_.3), custom_call_target="tpu_custom_call" | custom-call | bytes 1966080 | tf_op jit(solution)/shard_map/edges/pallas_call | solution.py:381
  2.2 6.7 %collective-permute-start.1 = (bf16[640,256]{1,0:T(8,128)(2,1)S(1)}, bf16[640,256]{1,0:T(8,128)(2,1)S(1)}, u32[]{:S(2)}, u32[]{:S(2)}) collective-permute-start(bf16[640,256]{1,0:T(8,128)(2,1)S(1)} %get-tuple-element.49._), channel_id=1, source_target_pairs={{4,8},{8,4},{12,16},{16,12},{20,24},{24,20},{28,32},{32,28},{36,40... | collective-permute-start | bytes 983048 | tf_op jit(solution)/shard_map/ppermute | solution.py:305
  8.9 4.3 %band.1 = (bf16[8,256,1536]{2,1,0:T(8,128)(2,1)S(1)}, bf16[640,256]{1,0:T(8,128)(2,1)S(1)}, bf16[640,256]{1,0:T(8,128)(2,1)S(1)}) custom-call(s32[1]{0:T(128)} %bitcast.slab, s32[1]{0:T(128)} %bitcast.1.core, bf16[640,256]{1,0:T(8,128)(2,1)S(1)} %get-tuple-element.49._, s32[16,9]{1,0:T(8,128)} %columns.3, ...), custom_call_target="tpu_custom_call", output_to_operand_aliasing={{0}: (6, {})} | custom-call | bytes 12582912 | tf_op jit(solution)/shard_map/band/pallas_call | solution.py:392
  13.2 1.4 %collective-permute-start.3 = (bf16[640,256]{1,0:T(8,128)(2,1)S(1)}, bf16[640,256]{1,0:T(8,128)(2,1)S(1)}, u32[]{:S(2)}, u32[]{:S(2)}) collective-permute-start(bf16[640,256]{1,0:T(8,128)(2,1)S(1)} %get-tuple-element.51._), channel_id=1, source_target_pairs={{4,8},{8,4},{12,16},{16,12},{20,24},{24,20},{28,32},{32,28},{36,40... | collective-permute-start | bytes 983048 | tf_op jit(solution)/shard_map/ppermute | solution.py:305
  14.7 0.8 %collective-permute-start.2 = (bf16[640,256]{1,0:T(8,128)(2,1)S(1)}, bf16[640,256]{1,0:T(8,128)(2,1)S(1)}, u32[]{:S(2)}, u32[]{:S(2)}) collective-permute-start(bf16[640,256]{1,0:T(8,128)(2,1)S(1)} %get-tuple-element.59), channel_id=1, source_target_pairs={{0,4},{4,0},{8,12},{12,8},{16,20},{20,16},{24,28},{28,24},{32,36},... | collective-permute-start | bytes 983048 | tf_op jit(solution)/shard_map/ppermute | solution.py:305
  15.4 0.3 weights.1._
  15.8 1.7 %middle.6 = (f32[2048,512]{1,0:T(8,128)S(1)}, bf16[768,256]{1,0:T(8,128)(2,1)S(1)}, f32[8,256]{1,0:T(8,128)S(1)}) custom-call(s32[1]{0:T(128)S(6)} %and.10.odd, f32[2048,512]{1,0:T(8,128)S(1)} %weights.1._, bf16[8,256,1536]{2,1,0:T(8,128)(2,1)S(1)} %get-tuple-element.52.banded, f32[2048,512]{1,0:T(8,128)S(1)} %weights.1._, f32[2048,512]{1,0:T(8,128)S(1)} %copy-done, ...), custom_call_target="tpu_custom_call" | custom-call | flops 1207959552 | bytes 8388608 | tf_op jit(solution)/shard_map/middle/pallas_call | solution.py:316
  17.5 0.2 collective-permute-done.evens_in
  17.6 0.8 %rims.6 = (f32[2048,512]{1,0:T(8,128)S(1)}, f32[8,256]{1,0:T(8,128)S(1)}, bf16[640,256]{1,0:T(8,128)(2,1)S(1)}, bf16[640,256]{1,0:T(8,128)(2,1)S(1)}) custom-call(s32[1]{0:T(128)S(6)} %and.10.odd, f32[8,256]{1,0:T(8,128)S(1)} %get-tuple-element.53._.partial, bf16[8,256,1536]{2,1,0:T(8,128)(2,1)S(1)} %get-tuple-element.52.banded, ...), custom_call_target="tpu_custom_call", output_to_operand_aliasing={{0}: (6, {})} | custom-call | flops 241591904 | bytes 2097152 | tf_op jit(solution)/shard_map/rims/pallas_call | solution.py:357
  18.4 1.7 %collective-permute-start.4 = (bf16[640,256]{1,0:T(8,128)(2,1)S(1)}, bf16[640,256]{1,0:T(8,128)(2,1)S(1)}, u32[]{:S(2)}, u32[]{:S(2)}) collective-permute-start(bf16[640,256]{1,0:T(8,128)(2,1)S(1)} %get-tuple-element.62.refs_0_), channel_id=1, source_target_pairs={{0,4},{4,0},{8,12},{12,8},{16,20},{20,16},{24,28},{28,24},{32,36},... | collective-permute-start | bytes 983048 | tf_op jit(solution)/shard_map/ppermute | solution.py:305
  20.1 4.4 %collective-permute-start.5 = (bf16[640,256]{1,0:T(8,128)(2,1)S(1)}, bf16[640,256]{1,0:T(8,128)(2,1)S(1)}, u32[]{:S(2)}, u32[]{:S(2)}) collective-permute-start(bf16[640,256]{1,0:T(8,128)(2,1)S(1)} %get-tuple-element.64.refs_2_), channel_id=1, source_target_pairs={{4,8},{8,4},{12,16},{16,12},{20,24},{24,20},{28,32},{32,28},{36,40... | collective-permute-start | bytes 983048 | tf_op jit(solution)/shard_map/ppermute | solution.py:305
  24.5 1.7 %middle.7 = (f32[2048,512]{1,0:T(8,128)S(1)}, bf16[768,256]{1,0:T(8,128)(2,1)S(1)}, f32[8,256]{1,0:T(8,128)S(1)}) custom-call(s32[1]{0:T(128)S(6)} %and.10.odd, f32[8,256]{1,0:T(8,128)S(1)} %get-tuple-element.56._.refs_0_, bf16[8,256,1536]{2,1,0:T(8,128)(2,1)S(1)} %get-tuple-element.52.banded, ...), custom_call_target="tpu_custom_call", output_to_operand_aliasing={{0}: (6, {})} | custom-call | flops 1207959552 | bytes 8388608 | tf_op jit(solution)/shard_map/middle/pallas_call | solution.py:316
  26.2 1.1 %collective-permute-done.3.odds_in = bf16[640,256]{1,0:T(8,128)(2,1)S(1)} collective-permute-done((bf16[640,256]{1,0:T(8,128)(2,1)S(1)}, bf16[640,256]{1,0:T(8,128)(2,1)S(1)}, u32[]{:S(2)}, u32[]{:S(2)}) %collective-permute-start.3) | collective-permute-done | bytes 327712 | tf_op jit(solution)/shard_map/ppermute | solution.py:305
  27.3 0.8 %rims.7 = (f32[2048,512]{1,0:T(8,128)S(1)}, f32[8,256]{1,0:T(8,128)S(1)}, bf16[640,256]{1,0:T(8,128)(2,1)S(1)}, bf16[640,256]{1,0:T(8,128)(2,1)S(1)}) custom-call(s32[1]{0:T(128)S(6)} %and.10.odd, f32[8,256]{1,0:T(8,128)S(1)} %get-tuple-element.58._.partial, bf16[8,256,1536]{2,1,0:T(8,128)(2,1)S(1)} %get-tuple-element.52.banded, ...), custom_call_target="tpu_custom_call", output_to_operand_aliasing={{0}: (6, {})} | custom-call | flops 241591904 | bytes 2097152 | tf_op jit(solution)/shard_map/rims/pallas_call | solution.py:357
  28.1 0.1 collective-permute-start.6
  28.2 2.5 %collective-permute-start.7 = (bf16[640,256]{1,0:T(8,128)(2,1)S(1)}, bf16[640,256]{1,0:T(8,128)(2,1)S(1)}, u32[]{:S(2)}, u32[]{:S(2)}) collective-permute-start(bf16[640,256]{1,0:T(8,128)(2,1)S(1)} %get-tuple-element.70.refs_2_), channel_id=1, source_target_pairs={{4,8},{8,4},{12,16},{16,12},{20,24},{24,20},{28,32},{32,28},{36,40... | collective-permute-start | bytes 983048 | tf_op jit(solution)/shard_map/ppermute | solution.py:305
  30.7 1.7 %middle.8 = (f32[2048,512]{1,0:T(8,128)S(1)}, bf16[768,256]{1,0:T(8,128)(2,1)S(1)}, f32[8,256]{1,0:T(8,128)S(1)}) custom-call(s32[1]{0:T(128)S(6)} %and.10.odd, f32[8,256]{1,0:T(8,128)S(1)} %get-tuple-element.61._.refs_1_, bf16[8,256,1536]{2,1,0:T(8,128)(2,1)S(1)} %get-tuple-element.52.banded, f32[2048,512]{1,0:T(8,128)S(1)} %weights.1._, ...), custom_call_target="tpu_custom_call" | custom-call | flops 1207959552 | bytes 8388608 | tf_op jit(solution)/shard_map/middle/pallas_call | solution.py:316
  32.4 1.8 %collective-permute-done.5.odds_in = bf16[640,256]{1,0:T(8,128)(2,1)S(1)} collective-permute-done((bf16[640,256]{1,0:T(8,128)(2,1)S(1)}, bf16[640,256]{1,0:T(8,128)(2,1)S(1)}, u32[]{:S(2)}, u32[]{:S(2)}) %collective-permute-start.5) | collective-permute-done | bytes 327712 | tf_op jit(solution)/shard_map/ppermute | solution.py:305
  34.3 0.8 %rims.8 = (f32[2048,512]{1,0:T(8,128)S(1)}, f32[8,256]{1,0:T(8,128)S(1)}, bf16[640,256]{1,0:T(8,128)(2,1)S(1)}, bf16[640,256]{1,0:T(8,128)(2,1)S(1)}) custom-call(s32[1]{0:T(128)S(6)} %and.10.odd, f32[8,256]{1,0:T(8,128)S(1)} %get-tuple-element.65._.partial, bf16[8,256,1536]{2,1,0:T(8,128)(2,1)S(1)} %get-tuple-element.52.banded, ...), custom_call_target="tpu_custom_call", output_to_operand_aliasing={{0}: (6, {})} | custom-call | flops 241591904 | bytes 2097152 | tf_op jit(solution)/shard_map/rims/pallas_call | solution.py:357
  35.1 4.8 %collective-permute-start.9 = (bf16[640,256]{1,0:T(8,128)(2,1)S(1)}, bf16[640,256]{1,0:T(8,128)(2,1)S(1)}, u32[]{:S(2)}, u32[]{:S(2)}) collective-permute-start(bf16[640,256]{1,0:T(8,128)(2,1)S(1)} %get-tuple-element.77.refs_2_), channel_id=1, source_target_pairs={{4,8},{8,4},{12,16},{16,12},{20,24},{24,20},{28,32},{32,28},{36,40... | collective-permute-start | bytes 983048 | tf_op jit(solution)/shard_map/ppermute | solution.py:305
  39.9 1.7 %middle.9 = (f32[2048,512]{1,0:T(8,128)S(1)}, bf16[768,256]{1,0:T(8,128)(2,1)S(1)}, f32[8,256]{1,0:T(8,128)S(1)}) custom-call(s32[1]{0:T(128)S(6)} %and.10.odd, f32[8,256]{1,0:T(8,128)S(1)} %get-tuple-element.67._.refs_2_, bf16[8,256,1536]{2,1,0:T(8,128)(2,1)S(1)} %get-tuple-element.52.banded, ...), custom_call_target="tpu_custom_call", output_to_operand_aliasing={{0}: (8, {})} | custom-call | flops 1207959552 | bytes 8388608 | tf_op jit(solution)/shard_map/middle/pallas_call | solution.py:316
  41.6 1.0 %collective-permute-done.7.odds_in = bf16[640,256]{1,0:T(8,128)(2,1)S(1)} collective-permute-done((bf16[640,256]{1,0:T(8,128)(2,1)S(1)}, bf16[640,256]{1,0:T(8,128)(2,1)S(1)}, u32[]{:S(2)}, u32[]{:S(2)}) %collective-permute-start.7) | collective-permute-done | bytes 327712 | tf_op jit(solution)/shard_map/ppermute | solution.py:305
  42.6 0.8 %rims.9 = (f32[2048,512]{1,0:T(8,128)S(1)}, f32[8,256]{1,0:T(8,128)S(1)}, bf16[640,256]{1,0:T(8,128)(2,1)S(1)}, bf16[640,256]{1,0:T(8,128)(2,1)S(1)}) custom-call(s32[1]{0:T(128)S(6)} %and.10.odd, f32[8,256]{1,0:T(8,128)S(1)} %get-tuple-element.72._.partial, bf16[8,256,1536]{2,1,0:T(8,128)(2,1)S(1)} %get-tuple-element.52.banded, ...), custom_call_target="tpu_custom_call", output_to_operand_aliasing={{0}: (6, {})} | custom-call | flops 241591904 | bytes 2097152 | tf_op jit(solution)/shard_map/rims/pallas_call | solution.py:357
  43.5 3.6 %collective-permute-start.11 = (bf16[640,256]{1,0:T(8,128)(2,1)S(1)}, bf16[640,256]{1,0:T(8,128)(2,1)S(1)}, u32[]{:S(2)}, u32[]{:S(2)}) collective-permute-start(bf16[640,256]{1,0:T(8,128)(2,1)S(1)} %get-tuple-element.82.refs_2_), channel_id=1, source_target_pairs={{4,8},{8,4},{12,16},{16,12},{20,24},{24,20},{28,32},{32,28},{36,40... | collective-permute-start | bytes 983048 | tf_op jit(solution)/shard_map/ppermute | solution.py:305
  47.1 1.7 %middle.10 = (f32[2048,512]{1,0:T(8,128)S(1)}, f32[8,256]{1,0:T(8,128)S(1)}) custom-call(s32[1]{0:T(128)S(6)} %and.10.odd, f32[8,256]{1,0:T(8,128)S(1)} %get-tuple-element.74._.refs_3_, bf16[8,256,1536]{2,1,0:T(8,128)(2,1)S(1)} %get-tuple-element.52.banded, f32[2048,512]{1,0:T(8,128)S(1)} %weights.1._, bf16[640,256]{1,0:T(8,128)(2,1)S(1)} %get-tuple-element.75.refs_0_, ...), custom_call_target="tpu_custom_call" | custom-call | flops 1207959552 | bytes 8388608 | tf_op jit(solution)/shard_map/middle/pallas_call | solution.py:316
  48.8 1.7 %middle.11 = (f32[2048,512]{1,0:T(8,128)S(1)}, f32[8,256]{1,0:T(8,128)S(1)}) custom-call(s32[1]{0:T(128)S(6)} %and.10.odd, f32[8,256]{1,0:T(8,128)S(1)} %get-tuple-element.79._.partial, bf16[8,256,1536]{2,1,0:T(8,128)(2,1)S(1)} %get-tuple-element.52.banded, f32[2048,512]{1,0:T(8,128)S(1)} %weights.1._, ...), custom_call_target="tpu_custom_call", output_to_operand_aliasing={{0}: (8, {})} | custom-call | flops 1207959552 | bytes 8388608 | tf_op jit(solution)/shard_map/middle/pallas_call | solution.py:316
  50.5 2.5 %store.1 = (f32[2048,512]{1,0:T(8,128)}, f32[2048,512]{1,0:T(8,128)}) custom-call(f32[8,256]{1,0:T(8,128)S(1)} %get-tuple-element.84._.partial, f32[2048,512]{1,0:T(8,128)S(1)} %get-tuple-element.85.previous, f32[2048,512]{1,0:T(8,128)S(1)} %get-tuple-element.86.current.begun), custom_call_target="tpu_custom_call" | custom-call | bytes 16777216 | tf_op jit(solution)/shard_map/store/pallas_call | solution.py:443
  53.1 1.4 %rims.10 = (f32[2048,512]{1,0:T(8,128)}, f32[8,256]{1,0:T(8,128)S(1)}) custom-call(s32[1]{0:T(128)S(6)} %and.10.odd, f32[8,256]{1,0:T(8,128)S(1)} %get-tuple-element.84._.partial, bf16[8,256,1536]{2,1,0:T(8,128)(2,1)S(1)} %get-tuple-element.52.banded, f32[2048,512]{1,0:T(8,128)S(1)} %weights.1._, ...), custom_call_target="tpu_custom_call", output_to_operand_aliasing={{0}: (8, {})} | custom-call | flops 241591904 | bytes 2097152 | tf_op jit(solution)/shard_map/rims/pallas_call | solution.py:357
  54.5 2.8 %collective-permute-done.11.odds_in = bf16[640,256]{1,0:T(8,128)(2,1)S(1)} collective-permute-done((bf16[640,256]{1,0:T(8,128)(2,1)S(1)}, bf16[640,256]{1,0:T(8,128)(2,1)S(1)}, u32[]{:S(2)}, u32[]{:S(2)}) %collective-permute-start.11) | collective-permute-done | bytes 327712 | tf_op jit(solution)/shard_map/ppermute | solution.py:305
  57.3 0.6 rims.11
  57.9 14.6 %all_to_all.5.parts = f32[32,1,1536]{2,1,0:T(1,128)S(1)} all-to-all(f32[32,1,1536]{2,1,0:T(1,128)S(1)} %get-tuple-element.90), channel_id=1, replica_groups=mesh['slab'=32,'col'=4] {'slab'}, dimensions={0} | all-to-all | bytes 393216 | tf_op jit(solution)/shard_map/all_to_all | solution.py:453
  72.5 1.1 %sums.1 = (f32[3,512]{1,0:T(4,128)}, f32[2048,512]{1,0:T(8,128)}) custom-call(f32[32,1,1536]{2,1,0:T(1,128)S(1)} %all_to_all.5.parts, f32[2,640,256]{2,1,0:T(8,128)S(1)} %get-tuple-element.91.rims, f32[2048,512]{1,0:T(8,128)} %get-tuple-element.92._), custom_call_target="tpu_custom_call", output_to_operand_aliasing={{1}: (2, {})} | custom-call | tf_op jit(solution)/shard_map/sums/pallas_call | solution.py:455
  (18 shorter events, 0.2 us)
Async XLA Ops:
  2.2 15.3 %collective-permute-start.1 = (bf16[640,256]{1,0:T(8,128)(2,1)S(1)}, bf16[640,256]{1,0:T(8,128)(2,1)S(1)}, u32[]{:S(2)}, u32[]{:S(2)}) collective-permute-start(bf16[640,256]{1,0:T(8,128)(2,1)S(1)} %get-tuple-element.49._), channel_id=1, source_target_pairs={{4,8},{8,4},{12,16},{16,12},{20,24},{24,20},{28,32},{32,28},{36,40... | collective-permute-start | bytes 983048 | tf_op jit(solution)/shard_map/ppermute | solution.py:305
  8.9 8.7 %collective-permute-start = (bf16[640,256]{1,0:T(8,128)(2,1)S(1)}, bf16[640,256]{1,0:T(8,128)(2,1)S(1)}, u32[]{:S(2)}, u32[]{:S(2)}) collective-permute-start(bf16[640,256]{1,0:T(8,128)(2,1)S(1)} %get-tuple-element.54), channel_id=1, source_target_pairs={{0,4},{4,0},{8,12},{12,8},{16,20},{20,16},{24,28},{28,24},{32,36},... | collective-permute-start | bytes 983048 | tf_op jit(solution)/shard_map/ppermute | solution.py:305
  8.9 6.5 %copy-start.2 = (bf16[2048,512]{1,0:T(8,128)(2,1)S(1)}, bf16[2048,512]{1,0:T(8,128)(2,1)}, u32[]{:S(2)}) copy-start(bf16[2048,512]{1,0:T(8,128)(2,1)} %probe.1) | copy-start | bytes 6291460
  8.9 6.5 %copy-start.3 = (f32[2048]{0:T(1024)S(1)}, f32[2048]{0:T(1024)}, u32[]{:S(2)}) copy-start(f32[2048]{0:T(1024)} %param.11) | copy-start | bytes 24580
  8.9 6.9 %copy-start.1 = (f32[2048,512]{1,0:T(8,128)S(1)}, f32[2048,512]{1,0:T(8,128)}, u32[]{:S(2)}) copy-start(f32[2048,512]{1,0:T(8,128)} %refs_1_.3) | copy-start | bytes 12582916
  13.2 2.6 %copy-start = (f32[2048,512]{1,0:T(8,128)S(1)}, f32[2048,512]{1,0:T(8,128)}, u32[]{:S(2)}) copy-start(f32[2048,512]{1,0:T(8,128)} %refs_3_.3) | copy-start | bytes 12582916
  13.2 14.1 %collective-permute-start.3 = (bf16[640,256]{1,0:T(8,128)(2,1)S(1)}, bf16[640,256]{1,0:T(8,128)(2,1)S(1)}, u32[]{:S(2)}, u32[]{:S(2)}) collective-permute-start(bf16[640,256]{1,0:T(8,128)(2,1)S(1)} %get-tuple-element.51._), channel_id=1, source_target_pairs={{4,8},{8,4},{12,16},{16,12},{20,24},{24,20},{28,32},{32,28},{36,40... | collective-permute-start | bytes 983048 | tf_op jit(solution)/shard_map/ppermute | solution.py:305
  14.7 12.6 %collective-permute-start.2 = (bf16[640,256]{1,0:T(8,128)(2,1)S(1)}, bf16[640,256]{1,0:T(8,128)(2,1)S(1)}, u32[]{:S(2)}, u32[]{:S(2)}) collective-permute-start(bf16[640,256]{1,0:T(8,128)(2,1)S(1)} %get-tuple-element.59), channel_id=1, source_target_pairs={{0,4},{4,0},{8,12},{12,8},{16,20},{20,16},{24,28},{28,24},{32,36},... | collective-permute-start | bytes 983048 | tf_op jit(solution)/shard_map/ppermute | solution.py:305
  18.4 14.0 %collective-permute-start.4 = (bf16[640,256]{1,0:T(8,128)(2,1)S(1)}, bf16[640,256]{1,0:T(8,128)(2,1)S(1)}, u32[]{:S(2)}, u32[]{:S(2)}) collective-permute-start(bf16[640,256]{1,0:T(8,128)(2,1)S(1)} %get-tuple-element.62.refs_0_), channel_id=1, source_target_pairs={{0,4},{4,0},{8,12},{12,8},{16,20},{20,16},{24,28},{28,24},{32,36},... | collective-permute-start | bytes 983048 | tf_op jit(solution)/shard_map/ppermute | solution.py:305
  20.1 14.2 %collective-permute-start.5 = (bf16[640,256]{1,0:T(8,128)(2,1)S(1)}, bf16[640,256]{1,0:T(8,128)(2,1)S(1)}, u32[]{:S(2)}, u32[]{:S(2)}) collective-permute-start(bf16[640,256]{1,0:T(8,128)(2,1)S(1)} %get-tuple-element.64.refs_2_), channel_id=1, source_target_pairs={{4,8},{8,4},{12,16},{16,12},{20,24},{24,20},{28,32},{32,28},{36,40... | collective-permute-start | bytes 983048 | tf_op jit(solution)/shard_map/ppermute | solution.py:305
  28.1 13.5 %collective-permute-start.6 = (bf16[640,256]{1,0:T(8,128)(2,1)S(1)}, bf16[640,256]{1,0:T(8,128)(2,1)S(1)}, u32[]{:S(2)}, u32[]{:S(2)}) collective-permute-start(bf16[640,256]{1,0:T(8,128)(2,1)S(1)} %get-tuple-element.68.refs_0_), channel_id=1, source_target_pairs={{0,4},{4,0},{8,12},{12,8},{16,20},{20,16},{24,28},{28,24},{32,36},... | collective-permute-start | bytes 983048 | tf_op jit(solution)/shard_map/ppermute | solution.py:305
  28.2 14.4 %collective-permute-start.7 = (bf16[640,256]{1,0:T(8,128)(2,1)S(1)}, bf16[640,256]{1,0:T(8,128)(2,1)S(1)}, u32[]{:S(2)}, u32[]{:S(2)}) collective-permute-start(bf16[640,256]{1,0:T(8,128)(2,1)S(1)} %get-tuple-element.70.refs_2_), channel_id=1, source_target_pairs={{4,8},{8,4},{12,16},{16,12},{20,24},{24,20},{28,32},{32,28},{36,40... | collective-permute-start | bytes 983048 | tf_op jit(solution)/shard_map/ppermute | solution.py:305
  35.0 18.1 %collective-permute-start.8 = (bf16[640,256]{1,0:T(8,128)(2,1)S(1)}, bf16[640,256]{1,0:T(8,128)(2,1)S(1)}, u32[]{:S(2)}, u32[]{:S(2)}) collective-permute-start(bf16[640,256]{1,0:T(8,128)(2,1)S(1)} %get-tuple-element.75.refs_0_), channel_id=1, source_target_pairs={{0,4},{4,0},{8,12},{12,8},{16,20},{20,16},{24,28},{28,24},{32,36},... | collective-permute-start | bytes 983048 | tf_op jit(solution)/shard_map/ppermute | solution.py:305
  35.1 18.0 %collective-permute-start.9 = (bf16[640,256]{1,0:T(8,128)(2,1)S(1)}, bf16[640,256]{1,0:T(8,128)(2,1)S(1)}, u32[]{:S(2)}, u32[]{:S(2)}) collective-permute-start(bf16[640,256]{1,0:T(8,128)(2,1)S(1)} %get-tuple-element.77.refs_2_), channel_id=1, source_target_pairs={{4,8},{8,4},{12,16},{16,12},{20,24},{24,20},{28,32},{32,28},{36,40... | collective-permute-start | bytes 983048 | tf_op jit(solution)/shard_map/ppermute | solution.py:305
  43.4 11.2 %collective-permute-start.10 = (bf16[640,256]{1,0:T(8,128)(2,1)S(1)}, bf16[640,256]{1,0:T(8,128)(2,1)S(1)}, u32[]{:S(2)}, u32[]{:S(2)}) collective-permute-start(bf16[640,256]{1,0:T(8,128)(2,1)S(1)} %get-tuple-element.80.refs_0_), channel_id=1, source_target_pairs={{0,4},{4,0},{8,12},{12,8},{16,20},{20,16},{24,28},{28,24},{32,36},... | collective-permute-start | bytes 983048 | tf_op jit(solution)/shard_map/ppermute | solution.py:305
  43.5 13.8 %collective-permute-start.11 = (bf16[640,256]{1,0:T(8,128)(2,1)S(1)}, bf16[640,256]{1,0:T(8,128)(2,1)S(1)}, u32[]{:S(2)}, u32[]{:S(2)}) collective-permute-start(bf16[640,256]{1,0:T(8,128)(2,1)S(1)} %get-tuple-element.82.refs_2_), channel_id=1, source_target_pairs={{4,8},{8,4},{12,16},{16,12},{20,24},{24,20},{28,32},{32,28},{36,40... | collective-permute-start | bytes 983048 | tf_op jit(solution)/shard_map/ppermute | solution.py:305

commit v9 on v7

--- a/solution.py
+++ b/solution.py
@@ -64,8 +64,22 @@
     return take
 
 
-def edge_kernel(first, cols, odd, current, evens, odds, held, sems):
-    hand_out(odd, fetch_rims(current, first, cols, held, sems), evens, odds)
+def edge_kernel(which, cols, odd, _, current, out, held, sems):
+    rim = held.shape[0]
+    piece = rim // sems.shape[0]
+    side = odd[0] if which else 1 - odd[0]
+    copies = []
+    for i in range(sems.shape[0]):
+        start = pl.multiple_of(side * (current.shape[0] - rim) + i * piece, piece)
+        here = pl.ds(i * piece, piece)
+        copies.append(
+            pltpu.make_async_copy(current.at[pl.ds(start, piece), pl.ds(0, cols)], held.at[here], sems.at[i])
+        )
+        copies[-1].start()
+    for i, copy in enumerate(copies):
+        copy.wait()
+        here = pl.ds(i * piece, piece)
+        out[here] = held[here].astype(BF16)
 
 
 def band_kernel(first, cols, odd, _, places, blocks, current, banded, evens, odds, sems, rims, rim_sems):
@@ -157,13 +171,16 @@
     return parts
 
 
-def rim_sums(first, cols, width, rows_blk, odd, banded, weights, evens, odds, begun, partial, keep):
+def rim_sums(first, cols, width, rows_blk, odd, banded, weights, evens, odds, begun, partial, keep, only=None):
     columns = pl.ds(first, cols)
     total = partial[...]
     for part, (side, pair, a, b, left, right, at) in enumerate(rim_parts(rows_blk)):
+        if only not in (None, side):
+            continue
+        halo = slice(at * width, (at + right - left) * width)
         product = jnp.dot(
             banded[pair, a * width : b * width, left * width : right * width],
-            pick(odd, side, (evens, odds), slice(at * width, (at + right - left) * width)),
+            evens[halo] if only is not None else pick(odd, side, (evens, odds), halo),
             preferred_element_type=F32,
         )
         here = pl.ds((2 * pair + a) * width, (b - a) * width)
@@ -210,18 +227,38 @@
         copy.wait()
 
 
-def last_rim_kernel(first, cols, width, rows_blk, odd, _, banded, weights, evens_in, odds_in, begun, partial, *refs):
-    *earlier, moments, rims = refs
-    rim = rims.shape[1]
-
-    def keep(part, side, here, columns, result):
-        base = here.start - (0 if side == 0 else rows_blk * width - rim)
-        rims[side, base : base + here.size] = result
-
-    total = rim_sums(
-        first, cols, width, rows_blk, odd, banded, weights, evens_in, odds_in, begun, partial, keep
-    )
-    parts = [jnp.sum(one, axis=0, keepdims=True) for one in [*(ref[...] for ref in earlier), total]]
+def last_side(which, bound, odd, banded, weights, halo, begun, partial, moments, held, done=None):
+    for parity in range(2):
+        side = parity if which else 1 - parity
+        top = 0 if side == 0 else begun.shape[0] - held.shape[0]
+
+        def keep(part, side, here, columns, result, top=top):
+            held[here.start - top : here.start - top + here.size] = result
+
+        @pl.when(odd[0] == parity)
+        def _():
+            moments[...] = rim_sums(
+                *bound, odd, banded, weights, halo, None, begun, partial, keep, only=side
+            )
+            if done is not None:
+                done(top)
+
+
+def even_rim_kernel(first, cols, width, rows_blk, odd, _, banded, weights, halo, begun, partial, __, out, moments, held, sem):
+    def done(top):
+        copy = pltpu.make_async_copy(held, out.at[pl.ds(top, held.shape[0]), pl.ds(first, cols)], sem)
+        copy.start()
+        copy.wait()
+
+    bound = (first, cols, width, rows_blk)
+    last_side(0, bound, odd, banded, weights, halo, begun, partial, moments, held, done)
+
+
+def odd_rim_kernel(first, cols, width, rows_blk, odd, _, banded, weights, halo, begun, partial, *refs):
+    *earlier, moments, held, total = refs
+    bound = (first, cols, width, rows_blk)
+    last_side(1, bound, odd, banded, weights, halo, begun, partial, total, held)
+    parts = [jnp.sum(one[...], axis=0, keepdims=True) for one in [*earlier, total]]
     row = jnp.concatenate(parts, axis=1)
     for slab in range(moments.shape[0]):
         moments[slab] = row
@@ -239,22 +276,18 @@
         copy.wait()
 
 
-def sum_kernel(first, parts, rims, _, out, out_current, held, sems):
-    _, rim, cols = rims.shape
-    starts = (0, out_current.shape[0] - rim)
+def sum_kernel(first, odd, parts, rims, _, out, out_current, held, sems):
+    rim, cols = rims.shape
+    top = pl.multiple_of(odd[0] * (out_current.shape[0] - rim), rim // BAND)
     copies = [
-        pltpu.make_async_copy(
-            rims.at[side], out_current.at[pl.ds(start, rim), pl.ds(first, cols)], sems.at[side]
-        )
-        for side, start in enumerate(starts)
+        pltpu.make_async_copy(rims, out_current.at[pl.ds(top, rim), pl.ds(first, cols)], sems.at[0])
     ]
-    for copy in copies:
-        copy.start()
+    copies[0].start()
     total = jnp.sum(parts[...], axis=0)
     every = held.shape[1]
     for term in range(held.shape[0]):
         held[term : term + 1] = total[:, term * every : (term + 1) * every]
-    copies.append(pltpu.make_async_copy(held, out, sems.at[2]))
+    copies.append(pltpu.make_async_copy(held, out, sems.at[1]))
     copies[-1].start()
     for copy in copies:
         copy.wait()
@@ -316,7 +349,7 @@
             out_specs = (VMEM,) * 4
             scratch = [pltpu.VMEM((2, rim, cols), BF16)]
             aliases = {6: 0}
-        elif chunk < CHUNKS - 1:
+        else:
             kernel = functools.partial(store_rim_kernel, *bound)
             aliases = {len(args): 0}
             args.append(outputs[1])
@@ -325,14 +358,6 @@
             out_specs = (HBM, VMEM)
             count = len(rim_parts(rows_blk))
             scratch = [pltpu.VMEM((count, 2 * width, cols), F32), pltpu.SemaphoreType.DMA((count,))]
-        else:
-            kernel = functools.partial(last_rim_kernel, *bound)
-            aliases = {}
-            args += sums
-            specs += [VMEM] * len(sums)
-            outs = (shape((slabs, 1, TERMS * all_cols), F32), shape((2, rim, cols), F32))
-            out_specs = (VMEM, VMEM)
-            scratch = []
         return pl.pallas_call(
             kernel,
             out_shape=outs,
@@ -351,17 +376,24 @@
     pairs = rows_blk // 2
 
     rim_scratch = [pltpu.VMEM((2, rim, cols), F32), pltpu.SemaphoreType.DMA((2, BAND))]
-    opening = pl.pallas_call(
-        functools.partial(edge_kernel, 0, cols),
-        out_shape=(edge_shape, edge_shape),
-        in_specs=[SMEM, HBM],
-        out_specs=(VMEM, VMEM),
-        scratch_shapes=rim_scratch,
-        compiler_params=params(),
-        cost_estimate=cost(0, 6 * 2 * rim * cols),
-        name="edges",
-    )(odd, in_hbm(current))
-    halos = [exchange(*opening)]
+
+    def edge(token, which):
+        return pl.pallas_call(
+            functools.partial(edge_kernel, which, cols),
+            out_shape=edge_shape,
+            in_specs=[SMEM, VMEM, HBM],
+            out_specs=VMEM,
+            scratch_shapes=[pltpu.VMEM((rim, cols), F32), pltpu.SemaphoreType.DMA((BAND,))],
+            compiler_params=params(),
+            cost_estimate=cost(0, 6 * rim * cols),
+            name="edge",
+        )(odd, token, in_hbm(current))
+
+    odds = edge(jnp.zeros((8, 128), F32), 1)
+    from_odds = lax.ppermute(odds, "slab", pairs_of[1])
+    evens = edge(odds, 0)
+    halos = [(lax.ppermute(evens, "slab", pairs_of[0]), from_odds)]
+    opening = (odds, evens)
     banded, *opening = pl.pallas_call(
         functools.partial(band_kernel, cols, cols),
         out_shape=(
@@ -412,7 +444,7 @@
             last_current, token = rims(token, term, chunk)
             outputs = (outputs[0], last_current)
         else:
-            scattered, ends = rims(token, term, chunk)
+            break
         sums.append(token)
         if step + 1 < ahead:
             token = begin(token, *order[step + 1])
@@ -429,18 +461,42 @@
                 cost_estimate=cost(0, 16 * 1024 * 1024),
                 name="store",
             )(token, terms[-2], terms[-1])
+    bound = (chunk * cols, cols, width, rows_blk)
+    args = [odd, token, banded, weights, halos[chunk][0], terms[-1], begun[chunk][-1], outputs[1]]
+    last_current, token = pl.pallas_call(
+        functools.partial(even_rim_kernel, *bound),
+        out_shape=(full_shape, part_shape),
+        in_specs=[SMEM] + [VMEM] * 6 + [HBM],
+        out_specs=(HBM, VMEM),
+        scratch_shapes=[pltpu.VMEM((rim, cols), F32), pltpu.SemaphoreType.DMA],
+        input_output_aliases={7: 0},
+        compiler_params=params(),
+        cost_estimate=cost(flops // 10, 1024 * 1024),
+        name="even_rims",
+    )(*args)
+    args = [odd, token, banded, weights, halos[chunk][1], terms[-1], token, *sums]
+    scattered, ends = pl.pallas_call(
+        functools.partial(odd_rim_kernel, *bound),
+        out_shape=(shape((slabs, 1, TERMS * all_cols), F32), shape((rim, cols), F32)),
+        in_specs=[SMEM] + [VMEM] * (len(args) - 1),
+        out_specs=(VMEM, VMEM),
+        scratch_shapes=[pltpu.VMEM(part_shape.shape, F32)],
+        compiler_params=params(),
+        cost_estimate=cost(flops // 10, 1024 * 1024),
+        name="odd_rims",
+    )(*args)
     gathered = lax.all_to_all(scattered, "slab", 0, 0)
     moments_shape = shape((TERMS, all_cols), F32)
     moments, last_current = pl.pallas_call(
         functools.partial(sum_kernel, all_cols - cols),
         out_shape=(moments_shape, full_shape),
-        in_specs=[VMEM, VMEM, HBM],
+        in_specs=[SMEM, VMEM, VMEM, HBM],
         out_specs=(HBM, HBM),
-        scratch_shapes=[pltpu.VMEM(moments_shape.shape, F32), pltpu.SemaphoreType.DMA((3,))],
-        input_output_aliases={2: 1},
+        scratch_shapes=[pltpu.VMEM(moments_shape.shape, F32), pltpu.SemaphoreType.DMA((2,))],
+        input_output_aliases={3: 1},
         compiler_params=params(),
         name="sums",
-    )(gathered, ends, outputs[1])
+    )(odd, gathered, ends, last_current)
     return outputs[0], last_current, moments
 
 

time: 70.3 us -> 70.6 us (level)
  Pallas kernels: 24.3 us -> 26.3 us
  waiting for transfers between devices: 6.7 us -> 5.87 us
  blocking collectives: 13.9 us -> 13.1 us
    ppermute x6 -> x5, starting transfers between devices: 23 us -> 16.1 us  [exchange(): lax.ppermute(odds, 'slab', pairs_of[1])]
    ppermute x0 -> x2, starting transfers between devices: none -> 6.81 us  [the longest x1 6.72 us: local(): from_odds = lax.ppermute(odds, 'slab', pairs_of[1])]
    ppermute x6 -> x5, waiting for transfers between devices: 4.42 us -> 1.04 us  [exchange(): lax.ppermute(evens, 'slab', pairs_of[0])]
    pallas_call x1 -> x4, Pallas kernels: 1.46 us -> 4.05 us  [the longest x2 2.43 us: edge(): pl.pallas_call(functools.partial(edge_kernel, which, cols), out_shape=edg...]
    ppermute x0 -> x2, waiting for transfers between devices: none -> 2.42 us  [the longest x1 2.42 us: local(): halos = [(lax.ppermute(evens, 'slab', pairs_of[0]), from_odds)]]
    all_to_all x1, blocking collectives: 13.9 us -> 13.1 us  [local(): gathered = lax.all_to_all(scattered, 'slab', 0, 0)]
    pallas_call x6 -> x5, Pallas kernels: 5.01 us -> 4.45 us  [rims(): pl.pallas_call(kernel, out_shape=outs, in_specs=specs, out_specs=out_spec...]
    ppermute x6 -> x5, waiting for transfers between devices: 2.28 us -> 2.41 us  [exchange(): lax.ppermute(odds, 'slab', pairs_of[1])]
  transfers between devices with their start and end apart: 12 -> 12, of which waited for: 7 -> 5; matrix products, arithmetic and copies ran while one was open for 0% -> 0% of each run, Pallas kernels for 30% -> 34%
where the time goes in v9:
time: 70.6 us; the launch traced here: 70.4 us
  Pallas kernels  26.3 us (37%)
  starting transfers between devices  24 us (34%)
  blocking collectives  13.1 us (19%)
  waiting for transfers between devices  5.87 us (8%)
  between operations  1.11 us (2%)
    ppermute x5, starting transfers between devices, exchange(): lax.ppermute(odds, 'slab', pairs_of[1])  16.1 us
    all_to_all x1, blocking collectives, local(): gathered = lax.all_to_all(scattered, 'slab', 0, 0)  13.1 us
    pallas_call x6, Pallas kernels, middle(): pl.pallas_call(functools.partial(middle_kernel, len(sources[chunk]), chun...  10.2 us
    ppermute x1, starting transfers between devices, local(): from_odds = lax.ppermute(odds, 'slab', pairs_of[1])  6.72 us
    pallas_call x5, Pallas kernels, rims(): pl.pallas_call(kernel, out_shape=outs, in_specs=specs, out_specs=out_spec...  4.45 us
    pallas_call x1, Pallas kernels, local(): pl.pallas_call(functools.partial(band_kernel, cols, cols), out_shape=(sha...  3.87 us
    pallas_call x1, Pallas kernels, local(): pl.pallas_call(functools.partial(store_kernel, rim), out_shape=(full_shap...  2.54 us
    pallas_call x2, Pallas kernels, edge(): pl.pallas_call(functools.partial(edge_kernel, which, cols), out_shape=edg...  2.43 us
  transfers between devices with their start and end apart: 12, of which 5 were waited for; matrix products, arithmetic and copies ran while one was open for 0% of the time, Pallas kernels for 34%

profile of v9, /device:TPU:0, one launch (start us, length us, event | category | flops | bytes accessed | tf_op | source)
XLA Modules:
  0.0 70.4 jit_solution(10515065354002629623)
XLA Ops:
  0.7 1.2 %edge.2._ = bf16[640,256]{1,0:T(8,128)(2,1)S(1)} custom-call(s32[1]{0:T(128)} %bitcast.odd, f32[8,128]{1,0:T(8,128)S(1)} %broadcast_in_dim.2._, f32[2048,512]{1,0:T(8,128)} %refs_3_.3), custom_call_target="tpu_custom_call" | custom-call | bytes 983040 | tf_op jit(solution)/shard_map/edge/pallas_call | solution.py:381
  1.9 6.7 %collective-permute-start.1 = (bf16[640,256]{1,0:T(8,128)(2,1)S(1)}, bf16[640,256]{1,0:T(8,128)(2,1)S(1)}, u32[]{:S(2)}, u32[]{:S(2)}) collective-permute-start(bf16[640,256]{1,0:T(8,128)(2,1)S(1)} %edge.2._), channel_id=1, source_target_pairs={{4,8},{8,4},{12,16},{16,12},{20,24},{24,20},{28,32},{32,28},{36,40... | collective-permute-start | bytes 983048 | tf_op jit(solution)/shard_map/ppermute | solution.py:393
  8.6 1.2 %edge.3._ = bf16[640,256]{1,0:T(8,128)(2,1)S(1)} custom-call(s32[1]{0:T(128)} %bitcast.odd, bf16[640,256]{1,0:T(8,128)(2,1)S(1)} %edge.2._, f32[2048,512]{1,0:T(8,128)} %refs_3_.3), custom_call_target="tpu_custom_call" | custom-call | bytes 983040 | tf_op jit(solution)/shard_map/edge/pallas_call | solution.py:381
  10.1 3.9 %band.1 = (bf16[8,256,1536]{2,1,0:T(8,128)(2,1)S(1)}, bf16[640,256]{1,0:T(8,128)(2,1)S(1)}, bf16[640,256]{1,0:T(8,128)(2,1)S(1)}) custom-call(s32[1]{0:T(128)} %bitcast.odd, bf16[640,256]{1,0:T(8,128)(2,1)S(1)} %edge.3._, s32[16,9]{1,0:T(8,128)S(1)} %add_select_fusion.places, bf16[16,9,128,128]{3,2,1,0:T(8,128)(2,1)} %blocks.1, f32[2048,512]{1,0:T(8,128)} %refs_3_.3), custom_call_target="tpu_custom_call" | custom-call | bytes 12582912 | tf_op jit(solution)/shard_map/band/pallas_call | solution.py:397
  14.0 1.4 %collective-permute-start.3 = (bf16[640,256]{1,0:T(8,128)(2,1)S(1)}, bf16[640,256]{1,0:T(8,128)(2,1)S(1)}, u32[]{:S(2)}, u32[]{:S(2)}) collective-permute-start(bf16[640,256]{1,0:T(8,128)(2,1)S(1)} %get-tuple-element.48._), channel_id=1, source_target_pairs={{4,8},{8,4},{12,16},{16,12},{20,24},{24,20},{28,32},{32,28},{36,40... | collective-permute-start | bytes 983048 | tf_op jit(solution)/shard_map/ppermute | solution.py:317
  15.4 0.8 %collective-permute-start.2 = (bf16[640,256]{1,0:T(8,128)(2,1)S(1)}, bf16[640,256]{1,0:T(8,128)(2,1)S(1)}, u32[]{:S(2)}, u32[]{:S(2)}) collective-permute-start(bf16[640,256]{1,0:T(8,128)(2,1)S(1)} %get-tuple-element.55), channel_id=1, source_target_pairs={{0,4},{4,0},{8,12},{12,8},{16,20},{20,16},{24,28},{28,24},{32,36},... | collective-permute-start | bytes 983048 | tf_op jit(solution)/shard_map/ppermute | solution.py:317
  16.1 0.3 weights.1._
  16.5 1.6 %middle.6 = (f32[2048,512]{1,0:T(8,128)S(1)}, bf16[768,256]{1,0:T(8,128)(2,1)S(1)}, f32[8,256]{1,0:T(8,128)S(1)}) custom-call(s32[1]{0:T(128)} %bitcast.odd, f32[2048,512]{1,0:T(8,128)S(1)} %weights.1._, bf16[8,256,1536]{2,1,0:T(8,128)(2,1)S(1)} %get-tuple-element.49.banded, f32[2048,512]{1,0:T(8,128)S(1)} %weights.1._, f32[2048,512]{1,0:T(8,128)S(1)} %copy-done, ...), custom_call_target="tpu_custom_call" | custom-call | flops 1207959552 | bytes 8388608 | tf_op jit(solution)/shard_map/middle/pallas_call | solution.py:328
  18.1 2.4 %collective-permute-done.evens_in = bf16[640,256]{1,0:T(8,128)(2,1)S(1)} collective-permute-done((bf16[640,256]{1,0:T(8,128)(2,1)S(1)}, bf16[640,256]{1,0:T(8,128)(2,1)S(1)}, u32[]{:S(2)}, u32[]{:S(2)}) %collective-permute-start) | collective-permute-done | bytes 327712 | tf_op jit(solution)/shard_map/ppermute | solution.py:395
  20.5 0.8 %rims.5 = (f32[2048,512]{1,0:T(8,128)S(1)}, f32[8,256]{1,0:T(8,128)S(1)}, bf16[640,256]{1,0:T(8,128)(2,1)S(1)}, bf16[640,256]{1,0:T(8,128)(2,1)S(1)}) custom-call(s32[1]{0:T(128)} %bitcast.odd, f32[8,256]{1,0:T(8,128)S(1)} %get-tuple-element.50._.partial, bf16[8,256,1536]{2,1,0:T(8,128)(2,1)S(1)} %get-tuple-element.49.banded, ...), custom_call_target="tpu_custom_call", output_to_operand_aliasing={{0}: (6, {})} | custom-call | flops 241591904 | bytes 2097152 | tf_op jit(solution)/shard_map/rims/pallas_call | solution.py:361
  21.4 3.8 %collective-permute-start.5 = (bf16[640,256]{1,0:T(8,128)(2,1)S(1)}, bf16[640,256]{1,0:T(8,128)(2,1)S(1)}, u32[]{:S(2)}, u32[]{:S(2)}) collective-permute-start(bf16[640,256]{1,0:T(8,128)(2,1)S(1)} %get-tuple-element.60.refs_2_), channel_id=1, source_target_pairs={{4,8},{8,4},{12,16},{16,12},{20,24},{24,20},{28,32},{32,28},{36,40... | collective-permute-start | bytes 983048 | tf_op jit(solution)/shard_map/ppermute | solution.py:317
  25.2 1.6 %middle.7 = (f32[2048,512]{1,0:T(8,128)S(1)}, bf16[768,256]{1,0:T(8,128)(2,1)S(1)}, f32[8,256]{1,0:T(8,128)S(1)}) custom-call(s32[1]{0:T(128)} %bitcast.odd, f32[8,256]{1,0:T(8,128)S(1)} %get-tuple-element.52._.refs_0_, bf16[8,256,1536]{2,1,0:T(8,128)(2,1)S(1)} %get-tuple-element.49.banded, ...), custom_call_target="tpu_custom_call", output_to_operand_aliasing={{0}: (6, {})} | custom-call | flops 1207959552 | bytes 8388608 | tf_op jit(solution)/shard_map/middle/pallas_call | solution.py:328
  26.8 1.3 %collective-permute-done.3.odds_in = bf16[640,256]{1,0:T(8,128)(2,1)S(1)} collective-permute-done((bf16[640,256]{1,0:T(8,128)(2,1)S(1)}, bf16[640,256]{1,0:T(8,128)(2,1)S(1)}, u32[]{:S(2)}, u32[]{:S(2)}) %collective-permute-start.3) | collective-permute-done | bytes 327712 | tf_op jit(solution)/shard_map/ppermute | solution.py:317
  28.1 0.8 %rims.6 = (f32[2048,512]{1,0:T(8,128)S(1)}, f32[8,256]{1,0:T(8,128)S(1)}, bf16[640,256]{1,0:T(8,128)(2,1)S(1)}, bf16[640,256]{1,0:T(8,128)(2,1)S(1)}) custom-call(s32[1]{0:T(128)} %bitcast.odd, f32[8,256]{1,0:T(8,128)S(1)} %get-tuple-element.54._.partial, bf16[8,256,1536]{2,1,0:T(8,128)(2,1)S(1)} %get-tuple-element.49.banded, ...), custom_call_target="tpu_custom_call", output_to_operand_aliasing={{0}: (6, {})} | custom-call | flops 241591904 | bytes 2097152 | tf_op jit(solution)/shard_map/rims/pallas_call | solution.py:361
  29.0 2.9 %collective-permute-start.7 = (bf16[640,256]{1,0:T(8,128)(2,1)S(1)}, bf16[640,256]{1,0:T(8,128)(2,1)S(1)}, u32[]{:S(2)}, u32[]{:S(2)}) collective-permute-start(bf16[640,256]{1,0:T(8,128)(2,1)S(1)} %get-tuple-element.66.refs_2_), channel_id=1, source_target_pairs={{4,8},{8,4},{12,16},{16,12},{20,24},{24,20},{28,32},{32,28},{36,40... | collective-permute-start | bytes 983048 | tf_op jit(solution)/shard_map/ppermute | solution.py:317
  31.9 1.7 %middle.8 = (f32[2048,512]{1,0:T(8,128)S(1)}, bf16[768,256]{1,0:T(8,128)(2,1)S(1)}, f32[8,256]{1,0:T(8,128)S(1)}) custom-call(s32[1]{0:T(128)} %bitcast.odd, f32[8,256]{1,0:T(8,128)S(1)} %get-tuple-element.57._.refs_1_, bf16[8,256,1536]{2,1,0:T(8,128)(2,1)S(1)} %get-tuple-element.49.banded, f32[2048,512]{1,0:T(8,128)S(1)} %weights.1._, ...), custom_call_target="tpu_custom_call" | custom-call | flops 1207959552 | bytes 8388608 | tf_op jit(solution)/shard_map/middle/pallas_call | solution.py:328
  33.6 1.0 %collective-permute-done.4.evens_in = bf16[640,256]{1,0:T(8,128)(2,1)S(1)} collective-permute-done((bf16[640,256]{1,0:T(8,128)(2,1)S(1)}, bf16[640,256]{1,0:T(8,128)(2,1)S(1)}, u32[]{:S(2)}, u32[]{:S(2)}) %collective-permute-start.4) | collective-permute-done | bytes 327712 | tf_op jit(solution)/shard_map/ppermute | solution.py:317
  34.6 0.4 collective-permute-done.5.odds_in
  35.0 0.8 %rims.7 = (f32[2048,512]{1,0:T(8,128)S(1)}, f32[8,256]{1,0:T(8,128)S(1)}, bf16[640,256]{1,0:T(8,128)(2,1)S(1)}, bf16[640,256]{1,0:T(8,128)(2,1)S(1)}) custom-call(s32[1]{0:T(128)} %bitcast.odd, f32[8,256]{1,0:T(8,128)S(1)} %get-tuple-element.61._.partial, bf16[8,256,1536]{2,1,0:T(8,128)(2,1)S(1)} %get-tuple-element.49.banded, ...), custom_call_target="tpu_custom_call", output_to_operand_aliasing={{0}: (6, {})} | custom-call | flops 241591904 | bytes 2097152 | tf_op jit(solution)/shard_map/rims/pallas_call | solution.py:361
  35.9 4.2 %collective-permute-start.9 = (bf16[640,256]{1,0:T(8,128)(2,1)S(1)}, bf16[640,256]{1,0:T(8,128)(2,1)S(1)}, u32[]{:S(2)}, u32[]{:S(2)}) collective-permute-start(bf16[640,256]{1,0:T(8,128)(2,1)S(1)} %get-tuple-element.73.refs_2_), channel_id=1, source_target_pairs={{4,8},{8,4},{12,16},{16,12},{20,24},{24,20},{28,32},{32,28},{36,40... | collective-permute-start | bytes 983048 | tf_op jit(solution)/shard_map/ppermute | solution.py:317
  40.1 1.7 %middle.9 = (f32[2048,512]{1,0:T(8,128)S(1)}, bf16[768,256]{1,0:T(8,128)(2,1)S(1)}, f32[8,256]{1,0:T(8,128)S(1)}) custom-call(s32[1]{0:T(128)} %bitcast.odd, f32[8,256]{1,0:T(8,128)S(1)} %get-tuple-element.63._.refs_2_, bf16[8,256,1536]{2,1,0:T(8,128)(2,1)S(1)} %get-tuple-element.49.banded, ...), custom_call_target="tpu_custom_call", output_to_operand_aliasing={{0}: (8, {})} | custom-call | flops 1207959552 | bytes 8388608 | tf_op jit(solution)/shard_map/middle/pallas_call | solution.py:328
  41.8 0.7 collective-permute-done.7.odds_in
  42.5 0.8 %rims.8 = (f32[2048,512]{1,0:T(8,128)S(1)}, f32[8,256]{1,0:T(8,128)S(1)}, bf16[640,256]{1,0:T(8,128)(2,1)S(1)}, bf16[640,256]{1,0:T(8,128)(2,1)S(1)}) custom-call(s32[1]{0:T(128)} %bitcast.odd, f32[8,256]{1,0:T(8,128)S(1)} %get-tuple-element.68._.partial, bf16[8,256,1536]{2,1,0:T(8,128)(2,1)S(1)} %get-tuple-element.49.banded, ...), custom_call_target="tpu_custom_call", output_to_operand_aliasing={{0}: (6, {})} | custom-call | flops 241591904 | bytes 2097152 | tf_op jit(solution)/shard_map/rims/pallas_call | solution.py:361
  43.4 3.8 %collective-permute-start.11 = (bf16[640,256]{1,0:T(8,128)(2,1)S(1)}, bf16[640,256]{1,0:T(8,128)(2,1)S(1)}, u32[]{:S(2)}, u32[]{:S(2)}) collective-permute-start(bf16[640,256]{1,0:T(8,128)(2,1)S(1)} %get-tuple-element.78.refs_2_), channel_id=1, source_target_pairs={{4,8},{8,4},{12,16},{16,12},{20,24},{24,20},{28,32},{32,28},{36,40... | collective-permute-start | bytes 983048 | tf_op jit(solution)/shard_map/ppermute | solution.py:317
  47.1 1.9 %middle.10 = (f32[2048,512]{1,0:T(8,128)S(1)}, f32[8,256]{1,0:T(8,128)S(1)}) custom-call(s32[1]{0:T(128)} %bitcast.odd, f32[8,256]{1,0:T(8,128)S(1)} %get-tuple-element.70._.refs_3_, bf16[8,256,1536]{2,1,0:T(8,128)(2,1)S(1)} %get-tuple-element.49.banded, f32[2048,512]{1,0:T(8,128)S(1)} %weights.1._, bf16[640,256]{1,0:T(8,128)(2,1)S(1)} %get-tuple-element.71.refs_0_, ...), custom_call_target="tpu_custom_call" | custom-call | flops 1207959552 | bytes 8388608 | tf_op jit(solution)/shard_map/middle/pallas_call | solution.py:328
  49.0 1.7 %middle.11 = (f32[2048,512]{1,0:T(8,128)S(1)}, f32[8,256]{1,0:T(8,128)S(1)}) custom-call(s32[1]{0:T(128)} %bitcast.odd, f32[8,256]{1,0:T(8,128)S(1)} %get-tuple-element.75._.partial, bf16[8,256,1536]{2,1,0:T(8,128)(2,1)S(1)} %get-tuple-element.49.banded, f32[2048,512]{1,0:T(8,128)S(1)} %weights.1._, ...), custom_call_target="tpu_custom_call", output_to_operand_aliasing={{0}: (8, {})} | custom-call | flops 1207959552 | bytes 8388608 | tf_op jit(solution)/shard_map/middle/pallas_call | solution.py:328
  50.7 2.5 %store.1 = (f32[2048,512]{1,0:T(8,128)}, f32[2048,512]{1,0:T(8,128)}) custom-call(f32[8,256]{1,0:T(8,128)S(1)} %get-tuple-element.80._.partial, f32[2048,512]{1,0:T(8,128)S(1)} %get-tuple-element.81.previous, f32[2048,512]{1,0:T(8,128)S(1)} %get-tuple-element.82.current.begun), custom_call_target="tpu_custom_call" | custom-call | bytes 16777216 | tf_op jit(solution)/shard_map/store/pallas_call | solution.py:454
  53.3 1.4 %rims.9 = (f32[2048,512]{1,0:T(8,128)}, f32[8,256]{1,0:T(8,128)S(1)}) custom-call(s32[1]{0:T(128)} %bitcast.odd, f32[8,256]{1,0:T(8,128)S(1)} %get-tuple-element.80._.partial, bf16[8,256,1536]{2,1,0:T(8,128)(2,1)S(1)} %get-tuple-element.49.banded, f32[2048,512]{1,0:T(8,128)S(1)} %weights.1._, ...), custom_call_target="tpu_custom_call", output_to_operand_aliasing={{0}: (8, {})} | custom-call | flops 241591904 | bytes 2097152 | tf_op jit(solution)/shard_map/rims/pallas_call | solution.py:361
  54.7 1.2 %even_rims.1 = (f32[2048,512]{1,0:T(8,128)}, f32[8,256]{1,0:T(8,128)S(1)}) custom-call(s32[1]{0:T(128)} %bitcast.odd, f32[8,256]{1,0:T(8,128)S(1)} %get-tuple-element.85._.refs_4_, bf16[8,256,1536]{2,1,0:T(8,128)(2,1)S(1)} %get-tuple-element.49.banded, f32[2048,512]{1,0:T(8,128)S(1)} %weights.1._, ...), custom_call_target="tpu_custom_call", output_to_operand_aliasing={{0}: (7, {})} | custom-call | flops 120795952 | bytes 1048576 | tf_op jit(solution)/shard_map/even_rims/pallas_call | solution.py:466
  55.9 0.4 odd_rims.1
  56.3 13.1 %all_to_all.5.parts = f32[32,1,1536]{2,1,0:T(1,128)S(1)} all-to-all(f32[32,1,1536]{2,1,0:T(1,128)S(1)} %get-tuple-element.88), channel_id=1, replica_groups=mesh['slab'=32,'col'=4] {'slab'}, dimensions={0} | all-to-all | bytes 393216 | tf_op jit(solution)/shard_map/all_to_all | solution.py:488
  69.4 0.9 %sums.1 = (f32[3,512]{1,0:T(4,128)}, f32[2048,512]{1,0:T(8,128)}) custom-call(s32[1]{0:T(128)} %bitcast.odd, f32[32,1,1536]{2,1,0:T(1,128)S(1)} %all_to_all.5.parts, f32[640,256]{1,0:T(8,128)S(1)} %get-tuple-element.89.rims, f32[2048,512]{1,0:T(8,128)} %get-tuple-element.90._), custom_call_target="tpu_custom_call", output_to_operand_aliasing={{1}: (3, {})} | custom-call | tf_op jit(solution)/shard_map/sums/pallas_call | solution.py:490
  (25 shorter events, 0.6 us)
Async XLA Ops:
  0.6 9.3 %copy-start.4 = (s32[16,9]{1,0:T(8,128)S(1)}, s32[16,9]{1,0:T(8,128)}, u32[]{:S(2)}) copy-start(s32[16,9]{1,0:T(8,128)} %param.7) | copy-start | bytes 1732
  1.9 18.7 %collective-permute-start.1 = (bf16[640,256]{1,0:T(8,128)(2,1)S(1)}, bf16[640,256]{1,0:T(8,128)(2,1)S(1)}, u32[]{:S(2)}, u32[]{:S(2)}) collective-permute-start(bf16[640,256]{1,0:T(8,128)(2,1)S(1)} %edge.2._), channel_id=1, source_target_pairs={{4,8},{8,4},{12,16},{16,12},{20,24},{24,20},{28,32},{32,28},{36,40... | collective-permute-start | bytes 983048 | tf_op jit(solution)/shard_map/ppermute | solution.py:393
  9.8 10.7 %collective-permute-start = (bf16[640,256]{1,0:T(8,128)(2,1)S(1)}, bf16[640,256]{1,0:T(8,128)(2,1)S(1)}, u32[]{:S(2)}, u32[]{:S(2)}) collective-permute-start(bf16[640,256]{1,0:T(8,128)(2,1)S(1)} %edge.3._), channel_id=1, source_target_pairs={{0,4},{4,0},{8,12},{12,8},{16,20},{20,16},{24,28},{28,24},{32,36},... | collective-permute-start | bytes 983048 | tf_op jit(solution)/shard_map/ppermute | solution.py:395
  10.0 6.1 %copy-start.2 = (bf16[2048,512]{1,0:T(8,128)(2,1)S(1)}, bf16[2048,512]{1,0:T(8,128)(2,1)}, u32[]{:S(2)}) copy-start(bf16[2048,512]{1,0:T(8,128)(2,1)} %probe.1) | copy-start | bytes 6291460
  10.0 6.1 %copy-start.3 = (f32[2048]{0:T(1024)S(1)}, f32[2048]{0:T(1024)}, u32[]{:S(2)}) copy-start(f32[2048]{0:T(1024)} %param.11) | copy-start | bytes 24580
  10.0 6.4 %copy-start.1 = (f32[2048,512]{1,0:T(8,128)S(1)}, f32[2048,512]{1,0:T(8,128)}, u32[]{:S(2)}) copy-start(f32[2048,512]{1,0:T(8,128)} %refs_1_.3) | copy-start | bytes 12582916
  13.9 2.5 %copy-start = (f32[2048,512]{1,0:T(8,128)S(1)}, f32[2048,512]{1,0:T(8,128)}, u32[]{:S(2)}) copy-start(f32[2048,512]{1,0:T(8,128)} %refs_3_.3) | copy-start | bytes 12582916
  14.0 14.2 %collective-permute-start.3 = (bf16[640,256]{1,0:T(8,128)(2,1)S(1)}, bf16[640,256]{1,0:T(8,128)(2,1)S(1)}, u32[]{:S(2)}, u32[]{:S(2)}) collective-permute-start(bf16[640,256]{1,0:T(8,128)(2,1)S(1)} %get-tuple-element.48._), channel_id=1, source_target_pairs={{4,8},{8,4},{12,16},{16,12},{20,24},{24,20},{28,32},{32,28},{36,40... | collective-permute-start | bytes 983048 | tf_op jit(solution)/shard_map/ppermute | solution.py:317
  15.4 12.8 %collective-permute-start.2 = (bf16[640,256]{1,0:T(8,128)(2,1)S(1)}, bf16[640,256]{1,0:T(8,128)(2,1)S(1)}, u32[]{:S(2)}, u32[]{:S(2)}) collective-permute-start(bf16[640,256]{1,0:T(8,128)(2,1)S(1)} %get-tuple-element.55), channel_id=1, source_target_pairs={{0,4},{4,0},{8,12},{12,8},{16,20},{20,16},{24,28},{28,24},{32,36},... | collective-permute-start | bytes 983048 | tf_op jit(solution)/shard_map/ppermute | solution.py:317
  21.3 13.3 %collective-permute-start.4 = (bf16[640,256]{1,0:T(8,128)(2,1)S(1)}, bf16[640,256]{1,0:T(8,128)(2,1)S(1)}, u32[]{:S(2)}, u32[]{:S(2)}) collective-permute-start(bf16[640,256]{1,0:T(8,128)(2,1)S(1)} %get-tuple-element.58.refs_0_), channel_id=1, source_target_pairs={{0,4},{4,0},{8,12},{12,8},{16,20},{20,16},{24,28},{28,24},{32,36},... | collective-permute-start | bytes 983048 | tf_op jit(solution)/shard_map/ppermute | solution.py:317
  21.4 13.6 %collective-permute-start.5 = (bf16[640,256]{1,0:T(8,128)(2,1)S(1)}, bf16[640,256]{1,0:T(8,128)(2,1)S(1)}, u32[]{:S(2)}, u32[]{:S(2)}) collective-permute-start(bf16[640,256]{1,0:T(8,128)(2,1)S(1)} %get-tuple-element.60.refs_2_), channel_id=1, source_target_pairs={{4,8},{8,4},{12,16},{16,12},{20,24},{24,20},{28,32},{32,28},{36,40... | collective-permute-start | bytes 983048 | tf_op jit(solution)/shard_map/ppermute | solution.py:317
  28.9 12.9 %collective-permute-start.6 = (bf16[640,256]{1,0:T(8,128)(2,1)S(1)}, bf16[640,256]{1,0:T(8,128)(2,1)S(1)}, u32[]{:S(2)}, u32[]{:S(2)}) collective-permute-start(bf16[640,256]{1,0:T(8,128)(2,1)S(1)} %get-tuple-element.64.refs_0_), channel_id=1, source_target_pairs={{0,4},{4,0},{8,12},{12,8},{16,20},{20,16},{24,28},{28,24},{32,36},... | collective-permute-start | bytes 983048 | tf_op jit(solution)/shard_map/ppermute | solution.py:317
  29.0 13.5 %collective-permute-start.7 = (bf16[640,256]{1,0:T(8,128)(2,1)S(1)}, bf16[640,256]{1,0:T(8,128)(2,1)S(1)}, u32[]{:S(2)}, u32[]{:S(2)}) collective-permute-start(bf16[640,256]{1,0:T(8,128)(2,1)S(1)} %get-tuple-element.66.refs_2_), channel_id=1, source_target_pairs={{4,8},{8,4},{12,16},{16,12},{20,24},{24,20},{28,32},{32,28},{36,40... | collective-permute-start | bytes 983048 | tf_op jit(solution)/shard_map/ppermute | solution.py:317
  35.8 17.5 %collective-permute-start.8 = (bf16[640,256]{1,0:T(8,128)(2,1)S(1)}, bf16[640,256]{1,0:T(8,128)(2,1)S(1)}, u32[]{:S(2)}, u32[]{:S(2)}) collective-permute-start(bf16[640,256]{1,0:T(8,128)(2,1)S(1)} %get-tuple-element.71.refs_0_), channel_id=1, source_target_pairs={{0,4},{4,0},{8,12},{12,8},{16,20},{20,16},{24,28},{28,24},{32,36},... | collective-permute-start | bytes 983048 | tf_op jit(solution)/shard_map/ppermute | solution.py:317
  35.9 17.4 %collective-permute-start.9 = (bf16[640,256]{1,0:T(8,128)(2,1)S(1)}, bf16[640,256]{1,0:T(8,128)(2,1)S(1)}, u32[]{:S(2)}, u32[]{:S(2)}) collective-permute-start(bf16[640,256]{1,0:T(8,128)(2,1)S(1)} %get-tuple-element.73.refs_2_), channel_id=1, source_target_pairs={{4,8},{8,4},{12,16},{16,12},{20,24},{24,20},{28,32},{32,28},{36,40... | collective-permute-start | bytes 983048 | tf_op jit(solution)/shard_map/ppermute | solution.py:317
  43.3 11.4 %collective-permute-start.10 = (bf16[640,256]{1,0:T(8,128)(2,1)S(1)}, bf16[640,256]{1,0:T(8,128)(2,1)S(1)}, u32[]{:S(2)}, u32[]{:S(2)}) collective-permute-start(bf16[640,256]{1,0:T(8,128)(2,1)S(1)} %get-tuple-element.76.refs_0_), channel_id=1, source_target_pairs={{0,4},{4,0},{8,12},{12,8},{16,20},{20,16},{24,28},{28,24},{32,36},... | collective-permute-start | bytes 983048 | tf_op jit(solution)/shard_map/ppermute | solution.py:317
  43.4 12.5 %collective-permute-start.11 = (bf16[640,256]{1,0:T(8,128)(2,1)S(1)}, bf16[640,256]{1,0:T(8,128)(2,1)S(1)}, u32[]{:S(2)}, u32[]{:S(2)}) collective-permute-start(bf16[640,256]{1,0:T(8,128)(2,1)S(1)} %get-tuple-element.78.refs_2_), channel_id=1, source_target_pairs={{4,8},{8,4},{12,16},{16,12},{20,24},{24,20},{28,32},{32,28},{36,40... | collective-permute-start | bytes 983048 | tf_op jit(solution)/shard_map/ppermute | solution.py:317

commit v10 on v9

--- a/solution.py
+++ b/solution.py
@@ -64,22 +64,8 @@
     return take
 
 
-def edge_kernel(which, cols, odd, _, current, out, held, sems):
-    rim = held.shape[0]
-    piece = rim // sems.shape[0]
-    side = odd[0] if which else 1 - odd[0]
-    copies = []
-    for i in range(sems.shape[0]):
-        start = pl.multiple_of(side * (current.shape[0] - rim) + i * piece, piece)
-        here = pl.ds(i * piece, piece)
-        copies.append(
-            pltpu.make_async_copy(current.at[pl.ds(start, piece), pl.ds(0, cols)], held.at[here], sems.at[i])
-        )
-        copies[-1].start()
-    for i, copy in enumerate(copies):
-        copy.wait()
-        here = pl.ds(i * piece, piece)
-        out[here] = held[here].astype(BF16)
+def edge_kernel(first, cols, odd, current, evens, odds, held, sems):
+    hand_out(odd, fetch_rims(current, first, cols, held, sems), evens, odds)
 
 
 def band_kernel(first, cols, odd, _, places, blocks, current, banded, evens, odds, sems, rims, rim_sems):
@@ -190,7 +176,7 @@
     return total
 
 
-def rim_kernel(first, cols, width, rows_blk, odd, _, banded, weights, evens_in, odds_in, begun, partial, *refs):
+def rim_kernel(first, cols, width, rows_blk, odd, _, banded, weights, odds_in, evens_in, begun, partial, *refs):
     upcoming, moments, evens, odds, rims = refs
     rim = rims.shape[1]
     rows = rows_blk * width
@@ -344,6 +330,7 @@
         specs = [SMEM] + [VMEM] * (len(args) - 1)
         bound = (chunk * cols, cols, width, rows_blk)
         if term < TERMS - 1:
+            args[4], args[5] = args[5], args[4]
             kernel = functools.partial(rim_kernel, *bound)
             outs = (full_shape, part_shape, edge_shape, edge_shape)
             out_specs = (VMEM,) * 4
@@ -376,24 +363,17 @@
     pairs = rows_blk // 2
 
     rim_scratch = [pltpu.VMEM((2, rim, cols), F32), pltpu.SemaphoreType.DMA((2, BAND))]
-
-    def edge(token, which):
-        return pl.pallas_call(
-            functools.partial(edge_kernel, which, cols),
-            out_shape=edge_shape,
-            in_specs=[SMEM, VMEM, HBM],
-            out_specs=VMEM,
-            scratch_shapes=[pltpu.VMEM((rim, cols), F32), pltpu.SemaphoreType.DMA((BAND,))],
-            compiler_params=params(),
-            cost_estimate=cost(0, 6 * rim * cols),
-            name="edge",
-        )(odd, token, in_hbm(current))
-
-    odds = edge(jnp.zeros((8, 128), F32), 1)
-    from_odds = lax.ppermute(odds, "slab", pairs_of[1])
-    evens = edge(odds, 0)
-    halos = [(lax.ppermute(evens, "slab", pairs_of[0]), from_odds)]
-    opening = (odds, evens)
+    opening = pl.pallas_call(
+        functools.partial(edge_kernel, 0, cols),
+        out_shape=(edge_shape, edge_shape),
+        in_specs=[SMEM, HBM],
+        out_specs=(VMEM, VMEM),
+        scratch_shapes=rim_scratch,
+        compiler_params=params(),
+        cost_estimate=cost(0, 6 * 2 * rim * cols),
+        name="edges",
+    )(odd, in_hbm(current))
+    halos = [exchange(*opening)]
     banded, *opening = pl.pallas_call(
         functools.partial(band_kernel, cols, cols),
         out_shape=(

time: 70.6 us -> 69.8 us (0.989)
  Pallas kernels: 26.3 us -> 25.1 us
    ppermute x5 -> x6, starting transfers between devices: 16.1 us -> 23.2 us  [exchange(): lax.ppermute(odds, 'slab', pairs_of[1])]
    ppermute x2 -> x0, starting transfers between devices: 6.81 us -> none  [the longest x1 6.72 us: local(): from_odds = lax.ppermute(odds, 'slab', pairs_of[1])]
    ppermute x2 -> x0, waiting for transfers between devices: 2.42 us -> none  [the longest x1 2.42 us: local(): halos = [(lax.ppermute(evens, 'slab', pairs_of[0]), from_odds)]]
    ppermute x5 -> x6, waiting for transfers between devices: 1.04 us -> 2.56 us  [exchange(): lax.ppermute(evens, 'slab', pairs_of[0])]
    pallas_call x2 -> x1, Pallas kernels: 2.43 us -> 1.46 us  [local(): pl.pallas_call(functools.partial(edge_kernel, 0, cols), out_shape=(edge_s...]
    ppermute x5 -> x6, waiting for transfers between devices: 2.41 us -> 3.25 us  [exchange(): lax.ppermute(odds, 'slab', pairs_of[1])]
  transfers between devices with their start and end apart: 12 -> 12, of which waited for: 5 -> 4; matrix products, arithmetic and copies ran while one was open for 0% -> 0% of each run, Pallas kernels for 34% -> 32%
where the time goes in v10:
time: 69.8 us; the launch traced here: 69.6 us
  Pallas kernels  25.1 us (36%)
  starting transfers between devices  24.6 us (35%)
  blocking collectives  12.9 us (18%)
  waiting for transfers between devices  5.82 us (8%)
  between operations  1.05 us (2%)
    ppermute x6, starting transfers between devices, exchange(): lax.ppermute(odds, 'slab', pairs_of[1])  23.2 us
    all_to_all x1, blocking collectives, local(): gathered = lax.all_to_all(scattered, 'slab', 0, 0)  12.9 us
    pallas_call x6, Pallas kernels, middle(): pl.pallas_call(functools.partial(middle_kernel, len(sources[chunk]), chun...  9.99 us
    pallas_call x5, Pallas kernels, rims(): pl.pallas_call(kernel, out_shape=outs, in_specs=specs, out_specs=out_spec...  4.45 us
    pallas_call x1, Pallas kernels, local(): pl.pallas_call(functools.partial(band_kernel, cols, cols), out_shape=(sha...  3.87 us
    ppermute x6, waiting for transfers between devices, exchange(): lax.ppermute(odds, 'slab', pairs_of[1])  3.25 us
    ppermute x6, waiting for transfers between devices, exchange(): lax.ppermute(evens, 'slab', pairs_of[0])  2.56 us
    pallas_call x1, Pallas kernels, local(): pl.pallas_call(functools.partial(store_kernel, rim), out_shape=(full_shap...  2.54 us
  transfers between devices with their start and end apart: 12, of which 4 were waited for; matrix products, arithmetic and copies ran while one was open for 0% of the time, Pallas kernels for 32%

profile of v10, /device:TPU:0, one launch (start us, length us, event | category | flops | bytes accessed | tf_op | source)
XLA Modules:
  0.0 69.6 jit_solution(9035706118181769623)
XLA Ops:
  0.6 1.5 %edges.1 = (bf16[640,256]{1,0:T(8,128)(2,1)S(1)}, bf16[640,256]{1,0:T(8,128)(2,1)S(1)}) custom-call(s32[1]{0:T(128)} %bitcast.odd, f32[2048,512]{1,0:T(8,128)} %refs_3_.3), custom_call_target="tpu_custom_call" | custom-call | bytes 1966080 | tf_op jit(solution)/shard_map/edges/pallas_call | solution.py:366
  2.1 6.7 %collective-permute-start = (bf16[640,256]{1,0:T(8,128)(2,1)S(1)}, bf16[640,256]{1,0:T(8,128)(2,1)S(1)}, u32[]{:S(2)}, u32[]{:S(2)}) collective-permute-start(bf16[640,256]{1,0:T(8,128)(2,1)S(1)} %get-tuple-element.50._), channel_id=1, source_target_pairs={{4,8},{8,4},{12,16},{16,12},{20,24},{24,20},{28,32},{32,28},{36,40... | collective-permute-start | bytes 983048 | tf_op jit(solution)/shard_map/ppermute | solution.py:303
  9.0 3.9 %band.1 = (bf16[8,256,1536]{2,1,0:T(8,128)(2,1)S(1)}, bf16[640,256]{1,0:T(8,128)(2,1)S(1)}, bf16[640,256]{1,0:T(8,128)(2,1)S(1)}) custom-call(s32[1]{0:T(128)} %bitcast.odd, bf16[640,256]{1,0:T(8,128)(2,1)S(1)} %get-tuple-element.50._, s32[16,9]{1,0:T(8,128)S(1)} %add_select_fusion.places, bf16[16,9,128,128]{3,2,1,0:T(8,128)(2,1)} %blocks.1, f32[2048,512]{1,0:T(8,128)} %refs_3_.3), custom_call_target="tpu_custom_call" | custom-call | bytes 12582912 | tf_op jit(solution)/shard_map/band/pallas_call | solution.py:377
  12.9 1.4 %collective-permute-start.2 = (bf16[640,256]{1,0:T(8,128)(2,1)S(1)}, bf16[640,256]{1,0:T(8,128)(2,1)S(1)}, u32[]{:S(2)}, u32[]{:S(2)}) collective-permute-start(bf16[640,256]{1,0:T(8,128)(2,1)S(1)} %get-tuple-element.51._), channel_id=1, source_target_pairs={{4,8},{8,4},{12,16},{16,12},{20,24},{24,20},{28,32},{32,28},{36,40... | collective-permute-start | bytes 983048 | tf_op jit(solution)/shard_map/ppermute | solution.py:303
  14.3 0.8 %collective-permute-start.3 = (bf16[640,256]{1,0:T(8,128)(2,1)S(1)}, bf16[640,256]{1,0:T(8,128)(2,1)S(1)}, u32[]{:S(2)}, u32[]{:S(2)}) collective-permute-start(bf16[640,256]{1,0:T(8,128)(2,1)S(1)} %get-tuple-element.59), channel_id=1, source_target_pairs={{0,4},{4,0},{8,12},{12,8},{16,20},{20,16},{24,28},{28,24},{32,36},... | collective-permute-start | bytes 983048 | tf_op jit(solution)/shard_map/ppermute | solution.py:303
  15.1 0.3 weights.1._
  15.4 1.6 %middle.6 = (f32[2048,512]{1,0:T(8,128)S(1)}, bf16[768,256]{1,0:T(8,128)(2,1)S(1)}, f32[8,256]{1,0:T(8,128)S(1)}) custom-call(s32[1]{0:T(128)} %bitcast.odd, f32[2048,512]{1,0:T(8,128)S(1)} %weights.1._, bf16[8,256,1536]{2,1,0:T(8,128)(2,1)S(1)} %get-tuple-element.52.banded, f32[2048,512]{1,0:T(8,128)S(1)} %weights.1._, f32[2048,512]{1,0:T(8,128)S(1)} %copy-done, ...), custom_call_target="tpu_custom_call" | custom-call | flops 1207959552 | bytes 8388608 | tf_op jit(solution)/shard_map/middle/pallas_call | solution.py:314
  17.1 2.4 %collective-permute-done.1.evens_in = bf16[640,256]{1,0:T(8,128)(2,1)S(1)} collective-permute-done((bf16[640,256]{1,0:T(8,128)(2,1)S(1)}, bf16[640,256]{1,0:T(8,128)(2,1)S(1)}, u32[]{:S(2)}, u32[]{:S(2)}) %collective-permute-start.1) | collective-permute-done | bytes 327712 | tf_op jit(solution)/shard_map/ppermute | solution.py:303
  19.5 0.8 %rims.5 = (f32[2048,512]{1,0:T(8,128)S(1)}, f32[8,256]{1,0:T(8,128)S(1)}, bf16[640,256]{1,0:T(8,128)(2,1)S(1)}, bf16[640,256]{1,0:T(8,128)(2,1)S(1)}) custom-call(s32[1]{0:T(128)} %bitcast.odd, f32[8,256]{1,0:T(8,128)S(1)} %get-tuple-element.53._.partial, bf16[8,256,1536]{2,1,0:T(8,128)(2,1)S(1)} %get-tuple-element.52.banded, ...), custom_call_target="tpu_custom_call", output_to_operand_aliasing={{0}: (6, {})} | custom-call | flops 241591904 | bytes 2097152 | tf_op jit(solution)/shard_map/rims/pallas_call | solution.py:348
  20.2 4.3 %collective-permute-start.4 = (bf16[640,256]{1,0:T(8,128)(2,1)S(1)}, bf16[640,256]{1,0:T(8,128)(2,1)S(1)}, u32[]{:S(2)}, u32[]{:S(2)}) collective-permute-start(bf16[640,256]{1,0:T(8,128)(2,1)S(1)} %get-tuple-element.64.refs_2_), channel_id=1, source_target_pairs={{4,8},{8,4},{12,16},{16,12},{20,24},{24,20},{28,32},{32,28},{36,40... | collective-permute-start | bytes 983048 | tf_op jit(solution)/shard_map/ppermute | solution.py:303
  24.5 1.6 %middle.7 = (f32[2048,512]{1,0:T(8,128)S(1)}, bf16[768,256]{1,0:T(8,128)(2,1)S(1)}, f32[8,256]{1,0:T(8,128)S(1)}) custom-call(s32[1]{0:T(128)} %bitcast.odd, f32[8,256]{1,0:T(8,128)S(1)} %get-tuple-element.56._.refs_0_, bf16[8,256,1536]{2,1,0:T(8,128)(2,1)S(1)} %get-tuple-element.52.banded, ...), custom_call_target="tpu_custom_call", output_to_operand_aliasing={{0}: (6, {})} | custom-call | flops 1207959552 | bytes 8388608 | tf_op jit(solution)/shard_map/middle/pallas_call | solution.py:314
  26.2 1.6 %collective-permute-done.2.odds_in = bf16[640,256]{1,0:T(8,128)(2,1)S(1)} collective-permute-done((bf16[640,256]{1,0:T(8,128)(2,1)S(1)}, bf16[640,256]{1,0:T(8,128)(2,1)S(1)}, u32[]{:S(2)}, u32[]{:S(2)}) %collective-permute-start.2) | collective-permute-done | bytes 327712 | tf_op jit(solution)/shard_map/ppermute | solution.py:303
  27.8 0.8 %rims.6 = (f32[2048,512]{1,0:T(8,128)S(1)}, f32[8,256]{1,0:T(8,128)S(1)}, bf16[640,256]{1,0:T(8,128)(2,1)S(1)}, bf16[640,256]{1,0:T(8,128)(2,1)S(1)}) custom-call(s32[1]{0:T(128)} %bitcast.odd, f32[8,256]{1,0:T(8,128)S(1)} %get-tuple-element.58._.partial, bf16[8,256,1536]{2,1,0:T(8,128)(2,1)S(1)} %get-tuple-element.52.banded, ...), custom_call_target="tpu_custom_call", output_to_operand_aliasing={{0}: (6, {})} | custom-call | flops 241591904 | bytes 2097152 | tf_op jit(solution)/shard_map/rims/pallas_call | solution.py:348
  28.6 2.1 %collective-permute-start.6 = (bf16[640,256]{1,0:T(8,128)(2,1)S(1)}, bf16[640,256]{1,0:T(8,128)(2,1)S(1)}, u32[]{:S(2)}, u32[]{:S(2)}) collective-permute-start(bf16[640,256]{1,0:T(8,128)(2,1)S(1)} %get-tuple-element.70.refs_2_), channel_id=1, source_target_pairs={{4,8},{8,4},{12,16},{16,12},{20,24},{24,20},{28,32},{32,28},{36,40... | collective-permute-start | bytes 983048 | tf_op jit(solution)/shard_map/ppermute | solution.py:303
  30.7 1.7 %middle.8 = (f32[2048,512]{1,0:T(8,128)S(1)}, bf16[768,256]{1,0:T(8,128)(2,1)S(1)}, f32[8,256]{1,0:T(8,128)S(1)}) custom-call(s32[1]{0:T(128)} %bitcast.odd, f32[8,256]{1,0:T(8,128)S(1)} %get-tuple-element.61._.refs_1_, bf16[8,256,1536]{2,1,0:T(8,128)(2,1)S(1)} %get-tuple-element.52.banded, f32[2048,512]{1,0:T(8,128)S(1)} %weights.1._, ...), custom_call_target="tpu_custom_call" | custom-call | flops 1207959552 | bytes 8388608 | tf_op jit(solution)/shard_map/middle/pallas_call | solution.py:314
  32.4 1.6 %collective-permute-done.4.odds_in = bf16[640,256]{1,0:T(8,128)(2,1)S(1)} collective-permute-done((bf16[640,256]{1,0:T(8,128)(2,1)S(1)}, bf16[640,256]{1,0:T(8,128)(2,1)S(1)}, u32[]{:S(2)}, u32[]{:S(2)}) %collective-permute-start.4) | collective-permute-done | bytes 327712 | tf_op jit(solution)/shard_map/ppermute | solution.py:303
  34.0 0.8 %rims.7 = (f32[2048,512]{1,0:T(8,128)S(1)}, f32[8,256]{1,0:T(8,128)S(1)}, bf16[640,256]{1,0:T(8,128)(2,1)S(1)}, bf16[640,256]{1,0:T(8,128)(2,1)S(1)}) custom-call(s32[1]{0:T(128)} %bitcast.odd, f32[8,256]{1,0:T(8,128)S(1)} %get-tuple-element.65._.partial, bf16[8,256,1536]{2,1,0:T(8,128)(2,1)S(1)} %get-tuple-element.52.banded, ...), custom_call_target="tpu_custom_call", output_to_operand_aliasing={{0}: (6, {})} | custom-call | flops 241591904 | bytes 2097152 | tf_op jit(solution)/shard_map/rims/pallas_call | solution.py:348
  34.8 0.5 collective-permute-start.8
  35.3 4.2 %collective-permute-start.9 = (bf16[640,256]{1,0:T(8,128)(2,1)S(1)}, bf16[640,256]{1,0:T(8,128)(2,1)S(1)}, u32[]{:S(2)}, u32[]{:S(2)}) collective-permute-start(bf16[640,256]{1,0:T(8,128)(2,1)S(1)} %get-tuple-element.77.refs_2_), channel_id=1, source_target_pairs={{4,8},{8,4},{12,16},{16,12},{20,24},{24,20},{28,32},{32,28},{36,40... | collective-permute-start | bytes 983048 | tf_op jit(solution)/shard_map/ppermute | solution.py:303
  39.5 1.7 %middle.9 = (f32[2048,512]{1,0:T(8,128)S(1)}, bf16[768,256]{1,0:T(8,128)(2,1)S(1)}, f32[8,256]{1,0:T(8,128)S(1)}) custom-call(s32[1]{0:T(128)} %bitcast.odd, f32[8,256]{1,0:T(8,128)S(1)} %get-tuple-element.67._.refs_2_, bf16[8,256,1536]{2,1,0:T(8,128)(2,1)S(1)} %get-tuple-element.52.banded, ...), custom_call_target="tpu_custom_call", output_to_operand_aliasing={{0}: (8, {})} | custom-call | flops 1207959552 | bytes 8388608 | tf_op jit(solution)/shard_map/middle/pallas_call | solution.py:314
  41.2 0.1 collective-permute-done.7.evens_in
  41.3 0.8 %rims.8 = (f32[2048,512]{1,0:T(8,128)S(1)}, f32[8,256]{1,0:T(8,128)S(1)}, bf16[640,256]{1,0:T(8,128)(2,1)S(1)}, bf16[640,256]{1,0:T(8,128)(2,1)S(1)}) custom-call(s32[1]{0:T(128)} %bitcast.odd, f32[8,256]{1,0:T(8,128)S(1)} %get-tuple-element.72._.partial, bf16[8,256,1536]{2,1,0:T(8,128)(2,1)S(1)} %get-tuple-element.52.banded, ...), custom_call_target="tpu_custom_call", output_to_operand_aliasing={{0}: (6, {})} | custom-call | flops 241591904 | bytes 2097152 | tf_op jit(solution)/shard_map/rims/pallas_call | solution.py:348
  42.1 0.1 collective-permute-start.10
  42.2 4.5 %collective-permute-start.11 = (bf16[640,256]{1,0:T(8,128)(2,1)S(1)}, bf16[640,256]{1,0:T(8,128)(2,1)S(1)}, u32[]{:S(2)}, u32[]{:S(2)}) collective-permute-start(bf16[640,256]{1,0:T(8,128)(2,1)S(1)} %get-tuple-element.82.refs_2_), channel_id=1, source_target_pairs={{4,8},{8,4},{12,16},{16,12},{20,24},{24,20},{28,32},{32,28},{36,40... | collective-permute-start | bytes 983048 | tf_op jit(solution)/shard_map/ppermute | solution.py:303
  46.7 1.7 %middle.10 = (f32[2048,512]{1,0:T(8,128)S(1)}, f32[8,256]{1,0:T(8,128)S(1)}) custom-call(s32[1]{0:T(128)} %bitcast.odd, f32[8,256]{1,0:T(8,128)S(1)} %get-tuple-element.74._.refs_3_, bf16[8,256,1536]{2,1,0:T(8,128)(2,1)S(1)} %get-tuple-element.52.banded, f32[2048,512]{1,0:T(8,128)S(1)} %weights.1._, bf16[640,256]{1,0:T(8,128)(2,1)S(1)} %get-tuple-element.75.refs_0_, ...), custom_call_target="tpu_custom_call" | custom-call | flops 1207959552 | bytes 8388608 | tf_op jit(solution)/shard_map/middle/pallas_call | solution.py:314
  48.4 1.7 %middle.11 = (f32[2048,512]{1,0:T(8,128)S(1)}, f32[8,256]{1,0:T(8,128)S(1)}) custom-call(s32[1]{0:T(128)} %bitcast.odd, f32[8,256]{1,0:T(8,128)S(1)} %get-tuple-element.79._.partial, bf16[8,256,1536]{2,1,0:T(8,128)(2,1)S(1)} %get-tuple-element.52.banded, f32[2048,512]{1,0:T(8,128)S(1)} %weights.1._, ...), custom_call_target="tpu_custom_call", output_to_operand_aliasing={{0}: (8, {})} | custom-call | flops 1207959552 | bytes 8388608 | tf_op jit(solution)/shard_map/middle/pallas_call | solution.py:314
  50.1 2.5 %store.1 = (f32[2048,512]{1,0:T(8,128)}, f32[2048,512]{1,0:T(8,128)}) custom-call(f32[8,256]{1,0:T(8,128)S(1)} %get-tuple-element.84._.partial, f32[2048,512]{1,0:T(8,128)S(1)} %get-tuple-element.85.previous, f32[2048,512]{1,0:T(8,128)S(1)} %get-tuple-element.86.current.begun), custom_call_target="tpu_custom_call" | custom-call | bytes 16777216 | tf_op jit(solution)/shard_map/store/pallas_call | solution.py:434
  52.7 1.4 %rims.9 = (f32[2048,512]{1,0:T(8,128)}, f32[8,256]{1,0:T(8,128)S(1)}) custom-call(s32[1]{0:T(128)} %bitcast.odd, f32[8,256]{1,0:T(8,128)S(1)} %get-tuple-element.84._.partial, bf16[8,256,1536]{2,1,0:T(8,128)(2,1)S(1)} %get-tuple-element.52.banded, f32[2048,512]{1,0:T(8,128)S(1)} %weights.1._, ...), custom_call_target="tpu_custom_call", output_to_operand_aliasing={{0}: (8, {})} | custom-call | flops 241591904 | bytes 2097152 | tf_op jit(solution)/shard_map/rims/pallas_call | solution.py:348
  54.1 1.2 %even_rims.1 = (f32[2048,512]{1,0:T(8,128)}, f32[8,256]{1,0:T(8,128)S(1)}) custom-call(s32[1]{0:T(128)} %bitcast.odd, f32[8,256]{1,0:T(8,128)S(1)} %get-tuple-element.89._.refs_4_, bf16[8,256,1536]{2,1,0:T(8,128)(2,1)S(1)} %get-tuple-element.52.banded, f32[2048,512]{1,0:T(8,128)S(1)} %weights.1._, ...), custom_call_target="tpu_custom_call", output_to_operand_aliasing={{0}: (7, {})} | custom-call | flops 120795952 | bytes 1048576 | tf_op jit(solution)/shard_map/even_rims/pallas_call | solution.py:446
  55.3 0.4 odd_rims.1
  55.7 12.9 %all_to_all.5.parts = f32[32,1,1536]{2,1,0:T(1,128)S(1)} all-to-all(f32[32,1,1536]{2,1,0:T(1,128)S(1)} %get-tuple-element.92), channel_id=1, replica_groups=mesh['slab'=32,'col'=4] {'slab'}, dimensions={0} | all-to-all | bytes 393216 | tf_op jit(solution)/shard_map/all_to_all | solution.py:468
  68.6 0.9 %sums.1 = (f32[3,512]{1,0:T(4,128)}, f32[2048,512]{1,0:T(8,128)}) custom-call(s32[1]{0:T(128)} %bitcast.odd, f32[32,1,1536]{2,1,0:T(1,128)S(1)} %all_to_all.5.parts, f32[640,256]{1,0:T(8,128)S(1)} %get-tuple-element.93.rims, f32[2048,512]{1,0:T(8,128)} %get-tuple-element.94._), custom_call_target="tpu_custom_call", output_to_operand_aliasing={{1}: (3, {})} | custom-call | tf_op jit(solution)/shard_map/sums/pallas_call | solution.py:470
  (23 shorter events, 0.1 us)
Async XLA Ops:
  0.6 8.2 %copy-start.4 = (s32[16,9]{1,0:T(8,128)S(1)}, s32[16,9]{1,0:T(8,128)}, u32[]{:S(2)}) copy-start(s32[16,9]{1,0:T(8,128)} %param.7) | copy-start | bytes 1732
  2.1 14.9 %collective-permute-start = (bf16[640,256]{1,0:T(8,128)(2,1)S(1)}, bf16[640,256]{1,0:T(8,128)(2,1)S(1)}, u32[]{:S(2)}, u32[]{:S(2)}) collective-permute-start(bf16[640,256]{1,0:T(8,128)(2,1)S(1)} %get-tuple-element.50._), channel_id=1, source_target_pairs={{4,8},{8,4},{12,16},{16,12},{20,24},{24,20},{28,32},{32,28},{36,40... | collective-permute-start | bytes 983048 | tf_op jit(solution)/shard_map/ppermute | solution.py:303
  8.8 10.6 %collective-permute-start.1 = (bf16[640,256]{1,0:T(8,128)(2,1)S(1)}, bf16[640,256]{1,0:T(8,128)(2,1)S(1)}, u32[]{:S(2)}, u32[]{:S(2)}) collective-permute-start(bf16[640,256]{1,0:T(8,128)(2,1)S(1)} %get-tuple-element.54), channel_id=1, source_target_pairs={{0,4},{4,0},{8,12},{12,8},{16,20},{20,16},{24,28},{28,24},{32,36},... | collective-permute-start | bytes 983048 | tf_op jit(solution)/shard_map/ppermute | solution.py:303
  8.9 6.1 %copy-start.2 = (bf16[2048,512]{1,0:T(8,128)(2,1)S(1)}, bf16[2048,512]{1,0:T(8,128)(2,1)}, u32[]{:S(2)}) copy-start(bf16[2048,512]{1,0:T(8,128)(2,1)} %probe.1) | copy-start | bytes 6291460
  8.9 6.1 %copy-start.3 = (f32[2048]{0:T(1024)S(1)}, f32[2048]{0:T(1024)}, u32[]{:S(2)}) copy-start(f32[2048]{0:T(1024)} %param.11) | copy-start | bytes 24580
  8.9 6.5 %copy-start.1 = (f32[2048,512]{1,0:T(8,128)S(1)}, f32[2048,512]{1,0:T(8,128)}, u32[]{:S(2)}) copy-start(f32[2048,512]{1,0:T(8,128)} %refs_1_.3) | copy-start | bytes 12582916
  12.8 2.6 %copy-start = (f32[2048,512]{1,0:T(8,128)S(1)}, f32[2048,512]{1,0:T(8,128)}, u32[]{:S(2)}) copy-start(f32[2048,512]{1,0:T(8,128)} %refs_3_.3) | copy-start | bytes 12582916
  12.9 14.9 %collective-permute-start.2 = (bf16[640,256]{1,0:T(8,128)(2,1)S(1)}, bf16[640,256]{1,0:T(8,128)(2,1)S(1)}, u32[]{:S(2)}, u32[]{:S(2)}) collective-permute-start(bf16[640,256]{1,0:T(8,128)(2,1)S(1)} %get-tuple-element.51._), channel_id=1, source_target_pairs={{4,8},{8,4},{12,16},{16,12},{20,24},{24,20},{28,32},{32,28},{36,40... | collective-permute-start | bytes 983048 | tf_op jit(solution)/shard_map/ppermute | solution.py:303
  14.3 13.5 %collective-permute-start.3 = (bf16[640,256]{1,0:T(8,128)(2,1)S(1)}, bf16[640,256]{1,0:T(8,128)(2,1)S(1)}, u32[]{:S(2)}, u32[]{:S(2)}) collective-permute-start(bf16[640,256]{1,0:T(8,128)(2,1)S(1)} %get-tuple-element.59), channel_id=1, source_target_pairs={{0,4},{4,0},{8,12},{12,8},{16,20},{20,16},{24,28},{28,24},{32,36},... | collective-permute-start | bytes 983048 | tf_op jit(solution)/shard_map/ppermute | solution.py:303
  20.2 13.7 %collective-permute-start.4 = (bf16[640,256]{1,0:T(8,128)(2,1)S(1)}, bf16[640,256]{1,0:T(8,128)(2,1)S(1)}, u32[]{:S(2)}, u32[]{:S(2)}) collective-permute-start(bf16[640,256]{1,0:T(8,128)(2,1)S(1)} %get-tuple-element.64.refs_2_), channel_id=1, source_target_pairs={{4,8},{8,4},{12,16},{16,12},{20,24},{24,20},{28,32},{32,28},{36,40... | collective-permute-start | bytes 983048 | tf_op jit(solution)/shard_map/ppermute | solution.py:303
  24.5 9.5 %collective-permute-start.5 = (bf16[640,256]{1,0:T(8,128)(2,1)S(1)}, bf16[640,256]{1,0:T(8,128)(2,1)S(1)}, u32[]{:S(2)}, u32[]{:S(2)}) collective-permute-start(bf16[640,256]{1,0:T(8,128)(2,1)S(1)} %get-tuple-element.62.refs_0_), channel_id=1, source_target_pairs={{0,4},{4,0},{8,12},{12,8},{16,20},{20,16},{24,28},{28,24},{32,36},... | collective-permute-start | bytes 983048 | tf_op jit(solution)/shard_map/ppermute | solution.py:303
  28.6 12.6 %collective-permute-start.6 = (bf16[640,256]{1,0:T(8,128)(2,1)S(1)}, bf16[640,256]{1,0:T(8,128)(2,1)S(1)}, u32[]{:S(2)}, u32[]{:S(2)}) collective-permute-start(bf16[640,256]{1,0:T(8,128)(2,1)S(1)} %get-tuple-element.70.refs_2_), channel_id=1, source_target_pairs={{4,8},{8,4},{12,16},{16,12},{20,24},{24,20},{28,32},{32,28},{36,40... | collective-permute-start | bytes 983048 | tf_op jit(solution)/shard_map/ppermute | solution.py:303
  30.7 10.6 %collective-permute-start.7 = (bf16[640,256]{1,0:T(8,128)(2,1)S(1)}, bf16[640,256]{1,0:T(8,128)(2,1)S(1)}, u32[]{:S(2)}, u32[]{:S(2)}) collective-permute-start(bf16[640,256]{1,0:T(8,128)(2,1)S(1)} %get-tuple-element.68.refs_0_), channel_id=1, source_target_pairs={{0,4},{4,0},{8,12},{12,8},{16,20},{20,16},{24,28},{28,24},{32,36},... | collective-permute-start | bytes 983048 | tf_op jit(solution)/shard_map/ppermute | solution.py:303
  34.8 17.9 %collective-permute-start.8 = (bf16[640,256]{1,0:T(8,128)(2,1)S(1)}, bf16[640,256]{1,0:T(8,128)(2,1)S(1)}, u32[]{:S(2)}, u32[]{:S(2)}) collective-permute-start(bf16[640,256]{1,0:T(8,128)(2,1)S(1)} %get-tuple-element.75.refs_0_), channel_id=1, source_target_pairs={{0,4},{4,0},{8,12},{12,8},{16,20},{20,16},{24,28},{28,24},{32,36},... | collective-permute-start | bytes 983048 | tf_op jit(solution)/shard_map/ppermute | solution.py:303
  35.3 17.4 %collective-permute-start.9 = (bf16[640,256]{1,0:T(8,128)(2,1)S(1)}, bf16[640,256]{1,0:T(8,128)(2,1)S(1)}, u32[]{:S(2)}, u32[]{:S(2)}) collective-permute-start(bf16[640,256]{1,0:T(8,128)(2,1)S(1)} %get-tuple-element.77.refs_2_), channel_id=1, source_target_pairs={{4,8},{8,4},{12,16},{16,12},{20,24},{24,20},{28,32},{32,28},{36,40... | collective-permute-start | bytes 983048 | tf_op jit(solution)/shard_map/ppermute | solution.py:303
  42.1 12.0 %collective-permute-start.10 = (bf16[640,256]{1,0:T(8,128)(2,1)S(1)}, bf16[640,256]{1,0:T(8,128)(2,1)S(1)}, u32[]{:S(2)}, u32[]{:S(2)}) collective-permute-start(bf16[640,256]{1,0:T(8,128)(2,1)S(1)} %get-tuple-element.80.refs_0_), channel_id=1, source_target_pairs={{0,4},{4,0},{8,12},{12,8},{16,20},{20,16},{24,28},{28,24},{32,36},... | collective-permute-start | bytes 983048 | tf_op jit(solution)/shard_map/ppermute | solution.py:303
  42.2 13.1 %collective-permute-start.11 = (bf16[640,256]{1,0:T(8,128)(2,1)S(1)}, bf16[640,256]{1,0:T(8,128)(2,1)S(1)}, u32[]{:S(2)}, u32[]{:S(2)}) collective-permute-start(bf16[640,256]{1,0:T(8,128)(2,1)S(1)} %get-tuple-element.82.refs_2_), channel_id=1, source_target_pairs={{4,8},{8,4},{12,16},{16,12},{20,24},{24,20},{28,32},{32,28},{36,40... | collective-permute-start | bytes 983048 | tf_op jit(solution)/shard_map/ppermute | solution.py:303

commit v11 on v10

--- a/solution.py
+++ b/solution.py
@@ -197,20 +197,16 @@
     hand_out(odd, take, evens, odds)
 
 
-def store_rim_kernel(first, cols, width, rows_blk, odd, _, banded, weights, evens_in, odds_in, begun, partial, __, out, moments, held, sems):
-    copies = []
+def plain_rim_kernel(first, cols, width, rows_blk, odd, _, banded, weights, evens_in, odds_in, begun, partial, moments, rims):
+    rim = rims.shape[1]
 
     def keep(part, side, here, columns, result):
-        slot = held.at[part, pl.ds(0, here.size)]
-        slot[...] = result
-        copies.append(pltpu.make_async_copy(slot, out.at[here, columns], sems.at[part]))
-        copies[-1].start()
+        base = here.start - (0 if side == 0 else rows_blk * width - rim)
+        rims[side, base : base + here.size] = result
 
     moments[...] = rim_sums(
         first, cols, width, rows_blk, odd, banded, weights, evens_in, odds_in, begun, partial, keep
     )
-    for copy in copies:
-        copy.wait()
 
 
 def last_side(which, bound, odd, banded, weights, halo, begun, partial, moments, held, done=None):
@@ -230,14 +226,26 @@
                 done(top)
 
 
-def even_rim_kernel(first, cols, width, rows_blk, odd, _, banded, weights, halo, begun, partial, __, out, moments, held, sem):
+def even_rim_kernel(first, cols, width, rows_blk, odd, _, banded, weights, halo, begun, partial, others, __, out, moments, held, sem, sems):
+    rim = held.shape[0]
+    copies = [
+        pltpu.make_async_copy(
+            others.at[side], out.at[pl.ds(start, rim), pl.ds(first - cols, cols)], sems.at[side]
+        )
+        for side, start in enumerate((0, rows_blk * width - rim))
+    ]
+    for copy in copies:
+        copy.start()
+
     def done(top):
-        copy = pltpu.make_async_copy(held, out.at[pl.ds(top, held.shape[0]), pl.ds(first, cols)], sem)
+        copy = pltpu.make_async_copy(held, out.at[pl.ds(top, rim), pl.ds(first, cols)], sem)
         copy.start()
         copy.wait()
 
     bound = (first, cols, width, rows_blk)
     last_side(0, bound, odd, banded, weights, halo, begun, partial, moments, held, done)
+    for copy in copies:
+        copy.wait()
 
 
 def odd_rim_kernel(first, cols, width, rows_blk, odd, _, banded, weights, halo, begun, partial, *refs):
@@ -337,14 +345,11 @@
             scratch = [pltpu.VMEM((2, rim, cols), BF16)]
             aliases = {6: 0}
         else:
-            kernel = functools.partial(store_rim_kernel, *bound)
-            aliases = {len(args): 0}
-            args.append(outputs[1])
-            specs.append(HBM)
-            outs = (full_shape, part_shape)
-            out_specs = (HBM, VMEM)
-            count = len(rim_parts(rows_blk))
-            scratch = [pltpu.VMEM((count, 2 * width, cols), F32), pltpu.SemaphoreType.DMA((count,))]
+            kernel = functools.partial(plain_rim_kernel, *bound)
+            outs = (part_shape, shape((2, rim, cols), F32))
+            out_specs = (VMEM, VMEM)
+            scratch = []
+            aliases = {}
         return pl.pallas_call(
             kernel,
             out_shape=outs,
@@ -421,8 +426,7 @@
             halos[chunk] = exchange(*sent)
             sources[chunk] = (sent[0], begun[chunk][0], sent[1])
         elif step + 1 < len(order):
-            last_current, token = rims(token, term, chunk)
-            outputs = (outputs[0], last_current)
+            token, others = rims(token, term, chunk)
         else:
             break
         sums.append(token)
@@ -442,14 +446,18 @@
                 name="store",
             )(token, terms[-2], terms[-1])
     bound = (chunk * cols, cols, width, rows_blk)
-    args = [odd, token, banded, weights, halos[chunk][0], terms[-1], begun[chunk][-1], outputs[1]]
+    args = [odd, token, banded, weights, halos[chunk][0], terms[-1], begun[chunk][-1], others, outputs[1]]
     last_current, token = pl.pallas_call(
         functools.partial(even_rim_kernel, *bound),
         out_shape=(full_shape, part_shape),
-        in_specs=[SMEM] + [VMEM] * 6 + [HBM],
+        in_specs=[SMEM] + [VMEM] * 7 + [HBM],
         out_specs=(HBM, VMEM),
-        scratch_shapes=[pltpu.VMEM((rim, cols), F32), pltpu.SemaphoreType.DMA],
-        input_output_aliases={7: 0},
+        scratch_shapes=[
+            pltpu.VMEM((rim, cols), F32),
+            pltpu.SemaphoreType.DMA,
+            pltpu.SemaphoreType.DMA((2,)),
+        ],
+        input_output_aliases={8: 0},
         compiler_params=params(),
         cost_estimate=cost(flops // 10, 1024 * 1024),
         name="even_rims",

time: 69.8 us -> 69.8 us (level)
  Pallas kernels: 25.1 us -> 24.4 us
  blocking collectives: 12.9 us -> 13.6 us
    pallas_call x5, Pallas kernels: 4.45 us -> 3.62 us  [rims(): pl.pallas_call(kernel, out_shape=outs, in_specs=specs, out_specs=out_spec...]
    all_to_all x1, blocking collectives: 12.9 us -> 13.6 us  [local(): gathered = lax.all_to_all(scattered, 'slab', 0, 0)]
  transfers between devices with their start and end apart: 12 -> 12, of which waited for: 4 -> 4; matrix products, arithmetic and copies ran while one was open for 0% -> 0% of each run, Pallas kernels for 32% -> 31%
where the time goes in v11:
time: 69.8 us; the launch traced here: 69.6 us
  starting transfers between devices  24.6 us (35%)
  Pallas kernels  24.4 us (35%)
  blocking collectives  13.6 us (19%)
  waiting for transfers between devices  5.82 us (8%)
  between operations  1.05 us (2%)
    ppermute x6, starting transfers between devices, exchange(): lax.ppermute(odds, 'slab', pairs_of[1])  23.2 us
    all_to_all x1, blocking collectives, local(): gathered = lax.all_to_all(scattered, 'slab', 0, 0)  13.6 us
    pallas_call x6, Pallas kernels, middle(): pl.pallas_call(functools.partial(middle_kernel, len(sources[chunk]), chun...  9.99 us
    pallas_call x1, Pallas kernels, local(): pl.pallas_call(functools.partial(band_kernel, cols, cols), out_shape=(sha...  3.87 us
    pallas_call x5, Pallas kernels, rims(): pl.pallas_call(kernel, out_shape=outs, in_specs=specs, out_specs=out_spec...  3.62 us
    ppermute x6, waiting for transfers between devices, exchange(): lax.ppermute(odds, 'slab', pairs_of[1])  3.25 us
    ppermute x6, waiting for transfers between devices, exchange(): lax.ppermute(evens, 'slab', pairs_of[0])  2.56 us
    pallas_call x1, Pallas kernels, local(): pl.pallas_call(functools.partial(store_kernel, rim), out_shape=(full_shap...  2.54 us
  transfers between devices with their start and end apart: 12, of which 4 were waited for; matrix products, arithmetic and copies ran while one was open for 0% of the time, Pallas kernels for 31%

profile of v11, /device:TPU:0, one launch (start us, length us, event | category | flops | bytes accessed | tf_op | source)
XLA Modules:
  0.0 69.6 jit_solution(8915488418880743510)
XLA Ops:
  0.6 1.5 %edges.1 = (bf16[640,256]{1,0:T(8,128)(2,1)S(1)}, bf16[640,256]{1,0:T(8,128)(2,1)S(1)}) custom-call(s32[1]{0:T(128)} %bitcast.odd, f32[2048,512]{1,0:T(8,128)} %refs_3_.3), custom_call_target="tpu_custom_call" | custom-call | bytes 1966080 | tf_op jit(solution)/shard_map/edges/pallas_call | solution.py:371
  2.1 6.7 %collective-permute-start = (bf16[640,256]{1,0:T(8,128)(2,1)S(1)}, bf16[640,256]{1,0:T(8,128)(2,1)S(1)}, u32[]{:S(2)}, u32[]{:S(2)}) collective-permute-start(bf16[640,256]{1,0:T(8,128)(2,1)S(1)} %get-tuple-element.50._), channel_id=1, source_target_pairs={{4,8},{8,4},{12,16},{16,12},{20,24},{24,20},{28,32},{32,28},{36,40... | collective-permute-start | bytes 983048 | tf_op jit(solution)/shard_map/ppermute | solution.py:311
  9.0 3.9 %band.1 = (bf16[8,256,1536]{2,1,0:T(8,128)(2,1)S(1)}, bf16[640,256]{1,0:T(8,128)(2,1)S(1)}, bf16[640,256]{1,0:T(8,128)(2,1)S(1)}) custom-call(s32[1]{0:T(128)} %bitcast.odd, bf16[640,256]{1,0:T(8,128)(2,1)S(1)} %get-tuple-element.50._, s32[16,9]{1,0:T(8,128)S(1)} %add_select_fusion.places, bf16[16,9,128,128]{3,2,1,0:T(8,128)(2,1)} %blocks.1, f32[2048,512]{1,0:T(8,128)} %refs_3_.3), custom_call_target="tpu_custom_call" | custom-call | bytes 12582912 | tf_op jit(solution)/shard_map/band/pallas_call | solution.py:382
  12.9 1.4 %collective-permute-start.2 = (bf16[640,256]{1,0:T(8,128)(2,1)S(1)}, bf16[640,256]{1,0:T(8,128)(2,1)S(1)}, u32[]{:S(2)}, u32[]{:S(2)}) collective-permute-start(bf16[640,256]{1,0:T(8,128)(2,1)S(1)} %get-tuple-element.51._), channel_id=1, source_target_pairs={{4,8},{8,4},{12,16},{16,12},{20,24},{24,20},{28,32},{32,28},{36,40... | collective-permute-start | bytes 983048 | tf_op jit(solution)/shard_map/ppermute | solution.py:311
  14.3 0.8 %collective-permute-start.3 = (bf16[640,256]{1,0:T(8,128)(2,1)S(1)}, bf16[640,256]{1,0:T(8,128)(2,1)S(1)}, u32[]{:S(2)}, u32[]{:S(2)}) collective-permute-start(bf16[640,256]{1,0:T(8,128)(2,1)S(1)} %get-tuple-element.59), channel_id=1, source_target_pairs={{0,4},{4,0},{8,12},{12,8},{16,20},{20,16},{24,28},{28,24},{32,36},... | collective-permute-start | bytes 983048 | tf_op jit(solution)/shard_map/ppermute | solution.py:311
  15.1 0.3 weights.1._
  15.4 1.6 %middle.6 = (f32[2048,512]{1,0:T(8,128)S(1)}, bf16[768,256]{1,0:T(8,128)(2,1)S(1)}, f32[8,256]{1,0:T(8,128)S(1)}) custom-call(s32[1]{0:T(128)} %bitcast.odd, f32[2048,512]{1,0:T(8,128)S(1)} %weights.1._, bf16[8,256,1536]{2,1,0:T(8,128)(2,1)S(1)} %get-tuple-element.52.banded, f32[2048,512]{1,0:T(8,128)S(1)} %weights.1._, f32[2048,512]{1,0:T(8,128)S(1)} %copy-done, ...), custom_call_target="tpu_custom_call" | custom-call | flops 1207959552 | bytes 8388608 | tf_op jit(solution)/shard_map/middle/pallas_call | solution.py:322
  17.1 2.4 %collective-permute-done.1.evens_in = bf16[640,256]{1,0:T(8,128)(2,1)S(1)} collective-permute-done((bf16[640,256]{1,0:T(8,128)(2,1)S(1)}, bf16[640,256]{1,0:T(8,128)(2,1)S(1)}, u32[]{:S(2)}, u32[]{:S(2)}) %collective-permute-start.1) | collective-permute-done | bytes 327712 | tf_op jit(solution)/shard_map/ppermute | solution.py:311
  19.5 0.8 %rims.5 = (f32[2048,512]{1,0:T(8,128)S(1)}, f32[8,256]{1,0:T(8,128)S(1)}, bf16[640,256]{1,0:T(8,128)(2,1)S(1)}, bf16[640,256]{1,0:T(8,128)(2,1)S(1)}) custom-call(s32[1]{0:T(128)} %bitcast.odd, f32[8,256]{1,0:T(8,128)S(1)} %get-tuple-element.53._.partial, bf16[8,256,1536]{2,1,0:T(8,128)(2,1)S(1)} %get-tuple-element.52.banded, ...), custom_call_target="tpu_custom_call", output_to_operand_aliasing={{0}: (6, {})} | custom-call | flops 241591904 | bytes 2097152 | tf_op jit(solution)/shard_map/rims/pallas_call | solution.py:353
  20.2 4.3 %collective-permute-start.4 = (bf16[640,256]{1,0:T(8,128)(2,1)S(1)}, bf16[640,256]{1,0:T(8,128)(2,1)S(1)}, u32[]{:S(2)}, u32[]{:S(2)}) collective-permute-start(bf16[640,256]{1,0:T(8,128)(2,1)S(1)} %get-tuple-element.64.refs_2_), channel_id=1, source_target_pairs={{4,8},{8,4},{12,16},{16,12},{20,24},{24,20},{28,32},{32,28},{36,40... | collective-permute-start | bytes 983048 | tf_op jit(solution)/shard_map/ppermute | solution.py:311
  24.5 1.6 %middle.7 = (f32[2048,512]{1,0:T(8,128)S(1)}, bf16[768,256]{1,0:T(8,128)(2,1)S(1)}, f32[8,256]{1,0:T(8,128)S(1)}) custom-call(s32[1]{0:T(128)} %bitcast.odd, f32[8,256]{1,0:T(8,128)S(1)} %get-tuple-element.56._.refs_0_, bf16[8,256,1536]{2,1,0:T(8,128)(2,1)S(1)} %get-tuple-element.52.banded, ...), custom_call_target="tpu_custom_call", output_to_operand_aliasing={{0}: (6, {})} | custom-call | flops 1207959552 | bytes 8388608 | tf_op jit(solution)/shard_map/middle/pallas_call | solution.py:322
  26.2 1.6 %collective-permute-done.2.odds_in = bf16[640,256]{1,0:T(8,128)(2,1)S(1)} collective-permute-done((bf16[640,256]{1,0:T(8,128)(2,1)S(1)}, bf16[640,256]{1,0:T(8,128)(2,1)S(1)}, u32[]{:S(2)}, u32[]{:S(2)}) %collective-permute-start.2) | collective-permute-done | bytes 327712 | tf_op jit(solution)/shard_map/ppermute | solution.py:311
  27.8 0.8 %rims.6 = (f32[2048,512]{1,0:T(8,128)S(1)}, f32[8,256]{1,0:T(8,128)S(1)}, bf16[640,256]{1,0:T(8,128)(2,1)S(1)}, bf16[640,256]{1,0:T(8,128)(2,1)S(1)}) custom-call(s32[1]{0:T(128)} %bitcast.odd, f32[8,256]{1,0:T(8,128)S(1)} %get-tuple-element.58._.partial, bf16[8,256,1536]{2,1,0:T(8,128)(2,1)S(1)} %get-tuple-element.52.banded, ...), custom_call_target="tpu_custom_call", output_to_operand_aliasing={{0}: (6, {})} | custom-call | flops 241591904 | bytes 2097152 | tf_op jit(solution)/shard_map/rims/pallas_call | solution.py:353
  28.6 2.1 %collective-permute-start.6 = (bf16[640,256]{1,0:T(8,128)(2,1)S(1)}, bf16[640,256]{1,0:T(8,128)(2,1)S(1)}, u32[]{:S(2)}, u32[]{:S(2)}) collective-permute-start(bf16[640,256]{1,0:T(8,128)(2,1)S(1)} %get-tuple-element.70.refs_2_), channel_id=1, source_target_pairs={{4,8},{8,4},{12,16},{16,12},{20,24},{24,20},{28,32},{32,28},{36,40... | collective-permute-start | bytes 983048 | tf_op jit(solution)/shard_map/ppermute | solution.py:311
  30.7 1.7 %middle.8 = (f32[2048,512]{1,0:T(8,128)S(1)}, bf16[768,256]{1,0:T(8,128)(2,1)S(1)}, f32[8,256]{1,0:T(8,128)S(1)}) custom-call(s32[1]{0:T(128)} %bitcast.odd, f32[8,256]{1,0:T(8,128)S(1)} %get-tuple-element.61._.refs_1_, bf16[8,256,1536]{2,1,0:T(8,128)(2,1)S(1)} %get-tuple-element.52.banded, f32[2048,512]{1,0:T(8,128)S(1)} %weights.1._, ...), custom_call_target="tpu_custom_call" | custom-call | flops 1207959552 | bytes 8388608 | tf_op jit(solution)/shard_map/middle/pallas_call | solution.py:322
  32.4 1.6 %collective-permute-done.4.odds_in = bf16[640,256]{1,0:T(8,128)(2,1)S(1)} collective-permute-done((bf16[640,256]{1,0:T(8,128)(2,1)S(1)}, bf16[640,256]{1,0:T(8,128)(2,1)S(1)}, u32[]{:S(2)}, u32[]{:S(2)}) %collective-permute-start.4) | collective-permute-done | bytes 327712 | tf_op jit(solution)/shard_map/ppermute | solution.py:311
  34.0 0.8 %rims.7 = (f32[2048,512]{1,0:T(8,128)S(1)}, f32[8,256]{1,0:T(8,128)S(1)}, bf16[640,256]{1,0:T(8,128)(2,1)S(1)}, bf16[640,256]{1,0:T(8,128)(2,1)S(1)}) custom-call(s32[1]{0:T(128)} %bitcast.odd, f32[8,256]{1,0:T(8,128)S(1)} %get-tuple-element.65._.partial, bf16[8,256,1536]{2,1,0:T(8,128)(2,1)S(1)} %get-tuple-element.52.banded, ...), custom_call_target="tpu_custom_call", output_to_operand_aliasing={{0}: (6, {})} | custom-call | flops 241591904 | bytes 2097152 | tf_op jit(solution)/shard_map/rims/pallas_call | solution.py:353
  34.8 0.5 collective-permute-start.8
  35.3 4.2 %collective-permute-start.9 = (bf16[640,256]{1,0:T(8,128)(2,1)S(1)}, bf16[640,256]{1,0:T(8,128)(2,1)S(1)}, u32[]{:S(2)}, u32[]{:S(2)}) collective-permute-start(bf16[640,256]{1,0:T(8,128)(2,1)S(1)} %get-tuple-element.77.refs_2_), channel_id=1, source_target_pairs={{4,8},{8,4},{12,16},{16,12},{20,24},{24,20},{28,32},{32,28},{36,40... | collective-permute-start | bytes 983048 | tf_op jit(solution)/shard_map/ppermute | solution.py:311
  39.5 1.7 %middle.9 = (f32[2048,512]{1,0:T(8,128)S(1)}, bf16[768,256]{1,0:T(8,128)(2,1)S(1)}, f32[8,256]{1,0:T(8,128)S(1)}) custom-call(s32[1]{0:T(128)} %bitcast.odd, f32[8,256]{1,0:T(8,128)S(1)} %get-tuple-element.67._.refs_2_, bf16[8,256,1536]{2,1,0:T(8,128)(2,1)S(1)} %get-tuple-element.52.banded, ...), custom_call_target="tpu_custom_call", output_to_operand_aliasing={{0}: (8, {})} | custom-call | flops 1207959552 | bytes 8388608 | tf_op jit(solution)/shard_map/middle/pallas_call | solution.py:322
  41.2 0.1 collective-permute-done.7.evens_in
  41.3 0.8 %rims.8 = (f32[2048,512]{1,0:T(8,128)S(1)}, f32[8,256]{1,0:T(8,128)S(1)}, bf16[640,256]{1,0:T(8,128)(2,1)S(1)}, bf16[640,256]{1,0:T(8,128)(2,1)S(1)}) custom-call(s32[1]{0:T(128)} %bitcast.odd, f32[8,256]{1,0:T(8,128)S(1)} %get-tuple-element.72._.partial, bf16[8,256,1536]{2,1,0:T(8,128)(2,1)S(1)} %get-tuple-element.52.banded, ...), custom_call_target="tpu_custom_call", output_to_operand_aliasing={{0}: (6, {})} | custom-call | flops 241591904 | bytes 2097152 | tf_op jit(solution)/shard_map/rims/pallas_call | solution.py:353
  42.1 0.1 collective-permute-start.10
  42.2 4.5 %collective-permute-start.11 = (bf16[640,256]{1,0:T(8,128)(2,1)S(1)}, bf16[640,256]{1,0:T(8,128)(2,1)S(1)}, u32[]{:S(2)}, u32[]{:S(2)}) collective-permute-start(bf16[640,256]{1,0:T(8,128)(2,1)S(1)} %get-tuple-element.82.refs_2_), channel_id=1, source_target_pairs={{4,8},{8,4},{12,16},{16,12},{20,24},{24,20},{28,32},{32,28},{36,40... | collective-permute-start | bytes 983048 | tf_op jit(solution)/shard_map/ppermute | solution.py:311
  46.7 1.7 %middle.10 = (f32[2048,512]{1,0:T(8,128)S(1)}, f32[8,256]{1,0:T(8,128)S(1)}) custom-call(s32[1]{0:T(128)} %bitcast.odd, f32[8,256]{1,0:T(8,128)S(1)} %get-tuple-element.74._.refs_3_, bf16[8,256,1536]{2,1,0:T(8,128)(2,1)S(1)} %get-tuple-element.52.banded, f32[2048,512]{1,0:T(8,128)S(1)} %weights.1._, bf16[640,256]{1,0:T(8,128)(2,1)S(1)} %get-tuple-element.75.refs_0_, ...), custom_call_target="tpu_custom_call" | custom-call | flops 1207959552 | bytes 8388608 | tf_op jit(solution)/shard_map/middle/pallas_call | solution.py:322
  48.4 1.7 %middle.11 = (f32[2048,512]{1,0:T(8,128)S(1)}, f32[8,256]{1,0:T(8,128)S(1)}) custom-call(s32[1]{0:T(128)} %bitcast.odd, f32[8,256]{1,0:T(8,128)S(1)} %get-tuple-element.79._.partial, bf16[8,256,1536]{2,1,0:T(8,128)(2,1)S(1)} %get-tuple-element.52.banded, f32[2048,512]{1,0:T(8,128)S(1)} %weights.1._, ...), custom_call_target="tpu_custom_call", output_to_operand_aliasing={{0}: (8, {})} | custom-call | flops 1207959552 | bytes 8388608 | tf_op jit(solution)/shard_map/middle/pallas_call | solution.py:322
  50.1 2.5 %store.1 = (f32[2048,512]{1,0:T(8,128)}, f32[2048,512]{1,0:T(8,128)}) custom-call(f32[8,256]{1,0:T(8,128)S(1)} %get-tuple-element.84._.partial, f32[2048,512]{1,0:T(8,128)S(1)} %get-tuple-element.85.previous, f32[2048,512]{1,0:T(8,128)S(1)} %get-tuple-element.86.current.begun), custom_call_target="tpu_custom_call" | custom-call | bytes 16777216 | tf_op jit(solution)/shard_map/store/pallas_call | solution.py:438
  52.7 0.6 rims.9
  53.2 1.3 %even_rims.1 = (f32[2048,512]{1,0:T(8,128)}, f32[8,256]{1,0:T(8,128)S(1)}) custom-call(s32[1]{0:T(128)} %bitcast.odd, f32[8,256]{1,0:T(8,128)S(1)} %get-tuple-element.88._.refs_4_, bf16[8,256,1536]{2,1,0:T(8,128)(2,1)S(1)} %get-tuple-element.52.banded, f32[2048,512]{1,0:T(8,128)S(1)} %weights.1._, ...), custom_call_target="tpu_custom_call", output_to_operand_aliasing={{0}: (8, {})} | custom-call | flops 120795952 | bytes 1048576 | tf_op jit(solution)/shard_map/even_rims/pallas_call | solution.py:450
  54.6 0.4 odd_rims.1
  55.0 13.6 %all_to_all.5.parts = f32[32,1,1536]{2,1,0:T(1,128)S(1)} all-to-all(f32[32,1,1536]{2,1,0:T(1,128)S(1)} %get-tuple-element.92), channel_id=1, replica_groups=mesh['slab'=32,'col'=4] {'slab'}, dimensions={0} | all-to-all | bytes 393216 | tf_op jit(solution)/shard_map/all_to_all | solution.py:476
  68.6 0.9 %sums.1 = (f32[3,512]{1,0:T(4,128)}, f32[2048,512]{1,0:T(8,128)}) custom-call(s32[1]{0:T(128)} %bitcast.odd, f32[32,1,1536]{2,1,0:T(1,128)S(1)} %all_to_all.5.parts, f32[640,256]{1,0:T(8,128)S(1)} %get-tuple-element.93.rims, f32[2048,512]{1,0:T(8,128)} %get-tuple-element.94._), custom_call_target="tpu_custom_call", output_to_operand_aliasing={{1}: (3, {})} | custom-call | tf_op jit(solution)/shard_map/sums/pallas_call | solution.py:478
  (23 shorter events, 0.1 us)
Async XLA Ops:
  0.6 8.2 %copy-start.4 = (s32[16,9]{1,0:T(8,128)S(1)}, s32[16,9]{1,0:T(8,128)}, u32[]{:S(2)}) copy-start(s32[16,9]{1,0:T(8,128)} %param.7) | copy-start | bytes 1732
  2.1 14.9 %collective-permute-start = (bf16[640,256]{1,0:T(8,128)(2,1)S(1)}, bf16[640,256]{1,0:T(8,128)(2,1)S(1)}, u32[]{:S(2)}, u32[]{:S(2)}) collective-permute-start(bf16[640,256]{1,0:T(8,128)(2,1)S(1)} %get-tuple-element.50._), channel_id=1, source_target_pairs={{4,8},{8,4},{12,16},{16,12},{20,24},{24,20},{28,32},{32,28},{36,40... | collective-permute-start | bytes 983048 | tf_op jit(solution)/shard_map/ppermute | solution.py:311
  8.8 10.6 %collective-permute-start.1 = (bf16[640,256]{1,0:T(8,128)(2,1)S(1)}, bf16[640,256]{1,0:T(8,128)(2,1)S(1)}, u32[]{:S(2)}, u32[]{:S(2)}) collective-permute-start(bf16[640,256]{1,0:T(8,128)(2,1)S(1)} %get-tuple-element.54), channel_id=1, source_target_pairs={{0,4},{4,0},{8,12},{12,8},{16,20},{20,16},{24,28},{28,24},{32,36},... | collective-permute-start | bytes 983048 | tf_op jit(solution)/shard_map/ppermute | solution.py:311
  8.9 6.1 %copy-start.2 = (bf16[2048,512]{1,0:T(8,128)(2,1)S(1)}, bf16[2048,512]{1,0:T(8,128)(2,1)}, u32[]{:S(2)}) copy-start(bf16[2048,512]{1,0:T(8,128)(2,1)} %probe.1) | copy-start | bytes 6291460
  8.9 6.1 %copy-start.3 = (f32[2048]{0:T(1024)S(1)}, f32[2048]{0:T(1024)}, u32[]{:S(2)}) copy-start(f32[2048]{0:T(1024)} %param.11) | copy-start | bytes 24580
  8.9 6.5 %copy-start.1 = (f32[2048,512]{1,0:T(8,128)S(1)}, f32[2048,512]{1,0:T(8,128)}, u32[]{:S(2)}) copy-start(f32[2048,512]{1,0:T(8,128)} %refs_1_.3) | copy-start | bytes 12582916
  12.8 2.6 %copy-start = (f32[2048,512]{1,0:T(8,128)S(1)}, f32[2048,512]{1,0:T(8,128)}, u32[]{:S(2)}) copy-start(f32[2048,512]{1,0:T(8,128)} %refs_3_.3) | copy-start | bytes 12582916
  12.9 14.9 %collective-permute-start.2 = (bf16[640,256]{1,0:T(8,128)(2,1)S(1)}, bf16[640,256]{1,0:T(8,128)(2,1)S(1)}, u32[]{:S(2)}, u32[]{:S(2)}) collective-permute-start(bf16[640,256]{1,0:T(8,128)(2,1)S(1)} %get-tuple-element.51._), channel_id=1, source_target_pairs={{4,8},{8,4},{12,16},{16,12},{20,24},{24,20},{28,32},{32,28},{36,40... | collective-permute-start | bytes 983048 | tf_op jit(solution)/shard_map/ppermute | solution.py:311
  14.3 13.5 %collective-permute-start.3 = (bf16[640,256]{1,0:T(8,128)(2,1)S(1)}, bf16[640,256]{1,0:T(8,128)(2,1)S(1)}, u32[]{:S(2)}, u32[]{:S(2)}) collective-permute-start(bf16[640,256]{1,0:T(8,128)(2,1)S(1)} %get-tuple-element.59), channel_id=1, source_target_pairs={{0,4},{4,0},{8,12},{12,8},{16,20},{20,16},{24,28},{28,24},{32,36},... | collective-permute-start | bytes 983048 | tf_op jit(solution)/shard_map/ppermute | solution.py:311
  20.2 13.7 %collective-permute-start.4 = (bf16[640,256]{1,0:T(8,128)(2,1)S(1)}, bf16[640,256]{1,0:T(8,128)(2,1)S(1)}, u32[]{:S(2)}, u32[]{:S(2)}) collective-permute-start(bf16[640,256]{1,0:T(8,128)(2,1)S(1)} %get-tuple-element.64.refs_2_), channel_id=1, source_target_pairs={{4,8},{8,4},{12,16},{16,12},{20,24},{24,20},{28,32},{32,28},{36,40... | collective-permute-start | bytes 983048 | tf_op jit(solution)/shard_map/ppermute | solution.py:311
  24.5 9.5 %collective-permute-start.5 = (bf16[640,256]{1,0:T(8,128)(2,1)S(1)}, bf16[640,256]{1,0:T(8,128)(2,1)S(1)}, u32[]{:S(2)}, u32[]{:S(2)}) collective-permute-start(bf16[640,256]{1,0:T(8,128)(2,1)S(1)} %get-tuple-element.62.refs_0_), channel_id=1, source_target_pairs={{0,4},{4,0},{8,12},{12,8},{16,20},{20,16},{24,28},{28,24},{32,36},... | collective-permute-start | bytes 983048 | tf_op jit(solution)/shard_map/ppermute | solution.py:311
  28.6 12.6 %collective-permute-start.6 = (bf16[640,256]{1,0:T(8,128)(2,1)S(1)}, bf16[640,256]{1,0:T(8,128)(2,1)S(1)}, u32[]{:S(2)}, u32[]{:S(2)}) collective-permute-start(bf16[640,256]{1,0:T(8,128)(2,1)S(1)} %get-tuple-element.70.refs_2_), channel_id=1, source_target_pairs={{4,8},{8,4},{12,16},{16,12},{20,24},{24,20},{28,32},{32,28},{36,40... | collective-permute-start | bytes 983048 | tf_op jit(solution)/shard_map/ppermute | solution.py:311
  30.7 10.6 %collective-permute-start.7 = (bf16[640,256]{1,0:T(8,128)(2,1)S(1)}, bf16[640,256]{1,0:T(8,128)(2,1)S(1)}, u32[]{:S(2)}, u32[]{:S(2)}) collective-permute-start(bf16[640,256]{1,0:T(8,128)(2,1)S(1)} %get-tuple-element.68.refs_0_), channel_id=1, source_target_pairs={{0,4},{4,0},{8,12},{12,8},{16,20},{20,16},{24,28},{28,24},{32,36},... | collective-permute-start | bytes 983048 | tf_op jit(solution)/shard_map/ppermute | solution.py:311
  34.8 17.9 %collective-permute-start.8 = (bf16[640,256]{1,0:T(8,128)(2,1)S(1)}, bf16[640,256]{1,0:T(8,128)(2,1)S(1)}, u32[]{:S(2)}, u32[]{:S(2)}) collective-permute-start(bf16[640,256]{1,0:T(8,128)(2,1)S(1)} %get-tuple-element.75.refs_0_), channel_id=1, source_target_pairs={{0,4},{4,0},{8,12},{12,8},{16,20},{20,16},{24,28},{28,24},{32,36},... | collective-permute-start | bytes 983048 | tf_op jit(solution)/shard_map/ppermute | solution.py:311
  35.3 17.4 %collective-permute-start.9 = (bf16[640,256]{1,0:T(8,128)(2,1)S(1)}, bf16[640,256]{1,0:T(8,128)(2,1)S(1)}, u32[]{:S(2)}, u32[]{:S(2)}) collective-permute-start(bf16[640,256]{1,0:T(8,128)(2,1)S(1)} %get-tuple-element.77.refs_2_), channel_id=1, source_target_pairs={{4,8},{8,4},{12,16},{16,12},{20,24},{24,20},{28,32},{32,28},{36,40... | collective-permute-start | bytes 983048 | tf_op jit(solution)/shard_map/ppermute | solution.py:311
  42.1 11.1 %collective-permute-start.10 = (bf16[640,256]{1,0:T(8,128)(2,1)S(1)}, bf16[640,256]{1,0:T(8,128)(2,1)S(1)}, u32[]{:S(2)}, u32[]{:S(2)}) collective-permute-start(bf16[640,256]{1,0:T(8,128)(2,1)S(1)} %get-tuple-element.80.refs_0_), channel_id=1, source_target_pairs={{0,4},{4,0},{8,12},{12,8},{16,20},{20,16},{24,28},{28,24},{32,36},... | collective-permute-start | bytes 983048 | tf_op jit(solution)/shard_map/ppermute | solution.py:311
  42.2 12.4 %collective-permute-start.11 = (bf16[640,256]{1,0:T(8,128)(2,1)S(1)}, bf16[640,256]{1,0:T(8,128)(2,1)S(1)}, u32[]{:S(2)}, u32[]{:S(2)}) collective-permute-start(bf16[640,256]{1,0:T(8,128)(2,1)S(1)} %get-tuple-element.82.refs_2_), channel_id=1, source_target_pairs={{4,8},{8,4},{12,16},{16,12},{20,24},{24,20},{28,32},{32,28},{36,40... | collective-permute-start | bytes 983048 | tf_op jit(solution)/shard_map/ppermute | solution.py:311
